TPU v7x, 32 devices: a whole 2x2x4 slice. The times are simulated.
32 devices in a mesh: seq: 8 (over z, x), fsdp: 4 (over y, core).
Axes of the slice: x: 2, y: 2, z: 4, core: 2. Of those that a mesh axis runs over, the one named last changes fastest.
Arguments:
- tokens: bfloat16 [6144, 6144], P('seq'), may hold values from -30 to 30
- w_query: bfloat16 [6144, 32, 128], P('seq', 'fsdp'), may hold values from -0.078125 to 0.078125
- w_keyval: bfloat16 [6144, 32, 256], P('seq', 'fsdp'), may hold values from -40 to 40
- doc_lengths: int32 [8], replicated, may hold values from 1 to 3072, 6144 in all
- norm_gain: bfloat16 [4096], P('fsdp'), may hold values from 0.25 to 1.75
Outputs:
- attended: bfloat16 [6144, 4096], P('seq', 'fsdp')
Inputs may be any that keep to these rules, and one draw needn't show every extreme that they name: `doc_lengths`: lengths are positive and sum to 6144; the longest document has exactly 3072 tokens.
All inputs are finite; a program needn't handle non-finite values.
Results may differ from a plain program's by a relative error of at most 0.0034.
Values may be sent and summed in bfloat16 or wider, within the bound.
No kernel may reach another device: no remote copies, remote signals or barrier semaphores. Data moves between devices by JAX's collectives and lax.ppermute only.
A program may use at most 128 MiB of HBM per device.

v0:
```python
import jax
import jax.numpy as jnp
from jax import lax
from jax.sharding import PartitionSpec as P


def doc_index(positions, doc_ends):
    return jnp.sum((positions[:, None] >= doc_ends[None, :]).astype(jnp.int32), axis=1)


def shards(tokens, w_query, w_keyval, doc_lengths, norm_gain):
    rows_here = tokens.shape[0]
    head_count = w_query.shape[1]
    head_size = w_query.shape[2]
    shard_index = lax.axis_index("seq")
    doc_ends = jnp.cumsum(doc_lengths)
    offsets = lax.iota(jnp.int32, rows_here)
    doc_ids = doc_index(shard_index * rows_here + offsets, doc_ends)
    first_doc = doc_ids[0]
    tail_doc = doc_ids[rows_here - 1]

    def project(panel_rows):
        panel = panel_rows.reshape(panel_rows.shape[0], panel_rows.shape[1] * panel_rows.shape[2])
        return jnp.dot(tokens, panel, preferred_element_type=jnp.float32)

    query_sum = project(lax.all_gather(w_query, "seq", axis=0, tiled=True))
    keyval_sum = project(lax.all_gather(w_keyval, "seq", axis=0, tiled=True))
    keyval = (
        jax.nn.silu(keyval_sum).astype(jnp.bfloat16).reshape(rows_here, head_count, 2 * head_size)
    )
    key_rows = keyval[:, :, :head_size]
    values = keyval[:, :, head_size:]
    tail_mask = (doc_ids == tail_doc).astype(jnp.bfloat16)
    tail_state = jnp.einsum(
        "thd,the->hde",
        key_rows * tail_mask[:, None, None],
        values,
        preferred_element_type=jnp.float32,
    )
    states = lax.all_gather(tail_state[None], "seq", axis=0, tiled=True)
    shard_ids = lax.iota(jnp.int32, states.shape[0])
    owner_docs = doc_index(shard_ids * rows_here + rows_here - 1, doc_ends)
    selected = ((shard_ids < shard_index) & (owner_docs == first_doc)).astype(jnp.float32)
    incoming = jnp.sum(selected[:, None, None, None] * states, axis=0)
    queries = jax.nn.silu(query_sum).astype(jnp.bfloat16).reshape(rows_here, head_count, head_size)
    scores = jnp.einsum("thd,shd->hts", queries, key_rows, preferred_element_type=jnp.float32)
    causal = (
        (offsets[:, None] >= offsets[None, :]) & (doc_ids[:, None] == doc_ids[None, :])
    ).astype(jnp.float32)
    weights = (scores * causal[None]).astype(jnp.bfloat16)
    within = jnp.einsum("hts,she->the", weights, values, preferred_element_type=jnp.float32)
    carried = jnp.einsum(
        "thd,hde->the", queries, incoming.astype(jnp.bfloat16), preferred_element_type=jnp.float32
    )
    carried = carried * (doc_ids == first_doc).astype(jnp.float32)[:, None, None]
    mixed = within + carried
    sum_squares = lax.psum(jnp.sum(mixed * mixed, axis=(1, 2)), "fsdp")
    inverse_rms = lax.rsqrt(sum_squares / (head_count * lax.axis_size("fsdp") * head_size) + 1e-06)
    flat = mixed.reshape(rows_here, head_count * head_size)
    return (flat * inverse_rms[:, None] * norm_gain.astype(jnp.float32)[None, :]).astype(
        jnp.bfloat16
    )


def solution(mesh):
    return jax.shard_map(
        shards,
        mesh=mesh,
        in_specs=(P("seq", None), P("seq", "fsdp", None), P("seq", "fsdp", None), P(), P("fsdp")),
        out_specs=P("seq", "fsdp"),
        check_vma=False,
    )
```

profile of v0, /device:TPU:0, one launch (start us, length us, event | category | flops | bytes accessed | tf_op | source)
XLA Modules:
  0.0 765.9 jit_solution(5795354679008302158)
XLA Ops:
  6.5 0.0 copy-start.3
  6.5 0.0 all-gather.5.cloned.1.call-start
  6.5 0.7 all-gather.5.cloned.1.call-update
  7.3 0.0 all-gather.7.cloned.1.call-start
  7.3 0.7 all-gather.7.cloned.1.call-update
  8.0 0.0 all-gather.9.cloned.1.call-start
  8.1 0.0 copy-done.3
  8.1 0.2 reduce-window.8
  8.3 0.1 convert_reduce_fusion
  8.3 0.6 fusion.29
  8.9 1.3 compare_convert_fusion.1
  10.2 481.8 %all-gather.5.cloned.1.call-done = bf16[6144,8,256]{2,1,0:T(8,128)(2,1)} async-done(((bf16[768,8,256]{2,1,0:T(8,128)(2,1)}), bf16[6144,8,256]{2,1,0:T(8,128)(2,1)}) %all-gather.5.cloned.1.call-update) | async-done | bytes 25165840 | tf_op jit(solution)/shard_map/all_gather | solution.py:27
  492.1 16.3 %copy.31 = bf16[768,8,8,256]{3,1,2,0:T(8,128)(2,1)S(1)} copy(bf16[768,8,8,256]{3,2,1,0:T(8,128)(2,1)} %bitcast.39) | data formatting | bytes 50331648
  508.4 23.2 %multiply_convert_fusion.2 = bf16[768,2048]{1,0:T(8,128)(2,1)} fusion(bf16[768,6144]{1,0:T(8,128)(2,1)} %param.5, bf16[6144,2048]{1,0:T(8,128)(2,1)S(1)} %bitcast.40), kind=kOutput, calls=%fused_computation.7 | convolution fusion | flops 19335217152 | bytes 37748736 | tf_op jit(solution)/shard_map/dot_general | solution.py:24
  531.6 3.0 copy.32
  534.5 1.3 fusion.28
  535.9 1.1 copy.28
  537.0 0.0 copy-start.1
  537.0 0.0 copy-start.2
  537.0 3.6 fusion.15
  540.6 0.0 all-gather.9.cloned.1.call-update
  540.6 0.0 copy-done.2
  540.7 0.2 convert_reduce_fusion.1
  540.8 0.6 and_convert_fusion
  541.5 1.7 fusion.9
  543.2 0.0 copy-done.1
  543.2 127.5 %all-gather.7.cloned.1.call-done = bf16[6144,8,128]{2,1,0:T(8,128)(2,1)} async-done(((bf16[768,8,128]{2,1,0:T(8,128)(2,1)}), bf16[6144,8,128]{2,1,0:T(8,128)(2,1)}) %all-gather.7.cloned.1.call-update) | async-done | bytes 12582928 | tf_op jit(solution)/shard_map/all_gather | solution.py:26
  670.7 17.0 %fusion.17 = bf16[96,8,8,128]{3,2,1,0:T(8,128)(2,1)} fusion(bf16[768,6144]{1,0:T(8,128)(2,1)} %param.5, bf16[768,8,8,128]{3,2,1,0:T(8,128)(2,1)} %bitcast.47), kind=kOutput, calls=%fused_computation.21 | convolution fusion | flops 9667608576 | bytes 23592960 | tf_op jit(solution)/shard_map/dot_general | solution.py:24
  687.7 8.8 %fusion.3 = f32[8,128,768]{2,1,0:T(8,128)S(1)} fusion(bf16[768,8,128]{0,2,1:T(8,128)(2,1)} %copy-done.1, f32[768,768]{1,0:T(8,128)} %fusion.9, bf16[96,8,8,128]{3,2,1,0:T(8,128)(2,1)} %fusion.17, bf16[768,8,128]{2,1,0:T(8,128)(2,1)} %get-tuple-element.5), kind=kOutput, calls=%fused_computation.4 | convolution fusion | flops 2425356288 | bytes 10223616 | tf_op jit(solution)/shard_map/hts,she->the/dot_general | solution.py:51
  696.5 48.0 %all-gather.9.cloned.1.call-done = f32[64,128,128]{2,1,0:T(8,128)} async-done(((f32[8,128,128]{2,1,0:T(8,128)}), f32[64,128,128]{2,1,0:T(8,128)}) %all-gather.9.cloned.1.call-update) | async-done | bytes 4194320 | tf_op jit(solution)/shard_map/all_gather | solution.py:40
  744.4 0.0 copy-start
  744.4 2.8 multiply_reduce_fusion
  747.2 0.0 copy-done
  747.3 2.5 fusion.7
  749.8 2.4 copy.24
  752.2 5.7 psum.7
  757.8 1.5 multiply_convert_fusion.3
  (4 shorter events, 0.0 us)
Async XLA Ops:
  6.5 1.5 copy-start.3
  6.5 485.5 %all-gather.5.cloned.1.call-start = ((), (), s32[]{:S(2)}) async-start(), calls=%async_computation | async-start | bytes 28311552 | tf_op jit(solution)/shard_map/all_gather | solution.py:27
  7.3 663.4 %all-gather.7.cloned.1.call-start = ((), (), s32[]{:S(2)}) async-start(), calls=%async_computation.1 | async-start | bytes 14155776 | tf_op jit(solution)/shard_map/all_gather | solution.py:26
  8.0 736.4 %all-gather.9.cloned.1.call-start = ((), (), s32[]{:S(2)}) async-start(), calls=%async_computation.2 | async-start | bytes 4718592 | tf_op jit(solution)/shard_map/all_gather | solution.py:40
  537.0 6.2 copy-start.1
  537.0 3.6 copy-start.2
  744.4 2.8 copy-start
Sparse Core Ops, SparseCore 0:
  8.9 483.1 all-gather.4
  494.2 176.3 all-gather.6
  672.8 71.5 all-gather.8
where the time goes:
time: 766 us
  waiting for transfers between devices  659 us (86%)
  matrix products  55 us (7%)
  local copies, waits for them, and re-layouts  24.7 us (3%)
  between operations  13.2 us (2%)
  other arithmetic  8.39 us (1%)
    all_gather x1, waiting for transfers between devices, shards(): keyval_sum = project(lax.all_gather(w_keyval, 'seq', axis=0, tiled=True))  482 us
    all_gather x1, waiting for transfers between devices, shards(): query_sum = project(lax.all_gather(w_query, 'seq', axis=0, tiled=True))  127 us
    all_gather x1, waiting for transfers between devices, shards(): states = lax.all_gather(tail_state[None], 'seq', axis=0, tiled=True)  48 us
    dot_general x2, matrix products, project(): return jnp.dot(tokens, panel, preferred_element_type=jnp.float32)  40.2 us
    unnamed x11, local copies, waits for them, and re-layouts  20.4 us
  transfers between devices with their start and end apart: 3, of which 3 were waited for; matrix products, arithmetic and copies ran while one was open for 10% of the time, Pallas kernels for 0%

commit v1 on v0

--- a/solution.py
+++ b/solution.py
@@ -1,14 +1,376 @@
+import functools
+
 import jax
 import jax.numpy as jnp
 from jax import lax
+from jax.experimental import pallas as pl
+from jax.experimental.pallas import tpu as pltpu
 from jax.sharding import PartitionSpec as P
+
+MEMBERS = 4
+VMEM = 60 * 1024 * 1024
 
 
 def doc_index(positions, doc_ends):
     return jnp.sum((positions[:, None] >= doc_ends[None, :]).astype(jnp.int32), axis=1)
 
 
-def shards(tokens, w_query, w_keyval, doc_lengths, norm_gain):
+def silu(v):
+    return v / (1.0 + jnp.exp(-v))
+
+
+def params():
+    return pltpu.CompilerParams(vmem_limit_bytes=VMEM)
+
+
+def project_body(parts, steps, has_acc, has_buffer, activate, where_ref, k_ref, *refs):
+    t_refs, refs = refs[:parts], refs[parts:]
+    w_ref, refs = refs[0], refs[1:]
+    if has_acc:
+        start_ref, refs = refs[0], refs[1:]
+    if has_buffer:
+        refs = refs[1:]
+    out_ref, total = refs
+    step = pl.program_id(0)
+    lhs = jnp.concatenate([r[...] for r in t_refs], axis=0) if parts > 1 else t_refs[0][...]
+    product = jnp.dot(lhs, w_ref[...], preferred_element_type=jnp.float32)
+
+    @pl.when(step == 0)
+    def _():
+        total[...] = product + start_ref[...] if has_acc else product
+
+    @pl.when(step > 0)
+    def _():
+        total[...] += product
+
+    @pl.when(step == steps - 1)
+    def _():
+        if not activate:
+            out_ref[...] = total[...]
+        else:
+            rows = t_refs[0].shape[0]
+            for e in range(parts):
+                at = pl.multiple_of((where_ref[1] ^ e) * rows, 16) if parts > 1 else 0
+                value = silu(total[pl.ds(e * rows, rows), :]).astype(out_ref.dtype)
+                out_ref[0, pl.ds(at, rows), :] = value
+
+
+def project(where, k_blocks, parts, w, depth, acc=None, buffer=None, place=0, activate=True):
+    steps = k_blocks.shape[0]
+    rows = sum(p.shape[0] for p in parts)
+    width = w.shape[1]
+    in_specs = [pl.BlockSpec((p.shape[0], depth), lambda k, wh, kb: (0, kb[k])) for p in parts]
+    in_specs.append(pl.BlockSpec((depth, width), lambda k, wh, kb: (k, 0)))
+    operands = list(parts) + [w]
+    if acc is not None:
+        in_specs.append(pl.BlockSpec((rows, width), lambda k, wh, kb: (0, 0)))
+        operands.append(acc)
+    aliases = {}
+    if buffer is not None:
+        aliases = {2 + len(operands): 0}
+        in_specs.append(pl.BlockSpec(memory_space=pl.ANY))
+        operands.append(buffer)
+    if activate:
+        out_shape = jax.ShapeDtypeStruct((MEMBERS, rows, width), jnp.bfloat16)
+        out_spec = pl.BlockSpec((1, rows, width), lambda k, wh, kb: (wh[0] ^ place, 0, 0))
+    else:
+        out_shape = jax.ShapeDtypeStruct((rows, width), jnp.float32)
+        out_spec = pl.BlockSpec((rows, width), lambda k, wh, kb: (0, 0))
+    return pl.pallas_call(
+        functools.partial(
+            project_body, len(parts), steps, acc is not None, buffer is not None, activate
+        ),
+        grid_spec=pltpu.PrefetchScalarGridSpec(
+            num_scalar_prefetch=2,
+            grid=(steps,),
+            in_specs=in_specs,
+            out_specs=out_spec,
+            scratch_shapes=[pltpu.VMEM((rows, width), jnp.float32)],
+        ),
+        out_shape=out_shape,
+        input_output_aliases=aliases,
+        compiler_params=params(),
+        cost_estimate=pl.CostEstimate(
+            flops=2 * rows * depth * steps * width,
+            bytes_accessed=2 * depth * steps * (rows + width),
+            transcendentals=0,
+        ),
+    )(where, k_blocks, *operands)
+
+
+def doc_of(positions, ends_ref):
+    total = jnp.zeros(positions.shape, jnp.int32)
+    for i in range(ends_ref.shape[0]):
+        total += (positions >= ends_ref[i]).astype(jnp.int32)
+    return total
+
+
+def doc_of_scalar(position, ends_ref):
+    total = jnp.int32(0)
+    for i in range(ends_ref.shape[0]):
+        total += (position >= ends_ref[i]).astype(jnp.int32)
+    return total
+
+
+def tails_body(where_ref, ends_ref, kv_ref, tails_ref, state_ref):
+    rows = kv_ref.shape[1]
+    size = kv_ref.shape[2] // 2
+    block = pl.program_id(1)
+    start = (where_ref[2] * MEMBERS + block) * rows
+    last = doc_of_scalar(start + rows - 1, ends_ref)
+    before = doc_of_scalar(start - 1, ends_ref)
+    docs = doc_of(start + lax.broadcasted_iota(jnp.int32, (rows, size), 0), ends_ref)
+    keys = jnp.where(docs == last, kv_ref[0, :, :size].astype(jnp.float32), 0.0).astype(jnp.bfloat16)
+    tail = lax.dot_general(
+        keys, kv_ref[0, :, size:], (((0,), (0,)), ((), ())), preferred_element_type=jnp.float32
+    )
+    tails_ref[0, 0] = tail
+
+    @pl.when(block == 0)
+    def _():
+        state_ref[0] = tail
+
+    @pl.when(block > 0)
+    def _():
+        state_ref[0] = tail + jnp.where(before == last, 1.0, 0.0) * state_ref[0]
+
+
+def tails(where, ends, kv, heads):
+    blocks, rows, width = kv.shape
+    size = width // heads // 2
+    return pl.pallas_call(
+        tails_body,
+        grid_spec=pltpu.PrefetchScalarGridSpec(
+            num_scalar_prefetch=2,
+            grid=(heads, blocks),
+            in_specs=[pl.BlockSpec((1, rows, 2 * size), lambda h, b, wh, en: (b, 0, h))],
+            out_specs=[
+                pl.BlockSpec((1, 1, size, size), lambda h, b, wh, en: (b, h, 0, 0)),
+                pl.BlockSpec((1, size, size), lambda h, b, wh, en: (h, 0, 0)),
+            ],
+        ),
+        out_shape=[
+            jax.ShapeDtypeStruct((blocks, heads, size, size), jnp.float32),
+            jax.ShapeDtypeStruct((heads, size, size), jnp.float32),
+        ],
+        compiler_params=params(),
+        cost_estimate=pl.CostEstimate(
+            flops=2 * blocks * rows * heads * size * size,
+            bytes_accessed=2 * blocks * rows * width,
+            transcendentals=0,
+        ),
+    )(where, ends, kv)
+
+
+def attend_body(cut, where_ref, ends_ref, q_ref, kv_ref, tail_ref, entry_ref, out_ref, state):
+    rows = kv_ref.shape[1]
+    size = kv_ref.shape[2] // 2
+    block = pl.program_id(1)
+    start = (where_ref[2] * MEMBERS + block) * rows
+    last = doc_of_scalar(start + rows - 1, ends_ref)
+    before = doc_of_scalar(start - 1, ends_ref)
+
+    @pl.when(block == 0)
+    def _():
+        state[...] = entry_ref[0]
+
+    incoming = state[...].astype(jnp.bfloat16)
+    row_docs = doc_of(start + lax.broadcasted_iota(jnp.int32, (1, rows), 1), ends_ref)
+    for begin in range(0, rows, cut):
+        seen = begin + cut
+        q = q_ref[0, begin:seen, :]
+        docs = doc_of(start + begin + lax.broadcasted_iota(jnp.int32, (cut, 1), 0), ends_ref)
+        at = begin + lax.broadcasted_iota(jnp.int32, (cut, seen), 0)
+        behind = lax.broadcasted_iota(jnp.int32, (cut, seen), 1)
+        mask = (at >= behind) & (docs == row_docs[:, :seen])
+        scores = lax.dot_general(
+            q, kv_ref[0, :seen, :size], (((1,), (1,)), ((), ())), preferred_element_type=jnp.float32
+        )
+        weights = jnp.where(mask, scores, 0.0).astype(jnp.bfloat16)
+        within = jnp.dot(weights, kv_ref[0, :seen, size:], preferred_element_type=jnp.float32)
+        carried = jnp.dot(q, incoming, preferred_element_type=jnp.float32)
+        out_ref[0, begin:seen, :] = within + jnp.where(docs == before, carried, 0.0)
+    state[...] = tail_ref[0, 0] + jnp.where(before == last, 1.0, 0.0) * state[...]
+
+
+def attend(where, ends, q, kv, tail, entry, heads):
+    blocks, rows, width = q.shape
+    size = width // heads
+    cut = rows // 3 if rows % 48 == 0 else rows
+    return pl.pallas_call(
+        functools.partial(attend_body, cut),
+        grid_spec=pltpu.PrefetchScalarGridSpec(
+            num_scalar_prefetch=2,
+            grid=(heads, blocks),
+            in_specs=[
+                pl.BlockSpec((1, rows, size), lambda h, b, wh, en: (b, 0, h)),
+                pl.BlockSpec((1, rows, 2 * size), lambda h, b, wh, en: (b, 0, h)),
+                pl.BlockSpec((1, 1, size, size), lambda h, b, wh, en: (b, h, 0, 0)),
+                pl.BlockSpec((1, size, size), lambda h, b, wh, en: (h, 0, 0)),
+            ],
+            out_specs=pl.BlockSpec((1, rows, size), lambda h, b, wh, en: (b, 0, h)),
+            scratch_shapes=[pltpu.VMEM((size, size), jnp.float32)],
+        ),
+        out_shape=jax.ShapeDtypeStruct((blocks, rows, width), jnp.float32),
+        compiler_params=params(),
+        cost_estimate=pl.CostEstimate(
+            flops=3 * blocks * rows * rows * heads * size,
+            bytes_accessed=12 * blocks * rows * width,
+            transcendentals=0,
+        ),
+    )(where, ends, q, kv, tail, entry)
+
+
+def place_body(where_ref, *refs):
+    out_ref = refs[-1]
+    for k in range(MEMBERS):
+
+        @pl.when(pl.program_id(0) == k)
+        def _():
+            out_ref[...] = refs[k][...]
+
+
+def place(where, parts):
+    rows, width = parts[0].shape
+    return pl.pallas_call(
+        place_body,
+        grid_spec=pltpu.PrefetchScalarGridSpec(
+            num_scalar_prefetch=1,
+            grid=(MEMBERS,),
+            in_specs=[pl.BlockSpec((rows, width), lambda k, wh: (0, 0)) for _ in parts],
+            out_specs=pl.BlockSpec((rows, width), lambda k, wh: (0, wh[0] ^ k)),
+        ),
+        out_shape=jax.ShapeDtypeStruct((rows, MEMBERS * width), parts[0].dtype),
+        compiler_params=params(),
+    )(where, *parts)
+
+
+def after(value, *others):
+    return lax.optimization_barrier((value, *others))[0]
+
+
+def grouped(seq_size, fsdp_size, tokens, w_query, w_keyval, doc_lengths, norm_gain):
+    rows, model = tokens.shape
+    depth, head_count, size = w_query.shape
+    heads = head_count // MEMBERS
+    groups = seq_size // MEMBERS
+    s = lax.axis_index("seq")
+    f = lax.axis_index("fsdp")
+    m = lax.rem(s, MEMBERS)
+    g = lax.div(s, MEMBERS)
+    where = jnp.stack([m, f, g]).astype(jnp.int32)
+    doc_ends = jnp.cumsum(doc_lengths)
+
+    def hop(value, k):
+        return lax.ppermute(value, "seq", [(i, i ^ k) for i in range(seq_size)])
+
+    def side(value, k):
+        return lax.ppermute(value, "fsdp", [(i, i ^ k) for i in range(fsdp_size)])
+
+    q_width, kv_width = heads * size, 2 * heads * size
+    wq = w_query.reshape(depth, head_count * size)
+    wkv = w_keyval.reshape(depth, head_count * 2 * size)
+
+    def columns(k):
+        at = m ^ k
+        return (
+            lax.dynamic_slice(wkv, (0, at * kv_width), (depth, kv_width)),
+            lax.dynamic_slice(wq, (0, at * q_width), (depth, q_width)),
+        )
+
+    kv_a, q_a = columns(0)
+    kv_b, q_b = columns(2)
+    kv_c, q_c = columns(1)
+    kv_d, q_d = columns(3)
+    piece_rows = rows // fsdp_size
+    own_piece = lax.dynamic_slice(tokens, (f * piece_rows, 0), (piece_rows, model))
+
+    kv = {0: kv_a}
+    q = {0: q_a}
+
+    first = 4
+    kv[4] = hop(kv_a, 4)
+    q[6] = hop(q_b, 6)
+    tz = hop(own_piece, 2)
+    tx = hop(own_piece, 1)
+
+    kv[1] = hop(after(kv_c, tx), 1)
+    kvx_b = hop(after(kv_d, tx), 1)
+    q[1] = hop(after(q_c, kv[1]), 1)
+    qx_b = hop(after(q_d, kvx_b), 1)
+    tzx = hop(after(tz, q[1], qx_b), 1)
+
+    kv[6] = hop(after(kv_b, q[6]), 6)
+    q[4] = hop(after(q_a, kv[4]), 4)
+    kv[5] = hop(after(kv[1], q[4]), 4)
+    kv[7] = hop(after(kvx_b, kv[6]), 6)
+    q[5] = hop(after(q[1], kv[5]), 4)
+    q[7] = hop(after(qx_b, kv[7]), 6)
+
+    kv[2] = hop(after(kv_b, tz), 2)
+    kv[3] = hop(after(kvx_b, kv[2]), 2)
+    q[2] = hop(after(q_b, kv[3]), 2)
+    q[3] = hop(after(qx_b, q[2]), 2)
+
+    def spread(piece, *waits):
+        pieces = [after(piece, *waits)] if waits else [piece]
+        bit = fsdp_size // 2
+        found = {0: pieces[0]}
+        while bit >= 1:
+            for e in sorted(found):
+                found[e | bit] = side(found[e], bit)
+            bit //= 2
+        return [found[e] for e in range(fsdp_size)]
+
+    px = spread(tx)
+    pz = spread(tz, px[2])
+    pzx = spread(tzx, pz[2])
+    parts = {0: [tokens], 1: px, 2: pz, 3: pzx}
+
+    total = sorted(kv)
+    w_kv = jnp.concatenate([kv[k] for k in total], axis=0)
+    k_all = jnp.stack([s ^ k for k in total]).astype(jnp.int32)
+    early = [k for k in total if k not in (5, 7)]
+    late = [5, 7]
+    w_q_early = jnp.concatenate([q[k] for k in early], axis=0)
+    w_q_late = jnp.concatenate([q[k] for k in late], axis=0)
+    k_early = jnp.stack([s ^ k for k in early]).astype(jnp.int32)
+    k_late = jnp.stack([s ^ k for k in late]).astype(jnp.int32)
+
+    keyval = None
+    for j in range(MEMBERS):
+        keyval = project(where, k_all, parts[j], w_kv, depth, buffer=keyval, place=j)
+    tail, state = tails(where, doc_ends, keyval, heads)
+    entry = jnp.zeros_like(state)
+    edge_doc = doc_index(g[None] * MEMBERS * rows - 1, doc_ends)[0]
+    for k in range(1, groups):
+        other = hop(state, MEMBERS * k)
+        owner = g ^ k
+        owner_doc = doc_index((owner[None] + 1) * MEMBERS * rows - 1, doc_ends)[0]
+        entry += jnp.where((owner < g) & (owner_doc == edge_doc), other, 0.0)
+
+    queries = None
+    for j in range(MEMBERS):
+        acc = project(where, k_early, parts[j], w_q_early, depth, activate=False)
+        queries = project(
+            where, k_late, parts[j], w_q_late, depth, acc=acc, buffer=queries, place=j
+        )
+    mixed = attend(where, doc_ends, queries, keyval, tail, entry, heads)
+
+    sums = lax.psum(jnp.sum(mixed * mixed, axis=2), "fsdp")
+    sums = sums + hop(sums, 1)
+    sums = sums + hop(sums, 2)
+    inverse = lax.rsqrt(sums / (head_count * fsdp_size * size) + 1e-06)
+    gain = lax.dynamic_slice(norm_gain, (m * q_width,), (q_width,)).astype(jnp.float32)
+    normed = (mixed * inverse[:, :, None] * gain[None, None, :]).astype(jnp.bfloat16)
+    outs = []
+    for k in range(MEMBERS):
+        part = lax.dynamic_index_in_dim(normed, m ^ k, 0, keepdims=False)
+        outs.append(hop(part, k) if k else part)
+    return place(where, outs)
+
+
+def plain(tokens, w_query, w_keyval, doc_lengths, norm_gain):
     rows_here = tokens.shape[0]
     head_count = w_query.shape[1]
     head_size = w_query.shape[2]
@@ -63,8 +425,13 @@
 
 
 def solution(mesh):
+    seq_size, fsdp_size = mesh.shape["seq"], mesh.shape["fsdp"]
+    if seq_size == 2 * MEMBERS:
+        body = functools.partial(grouped, seq_size, fsdp_size)
+    else:
+        body = plain
     return jax.shard_map(
-        shards,
+        body,
         mesh=mesh,
         in_specs=(P("seq", None), P("seq", "fsdp", None), P("seq", "fsdp", None), P(), P("fsdp")),
         out_specs=P("seq", "fsdp"),

time: 766 us -> 503 us (0.66)
  waiting for transfers between devices: 659 us -> 270 us
  Pallas kernels: 0 us -> 126 us
  matrix products: 55 us -> 0 us
  starting transfers between devices: 0.08 us -> 53.8 us
  between operations: 13.2 us -> 1.39 us
  local copies, waits for them, and re-layouts: 24.7 us -> 32.6 us
    all_gather x3 -> x0, waiting for transfers between devices: 657 us -> none  [the longest x1 482 us: shards(): keyval_sum = project(lax.all_gather(w_keyval, 'seq', axis=0, tiled=True))]
    ppermute x0 -> x34, waiting for transfers between devices: none -> 270 us  [the longest x25 270 us: hop(): return lax.ppermute(value, 'seq', [(i, i ^ k) for i in range(seq_size)])]
    pallas_call x0 -> x15, Pallas kernels: none -> 126 us  [the longest x12 103 us: project(): pl.pallas_call(functools.partial(project_body, len(parts), steps, acc is...]
    dot_general x5 -> x0, matrix products: 55 us -> none  [the longest x2 40.2 us: project(): return jnp.dot(tokens, panel, preferred_element_type=jnp.float32)]
    ppermute x0 -> x34, starting transfers between devices: none -> 53.8 us  [the longest x25 50 us: hop(): return lax.ppermute(value, 'seq', [(i, i ^ k) for i in range(seq_size)])]
    unnamed x11 -> x59, local copies, waits for them, and re-layouts: 20.4 us -> 25 us
  transfers between devices with their start and end apart: 3 -> 34, of which waited for: 3 -> 19; matrix products, arithmetic and copies ran while one was open for 10% -> 5% of each run, Pallas kernels for 0% -> 18%
where the time goes in v1:
time: 503 us; the launch traced here: 501 us
  waiting for transfers between devices  270 us (54%)
  Pallas kernels  126 us (25%)
  starting transfers between devices  53.8 us (11%)
  local copies, waits for them, and re-layouts  32.6 us (6%)
  blocking collectives  11.2 us (2%)
  other arithmetic  6.48 us (1%)
    ppermute x25, waiting for transfers between devices, hop(): return lax.ppermute(value, 'seq', [(i, i ^ k) for i in range(seq_size)])  270 us
    pallas_call x12, Pallas kernels, project(): pl.pallas_call(functools.partial(project_body, len(parts), steps, acc is...  103 us
    ppermute x25, starting transfers between devices, hop(): return lax.ppermute(value, 'seq', [(i, i ^ k) for i in range(seq_size)])  50 us
    unnamed x59, local copies, waits for them, and re-layouts  25 us
    psum x1, blocking collectives, grouped(): sums = lax.psum(jnp.sum(mixed * mixed, axis=2), 'fsdp')  11.2 us
    pallas_call x1, Pallas kernels, attend(): pl.pallas_call(functools.partial(attend_body, cut), grid_spec=pltpu.Prefe...  10.6 us
  transfers between devices with their start and end apart: 34, of which 19 were waited for; matrix products, arithmetic and copies ran while one was open for 5% of the time, Pallas kernels for 18%

profile of v1, /device:TPU:0, one launch (start us, length us, event | category | flops | bytes accessed | tf_op | source)
XLA Modules:
  0.0 501.4 jit_solution(16139363575607595663)
XLA Ops:
  0.0 3.4 constant_dynamic-slice_fusion.8
  3.4 2.9 collective-permute-start.1
  6.3 1.6 collective-permute-start
  7.9 50.0 %collective-permute-done.1.refs_0_ = bf16[192,6144]{1,0:T(8,128)(2,1)} collective-permute-done((bf16[192,6144]{1,0:T(8,128)(2,1)}, bf16[192,6144]{1,0:T(8,128)(2,1)}, u32[]{:S(2)}, u32[]{:S(2)}) %collective-permute-start.1) | collective-permute-done | bytes 2359328 | tf_op jit(solution)/shard_map/ppermute | solution.py:265
  57.9 1.8 collective-permute-start.7
  59.6 3.0 copy.13
  62.6 2.1 constant_dynamic-update-slice_fusion.15
  64.7 1.5 collective-permute-start.2
  66.7 3.0 copy.15
  69.7 1.5 constant_dynamic-update-slice_fusion.7
  71.2 14.1 %collective-permute-done.2 = bf16[768,512]{1,0:T(8,128)(2,1)S(1)} collective-permute-done((bf16[768,512]{1,0:T(8,128)(2,1)}, bf16[768,512]{1,0:T(8,128)(2,1)S(1)}, u32[]{:S(2)}, u32[]{:S(2)}) %collective-permute-start.2) | collective-permute-done | bytes 786464 | tf_op jit(solution)/shard_map/ppermute | solution.py:265
  85.4 1.5 collective-permute-start.3
  86.9 15.5 %collective-permute-done.4 = bf16[768,512]{1,0:T(8,128)(2,1)} collective-permute-done((bf16[768,512]{1,0:T(8,128)(2,1)}, bf16[768,512]{1,0:T(8,128)(2,1)}, u32[]{:S(2)}, u32[]{:S(2)}) %collective-permute-start.4) | collective-permute-done | bytes 786464 | tf_op jit(solution)/shard_map/ppermute | solution.py:265
  102.3 1.5 collective-permute-start.5
  103.8 6.8 %collective-permute-done.3 = bf16[768,256]{1,0:T(8,128)(2,1)S(1)} collective-permute-done((bf16[768,256]{1,0:T(8,128)(2,1)S(1)}, bf16[768,256]{1,0:T(8,128)(2,1)S(1)}, u32[]{:S(2)}, u32[]{:S(2)}) %collective-permute-start.3) | collective-permute-done | bytes 393248 | tf_op jit(solution)/shard_map/ppermute | solution.py:265
  110.7 6.1 %collective-permute-done.5 = bf16[768,256]{1,0:T(8,128)(2,1)S(1)} collective-permute-done((bf16[768,256]{1,0:T(8,128)(2,1)S(1)}, bf16[768,256]{1,0:T(8,128)(2,1)S(1)}, u32[]{:S(2)}, u32[]{:S(2)}) %collective-permute-start.5) | collective-permute-done | bytes 393248 | tf_op jit(solution)/shard_map/ppermute | solution.py:265
  116.7 1.5 collective-permute-start.6
  118.8 3.6 collective-permute-start.16
  123.1 9.5 %collective-permute-done.16 = bf16[768,256]{1,0:T(8,128)(2,1)S(1)} collective-permute-done((bf16[768,256]{1,0:T(8,128)(2,1)S(1)}, bf16[768,256]{1,0:T(8,128)(2,1)S(1)}, u32[]{:S(2)}, u32[]{:S(2)}) %collective-permute-start.16) | collective-permute-done | bytes 393248 | tf_op jit(solution)/shard_map/ppermute | solution.py:265
  133.4 34.5 %collective-permute-done.6.refs_0_ = bf16[192,6144]{1,0:T(8,128)(2,1)} collective-permute-done((bf16[192,6144]{1,0:T(8,128)(2,1)}, bf16[192,6144]{1,0:T(8,128)(2,1)}, u32[]{:S(2)}, u32[]{:S(2)}) %collective-permute-start.6) | collective-permute-done | bytes 2359328 | tf_op jit(solution)/shard_map/ppermute | solution.py:265
  168.0 3.6 collective-permute-start.17
  172.1 13.5 %collective-permute-done.12 = bf16[768,512]{1,0:T(8,128)(2,1)S(1)} collective-permute-done((bf16[768,512]{1,0:T(8,128)(2,1)}, bf16[768,512]{1,0:T(8,128)(2,1)S(1)}, u32[]{:S(2)}, u32[]{:S(2)}) %collective-permute-start.12) | collective-permute-done | bytes 786464 | tf_op jit(solution)/shard_map/ppermute | solution.py:265
  185.6 4.9 collective-permute-done.17
  190.5 3.6 collective-permute-start.18
  194.1 44.5 %collective-permute-done.13 = bf16[768,256]{1,0:T(8,128)(2,1)S(1)} collective-permute-done((bf16[768,256]{1,0:T(8,128)(2,1)S(1)}, bf16[768,256]{1,0:T(8,128)(2,1)S(1)}, u32[]{:S(2)}, u32[]{:S(2)}) %collective-permute-start.13) | collective-permute-done | bytes 393248 | tf_op jit(solution)/shard_map/ppermute | solution.py:265
  239.6 3.5 collective-permute-start.22
  248.3 39.9 %collective-permute-done.14 = bf16[768,512]{1,0:T(8,128)(2,1)} collective-permute-done((bf16[768,512]{1,0:T(8,128)(2,1)S(1)}, bf16[768,512]{1,0:T(8,128)(2,1)}, u32[]{:S(2)}, u32[]{:S(2)}) %collective-permute-start.14) | collective-permute-done | bytes 786464 | tf_op jit(solution)/shard_map/ppermute | solution.py:265
  288.3 2.5 collective-permute-start.19
  290.7 2.1 constant_dynamic-update-slice_fusion.13
  292.9 2.2 constant_dynamic-update-slice_fusion.12
  295.0 0.9 constant_dynamic-update-slice_fusion.11
  296.0 6.4 %collective-permute-done.19 = bf16[768,256]{1,0:T(8,128)(2,1)S(1)} collective-permute-done((bf16[768,256]{1,0:T(8,128)(2,1)}, bf16[768,256]{1,0:T(8,128)(2,1)S(1)}, u32[]{:S(2)}, u32[]{:S(2)}) %collective-permute-start.19) | collective-permute-done | bytes 393248 | tf_op jit(solution)/shard_map/ppermute | solution.py:265
  302.4 14.5 %collective-permute-start.23 = (bf16[768,256]{1,0:T(8,128)(2,1)S(1)}, bf16[768,256]{1,0:T(8,128)(2,1)S(1)}, u32[]{:S(2)}, u32[]{:S(2)}) collective-permute-start(bf16[768,256]{1,0:T(8,128)(2,1)S(1)} %copy-done.20), channel_id=1, source_target_pairs={{0,8},{4,12},{8,0},{12,4},{16,24},{20,28},{24,16},{28,20},{1,9},{5... | collective-permute-start | bytes 1179656 | tf_op jit(solution)/shard_map/ppermute | solution.py:265
  316.9 5.6 %collective-permute-done.15 = bf16[768,256]{1,0:T(8,128)(2,1)S(1)} collective-permute-done((bf16[768,256]{1,0:T(8,128)(2,1)}, bf16[768,256]{1,0:T(8,128)(2,1)S(1)}, u32[]{:S(2)}, u32[]{:S(2)}) %collective-permute-start.15) | collective-permute-done | bytes 393248 | tf_op jit(solution)/shard_map/ppermute | solution.py:265
  323.0 2.1 constant_dynamic-update-slice_fusion.10
  325.1 1.0 constant_dynamic-update-slice_fusion.9
  326.1 2.1 constant_dynamic-update-slice_fusion.8.refs_1_.refs_4_
  328.1 1.1 collective-permute-done.23
  329.7 13.1 %shard_map.63.refs_5_ = bf16[4,768,512]{2,1,0:T(8,128)(2,1)} custom-call(s32[3]{0:T(128)} %pad_add_fusion.where_ref, s32[8]{0:T(128)} %stack.67.k_ref, bf16[768,6144]{1,0:T(8,128)(2,1)} %refs_0_.5, bf16[6144,512]{1,0:T(8,128)(2,1)} %constant_dynamic-update-slice_fusion.8.refs_1_.refs_4_), custom_call_target="tpu_custom_call" | custom-call | flops 4831838208 | bytes 15728640 | tf_op jit(solution)/shard_map/pallas_call | solution.py:79
  342.8 1.1 constant_dynamic-update-slice_fusion.5
  344.0 1.3 constant_dynamic-update-slice_fusion.4
  345.4 1.4 copy-done
  346.8 8.2 %shard_map.58.refs_2_ = f32[768,256]{1,0:T(8,128)} custom-call(s32[3]{0:T(128)} %pad_add_fusion.where_ref, s32[6]{0:T(128)} %stack.66.k_ref, bf16[768,6144]{1,0:T(8,128)(2,1)} %refs_0_.5, bf16[4608,256]{1,0:T(8,128)(2,1)} %copy-done), custom_call_target="tpu_custom_call" | custom-call | flops 1811939328 | bytes 9437184 | tf_op jit(solution)/shard_map/pallas_call | solution.py:79
  355.0 4.4 shard_map.59.refs_6_
  359.4 8.3 %shard_map.57.refs_5_ = f32[768,256]{1,0:T(8,128)} custom-call(s32[3]{0:T(128)} %pad_add_fusion.where_ref, s32[6]{0:T(128)} %stack.66.k_ref, bf16[192,6144]{1,0:T(8,128)(2,1)} %collective-permute-done.1.refs_0_, bf16[192,6144]{1,0:T(8,128)(2,1)} %collective-permute-done.26.refs_1_, bf16[192,6144]{1,0:T(8,128)(2,1)} %collective-permute-done.7.refs_2_, ...), custom_call_target="tpu_custom_call" | custom-call | flops 1811939328 | bytes 9437184 | tf_op jit(solution)/shard_map/pallas_call | solution.py:79
  367.7 4.6 shard_map.60.refs_6_
  372.2 13.0 %shard_map.64.refs_5_ = bf16[4,768,512]{2,1,0:T(8,128)(2,1)} custom-call(s32[3]{0:T(128)} %pad_add_fusion.where_ref, s32[8]{0:T(128)} %stack.67.k_ref, bf16[192,6144]{1,0:T(8,128)(2,1)} %collective-permute-done.1.refs_0_, bf16[192,6144]{1,0:T(8,128)(2,1)} %collective-permute-done.26.refs_1_, ...), custom_call_target="tpu_custom_call", output_to_operand_aliasing={{}: (7, {})} | custom-call | flops 4831838208 | bytes 15728640 | tf_op jit(solution)/shard_map/pallas_call | solution.py:79
  385.3 8.2 %shard_map.56.refs_5_ = f32[768,256]{1,0:T(8,128)} custom-call(s32[3]{0:T(128)} %pad_add_fusion.where_ref, s32[6]{0:T(128)} %stack.66.k_ref, bf16[192,6144]{1,0:T(8,128)(2,1)} %collective-permute-done.refs_0_, bf16[192,6144]{1,0:T(8,128)(2,1)} %collective-permute-done.24.refs_1_, bf16[192,6144]{1,0:T(8,128)(2,1)} %collective-permute-done.8.refs_2_, ...), custom_call_target="tpu_custom_call" | custom-call | flops 1811939328 | bytes 9437184 | tf_op jit(solution)/shard_map/pallas_call | solution.py:79
  393.5 4.6 shard_map.61.refs_6_
  398.1 13.0 %shard_map.65.refs_5_ = bf16[4,768,512]{2,1,0:T(8,128)(2,1)} custom-call(s32[3]{0:T(128)} %pad_add_fusion.where_ref, s32[8]{0:T(128)} %stack.67.k_ref, bf16[192,6144]{1,0:T(8,128)(2,1)} %collective-permute-done.refs_0_, bf16[192,6144]{1,0:T(8,128)(2,1)} %collective-permute-done.24.refs_1_, ...), custom_call_target="tpu_custom_call", output_to_operand_aliasing={{}: (7, {})} | custom-call | flops 4831838208 | bytes 15728640 | tf_op jit(solution)/shard_map/pallas_call | solution.py:79
  411.1 13.0 %shard_map.66.kv_ref = bf16[4,768,512]{2,1,0:T(8,128)(2,1)} custom-call(s32[3]{0:T(128)} %pad_add_fusion.where_ref, s32[8]{0:T(128)} %stack.67.k_ref, bf16[192,6144]{1,0:T(8,128)(2,1)} %collective-permute-done.6.refs_0_, bf16[192,6144]{1,0:T(8,128)(2,1)} %collective-permute-done.9.refs_1_, ...), custom_call_target="tpu_custom_call", output_to_operand_aliasing={{}: (7, {})} | custom-call | flops 4831838208 | bytes 15728640 | tf_op jit(solution)/shard_map/pallas_call | solution.py:79
  424.1 8.5 %shard_map.67 = (f32[4,2,128,128]{3,2,1,0:T(8,128)}, f32[2,128,128]{2,1,0:T(8,128)}) custom-call(s32[3]{0:T(128)} %pad_add_fusion.where_ref, s32[8]{0:T(128)} %bitcast.32, bf16[4,768,512]{2,1,0:T(8,128)(2,1)} %shard_map.66.kv_ref), custom_call_target="tpu_custom_call" | custom-call | flops 201326592 | bytes 3145728 | tf_op jit(solution)/shard_map/pallas_call | solution.py:141
  433.2 8.2 %shard_map.55.refs_5_ = f32[768,256]{1,0:T(8,128)} custom-call(s32[3]{0:T(128)} %pad_add_fusion.where_ref, s32[6]{0:T(128)} %stack.66.k_ref, bf16[192,6144]{1,0:T(8,128)(2,1)} %collective-permute-done.6.refs_0_, bf16[192,6144]{1,0:T(8,128)(2,1)} %collective-permute-done.9.refs_1_, bf16[192,6144]{1,0:T(8,128)(2,1)} %collective-permute-done.10.refs_2_, ...), custom_call_target="tpu_custom_call" | custom-call | flops 1811939328 | bytes 9437184 | tf_op jit(solution)/shard_map/pallas_call | solution.py:79
  441.4 4.6 shard_map.62.q_ref
  446.7 10.6 %shard_map.68 = f32[4,768,256]{2,1,0:T(8,128)} custom-call(s32[3]{0:T(128)} %pad_add_fusion.where_ref, s32[8]{0:T(128)} %bitcast.33, bf16[4,768,256]{2,1,0:T(8,128)(2,1)} %shard_map.62.q_ref, bf16[4,768,512]{2,1,0:T(8,128)(2,1)} %shard_map.66.kv_ref, f32[4,2,128,128]{3,2,1,0:T(8,128)} %get-tuple-element.41.tail_ref, ...), custom_call_target="tpu_custom_call" | custom-call | flops 1811939328 | bytes 9437184 | tf_op jit(solution)/shard_map/pallas_call | solution.py:200
  457.3 2.5 multiply_reduce_fusion
  459.8 11.2 %psum.7 = f32[4,768]{1,0:T(4,128)S(1)} all-reduce(f32[4,768]{1,0:T(4,128)S(1)} %multiply_reduce_fusion), channel_id=1, replica_groups=mesh['seq'=8,'fsdp'=4] {'fsdp'}, use_global_device_ids=true, to_apply=%region_4.5 | all-reduce | flops 3072 | bytes 24576 | tf_op jit(solution)/shard_map/psum | solution.py:360
  471.4 3.3 collective-permute-done.29
  474.7 2.5 collective-permute-start.30
  480.2 1.9 collective-permute-start.33
  482.3 1.5 collective-permute-start.31
  483.7 9.0 %collective-permute-done.33.refs_3_ = bf16[768,256]{1,0:T(8,128)(2,1)S(1)} collective-permute-done((bf16[768,256]{1,0:T(8,128)(2,1)S(1)}, bf16[768,256]{1,0:T(8,128)(2,1)S(1)}, u32[]{:S(2)}, u32[]{:S(2)}) %collective-permute-start.33) | collective-permute-done | bytes 393248 | tf_op jit(solution)/shard_map/ppermute | solution.py:265
  492.8 4.0 collective-permute-done.32.refs_2_
  497.7 3.7 shard_map.69
  (96 shorter events, 15.2 us)
Async XLA Ops:
  3.4 54.5 %collective-permute-start.1 = (bf16[192,6144]{1,0:T(8,128)(2,1)}, bf16[192,6144]{1,0:T(8,128)(2,1)}, u32[]{:S(2)}, u32[]{:S(2)}) collective-permute-start(bf16[192,6144]{1,0:T(8,128)(2,1)} %constant_dynamic-slice_fusion.8), channel_id=1, source_target_pairs={{0,4},{4,0},{8,12},{12,8},{16,20},{20,16},{24,28},{28,24},{1,5},{5... | collective-permute-start | bytes 7077896 | tf_op jit(solution)/shard_map/ppermute | solution.py:265
  6.3 97.5 %collective-permute-start = (bf16[192,6144]{1,0:T(8,128)(2,1)}, bf16[192,6144]{1,0:T(8,128)(2,1)}, u32[]{:S(2)}, u32[]{:S(2)}) collective-permute-start(bf16[192,6144]{1,0:T(8,128)(2,1)} %constant_dynamic-slice_fusion.8), channel_id=1, source_target_pairs={{0,8},{4,12},{8,0},{12,4},{16,24},{20,28},{24,16},{28,20},{1,9},{5... | collective-permute-start | bytes 7077896 | tf_op jit(solution)/shard_map/ppermute | solution.py:265
  57.9 60.4 %collective-permute-start.7 = (bf16[192,6144]{1,0:T(8,128)(2,1)}, bf16[192,6144]{1,0:T(8,128)(2,1)}, u32[]{:S(2)}, u32[]{:S(2)}) collective-permute-start(bf16[192,6144]{1,0:T(8,128)(2,1)} %collective-permute-done.1.refs_0_), channel_id=1, source_target_pairs={{0,2},{1,3},{2,0},{3,1},{4,6},{5,7},{6,4},{7,5},{8,10},{9,11},{10,... | collective-permute-start | bytes 7077896 | tf_op jit(solution)/shard_map/ppermute | solution.py:268
  64.7 20.7 %collective-permute-start.2 = (bf16[768,512]{1,0:T(8,128)(2,1)}, bf16[768,512]{1,0:T(8,128)(2,1)S(1)}, u32[]{:S(2)}, u32[]{:S(2)}) collective-permute-start(bf16[768,512]{1,0:T(8,128)(2,1)} %get-tuple-element.24), channel_id=1, source_target_pairs={{0,4},{4,0},{8,12},{12,8},{16,20},{20,16},{24,28},{28,24},{1,5},{5... | collective-permute-start | bytes 2359304 | tf_op jit(solution)/shard_map/ppermute | solution.py:265
  66.2 36.2 %collective-permute-start.4 = (bf16[768,512]{1,0:T(8,128)(2,1)}, bf16[768,512]{1,0:T(8,128)(2,1)}, u32[]{:S(2)}, u32[]{:S(2)}) collective-permute-start(bf16[768,512]{1,0:T(8,128)(2,1)} %get-tuple-element.26), channel_id=1, source_target_pairs={{0,4},{4,0},{8,12},{12,8},{16,20},{20,16},{24,28},{28,24},{1,5},{5... | collective-permute-start | bytes 2359304 | tf_op jit(solution)/shard_map/ppermute | solution.py:265
  69.7 169.7 %copy-start.21 = (s32[8]{0:T(128)S(1)}, s32[8]{0:T(128)}, u32[]{:S(2)}) copy-start(s32[8]{0:T(128)} %param.8) | copy-start | bytes 100
  85.4 25.3 %collective-permute-start.3 = (bf16[768,256]{1,0:T(8,128)(2,1)S(1)}, bf16[768,256]{1,0:T(8,128)(2,1)S(1)}, u32[]{:S(2)}, u32[]{:S(2)}) collective-permute-start(bf16[768,256]{1,0:T(8,128)(2,1)S(1)} %get-tuple-element.25), channel_id=1, source_target_pairs={{0,4},{4,0},{8,12},{12,8},{16,20},{20,16},{24,28},{28,24},{1,5},{5... | collective-permute-start | bytes 1179656 | tf_op jit(solution)/shard_map/ppermute | solution.py:265
  102.3 14.4 %collective-permute-start.5 = (bf16[768,256]{1,0:T(8,128)(2,1)S(1)}, bf16[768,256]{1,0:T(8,128)(2,1)S(1)}, u32[]{:S(2)}, u32[]{:S(2)}) collective-permute-start(bf16[768,256]{1,0:T(8,128)(2,1)S(1)} %get-tuple-element.27), channel_id=1, source_target_pairs={{0,4},{4,0},{8,12},{12,8},{16,20},{20,16},{24,28},{28,24},{1,5},{5... | collective-permute-start | bytes 1179656 | tf_op jit(solution)/shard_map/ppermute | solution.py:265
  110.7 8.1 %copy-start.10 = (bf16[768,256]{1,0:T(8,128)(2,1)}, bf16[768,256]{1,0:T(8,128)(2,1)S(1)}, u32[]{:S(2)}) copy-start(bf16[768,256]{1,0:T(8,128)(2,1)S(1)} %collective-permute-done.3) | copy-start | bytes 1179652
  116.7 15.9 %copy-start.19 = (bf16[768,256]{1,0:T(8,128)(2,1)}, bf16[768,256]{1,0:T(8,128)(2,1)S(1)}, u32[]{:S(2)}) copy-start(bf16[768,256]{1,0:T(8,128)(2,1)S(1)} %collective-permute-done.5) | copy-start | bytes 1179652
  116.7 51.2 %collective-permute-start.6 = (bf16[192,6144]{1,0:T(8,128)(2,1)}, bf16[192,6144]{1,0:T(8,128)(2,1)}, u32[]{:S(2)}, u32[]{:S(2)}) collective-permute-start(bf16[192,6144]{1,0:T(8,128)(2,1)} %collective-permute-done.refs_0_), channel_id=1, source_target_pairs={{0,4},{4,0},{8,12},{12,8},{16,20},{20,16},{24,28},{28,24},{1,5},{5... | collective-permute-start | bytes 7077896 | tf_op jit(solution)/shard_map/ppermute | solution.py:265
  118.2 53.3 %collective-permute-start.8 = (bf16[192,6144]{1,0:T(8,128)(2,1)}, bf16[192,6144]{1,0:T(8,128)(2,1)}, u32[]{:S(2)}, u32[]{:S(2)}) collective-permute-start(bf16[192,6144]{1,0:T(8,128)(2,1)} %collective-permute-done.refs_0_), channel_id=1, source_target_pairs={{0,2},{1,3},{2,0},{3,1},{4,6},{5,7},{6,4},{7,5},{8,10},{9,11},{10,... | collective-permute-start | bytes 7077896 | tf_op jit(solution)/shard_map/ppermute | solution.py:268
  118.8 13.9 %collective-permute-start.16 = (bf16[768,256]{1,0:T(8,128)(2,1)S(1)}, bf16[768,256]{1,0:T(8,128)(2,1)S(1)}, u32[]{:S(2)}, u32[]{:S(2)}) collective-permute-start(bf16[768,256]{1,0:T(8,128)(2,1)S(1)} %get-tuple-element.39), channel_id=1, source_target_pairs={{0,24},{4,28},{8,16},{12,20},{16,8},{20,12},{24,0},{28,4},{1,25},{... | collective-permute-start | bytes 1179656 | tf_op jit(solution)/shard_map/ppermute | solution.py:265
  122.4 49.7 %collective-permute-start.20 = (bf16[768,512]{1,0:T(8,128)(2,1)}, bf16[768,512]{1,0:T(8,128)(2,1)S(1)}, u32[]{:S(2)}, u32[]{:S(2)}) collective-permute-start(bf16[768,512]{1,0:T(8,128)(2,1)} %get-tuple-element.37), channel_id=1, source_target_pairs={{0,8},{4,12},{8,0},{12,4},{16,24},{20,28},{24,16},{28,20},{1,9},{5... | collective-permute-start | bytes 2359304 | tf_op jit(solution)/shard_map/ppermute | solution.py:265
  122.4 63.3 %collective-permute-start.12 = (bf16[768,512]{1,0:T(8,128)(2,1)}, bf16[768,512]{1,0:T(8,128)(2,1)S(1)}, u32[]{:S(2)}, u32[]{:S(2)}) collective-permute-start(bf16[768,512]{1,0:T(8,128)(2,1)} %get-tuple-element.46), channel_id=1, source_target_pairs={{0,16},{4,20},{8,24},{12,28},{16,0},{20,4},{24,8},{28,12},{1,17},{... | collective-permute-start | bytes 2359304 | tf_op jit(solution)/shard_map/ppermute | solution.py:265
  132.7 0.8 copy-start.8
  132.7 189.8 %collective-permute-start.26 = (bf16[192,6144]{1,0:T(8,128)(2,1)}, bf16[192,6144]{1,0:T(8,128)(2,1)}, u32[]{:S(2)}, u32[]{:S(2)}) collective-permute-start(bf16[192,6144]{1,0:T(8,128)(2,1)} %collective-permute-done.1.refs_0_), channel_id=1, source_target_pairs={{0,1},{1,0},{2,3},{3,2},{4,5},{5,4},{6,7},{7,6},{8,9},{9,8},{10,11... | collective-permute-start | bytes 7077896 | tf_op jit(solution)/shard_map/ppermute | solution.py:268
  168.0 22.5 %collective-permute-start.17 = (bf16[768,512]{1,0:T(8,128)(2,1)}, bf16[768,512]{1,0:T(8,128)(2,1)S(1)}, u32[]{:S(2)}, u32[]{:S(2)}) collective-permute-start(bf16[768,512]{1,0:T(8,128)(2,1)} %get-tuple-element.37), channel_id=1, source_target_pairs={{0,24},{4,28},{8,16},{12,20},{16,8},{20,12},{24,0},{28,4},{1,25},{... | collective-permute-start | bytes 2359304 | tf_op jit(solution)/shard_map/ppermute | solution.py:265
  171.6 157.6 %collective-permute-start.10 = (bf16[192,6144]{1,0:T(8,128)(2,1)}, bf16[192,6144]{1,0:T(8,128)(2,1)}, u32[]{:S(2)}, u32[]{:S(2)}) collective-permute-start(bf16[192,6144]{1,0:T(8,128)(2,1)} %collective-permute-done.6.refs_0_), channel_id=1, source_target_pairs={{0,2},{1,3},{2,0},{3,1},{4,6},{5,7},{6,4},{7,5},{8,10},{9,11},{10,... | collective-permute-start | bytes 7077896 | tf_op jit(solution)/shard_map/ppermute | solution.py:268
  172.1 66.5 %copy-start.7 = (bf16[768,512]{1,0:T(8,128)(2,1)}, bf16[768,512]{1,0:T(8,128)(2,1)S(1)}, u32[]{:S(2)}) copy-start(bf16[768,512]{1,0:T(8,128)(2,1)S(1)} %collective-permute-done.20) | copy-start | bytes 2359300
  172.1 67.5 %collective-permute-start.21 = (bf16[768,512]{1,0:T(8,128)(2,1)}, bf16[768,512]{1,0:T(8,128)(2,1)}, u32[]{:S(2)}, u32[]{:S(2)}) collective-permute-start(bf16[768,512]{1,0:T(8,128)(2,1)} %collective-permute-done.4), channel_id=1, source_target_pairs={{0,8},{4,12},{8,0},{12,4},{16,24},{20,28},{24,16},{28,20},{1,9},{5... | collective-permute-start | bytes 2359304 | tf_op jit(solution)/shard_map/ppermute | solution.py:265
  185.6 53.0 %copy-start.5 = (bf16[768,512]{1,0:T(8,128)(2,1)}, bf16[768,512]{1,0:T(8,128)(2,1)S(1)}, u32[]{:S(2)}) copy-start(bf16[768,512]{1,0:T(8,128)(2,1)S(1)} %collective-permute-done.12) | copy-start | bytes 2359300
  185.6 53.0 %collective-permute-start.13 = (bf16[768,256]{1,0:T(8,128)(2,1)S(1)}, bf16[768,256]{1,0:T(8,128)(2,1)S(1)}, u32[]{:S(2)}, u32[]{:S(2)}) collective-permute-start(bf16[768,256]{1,0:T(8,128)(2,1)S(1)} %get-tuple-element.31), channel_id=1, source_target_pairs={{0,16},{4,20},{8,24},{12,28},{16,0},{20,4},{24,8},{28,12},{1,17},{... | collective-permute-start | bytes 1179656 | tf_op jit(solution)/shard_map/ppermute | solution.py:265
  190.5 3.6 copy-start.3
  190.5 56.9 %collective-permute-start.18 = (bf16[768,512]{1,0:T(8,128)(2,1)}, bf16[768,512]{1,0:T(8,128)(2,1)}, u32[]{:S(2)}, u32[]{:S(2)}) collective-permute-start(bf16[768,512]{1,0:T(8,128)(2,1)} %collective-permute-done.4), channel_id=1, source_target_pairs={{0,24},{4,28},{8,16},{12,20},{16,8},{20,12},{24,0},{28,4},{1,25},{... | collective-permute-start | bytes 2359304 | tf_op jit(solution)/shard_map/ppermute | solution.py:265
  238.6 0.8 copy-start.12
  239.4 48.9 %collective-permute-start.14 = (bf16[768,512]{1,0:T(8,128)(2,1)S(1)}, bf16[768,512]{1,0:T(8,128)(2,1)}, u32[]{:S(2)}, u32[]{:S(2)}) collective-permute-start(bf16[768,512]{1,0:T(8,128)(2,1)S(1)} %collective-permute-done.2), channel_id=1, source_target_pairs={{0,16},{4,20},{8,24},{12,28},{16,0},{20,4},{24,8},{28,12},{1,17},{... | collective-permute-start | bytes 2359304 | tf_op jit(solution)/shard_map/ppermute | solution.py:265
  239.6 55.5 %copy-start.18 = (s32[8,1]{0,1:T(1,128)}, s32[8,1]{0,1:T(1,128)S(1)}, u32[]{:S(2)}) copy-start(s32[8,1]{0,1:T(1,128)S(1)} %reduce-window.4) | copy-start | bytes 100
  239.6 51.2 %collective-permute-start.22 = (bf16[768,256]{1,0:T(8,128)(2,1)S(1)}, bf16[768,256]{1,0:T(8,128)(2,1)}, u32[]{:S(2)}, u32[]{:S(2)}) collective-permute-start(bf16[768,256]{1,0:T(8,128)(2,1)S(1)} %get-tuple-element.39), channel_id=1, source_target_pairs={{0,8},{4,12},{8,0},{12,4},{16,24},{20,28},{24,16},{28,20},{1,9},{5... | collective-permute-start | bytes 1179656 | tf_op jit(solution)/shard_map/ppermute | solution.py:265
  246.2 46.7 %copy-start.11 = (bf16[768,256]{1,0:T(8,128)(2,1)S(1)}, bf16[768,256]{1,0:T(8,128)(2,1)}, u32[]{:S(2)}) copy-start(bf16[768,256]{1,0:T(8,128)(2,1)} %copy-done.10) | copy-start | bytes 1179652
  247.4 112.0 %collective-permute-start.27 = (bf16[192,6144]{1,0:T(8,128)(2,1)}, bf16[192,6144]{1,0:T(8,128)(2,1)}, u32[]{:S(2)}, u32[]{:S(2)}) collective-permute-start(bf16[192,6144]{1,0:T(8,128)(2,1)} %collective-permute-done.7.refs_2_), channel_id=1, source_target_pairs={{0,1},{1,0},{2,3},{3,2},{4,5},{5,4},{6,7},{7,6},{8,9},{9,8},{10,11... | collective-permute-start | bytes 7077896 | tf_op jit(solution)/shard_map/ppermute | solution.py:268
  248.3 46.7 %copy-start.6 = (bf16[768,512]{1,0:T(8,128)(2,1)S(1)}, bf16[768,512]{1,0:T(8,128)(2,1)}, u32[]{:S(2)}) copy-start(bf16[768,512]{1,0:T(8,128)(2,1)} %copy-done.5) | copy-start | bytes 2359300
  288.3 14.1 %collective-permute-start.19 = (bf16[768,256]{1,0:T(8,128)(2,1)}, bf16[768,256]{1,0:T(8,128)(2,1)S(1)}, u32[]{:S(2)}, u32[]{:S(2)}) collective-permute-start(bf16[768,256]{1,0:T(8,128)(2,1)} %copy-done.19), channel_id=1, source_target_pairs={{0,24},{4,28},{8,16},{12,20},{16,8},{20,12},{24,0},{28,4},{1,25},{... | collective-permute-start | bytes 1179656 | tf_op jit(solution)/shard_map/ppermute | solution.py:265
  290.7 31.7 %collective-permute-start.15 = (bf16[768,256]{1,0:T(8,128)(2,1)}, bf16[768,256]{1,0:T(8,128)(2,1)S(1)}, u32[]{:S(2)}, u32[]{:S(2)}) collective-permute-start(bf16[768,256]{1,0:T(8,128)(2,1)} %copy-done.10), channel_id=1, source_target_pairs={{0,16},{4,20},{8,24},{12,28},{16,0},{20,4},{24,8},{28,12},{1,17},{... | collective-permute-start | bytes 1179656 | tf_op jit(solution)/shard_map/ppermute | solution.py:265
  292.8 9.6 %copy-start.20 = (bf16[768,256]{1,0:T(8,128)(2,1)S(1)}, bf16[768,256]{1,0:T(8,128)(2,1)}, u32[]{:S(2)}) copy-start(bf16[768,256]{1,0:T(8,128)(2,1)} %copy-done.19) | copy-start | bytes 1179652
  292.9 32.2 %copy-start.4 = (bf16[768,512]{1,0:T(8,128)(2,1)S(1)}, bf16[768,512]{1,0:T(8,128)(2,1)}, u32[]{:S(2)}) copy-start(bf16[768,512]{1,0:T(8,128)(2,1)} %copy-done.3) | copy-start | bytes 2359300
  302.4 26.8 %collective-permute-start.23 = (bf16[768,256]{1,0:T(8,128)(2,1)S(1)}, bf16[768,256]{1,0:T(8,128)(2,1)S(1)}, u32[]{:S(2)}, u32[]{:S(2)}) collective-permute-start(bf16[768,256]{1,0:T(8,128)(2,1)S(1)} %copy-done.20), channel_id=1, source_target_pairs={{0,8},{4,12},{8,0},{12,4},{16,24},{20,28},{24,16},{28,20},{1,9},{5... | collective-permute-start | bytes 1179656 | tf_op jit(solution)/shard_map/ppermute | solution.py:265
  322.5 62.8 %collective-permute-start.24 = (bf16[192,6144]{1,0:T(8,128)(2,1)}, bf16[192,6144]{1,0:T(8,128)(2,1)}, u32[]{:S(2)}, u32[]{:S(2)}) collective-permute-start(bf16[192,6144]{1,0:T(8,128)(2,1)} %collective-permute-done.refs_0_), channel_id=1, source_target_pairs={{0,1},{1,0},{2,3},{3,2},{4,5},{5,4},{6,7},{7,6},{8,9},{9,8},{10,11... | collective-permute-start | bytes 7077896 | tf_op jit(solution)/shard_map/ppermute | solution.py:268
  322.5 62.8 %collective-permute-start.25 = (bf16[192,6144]{1,0:T(8,128)(2,1)}, bf16[192,6144]{1,0:T(8,128)(2,1)}, u32[]{:S(2)}, u32[]{:S(2)}) collective-permute-start(bf16[192,6144]{1,0:T(8,128)(2,1)} %collective-permute-done.8.refs_2_), channel_id=1, source_target_pairs={{0,1},{1,0},{2,3},{3,2},{4,5},{5,4},{6,7},{7,6},{8,9},{9,8},{10,11... | collective-permute-start | bytes 7077896 | tf_op jit(solution)/shard_map/ppermute | solution.py:268
  329.2 13.6 %copy-start.14 = (bf16[768,256]{1,0:T(8,128)(2,1)}, bf16[768,256]{1,0:T(8,128)(2,1)S(1)}, u32[]{:S(2)}) copy-start(bf16[768,256]{1,0:T(8,128)(2,1)S(1)} %collective-permute-done.23) | copy-start | bytes 1179652
  329.2 81.9 %collective-permute-start.9 = (bf16[192,6144]{1,0:T(8,128)(2,1)}, bf16[192,6144]{1,0:T(8,128)(2,1)}, u32[]{:S(2)}, u32[]{:S(2)}) collective-permute-start(bf16[192,6144]{1,0:T(8,128)(2,1)} %collective-permute-done.6.refs_0_), channel_id=1, source_target_pairs={{0,1},{1,0},{2,3},{3,2},{4,5},{5,4},{6,7},{7,6},{8,9},{9,8},{10,11... | collective-permute-start | bytes 7077896 | tf_op jit(solution)/shard_map/ppermute | solution.py:268
  329.2 81.9 %collective-permute-start.11 = (bf16[192,6144]{1,0:T(8,128)(2,1)}, bf16[192,6144]{1,0:T(8,128)(2,1)}, u32[]{:S(2)}, u32[]{:S(2)}) collective-permute-start(bf16[192,6144]{1,0:T(8,128)(2,1)} %collective-permute-done.10.refs_2_), channel_id=1, source_target_pairs={{0,1},{1,0},{2,3},{3,2},{4,5},{5,4},{6,7},{7,6},{8,9},{9,8},{10,11... | collective-permute-start | bytes 7077896 | tf_op jit(solution)/shard_map/ppermute | solution.py:268
  342.8 2.5 copy-start.13
  342.8 2.5 copy-start.9
  344.0 11.0 %copy-start.2 = (bf16[1536,256]{1,0:T(8,128)(2,1)}, bf16[1536,256]{1,0:T(8,128)(2,1)S(1)}, u32[]{:S(2)}) copy-start(bf16[1536,256]{1,0:T(8,128)(2,1)S(1)} %constant_dynamic-update-slice_fusion.refs_1_.refs_4_) | copy-start | bytes 2359300
  345.4 1.4 copy-start
  432.6 13.4 %collective-permute-start.28 = (f32[2,128,128]{2,1,0:T(8,128)}, f32[2,128,128]{2,1,0:T(8,128)S(1)}, u32[]{:S(2)}, u32[]{:S(2)}) collective-permute-start(f32[2,128,128]{2,1,0:T(8,128)} %get-tuple-element.42), channel_id=1, source_target_pairs={{0,16},{4,20},{8,24},{12,28},{16,0},{20,4},{24,8},{28,12},{1,17},{... | collective-permute-start | bytes 393224 | tf_op jit(solution)/shard_map/ppermute | solution.py:265
  457.3 21.6 %copy-start.1 = (f32[4,768,256]{2,1,0:T(8,128)S(1)}, f32[4,768,256]{2,1,0:T(8,128)}, u32[]{:S(2)}) copy-start(f32[4,768,256]{2,1,0:T(8,128)} %shard_map.68) | copy-start | bytes 9437188
  471.0 3.7 collective-permute-start.29
  474.7 4.1 collective-permute-start.30
  480.2 12.5 %collective-permute-start.33 = (bf16[768,256]{1,0:T(8,128)(2,1)S(1)}, bf16[768,256]{1,0:T(8,128)(2,1)S(1)}, u32[]{:S(2)}, u32[]{:S(2)}) collective-permute-start(bf16[768,256]{1,0:T(8,128)(2,1)S(1)} %get-tuple-element.52), channel_id=1, source_target_pairs={{0,12},{4,8},{8,4},{12,0},{16,28},{20,24},{24,20},{28,16},{1,13},{... | collective-permute-start | bytes 1179656 | tf_op jit(solution)/shard_map/ppermute | solution.py:265
  482.1 14.6 %collective-permute-start.32 = (bf16[768,256]{1,0:T(8,128)(2,1)S(1)}, bf16[768,256]{1,0:T(8,128)(2,1)S(1)}, u32[]{:S(2)}, u32[]{:S(2)}) collective-permute-start(bf16[768,256]{1,0:T(8,128)(2,1)S(1)} %get-tuple-element.53), channel_id=1, source_target_pairs={{0,8},{4,12},{8,0},{12,4},{16,24},{20,28},{24,16},{28,20},{1,9},{5... | collective-permute-start | bytes 1179656 | tf_op jit(solution)/shard_map/ppermute | solution.py:265
  482.3 14.6 %collective-permute-start.31 = (bf16[768,256]{1,0:T(8,128)(2,1)S(1)}, bf16[768,256]{1,0:T(8,128)(2,1)S(1)}, u32[]{:S(2)}, u32[]{:S(2)}) collective-permute-start(bf16[768,256]{1,0:T(8,128)(2,1)S(1)} %get-tuple-element.54), channel_id=1, source_target_pairs={{0,4},{4,0},{8,12},{12,8},{16,20},{20,16},{24,28},{28,24},{1,5},{5... | collective-permute-start | bytes 1179656 | tf_op jit(solution)/shard_map/ppermute | solution.py:265
  492.8 4.1 copy-start.15
  496.8 0.7 copy-start.16
  496.9 0.8 copy-start.17

commit v2 on v0

--- a/solution.py
+++ b/solution.py
@@ -1,14 +1,529 @@
+import functools
+
 import jax
 import jax.numpy as jnp
 from jax import lax
+from jax.experimental import pallas as pl
+from jax.experimental.pallas import tpu as pltpu
 from jax.sharding import PartitionSpec as P
+
+MEMBERS = 4
+VMEM = 60 * 1024 * 1024
 
 
 def doc_index(positions, doc_ends):
     return jnp.sum((positions[:, None] >= doc_ends[None, :]).astype(jnp.int32), axis=1)
 
 
-def shards(tokens, w_query, w_keyval, doc_lengths, norm_gain):
+def silu(v):
+    return v / (1.0 + jnp.exp(-v))
+
+
+def params():
+    return pltpu.CompilerParams(vmem_limit_bytes=VMEM)
+
+
+def project_body(places, fsdp_size, steps, starts, activate, where_ref, k_ref, *refs):
+    parts = len(places)
+    t_refs, w_ref, start_refs, out_ref = refs[:parts], refs[parts], refs[parts + 1 : -1], refs[-1]
+    total = out_ref
+    if activate:
+        start_refs, out_ref, total = refs[parts + 1 : -2], refs[-2], refs[-1]
+    step = pl.program_id(0)
+    lhs = jnp.concatenate([r[...] for r in t_refs], axis=0) if parts > 1 else t_refs[0][...]
+    product = jnp.dot(lhs, w_ref[...], preferred_element_type=jnp.float32)
+
+    @pl.when(step == 0)
+    def _():
+        if not starts:
+            total[...] = product
+        at = 0
+        for ref in start_refs:
+            rows = ref.shape[0]
+            total[at : at + rows, :] = product[at : at + rows] + ref[...]
+            at += rows
+
+    @pl.when(step > 0)
+    def _():
+        total[...] += product
+
+    if activate:
+
+        @pl.when(step == steps - 1)
+        def _():
+            m, f = where_ref[0], where_ref[1]
+            block_rows = out_ref.shape[0] // MEMBERS
+            at = 0
+            for ref, (j, spots) in zip(t_refs, places):
+                rows = ref.shape[0] // len(spots)
+                for e, offset in spots:
+                    to = (m ^ j) * block_rows
+                    if e is not None:
+                        to = to + (f ^ e) * (block_rows // fsdp_size) + offset
+                    to = pl.multiple_of(to, 16)
+                    value = silu(total[at : at + rows, :])
+                    out_ref[pl.ds(to, rows), :] = value.astype(out_ref.dtype)
+                    at += rows
+
+
+def part_rows(part, depth):
+    return part.shape[0] * part.shape[1] // (depth * lax.axis_size("seq"))
+
+
+def part_spec(part, depth, block):
+    if part.shape[1] == depth:
+        return pl.BlockSpec((part_rows(part, depth), depth), lambda *a: (block(*a), 0))
+    return pl.BlockSpec((part.shape[0], depth), lambda *a: (0, block(*a)))
+
+
+def project(where, k_blocks, parts, w, column, width, starts=(), start_column=0, activate=True):
+    steps = k_blocks.shape[0]
+    depth = w.shape[0] // steps
+    rows = sum(part_rows(p, depth) for p, _ in parts)
+    in_specs = [part_spec(p, depth, lambda k, wh, kb: kb[k]) for p, _ in parts]
+    in_specs.append(pl.BlockSpec((depth, width), lambda k, wh, kb: (k, column)))
+    in_specs += [
+        pl.BlockSpec((a.shape[0], width), lambda k, wh, kb: (0, start_column)) for a in starts
+    ]
+    kind = jnp.bfloat16 if activate else jnp.float32
+    return pl.pallas_call(
+        functools.partial(
+            project_body, [p for _, p in parts], lax.axis_size("fsdp"), steps, len(starts), activate
+        ),
+        grid_spec=pltpu.PrefetchScalarGridSpec(
+            num_scalar_prefetch=2,
+            grid=(steps,),
+            in_specs=in_specs,
+            out_specs=pl.BlockSpec((rows, width), lambda k, wh, kb: (0, 0)),
+            scratch_shapes=[pltpu.VMEM((rows, width), jnp.float32)] if activate else [],
+        ),
+        out_shape=jax.ShapeDtypeStruct((rows, width), kind),
+        compiler_params=params(),
+        cost_estimate=pl.CostEstimate(
+            flops=2 * rows * depth * steps * width,
+            bytes_accessed=2 * depth * steps * (rows + width),
+            transcendentals=0,
+        ),
+    )(where, k_blocks, *[p for p, _ in parts], w, *starts)
+
+
+def doc_of(positions, ends_ref):
+    total = jnp.zeros(positions.shape, jnp.int32)
+    for i in range(ends_ref.shape[0]):
+        total += (positions >= ends_ref[i]).astype(jnp.int32)
+    return total
+
+
+def doc_of_scalar(position, ends_ref):
+    total = jnp.int32(0)
+    for i in range(ends_ref.shape[0]):
+        total += (position >= ends_ref[i]).astype(jnp.int32)
+    return total
+
+
+def tails_body(heads, where_ref, ends_ref, kv_ref, tails_ref, state_ref):
+    rows = kv_ref.shape[1]
+    size = kv_ref.shape[2] // heads // 2
+    block = pl.program_id(0)
+    start = (where_ref[2] * MEMBERS + block) * rows
+    last = doc_of_scalar(start + rows - 1, ends_ref)
+    before = doc_of_scalar(start - 1, ends_ref)
+    docs = doc_of(start + lax.broadcasted_iota(jnp.int32, (rows, size), 0), ends_ref)
+    kept = jnp.where((before == last) & (block > 0), 1.0, 0.0)
+    for h in range(heads):
+        at = 2 * h * size
+        keys = kv_ref[0, :, at : at + size].astype(jnp.float32)
+        keys = jnp.where(docs == last, keys, 0.0).astype(jnp.bfloat16)
+        values = kv_ref[0, :, at + size : at + 2 * size]
+        tail = lax.dot_general(
+            keys, values, (((0,), (0,)), ((), ())), preferred_element_type=jnp.float32
+        )
+        tails_ref[0, h] = tail
+
+        @pl.when(block == 0)
+        def _():
+            state_ref[h] = tail
+
+        @pl.when(block > 0)
+        def _():
+            state_ref[h] = tail + kept * state_ref[h]
+
+
+def tails(where, ends, kv, heads):
+    blocks, rows, width = kv.shape
+    size = width // heads // 2
+    return pl.pallas_call(
+        functools.partial(tails_body, heads),
+        grid_spec=pltpu.PrefetchScalarGridSpec(
+            num_scalar_prefetch=2,
+            grid=(blocks,),
+            in_specs=[pl.BlockSpec((1, rows, width), lambda b, wh, en: (b, 0, 0))],
+            out_specs=[
+                pl.BlockSpec((1, heads, size, size), lambda b, wh, en: (b, 0, 0, 0)),
+                pl.BlockSpec((heads, size, size), lambda b, wh, en: (0, 0, 0)),
+            ],
+        ),
+        out_shape=[
+            jax.ShapeDtypeStruct((blocks, heads, size, size), jnp.float32),
+            jax.ShapeDtypeStruct((heads, size, size), jnp.float32),
+        ],
+        compiler_params=params(),
+        cost_estimate=pl.CostEstimate(
+            flops=2 * blocks * rows * heads * size * size,
+            bytes_accessed=2 * blocks * rows * width,
+            transcendentals=0,
+        ),
+    )(where, ends, kv)
+
+
+def incoming_body(rows, where_ref, ends_ref, tails_ref, other_ref, out_ref):
+    blocks = tails_ref.shape[0]
+    g = where_ref[2]
+    start = g * blocks * rows
+    edge = doc_of_scalar(start - 1, ends_ref)
+    owner = doc_of_scalar((g ^ 1) * blocks * rows + blocks * rows - 1, ends_ref)
+    state = jnp.where((g == 1) & (owner == edge), 1.0, 0.0) * other_ref[...]
+    for b in range(blocks):
+        out_ref[b] = state.astype(out_ref.dtype)
+        before = doc_of_scalar(start + b * rows - 1, ends_ref)
+        last = doc_of_scalar(start + (b + 1) * rows - 1, ends_ref)
+        state = tails_ref[b] + jnp.where(before == last, 1.0, 0.0) * state
+
+
+def incoming_states(where, ends, tail, other, rows):
+    return pl.pallas_call(
+        functools.partial(incoming_body, rows),
+        grid_spec=pltpu.PrefetchScalarGridSpec(
+            num_scalar_prefetch=2,
+            grid=(1,),
+            in_specs=[
+                pl.BlockSpec(tail.shape, lambda i, wh, en: (0, 0, 0, 0)),
+                pl.BlockSpec(other.shape, lambda i, wh, en: (0, 0, 0)),
+            ],
+            out_specs=pl.BlockSpec(tail.shape, lambda i, wh, en: (0, 0, 0, 0)),
+        ),
+        out_shape=jax.ShapeDtypeStruct(tail.shape, jnp.bfloat16),
+        compiler_params=params(),
+    )(where, ends, tail, other)
+
+
+def attend_body(
+    places, fsdp_size, steps, heads, cut, where_ref, ends_ref, k_ref, *refs
+):
+    parts = len(places)
+    t_refs = refs[:parts]
+    w_ref, start_ref, kv_ref, state_ref, out_ref, square_ref, total, q_ref = refs[parts:]
+    step = pl.program_id(0)
+    lhs = jnp.concatenate([r[...] for r in t_refs], axis=0) if parts > 1 else t_refs[0][...]
+    product = jnp.dot(lhs, w_ref[...], preferred_element_type=jnp.float32)
+
+    @pl.when(step == 0)
+    def _():
+        total[...] = product + start_ref[...]
+
+    @pl.when(step > 0)
+    def _():
+        total[...] += product
+
+    @pl.when(step == steps - 1)
+    def _():
+        m, f, g = where_ref[0], where_ref[1], where_ref[2]
+        rows, width = q_ref.shape
+        size = width // heads
+        place = places[0][0]
+        at = 0
+        for ref, (_, spots) in zip(t_refs, places):
+            count = ref.shape[0] // len(spots)
+            for e, offset in spots:
+                to = 0
+                if e is not None:
+                    to = pl.multiple_of((f ^ e) * (rows // fsdp_size) + offset, 16)
+                q_ref[pl.ds(to, count), :] = silu(total[at : at + count, :]).astype(q_ref.dtype)
+                at += count
+        start = (g * MEMBERS + (m ^ place)) * rows
+        before = doc_of_scalar(start - 1, ends_ref)
+        row_docs = doc_of(start + lax.broadcasted_iota(jnp.int32, (1, rows), 1), ends_ref)
+        for begin in range(0, rows, cut):
+            seen = begin + cut
+            docs = doc_of(start + begin + lax.broadcasted_iota(jnp.int32, (cut, 1), 0), ends_ref)
+            at = begin + lax.broadcasted_iota(jnp.int32, (cut, seen), 0)
+            behind = lax.broadcasted_iota(jnp.int32, (cut, seen), 1)
+            mask = (at >= behind) & (docs == row_docs[:, :seen])
+            mixed = []
+            for h in range(heads):
+                k_at, v_at = 2 * h * size, (2 * h + 1) * size
+                q = q_ref[begin:seen, h * size : (h + 1) * size]
+                scores = lax.dot_general(
+                    q, kv_ref[0, :seen, k_at : k_at + size], (((1,), (1,)), ((), ())),
+                    preferred_element_type=jnp.float32,
+                )
+                weights = jnp.where(mask, scores, 0.0).astype(jnp.bfloat16)
+                within = jnp.dot(
+                    weights, kv_ref[0, :seen, v_at : v_at + size],
+                    preferred_element_type=jnp.float32,
+                )
+                carried = jnp.dot(q, state_ref[0, h], preferred_element_type=jnp.float32)
+                mixed.append(within + jnp.where(docs == before, carried, 0.0))
+            mixed = jnp.concatenate(mixed, axis=1)
+            out_ref[begin:seen, :] = mixed.astype(out_ref.dtype)
+            square_ref[:, begin:seen] = lax.dot_general(
+                jnp.ones((8, width), jnp.float32), mixed * mixed, (((1,), (1,)), ((), ())),
+                precision=lax.Precision.HIGHEST, preferred_element_type=jnp.float32,
+            )
+
+
+def attend(where, ends, k_blocks, parts, w, acc, acc_at, acc_column, kv, states):
+    steps = k_blocks.shape[0]
+    depth, width = w.shape[0] // steps, w.shape[1]
+    heads = states.shape[1]
+    rows = kv.shape[1]
+    size = width // heads
+    place = parts[0][1][0]
+    cut = rows // 3 if rows % 384 == 0 else rows
+    in_specs = [part_spec(p, depth, lambda k, wh, en, kb: kb[k]) for p, _ in parts]
+    in_specs += [
+        pl.BlockSpec((depth, width), lambda k, wh, en, kb: (k, 0)),
+        pl.BlockSpec((rows, width), lambda k, wh, en, kb: (acc_at, acc_column)),
+        pl.BlockSpec((1, rows, kv.shape[2]), lambda k, wh, en, kb: (wh[0] ^ place, 0, 0)),
+        pl.BlockSpec((1, heads, size, size), lambda k, wh, en, kb: (wh[0] ^ place, 0, 0, 0)),
+    ]
+    return pl.pallas_call(
+        functools.partial(
+            attend_body, [p for _, p in parts], lax.axis_size("fsdp"), steps, heads, cut
+        ),
+        grid_spec=pltpu.PrefetchScalarGridSpec(
+            num_scalar_prefetch=3,
+            grid=(steps,),
+            in_specs=in_specs,
+            out_specs=[
+                pl.BlockSpec((rows, width), lambda k, wh, en, kb: (0, 0)),
+                pl.BlockSpec((8, rows), lambda k, wh, en, kb: (0, 0)),
+            ],
+            scratch_shapes=[
+                pltpu.VMEM((rows, width), jnp.float32),
+                pltpu.VMEM((rows, width), jnp.bfloat16),
+            ],
+        ),
+        out_shape=[
+            jax.ShapeDtypeStruct((rows, width), jnp.bfloat16),
+            jax.ShapeDtypeStruct((8, rows), jnp.float32),
+        ],
+        compiler_params=params(),
+        cost_estimate=pl.CostEstimate(
+            flops=2 * rows * depth * steps * width + 3 * rows * rows * width,
+            bytes_accessed=2 * depth * steps * (rows + width) + 12 * rows * width,
+            transcendentals=rows * width,
+        ),
+    )(where, ends, k_blocks, *[p for p, _ in parts], w, acc, kv, states)
+
+
+def finish_body(where_ref, *refs):
+    inverse_ref, gain_ref, out_ref = refs[MEMBERS:]
+    width = refs[0].shape[1]
+    for k in range(MEMBERS):
+        at = pl.multiple_of((where_ref[0] ^ k) * width, width)
+        gain = gain_ref[:, pl.ds(at, width)].astype(jnp.float32)
+        value = refs[k][...].astype(jnp.float32) * inverse_ref[...] * gain
+        out_ref[:, pl.ds(at, width)] = value.astype(out_ref.dtype)
+
+
+def finish(where, parts, inverse, gain):
+    rows, width = parts[0].shape
+    whole = lambda shape: pl.BlockSpec(shape, lambda i, wh: (0, 0))
+    return pl.pallas_call(
+        finish_body,
+        grid_spec=pltpu.PrefetchScalarGridSpec(
+            num_scalar_prefetch=1,
+            grid=(1,),
+            in_specs=[whole((rows, width)) for _ in parts]
+            + [whole((rows, 1)), whole((1, MEMBERS * width))],
+            out_specs=whole((rows, MEMBERS * width)),
+        ),
+        out_shape=jax.ShapeDtypeStruct((rows, MEMBERS * width), jnp.bfloat16),
+        compiler_params=params(),
+    )(where, *parts, inverse, gain)
+
+
+def grouped(seq_size, fsdp_size, tokens, w_query, w_keyval, doc_lengths, norm_gain):
+    rows, model = tokens.shape
+    depth, head_count, size = w_query.shape
+    heads = head_count // MEMBERS
+    s = lax.axis_index("seq")
+    f = lax.axis_index("fsdp")
+    m = lax.rem(s, MEMBERS)
+    g = lax.div(s, MEMBERS)
+    where = jnp.stack([m, f, g]).astype(jnp.int32)
+    doc_ends = jnp.cumsum(doc_lengths)
+
+    inner = ((s >> 1) ^ (s >> 2)) & 1 == 1
+    inner_seq = [i for i in range(seq_size) if ((i >> 1) ^ (i >> 2)) & 1 == 1]
+    outer_seq = [i for i in range(seq_size) if i not in inner_seq]
+
+    def hop(value, k, only=range(seq_size)):
+        return lax.ppermute(value, "seq", [(i, i ^ k) for i in only])
+
+    def side(value, k):
+        return lax.ppermute(value, "fsdp", [(i, i ^ k) for i in range(fsdp_size)])
+
+    q_width, kv_width = heads * size, 2 * heads * size
+    width = kv_width + q_width
+    q_block = kv_width // q_width
+    flat_kv = w_keyval.reshape(depth, head_count * 2 * size)
+    flat_q = w_query.reshape(depth, head_count * size)
+
+    def columns(k):
+        at = m ^ k
+        return jnp.concatenate(
+            [
+                lax.dynamic_slice(flat_kv, (0, at * kv_width), (depth, kv_width)),
+                lax.dynamic_slice(flat_q, (0, at * q_width), (depth, q_width)),
+            ],
+            axis=1,
+        )
+
+    half = rows // fsdp_size // 2
+
+    def own(i):
+        chunk = lax.dynamic_slice(tokens, ((2 * f + i) * half, 0), (half, model))
+        return chunk.reshape(half, seq_size, depth).transpose(1, 0, 2).reshape(-1, depth)
+
+    def stage(done, operands):
+        return lax.optimization_barrier((tuple(operands), tuple(done)))[0]
+
+    def blocks(ks):
+        return jnp.stack([s ^ k for k in ks]).astype(jnp.int32)
+
+    def pairs(inner_hop, outer_hop):
+        moves = [(i, i ^ inner_hop) for i in inner_seq if inner_hop]
+        moves += [(i, i ^ outer_hop) for i in outer_seq if outer_hop]
+        return lambda value: lax.ppermute(value, "seq", moves)
+
+    def pick(a, b):
+        return jnp.where(inner, a, b)
+
+    def spread(j, first, second):
+        found = []
+        for offset, pieces in ((0, first), (half, second)):
+            found += [(p, (j, [(e, offset)])) for e, p in zip((0, 2, 1, 3), pieces)]
+        return found
+
+    def x(value):
+        return hop(value, 1)
+
+    def y(value):
+        return side(value, 2)
+
+    def c(value):
+        return side(value, 1)
+
+    both_ways = pairs(2, 2)
+    own1 = own(0)
+    tz1 = both_ways(own1)
+    tx1 = x(own1)
+    wb = columns(2)
+    r1 = pairs(6, 0)(wb)
+    wa, wc, wd, own2 = columns(0), columns(1), columns(3), own(1)
+    in2, in3 = pick(wa, own2), pick(own2, wa)
+    o = stage([r1, tz1, tx1, wc, wd, own2, in3], [in2, own2, tx1, tx1, tz1])
+    r2 = pairs(4, 2)(o[0])
+    tx2 = x(o[1])
+    yx1 = y(o[2])
+    cx1 = c(o[3])
+    cz1 = c(o[4])
+    o = stage([r2, tx2, yx1, cx1, cz1], [in3, wd, tx2, tx2, yx1])
+    r3 = pairs(2, 4)(o[0])
+    rxb = x(o[1])
+    yx2 = y(o[2])
+    cx2 = c(o[3])
+    dx1 = c(o[4])
+    o = stage([r3, rxb, yx2, cx2, dx1], [wb, tz1, tz1, yx2])
+    r4 = pairs(0, 6)(o[0])
+    tzx1 = x(o[1])
+    yz1 = y(o[2])
+    dx2 = c(o[3])
+    tz2 = pick(r2, r3)
+    w4 = pick(r3, r2)
+    o = stage([r4, tzx1, yz1, dx2, tz2, w4], [rxb, wb, wc, tzx1, yz1])
+    r5 = pairs(6, 0)(o[0])
+    z5 = both_ways(o[1])
+    rxa = x(o[2])
+    yzx1 = y(o[3])
+    dz1 = c(o[4])
+    w6 = pick(r1, r4)
+    o = stage([r5, z5, rxa, yzx1, dz1, w6], [pick(rxa, rxb), tz2, tz2, tzx1, yzx1])
+    r6 = pairs(4, 2)(o[0])
+    tzx2 = x(o[1])
+    yz2 = y(o[2])
+    czx1 = c(o[3])
+    dzx1 = c(o[4])
+    in7 = pick(rxb, rxa)
+    in7_kv, in7_q = in7[:, :kv_width], in7[:, kv_width:]
+    rxb_kv, rxb_q = rxb[:, :kv_width], rxb[:, kv_width:]
+    w_early = jnp.concatenate([wa, rxa, z5, w4, w6], axis=0)
+    early = [0, 1, 2, 4, 6]
+    part0 = [(tokens, (0, [(None, 0)]))]
+    part1 = spread(1, (tx1, yx1, cx1, dx1), (tx2, yx2, cx2, dx2))
+    acc01 = project(where, blocks(early), part0 + part1, w_early, 0, width, activate=False)
+    o = stage(
+        [r6, tzx2, yz2, czx1, dzx1, acc01, rxb_kv, rxb_q, in7_q], [in7_kv, tzx2, tz2, tzx2, yz2]
+    )
+    r7 = pairs(2, 4)(o[0])
+    yzx2 = y(o[1])
+    cz2 = c(o[2])
+    czx2 = c(o[3])
+    dz2 = c(o[4])
+    sixth = s ^ pick(3, 5)
+    acc01 = project(
+        where, sixth[None].astype(jnp.int32), part0 + part1, r6, 0, width,
+        starts=(acc01,), activate=False,
+    )
+    w_more = jnp.concatenate([w_early, r6], axis=0)
+    k_more = jnp.concatenate([blocks(early), sixth[None].astype(jnp.int32)])
+    o = stage([r7, yzx2, cz2, czx2, dz2, acc01, w_more], [rxb_kv, yzx2])
+    r8 = pairs(0, 6)(o[0])
+    dzx2 = c(o[1])
+    part2 = spread(2, (tz1, yz1, cz1, dz1), (tz2, yz2, cz2, dz2))
+    acc2 = project(where, k_more, part2, w_more, 0, width, activate=False)
+    o = stage([r8, dzx2, acc2], [in7_q, rxb_q])
+    r7q = pairs(2, 4)(o[0])
+    r8q = pairs(0, 6)(o[1])
+    part3 = spread(3, (tzx1, yzx1, czx1, dzx1), (tzx2, yzx2, czx2, dzx2))
+    acc3 = project(where, k_more, part3, w_more, 0, width, activate=False)
+
+    accs = (acc01, acc2, acc3)
+    all_parts = part0 + part1 + part2 + part3
+    last = jnp.stack([s ^ pick(5, 3), s ^ 7]).astype(jnp.int32)
+    w_late = jnp.concatenate([r7, pick(r5[:, :kv_width], r8)], axis=0)
+    keyval = project(where, last, all_parts, w_late, 0, kv_width, starts=accs)
+    keyval = keyval.reshape(MEMBERS, rows, kv_width)
+    tail, state = tails(where, doc_ends, keyval, heads)
+    other = hop(state, MEMBERS)
+    states = incoming_states(where, doc_ends, tail, other, rows)
+
+    w_last = jnp.concatenate([r7q, pick(r5[:, kv_width:], r8q)], axis=0)
+    outs, squares = {}, 0.0
+    before = ()
+    for k, part, acc, acc_at in (
+        (3, part3, acc3, 0), (2, part2, acc2, 0), (1, part1, acc01, 1), (0, part0, acc01, 0)
+    ):
+        if before:
+            w_last = stage(before, [w_last])[0]
+        outs[k], square = attend(
+            where, doc_ends, last, part, w_last, acc, acc_at, q_block, keyval, states
+        )
+        before = (outs[k],)
+        if k:
+            outs[k], square = hop(outs[k], k), hop(square[:1], k)
+        else:
+            square = square[:1]
+        squares = squares + square
+    squares = squares + side(squares, 2)
+    squares = squares + side(squares, 1)
+    inverse = lax.rsqrt(squares / (head_count * fsdp_size * size) + 1e-06).reshape(rows, 1)
+    return finish(where, [outs[k] for k in range(MEMBERS)], inverse, norm_gain[None, :])
+
+
+def plain(tokens, w_query, w_keyval, doc_lengths, norm_gain):
     rows_here = tokens.shape[0]
     head_count = w_query.shape[1]
     head_size = w_query.shape[2]
@@ -63,8 +578,13 @@
 
 
 def solution(mesh):
+    seq_size, fsdp_size = mesh.shape["seq"], mesh.shape["fsdp"]
+    if seq_size == 2 * MEMBERS:
+        body = functools.partial(grouped, seq_size, fsdp_size)
+    else:
+        body = plain
     return jax.shard_map(
-        shards,
+        body,
         mesh=mesh,
         in_specs=(P("seq", None), P("seq", "fsdp", None), P("seq", "fsdp", None), P(), P("fsdp")),
         out_specs=P("seq", "fsdp"),

time: 766 us -> 368 us (0.48)
  waiting for transfers between devices: 659 us -> 144 us
  Pallas kernels: 0 us -> 110 us
  starting transfers between devices: 0.08 us -> 60.8 us
  matrix products: 55 us -> 0 us
  between operations: 13.2 us -> 0.89 us
    all_gather x3 -> x0, waiting for transfers between devices: 657 us -> none  [the longest x1 482 us: shards(): keyval_sum = project(lax.all_gather(w_keyval, 'seq', axis=0, tiled=True))]
    ppermute x0 -> x45, waiting for transfers between devices: none -> 144 us  [the longest x13 95.1 us: hop(): return lax.ppermute(value, 'seq', [(i, i ^ k) for i in only])]
    pallas_call x0 -> x12, Pallas kernels: none -> 110 us  [the longest x5 67.1 us: project(): pl.pallas_call(functools.partial(project_body, [p for _, p in parts], lax...]
    ppermute x0 -> x45, starting transfers between devices: none -> 60.8 us  [the longest x12 35.8 us: pairs(): return lambda value: lax.ppermute(value, 'seq', moves)]
    dot_general x5 -> x0, matrix products: 55 us -> none  [the longest x2 40.2 us: project(): return jnp.dot(tokens, panel, preferred_element_type=jnp.float32)]
    unnamed x11 -> x80, local copies, waits for them, and re-layouts: 20.4 us -> 11.9 us
  transfers between devices with their start and end apart: 3 -> 45, of which waited for: 3 -> 18; matrix products, arithmetic and copies ran while one was open for 10% -> 8% of each run, Pallas kernels for 0% -> 23%
where the time goes in v2:
time: 368 us; the launch traced here: 361 us
  waiting for transfers between devices  144 us (39%)
  Pallas kernels  110 us (30%)
  starting transfers between devices  60.8 us (17%)
  local copies, waits for them, and re-layouts  31 us (8%)
  other arithmetic  14.1 us (4%)
    ppermute x13, waiting for transfers between devices, hop(): return lax.ppermute(value, 'seq', [(i, i ^ k) for i in only])  95.1 us
    pallas_call x5, Pallas kernels, project(): pl.pallas_call(functools.partial(project_body, [p for _, p in parts], lax...  67.1 us
    ppermute x12, waiting for transfers between devices, pairs(): return lambda value: lax.ppermute(value, 'seq', moves)  43.2 us
    ppermute x12, starting transfers between devices, pairs(): return lambda value: lax.ppermute(value, 'seq', moves)  35.8 us
    pallas_call x4, Pallas kernels, attend(): pl.pallas_call(functools.partial(attend_body, [p for _, p in parts], lax....  30.4 us
    ppermute x13, starting transfers between devices, hop(): return lax.ppermute(value, 'seq', [(i, i ^ k) for i in only])  16 us
    unnamed x80, local copies, waits for them, and re-layouts  11.9 us
    ppermute x20, starting transfers between devices, side(): return lax.ppermute(value, 'fsdp', [(i, i ^ k) for i in range(fsdp_size)])  8.94 us
  transfers between devices with their start and end apart: 45, of which 18 were waited for; matrix products, arithmetic and copies ran while one was open for 8% of the time, Pallas kernels for 23%

profile of v2, /device:TPU:0, one launch (start us, length us, event | category | flops | bytes accessed | tf_op | source)
XLA Modules:
  0.0 360.6 jit_solution(12037416766096015741)
XLA Ops:
  0.0 3.1 copy.10
  3.1 1.6 copy.14
  4.7 1.5 constant_dynamic-slice_fusion.1
  7.2 1.1 pad_maximum_fusion.3
  8.3 1.7 collective-permute-start.2
  10.0 1.8 constant_dynamic-slice_fusion.4
  12.0 1.2 copy.7
  13.3 2.9 collective-permute-start
  16.2 3.4 collective-permute-start.1
  21.3 1.0 copy-done.20
  22.9 19.5 %collective-permute-done.refs_1_.refs_0_ = bf16[768,768]{1,0:T(8,128)(2,1)S(1)} collective-permute-done((bf16[768,768]{1,0:T(8,128)(2,1)}, bf16[768,768]{1,0:T(8,128)(2,1)S(1)}, u32[]{:S(2)}, u32[]{:S(2)}) %collective-permute-start) | collective-permute-done | bytes 1179680 | tf_op jit(solution)/shard_map/ppermute | solution.py:363
  42.4 3.0 collective-permute-done.1.refs_0_.refs_9_
  45.9 1.5 collective-permute-start.4
  47.4 1.7 collective-permute-start.5
  49.6 22.2 %collective-permute-done.3.refs_5_.refs_4_ = bf16[768,768]{1,0:T(8,128)(2,1)S(1)} collective-permute-done((bf16[768,768]{1,0:T(8,128)(2,1)S(1)}, bf16[768,768]{1,0:T(8,128)(2,1)S(1)}, u32[]{:S(2)}, u32[]{:S(2)}) %collective-permute-start.3) | collective-permute-done | bytes 1179680 | tf_op jit(solution)/shard_map/ppermute | solution.py:363
  72.1 2.1 collective-permute-done.5
  74.3 1.1 copy-done.10
  76.3 1.4 collective-permute-start.8
  78.4 22.0 %collective-permute-done.10 = bf16[768,768]{1,0:T(8,128)(2,1)S(1)} collective-permute-done((bf16[768,768]{1,0:T(8,128)(2,1)S(1)}, bf16[768,768]{1,0:T(8,128)(2,1)S(1)}, u32[]{:S(2)}, u32[]{:S(2)}) %collective-permute-start.10) | collective-permute-done | bytes 1179680 | tf_op jit(solution)/shard_map/ppermute | solution.py:399
  100.4 3.8 %collective-permute-done.8 = bf16[768,768]{1,0:T(8,128)(2,1)S(1)} collective-permute-done((bf16[768,768]{1,0:T(8,128)(2,1)S(1)}, bf16[768,768]{1,0:T(8,128)(2,1)S(1)}, u32[]{:S(2)}, u32[]{:S(2)}) %collective-permute-start.8) | collective-permute-done | bytes 1179680 | tf_op jit(solution)/shard_map/ppermute | solution.py:363
  104.2 1.2 collective-permute-done.9.refs_6_.refs_5_
  106.6 4.4 %collective-permute-start.15 = (bf16[768,768]{1,0:T(8,128)(2,1)}, bf16[768,768]{1,0:T(8,128)(2,1)S(1)}, u32[]{:S(2)}, u32[]{:S(2)}) collective-permute-start(bf16[768,768]{1,0:T(8,128)(2,1)} %pad_maximum_fusion.3), channel_id=1, source_target_pairs={{0,24},{4,28},{24,0},{28,4},{1,25},{5,29},{25,1},{29,5},{2,26},{6,... | collective-permute-start | bytes 3538952 | tf_op jit(solution)/shard_map/ppermute | solution.py:399
  111.3 21.1 %collective-permute-done.13.refs_0_.refs_17_ = bf16[768,768]{1,0:T(8,128)(2,1)} collective-permute-done((bf16[768,768]{1,0:T(8,128)(2,1)}, bf16[768,768]{1,0:T(8,128)(2,1)}, u32[]{:S(2)}, u32[]{:S(2)}) %collective-permute-start.13) | collective-permute-done | bytes 1179680 | tf_op jit(solution)/shard_map/ppermute | solution.py:363
  132.6 4.0 %collective-permute-done.15 = bf16[768,768]{1,0:T(8,128)(2,1)S(1)} collective-permute-done((bf16[768,768]{1,0:T(8,128)(2,1)}, bf16[768,768]{1,0:T(8,128)(2,1)S(1)}, u32[]{:S(2)}, u32[]{:S(2)}) %collective-permute-start.15) | collective-permute-done | bytes 1179680 | tf_op jit(solution)/shard_map/ppermute | solution.py:399
  136.7 1.0 copy-done.8
  137.7 1.4 collective-permute-start.17
  139.0 1.4 collective-permute-start.18
  141.3 21.7 %collective-permute-done.17 = bf16[768,768]{1,0:T(8,128)(2,1)S(1)} collective-permute-done((bf16[768,768]{1,0:T(8,128)(2,1)S(1)}, bf16[768,768]{1,0:T(8,128)(2,1)S(1)}, u32[]{:S(2)}, u32[]{:S(2)}) %collective-permute-start.17) | collective-permute-done | bytes 1179680 | tf_op jit(solution)/shard_map/ppermute | solution.py:363
  162.9 1.9 constant_dynamic-update-slice_fusion.3
  165.2 1.6 constant_dynamic-update-slice_fusion.6
  166.8 3.0 collective-permute-start.24
  172.3 2.2 slice.42
  174.5 1.8 slice.41
  176.2 0.9 slice.43
  178.0 1.1 constant_dynamic-update-slice_fusion.refs_9_
  179.1 17.8 %shard_map.55.refs_10_ = f32[1536,768]{1,0:T(8,128)} custom-call(s32[3]{0:T(128)} %pad_add_fusion.where_ref, s32[5]{0:T(128)} %stack.56.k_ref, bf16[768,6144]{1,0:T(8,128)(2,1)} %refs_0_.7, bf16[768,768]{1,0:T(8,128)(2,1)} %copy-done.1, bf16[768,768]{1,0:T(8,128)(2,1)} %copy-done.3, bf16[768,768]{1,0:T(8,128)(2,1)} %copy-done.4, bf16[768,768]{1,0:T(8,128)(2,1)} %copy-done.6, ...), custom_call_target="tpu_custom_call" | custom-call | flops 9059696640 | bytes 17694720 | tf_op jit(solution)/shard_map/pallas_call | solution.py:89
  196.9 1.6 collective-permute-start.27
  199.0 11.6 %collective-permute-start.28 = (bf16[768,512]{1,0:T(8,128)(2,1)}, bf16[768,512]{1,0:T(8,128)(2,1)}, u32[]{:S(2)}, u32[]{:S(2)}) collective-permute-start(bf16[768,512]{1,0:T(8,128)(2,1)} %slice.43), channel_id=1, source_target_pairs={{8,0},{12,4},{16,24},{20,28},{0,16},{4,20},{24,8},{28,12},{9,1},{1... | collective-permute-start | bytes 2359304 | tf_op jit(solution)/shard_map/ppermute | solution.py:399
  210.7 2.4 constant_dynamic-update-slice_fusion.5.refs_8_
  213.1 8.6 %shard_map.56.refs_26_.refs_9_.refs_2_ = f32[1536,768]{1,0:T(8,128)} custom-call(s32[3]{0:T(128)} %pad_add_fusion.where_ref, s32[1]{0:T(128)} %bitcast.16.k_ref, bf16[768,6144]{1,0:T(8,128)(2,1)} %refs_0_.7, bf16[768,768]{1,0:T(8,128)(2,1)} %copy-done.1, bf16[768,768]{1,0:T(8,128)(2,1)} %copy-done.3, bf16[768,768]{1,0:T(8,128)(2,1)} %copy-done.4, ...), custom_call_target="tpu_custom_call" | custom-call | flops 1811939328 | bytes 3538944 | tf_op jit(solution)/shard_map/pallas_call | solution.py:89
  221.6 7.8 %collective-permute-done.28 = bf16[768,512]{1,0:T(8,128)(2,1)} collective-permute-done((bf16[768,512]{1,0:T(8,128)(2,1)}, bf16[768,512]{1,0:T(8,128)(2,1)}, u32[]{:S(2)}, u32[]{:S(2)}) %collective-permute-start.28) | collective-permute-done | bytes 786464 | tf_op jit(solution)/shard_map/ppermute | solution.py:399
  229.5 4.4 %collective-permute-start.32 = (bf16[768,512]{1,0:T(8,128)(2,1)}, bf16[768,512]{1,0:T(8,128)(2,1)}, u32[]{:S(2)}, u32[]{:S(2)}) collective-permute-start(bf16[768,512]{1,0:T(8,128)(2,1)} %slice.42), channel_id=1, source_target_pairs={{0,24},{4,28},{24,0},{28,4},{1,25},{5,29},{25,1},{29,5},{2,26},{6,... | collective-permute-start | bytes 2359304 | tf_op jit(solution)/shard_map/ppermute | solution.py:399
  235.8 12.6 %shard_map.57.refs_27_.refs_9_ = f32[768,768]{1,0:T(8,128)} custom-call(s32[3]{0:T(128)} %pad_add_fusion.where_ref, s32[6]{0:T(128)} %concatenate.34.k_ref, bf16[768,768]{1,0:T(8,128)(2,1)} %collective-permute-done.1.refs_0_.refs_9_, bf16[768,768]{1,0:T(8,128)(2,1)} %copy-done.11, bf16[768,768]{1,0:T(8,128)(2,1)} %copy-done.10, bf16[768,768]{1,0:T(8,128)(2,1)} %copy-done.12, ...), custom_call_target="tpu_custom_call" | custom-call | flops 5435817984 | bytes 14155776 | tf_op jit(solution)/shard_map/pallas_call | solution.py:89
  248.4 4.3 %collective-permute-done.32 = bf16[768,512]{1,0:T(8,128)(2,1)} collective-permute-done((bf16[768,512]{1,0:T(8,128)(2,1)}, bf16[768,512]{1,0:T(8,128)(2,1)}, u32[]{:S(2)}, u32[]{:S(2)}) %collective-permute-start.32) | collective-permute-done | bytes 786464 | tf_op jit(solution)/shard_map/ppermute | solution.py:399
  252.7 1.5 slice_select_fusion
  254.1 2.4 pad_maximum_fusion.refs_25_
  256.6 4.4 %collective-permute-start.35 = (bf16[768,256]{1,0:T(8,128)(2,1)S(1)}, bf16[768,256]{1,0:T(8,128)(2,1)S(1)}, u32[]{:S(2)}, u32[]{:S(2)}) collective-permute-start(bf16[768,256]{1,0:T(8,128)(2,1)S(1)} %copy-done.29), channel_id=1, source_target_pairs={{0,24},{4,28},{24,0},{28,4},{1,25},{5,29},{25,1},{29,5},{2,26},{6,... | collective-permute-start | bytes 1179656 | tf_op jit(solution)/shard_map/ppermute | solution.py:399
  261.1 12.6 %shard_map.58.refs_28_.refs_9_ = f32[768,768]{1,0:T(8,128)} custom-call(s32[3]{0:T(128)} %pad_add_fusion.where_ref, s32[6]{0:T(128)} %concatenate.34.k_ref, bf16[768,768]{1,0:T(8,128)(2,1)} %collective-permute-done.13.refs_0_.refs_17_, bf16[768,768]{1,0:T(8,128)(2,1)} %copy-done.13, bf16[768,768]{1,0:T(8,128)(2,1)} %collective-permute-done.25.refs_2_.refs_19_, ...), custom_call_target="tpu_custom_call" | custom-call | flops 5435817984 | bytes 14155776 | tf_op jit(solution)/shard_map/pallas_call | solution.py:89
  273.6 15.6 %shard_map.59 = bf16[3072,512]{1,0:T(8,128)(2,1)} custom-call(s32[3]{0:T(128)} %pad_add_fusion.where_ref, s32[2]{0:T(128)} %pad_add_fusion.1.k_ref, bf16[768,6144]{1,0:T(8,128)(2,1)} %refs_0_.7, bf16[768,768]{1,0:T(8,128)(2,1)} %copy-done.1, bf16[768,768]{1,0:T(8,128)(2,1)} %copy-done.3, bf16[768,768]{1,0:T(8,128)(2,1)} %copy-done.4, ...), custom_call_target="tpu_custom_call" | custom-call | flops 4831838208 | bytes 11010048 | tf_op jit(solution)/shard_map/pallas_call | solution.py:89
  289.3 6.3 %shard_map.60 = (f32[4,2,128,128]{3,2,1,0:T(8,128)}, f32[2,128,128]{2,1,0:T(8,128)}) custom-call(s32[3]{0:T(128)} %pad_add_fusion.where_ref, s32[8]{0:T(128)} %bitcast.48, bf16[4,768,512]{2,1,0:T(8,128)(2,1)} %bitcast.34), custom_call_target="tpu_custom_call" | custom-call | flops 201326592 | bytes 3145728 | tf_op jit(solution)/shard_map/pallas_call | solution.py:155
  295.6 1.9 collective-permute-start.36
  297.4 6.0 %collective-permute-done.36.other_ref = f32[2,128,128]{2,1,0:T(8,128)S(1)} collective-permute-done((f32[2,128,128]{2,1,0:T(8,128)}, f32[2,128,128]{2,1,0:T(8,128)S(1)}, u32[]{:S(2)}, u32[]{:S(2)}) %collective-permute-start.36) | collective-permute-done | bytes 131104 | tf_op jit(solution)/shard_map/ppermute | solution.py:363
  304.1 2.5 shard_map.61.refs_11_.refs_4_
  306.6 1.0 slice_select_fusion.1
  308.6 7.7 %shard_map.62 = (bf16[768,256]{1,0:T(8,128)(2,1)}, f32[8,768]{1,0:T(8,128)}) custom-call(s32[3]{0:T(128)} %pad_add_fusion.where_ref, s32[8]{0:T(128)} %bitcast.50, s32[2]{0:T(128)} %pad_add_fusion.1.k_ref, bf16[768,768]{1,0:T(8,128)(2,1)} %collective-permute-done.13.refs_0_.refs_17_, bf16[768,768]{1,0:T(8,128)(2,1)} %copy-done.13, ...), custom_call_target="tpu_custom_call" | custom-call | flops 1056964608 | bytes 5505024 | tf_op jit(solution)/shard_map/pallas_call | solution.py:290
  316.3 7.9 %shard_map.63 = (bf16[768,256]{1,0:T(8,128)(2,1)}, f32[8,768]{1,0:T(8,128)}) custom-call(s32[3]{0:T(128)} %pad_add_fusion.where_ref, s32[8]{0:T(128)} %bitcast.51, s32[2]{0:T(128)} %pad_add_fusion.1.k_ref, bf16[768,768]{1,0:T(8,128)(2,1)} %collective-permute-done.1.refs_0_.refs_9_, bf16[768,768]{1,0:T(8,128)(2,1)} %copy-done.11, ...), custom_call_target="tpu_custom_call" | custom-call | flops 1056964608 | bytes 5505024 | tf_op jit(solution)/shard_map/pallas_call | solution.py:290
  324.1 7.9 %shard_map.64 = (bf16[768,256]{1,0:T(8,128)(2,1)}, f32[8,768]{1,0:T(8,128)}) custom-call(s32[3]{0:T(128)} %pad_add_fusion.where_ref, s32[8]{0:T(128)} %bitcast.52, s32[2]{0:T(128)} %pad_add_fusion.1.k_ref, bf16[768,768]{1,0:T(8,128)(2,1)} %copy-done.1, bf16[768,768]{1,0:T(8,128)(2,1)} %copy-done.3, bf16[768,768]{1,0:T(8,128)(2,1)} %copy-done.4, ...), custom_call_target="tpu_custom_call" | custom-call | flops 1056964608 | bytes 5505024 | tf_op jit(solution)/shard_map/pallas_call | solution.py:290
  332.0 1.9 collective-permute-start.37
  335.9 1.7 collective-permute-start.41
  338.3 1.6 collective-permute-start.40
  339.9 7.0 %shard_map.65 = (bf16[768,256]{1,0:T(8,128)(2,1)}, f32[8,768]{1,0:T(8,128)}) custom-call(s32[3]{0:T(128)} %pad_add_fusion.where_ref, s32[8]{0:T(128)} %bitcast.53, s32[2]{0:T(128)} %pad_add_fusion.1.k_ref, bf16[768,6144]{1,0:T(8,128)(2,1)} %refs_0_.7, bf16[1536,256]{1,0:T(8,128)(2,1)} %pad_maximum_fusion.5.refs_8_.refs_1_, ...), custom_call_target="tpu_custom_call" | custom-call | flops 1056964608 | bytes 5505024 | tf_op jit(solution)/shard_map/pallas_call | solution.py:290
  346.9 1.4 collective-permute-start.39
  349.6 3.1 collective-permute-done.43
  356.4 3.8 %shard_map.66 = bf16[768,1024]{1,0:T(8,128)(2,1)} custom-call(s32[3]{0:T(128)} %pad_add_fusion.where_ref, bf16[768,256]{1,0:T(8,128)(2,1)} %get-tuple-element.92.refs_0_, bf16[768,256]{1,0:T(8,128)(2,1)} %copy-done.25, bf16[768,256]{1,0:T(8,128)(2,1)} %copy-done.26, bf16[768,256]{1,0:T(8,128)(2,1)} %copy-done.27, f32[768,1]{1,0:T(8,128)} %copy.8.refs_4_, ...), custom_call_target="tpu_custom_call" | custom-call | tf_op jit(solution)/shard_map/pallas_call | solution.py:333
  (152 shorter events, 24.3 us)
Async XLA Ops:
  8.3 14.5 %collective-permute-start.2 = (bf16[768,768]{1,0:T(8,128)(2,1)}, bf16[768,768]{1,0:T(8,128)(2,1)}, u32[]{:S(2)}, u32[]{:S(2)}) collective-permute-start(bf16[768,768]{1,0:T(8,128)(2,1)} %pad_maximum_fusion.3), channel_id=1, source_target_pairs={{8,16},{12,20},{16,8},{20,12},{9,17},{13,21},{17,9},{21,13},{10,18... | collective-permute-start | bytes 3538952 | tf_op jit(solution)/shard_map/ppermute | solution.py:399
  13.3 29.1 %collective-permute-start = (bf16[768,768]{1,0:T(8,128)(2,1)}, bf16[768,768]{1,0:T(8,128)(2,1)S(1)}, u32[]{:S(2)}, u32[]{:S(2)}) collective-permute-start(bf16[768,768]{1,0:T(8,128)(2,1)} %bitcast.10), channel_id=1, source_target_pairs={{0,4},{4,0},{8,12},{12,8},{16,20},{20,16},{24,28},{28,24},{1,5},{5... | collective-permute-start | bytes 3538952 | tf_op jit(solution)/shard_map/ppermute | solution.py:363
  16.2 29.1 %collective-permute-start.1 = (bf16[768,768]{1,0:T(8,128)(2,1)}, bf16[768,768]{1,0:T(8,128)(2,1)}, u32[]{:S(2)}, u32[]{:S(2)}) collective-permute-start(bf16[768,768]{1,0:T(8,128)(2,1)} %bitcast.10), channel_id=1, source_target_pairs={{8,0},{12,4},{16,24},{20,28},{0,8},{4,12},{24,16},{28,20},{9,1},{1... | collective-permute-start | bytes 3538952 | tf_op jit(solution)/shard_map/ppermute | solution.py:399
  42.4 68.9 %copy-start.1 = (bf16[768,768]{1,0:T(8,128)(2,1)}, bf16[768,768]{1,0:T(8,128)(2,1)S(1)}, u32[]{:S(2)}) copy-start(bf16[768,768]{1,0:T(8,128)(2,1)S(1)} %collective-permute-done.refs_1_.refs_0_) | copy-start | bytes 3538948
  45.3 26.5 %collective-permute-start.3 = (bf16[768,768]{1,0:T(8,128)(2,1)S(1)}, bf16[768,768]{1,0:T(8,128)(2,1)S(1)}, u32[]{:S(2)}, u32[]{:S(2)}) collective-permute-start(bf16[768,768]{1,0:T(8,128)(2,1)S(1)} %bitcast.41), channel_id=1, source_target_pairs={{0,4},{4,0},{8,12},{12,8},{16,20},{20,16},{24,28},{28,24},{1,5},{5... | collective-permute-start | bytes 3538952 | tf_op jit(solution)/shard_map/ppermute | solution.py:363
  45.9 26.2 %collective-permute-start.4 = (bf16[768,768]{1,0:T(8,128)(2,1)S(1)}, bf16[768,768]{1,0:T(8,128)(2,1)S(1)}, u32[]{:S(2)}, u32[]{:S(2)}) collective-permute-start(bf16[768,768]{1,0:T(8,128)(2,1)S(1)} %collective-permute-done.refs_1_.refs_0_), channel_id=1, source_target_pairs={{0,2},{1,3},{2,0},{3,1},{4,6},{5,7},{6,4},{7,5},{8,10},{9,11},{10,... | collective-permute-start | bytes 3538952 | tf_op jit(solution)/shard_map/ppermute | solution.py:366
  47.4 26.9 %collective-permute-start.5 = (bf16[768,768]{1,0:T(8,128)(2,1)S(1)}, bf16[768,768]{1,0:T(8,128)(2,1)S(1)}, u32[]{:S(2)}, u32[]{:S(2)}) collective-permute-start(bf16[768,768]{1,0:T(8,128)(2,1)S(1)} %get-tuple-element.53), channel_id=1, source_target_pairs={{8,24},{12,28},{16,0},{20,4},{0,8},{4,12},{24,16},{28,20},{9,25},{... | collective-permute-start | bytes 3538952 | tf_op jit(solution)/shard_map/ppermute | solution.py:399
  49.1 25.1 %collective-permute-start.6 = (bf16[768,768]{1,0:T(8,128)(2,1)S(1)}, bf16[768,768]{1,0:T(8,128)(2,1)S(1)}, u32[]{:S(2)}, u32[]{:S(2)}) collective-permute-start(bf16[768,768]{1,0:T(8,128)(2,1)S(1)} %collective-permute-done.refs_1_.refs_0_), channel_id=1, source_target_pairs={{0,1},{1,0},{2,3},{3,2},{4,5},{5,4},{6,7},{7,6},{8,9},{9,8},{10,11... | collective-permute-start | bytes 3538952 | tf_op jit(solution)/shard_map/ppermute | solution.py:366
  49.1 25.2 %collective-permute-start.7 = (bf16[768,768]{1,0:T(8,128)(2,1)}, bf16[768,768]{1,0:T(8,128)(2,1)S(1)}, u32[]{:S(2)}, u32[]{:S(2)}) collective-permute-start(bf16[768,768]{1,0:T(8,128)(2,1)} %collective-permute-done.1.refs_0_.refs_9_), channel_id=1, source_target_pairs={{0,1},{1,0},{2,3},{3,2},{4,5},{5,4},{6,7},{7,6},{8,9},{9,8},{10,11... | collective-permute-start | bytes 3538952 | tf_op jit(solution)/shard_map/ppermute | solution.py:366
  71.8 39.4 %copy-start.2 = (bf16[768,768]{1,0:T(8,128)(2,1)}, bf16[768,768]{1,0:T(8,128)(2,1)S(1)}, u32[]{:S(2)}) copy-start(bf16[768,768]{1,0:T(8,128)(2,1)S(1)} %collective-permute-done.3.refs_5_.refs_4_) | copy-start | bytes 3538948
  72.1 38.9 %copy-start.3 = (bf16[768,768]{1,0:T(8,128)(2,1)}, bf16[768,768]{1,0:T(8,128)(2,1)S(1)}, u32[]{:S(2)}) copy-start(bf16[768,768]{1,0:T(8,128)(2,1)S(1)} %collective-permute-done.4.refs_2_.refs_1_) | copy-start | bytes 3538948
  74.2 36.7 %copy-start.4 = (bf16[768,768]{1,0:T(8,128)(2,1)}, bf16[768,768]{1,0:T(8,128)(2,1)S(1)}, u32[]{:S(2)}) copy-start(bf16[768,768]{1,0:T(8,128)(2,1)S(1)} %collective-permute-done.6.refs_3_.refs_2_) | copy-start | bytes 3538948
  75.3 25.0 %collective-permute-start.10 = (bf16[768,768]{1,0:T(8,128)(2,1)S(1)}, bf16[768,768]{1,0:T(8,128)(2,1)S(1)}, u32[]{:S(2)}, u32[]{:S(2)}) collective-permute-start(bf16[768,768]{1,0:T(8,128)(2,1)S(1)} %get-tuple-element.58), channel_id=1, source_target_pairs={{8,0},{12,4},{16,24},{20,28},{0,16},{4,20},{24,8},{28,12},{9,1},{1... | collective-permute-start | bytes 3538952 | tf_op jit(solution)/shard_map/ppermute | solution.py:399
  75.8 24.6 %collective-permute-start.11 = (bf16[768,768]{1,0:T(8,128)(2,1)S(1)}, bf16[768,768]{1,0:T(8,128)(2,1)S(1)}, u32[]{:S(2)}, u32[]{:S(2)}) collective-permute-start(bf16[768,768]{1,0:T(8,128)(2,1)S(1)} %collective-permute-done.3.refs_5_.refs_4_), channel_id=1, source_target_pairs={{0,1},{1,0},{2,3},{3,2},{4,5},{5,4},{6,7},{7,6},{8,9},{9,8},{10,11... | collective-permute-start | bytes 3538952 | tf_op jit(solution)/shard_map/ppermute | solution.py:366
  75.8 24.6 %collective-permute-start.12 = (bf16[768,768]{1,0:T(8,128)(2,1)S(1)}, bf16[768,768]{1,0:T(8,128)(2,1)S(1)}, u32[]{:S(2)}, u32[]{:S(2)}) collective-permute-start(bf16[768,768]{1,0:T(8,128)(2,1)S(1)} %collective-permute-done.4.refs_2_.refs_1_), channel_id=1, source_target_pairs={{0,1},{1,0},{2,3},{3,2},{4,5},{5,4},{6,7},{7,6},{8,9},{9,8},{10,11... | collective-permute-start | bytes 3538952 | tf_op jit(solution)/shard_map/ppermute | solution.py:366
  76.3 27.9 %collective-permute-start.8 = (bf16[768,768]{1,0:T(8,128)(2,1)S(1)}, bf16[768,768]{1,0:T(8,128)(2,1)S(1)}, u32[]{:S(2)}, u32[]{:S(2)}) collective-permute-start(bf16[768,768]{1,0:T(8,128)(2,1)S(1)} %get-tuple-element.56), channel_id=1, source_target_pairs={{0,4},{4,0},{8,12},{12,8},{16,20},{20,16},{24,28},{28,24},{1,5},{5... | collective-permute-start | bytes 3538952 | tf_op jit(solution)/shard_map/ppermute | solution.py:363
  77.7 27.6 %collective-permute-start.9 = (bf16[768,768]{1,0:T(8,128)(2,1)S(1)}, bf16[768,768]{1,0:T(8,128)(2,1)S(1)}, u32[]{:S(2)}, u32[]{:S(2)}) collective-permute-start(bf16[768,768]{1,0:T(8,128)(2,1)S(1)} %collective-permute-done.3.refs_5_.refs_4_), channel_id=1, source_target_pairs={{0,2},{1,3},{2,0},{3,1},{4,6},{5,7},{6,4},{7,5},{8,10},{9,11},{10,... | collective-permute-start | bytes 3538952 | tf_op jit(solution)/shard_map/ppermute | solution.py:366
  100.4 10.6 %copy-start.5 = (bf16[768,768]{1,0:T(8,128)(2,1)}, bf16[768,768]{1,0:T(8,128)(2,1)S(1)}, u32[]{:S(2)}) copy-start(bf16[768,768]{1,0:T(8,128)(2,1)S(1)} %collective-permute-done.11.refs_7_.refs_6_) | copy-start | bytes 3538948
  100.4 10.6 %copy-start.6 = (bf16[768,768]{1,0:T(8,128)(2,1)}, bf16[768,768]{1,0:T(8,128)(2,1)S(1)}, u32[]{:S(2)}) copy-start(bf16[768,768]{1,0:T(8,128)(2,1)S(1)} %collective-permute-done.12.refs_4_.refs_3_) | copy-start | bytes 3538948
  104.2 58.8 %copy-start.18 = (bf16[768,768]{1,0:T(8,128)(2,1)}, bf16[768,768]{1,0:T(8,128)(2,1)S(1)}, u32[]{:S(2)}) copy-start(bf16[768,768]{1,0:T(8,128)(2,1)S(1)} %collective-permute-done.8) | copy-start | bytes 3538948
  105.3 5.9 %copy-start.7 = (bf16[768,768]{1,0:T(8,128)(2,1)}, bf16[768,768]{1,0:T(8,128)(2,1)S(1)}, u32[]{:S(2)}) copy-start(bf16[768,768]{1,0:T(8,128)(2,1)S(1)} %collective-permute-done.9.refs_6_.refs_5_) | copy-start | bytes 3538948
  105.3 27.0 %collective-permute-start.13 = (bf16[768,768]{1,0:T(8,128)(2,1)}, bf16[768,768]{1,0:T(8,128)(2,1)}, u32[]{:S(2)}, u32[]{:S(2)}) collective-permute-start(bf16[768,768]{1,0:T(8,128)(2,1)} %collective-permute-done.1.refs_0_.refs_9_), channel_id=1, source_target_pairs={{0,4},{4,0},{8,12},{12,8},{16,20},{20,16},{24,28},{28,24},{1,5},{5... | collective-permute-start | bytes 3538952 | tf_op jit(solution)/shard_map/ppermute | solution.py:363
  105.9 26.7 %collective-permute-start.14 = (bf16[768,768]{1,0:T(8,128)(2,1)}, bf16[768,768]{1,0:T(8,128)(2,1)S(1)}, u32[]{:S(2)}, u32[]{:S(2)}) collective-permute-start(bf16[768,768]{1,0:T(8,128)(2,1)} %collective-permute-done.1.refs_0_.refs_9_), channel_id=1, source_target_pairs={{0,2},{1,3},{2,0},{3,1},{4,6},{5,7},{6,4},{7,5},{8,10},{9,11},{10,... | collective-permute-start | bytes 3538952 | tf_op jit(solution)/shard_map/ppermute | solution.py:366
  106.6 30.1 %collective-permute-start.15 = (bf16[768,768]{1,0:T(8,128)(2,1)}, bf16[768,768]{1,0:T(8,128)(2,1)S(1)}, u32[]{:S(2)}, u32[]{:S(2)}) collective-permute-start(bf16[768,768]{1,0:T(8,128)(2,1)} %pad_maximum_fusion.3), channel_id=1, source_target_pairs={{0,24},{4,28},{24,0},{28,4},{1,25},{5,29},{25,1},{29,5},{2,26},{6,... | collective-permute-start | bytes 3538952 | tf_op jit(solution)/shard_map/ppermute | solution.py:399
  111.0 25.6 %collective-permute-start.16 = (bf16[768,768]{1,0:T(8,128)(2,1)S(1)}, bf16[768,768]{1,0:T(8,128)(2,1)S(1)}, u32[]{:S(2)}, u32[]{:S(2)}) collective-permute-start(bf16[768,768]{1,0:T(8,128)(2,1)S(1)} %collective-permute-done.9.refs_6_.refs_5_), channel_id=1, source_target_pairs={{0,1},{1,0},{2,3},{3,2},{4,5},{5,4},{6,7},{7,6},{8,9},{9,8},{10,11... | collective-permute-start | bytes 3538952 | tf_op jit(solution)/shard_map/ppermute | solution.py:366
  111.3 87.2 %copy-start = (bf16[768,768]{1,0:T(8,128)(2,1)}, bf16[768,768]{1,0:T(8,128)(2,1)S(1)}, u32[]{:S(2)}) copy-start(bf16[768,768]{1,0:T(8,128)(2,1)S(1)} %get-tuple-element.77.refs_4_.refs_13_) | copy-start | bytes 3538948
  132.6 32.2 %copy-start.11 = (bf16[768,768]{1,0:T(8,128)(2,1)}, bf16[768,768]{1,0:T(8,128)(2,1)S(1)}, u32[]{:S(2)}) copy-start(bf16[768,768]{1,0:T(8,128)(2,1)S(1)} %collective-permute-done.14.refs_1_.refs_10_) | copy-start | bytes 3538948
  137.7 25.3 %collective-permute-start.17 = (bf16[768,768]{1,0:T(8,128)(2,1)S(1)}, bf16[768,768]{1,0:T(8,128)(2,1)S(1)}, u32[]{:S(2)}, u32[]{:S(2)}) collective-permute-start(bf16[768,768]{1,0:T(8,128)(2,1)S(1)} %get-tuple-element.65), channel_id=1, source_target_pairs={{0,4},{4,0},{8,12},{12,8},{16,20},{20,16},{24,28},{28,24},{1,5},{5... | collective-permute-start | bytes 3538952 | tf_op jit(solution)/shard_map/ppermute | solution.py:363
  139.0 25.8 %collective-permute-start.20 = (bf16[768,768]{1,0:T(8,128)(2,1)}, bf16[768,768]{1,0:T(8,128)(2,1)S(1)}, u32[]{:S(2)}, u32[]{:S(2)}) collective-permute-start(bf16[768,768]{1,0:T(8,128)(2,1)} %pad_maximum_fusion.3), channel_id=1, source_target_pairs={{8,0},{12,4},{16,24},{20,28},{0,8},{4,12},{24,16},{28,20},{9,1},{1... | collective-permute-start | bytes 3538952 | tf_op jit(solution)/shard_map/ppermute | solution.py:399
  139.0 27.7 %collective-permute-start.18 = (bf16[768,768]{1,0:T(8,128)(2,1)}, bf16[768,768]{1,0:T(8,128)(2,1)S(1)}, u32[]{:S(2)}, u32[]{:S(2)}) collective-permute-start(bf16[768,768]{1,0:T(8,128)(2,1)} %collective-permute-done.13.refs_0_.refs_17_), channel_id=1, source_target_pairs={{0,2},{1,3},{2,0},{3,1},{4,6},{5,7},{6,4},{7,5},{8,10},{9,11},{10,... | collective-permute-start | bytes 3538952 | tf_op jit(solution)/shard_map/ppermute | solution.py:366
  140.4 26.3 %collective-permute-start.19 = (bf16[768,768]{1,0:T(8,128)(2,1)S(1)}, bf16[768,768]{1,0:T(8,128)(2,1)S(1)}, u32[]{:S(2)}, u32[]{:S(2)}) collective-permute-start(bf16[768,768]{1,0:T(8,128)(2,1)S(1)} %collective-permute-done.8), channel_id=1, source_target_pairs={{8,16},{12,20},{16,8},{20,12},{9,17},{13,21},{17,9},{21,13},{10,18... | collective-permute-start | bytes 3538952 | tf_op jit(solution)/shard_map/ppermute | solution.py:399
  141.2 25.6 %collective-permute-start.21 = (bf16[768,768]{1,0:T(8,128)(2,1)S(1)}, bf16[768,768]{1,0:T(8,128)(2,1)S(1)}, u32[]{:S(2)}, u32[]{:S(2)}) collective-permute-start(bf16[768,768]{1,0:T(8,128)(2,1)S(1)} %collective-permute-done.14.refs_1_.refs_10_), channel_id=1, source_target_pairs={{0,1},{1,0},{2,3},{3,2},{4,5},{5,4},{6,7},{7,6},{8,9},{9,8},{10,11... | collective-permute-start | bytes 3538952 | tf_op jit(solution)/shard_map/ppermute | solution.py:366
  166.8 9.5 %copy-start.13 = (bf16[768,768]{1,0:T(8,128)(2,1)}, bf16[768,768]{1,0:T(8,128)(2,1)S(1)}, u32[]{:S(2)}) copy-start(bf16[768,768]{1,0:T(8,128)(2,1)S(1)} %collective-permute-done.18.refs_1_.refs_18_) | copy-start | bytes 3538948
  166.8 9.4 %copy-start.12 = (bf16[768,768]{1,0:T(8,128)(2,1)}, bf16[768,768]{1,0:T(8,128)(2,1)S(1)}, u32[]{:S(2)}) copy-start(bf16[768,768]{1,0:T(8,128)(2,1)S(1)} %collective-permute-done.21.refs_3_.refs_12_) | copy-start | bytes 3538948
  166.8 30.0 %collective-permute-start.24 = (bf16[768,768]{1,0:T(8,128)(2,1)}, bf16[768,768]{1,0:T(8,128)(2,1)}, u32[]{:S(2)}, u32[]{:S(2)}) collective-permute-start(bf16[768,768]{1,0:T(8,128)(2,1)} %get-tuple-element.72), channel_id=1, source_target_pairs={{8,24},{12,28},{16,0},{20,4},{0,8},{4,12},{24,16},{28,20},{9,25},{... | collective-permute-start | bytes 3538952 | tf_op jit(solution)/shard_map/ppermute | solution.py:399
  169.9 27.0 %collective-permute-start.22 = (bf16[768,768]{1,0:T(8,128)(2,1)S(1)}, bf16[768,768]{1,0:T(8,128)(2,1)}, u32[]{:S(2)}, u32[]{:S(2)}) collective-permute-start(bf16[768,768]{1,0:T(8,128)(2,1)S(1)} %get-tuple-element.77.refs_4_.refs_13_), channel_id=1, source_target_pairs={{0,4},{4,0},{8,12},{12,8},{16,20},{20,16},{24,28},{28,24},{1,5},{5... | collective-permute-start | bytes 3538952 | tf_op jit(solution)/shard_map/ppermute | solution.py:363
  170.0 26.8 %collective-permute-start.23 = (bf16[768,768]{1,0:T(8,128)(2,1)S(1)}, bf16[768,768]{1,0:T(8,128)(2,1)}, u32[]{:S(2)}, u32[]{:S(2)}) collective-permute-start(bf16[768,768]{1,0:T(8,128)(2,1)S(1)} %get-tuple-element.77.refs_4_.refs_13_), channel_id=1, source_target_pairs={{0,2},{1,3},{2,0},{3,1},{4,6},{5,7},{6,4},{7,5},{8,10},{9,11},{10,... | collective-permute-start | bytes 3538952 | tf_op jit(solution)/shard_map/ppermute | solution.py:366
  170.5 26.4 %collective-permute-start.25 = (bf16[768,768]{1,0:T(8,128)(2,1)}, bf16[768,768]{1,0:T(8,128)(2,1)}, u32[]{:S(2)}, u32[]{:S(2)}) collective-permute-start(bf16[768,768]{1,0:T(8,128)(2,1)} %collective-permute-done.13.refs_0_.refs_17_), channel_id=1, source_target_pairs={{0,1},{1,0},{2,3},{3,2},{4,5},{5,4},{6,7},{7,6},{8,9},{9,8},{10,11... | collective-permute-start | bytes 3538952 | tf_op jit(solution)/shard_map/ppermute | solution.py:366
  170.5 26.4 %collective-permute-start.26 = (bf16[768,768]{1,0:T(8,128)(2,1)S(1)}, bf16[768,768]{1,0:T(8,128)(2,1)}, u32[]{:S(2)}, u32[]{:S(2)}) collective-permute-start(bf16[768,768]{1,0:T(8,128)(2,1)S(1)} %collective-permute-done.18.refs_1_.refs_18_), channel_id=1, source_target_pairs={{0,1},{1,0},{2,3},{3,2},{4,5},{5,4},{6,7},{7,6},{8,9},{9,8},{10,11... | collective-permute-start | bytes 3538952 | tf_op jit(solution)/shard_map/ppermute | solution.py:366
  196.9 32.6 %collective-permute-start.27 = (bf16[768,768]{1,0:T(8,128)(2,1)}, bf16[768,768]{1,0:T(8,128)(2,1)}, u32[]{:S(2)}, u32[]{:S(2)}) collective-permute-start(bf16[768,768]{1,0:T(8,128)(2,1)} %collective-permute-done.22.refs_4_.refs_21_), channel_id=1, source_target_pairs={{0,2},{1,3},{2,0},{3,1},{4,6},{5,7},{6,4},{7,5},{8,10},{9,11},{10,... | collective-permute-start | bytes 3538952 | tf_op jit(solution)/shard_map/ppermute | solution.py:366
  198.5 30.9 %collective-permute-start.29 = (bf16[768,768]{1,0:T(8,128)(2,1)S(1)}, bf16[768,768]{1,0:T(8,128)(2,1)S(1)}, u32[]{:S(2)}, u32[]{:S(2)}) collective-permute-start(bf16[768,768]{1,0:T(8,128)(2,1)S(1)} %get-tuple-element.77.refs_4_.refs_13_), channel_id=1, source_target_pairs={{0,1},{1,0},{2,3},{3,2},{4,5},{5,4},{6,7},{7,6},{8,9},{9,8},{10,11... | collective-permute-start | bytes 3538952 | tf_op jit(solution)/shard_map/ppermute | solution.py:366
  198.5 30.9 %collective-permute-start.30 = (bf16[768,768]{1,0:T(8,128)(2,1)}, bf16[768,768]{1,0:T(8,128)(2,1)}, u32[]{:S(2)}, u32[]{:S(2)}) collective-permute-start(bf16[768,768]{1,0:T(8,128)(2,1)} %collective-permute-done.22.refs_4_.refs_21_), channel_id=1, source_target_pairs={{0,1},{1,0},{2,3},{3,2},{4,5},{5,4},{6,7},{7,6},{8,9},{9,8},{10,11... | collective-permute-start | bytes 3538952 | tf_op jit(solution)/shard_map/ppermute | solution.py:366
  199.0 30.4 %collective-permute-start.31 = (bf16[768,768]{1,0:T(8,128)(2,1)}, bf16[768,768]{1,0:T(8,128)(2,1)S(1)}, u32[]{:S(2)}, u32[]{:S(2)}) collective-permute-start(bf16[768,768]{1,0:T(8,128)(2,1)} %collective-permute-done.23.refs_5_.refs_14_), channel_id=1, source_target_pairs={{0,1},{1,0},{2,3},{3,2},{4,5},{5,4},{6,7},{7,6},{8,9},{9,8},{10,11... | collective-permute-start | bytes 3538952 | tf_op jit(solution)/shard_map/ppermute | solution.py:366
  199.0 30.4 %collective-permute-start.28 = (bf16[768,512]{1,0:T(8,128)(2,1)}, bf16[768,512]{1,0:T(8,128)(2,1)}, u32[]{:S(2)}, u32[]{:S(2)}) collective-permute-start(bf16[768,512]{1,0:T(8,128)(2,1)} %slice.43), channel_id=1, source_target_pairs={{8,0},{12,4},{16,24},{20,28},{0,16},{4,20},{24,8},{28,12},{9,1},{1... | collective-permute-start | bytes 2359304 | tf_op jit(solution)/shard_map/ppermute | solution.py:399
  213.1 21.4 %copy-start.36 = (s32[8]{0:T(128)S(1)}, s32[8]{0:T(128)}, u32[]{:S(2)}) copy-start(s32[8]{0:T(128)} %param.8) | copy-start | bytes 100
  229.4 6.4 %copy-start.14 = (bf16[768,768]{1,0:T(8,128)(2,1)}, bf16[768,768]{1,0:T(8,128)(2,1)S(1)}, u32[]{:S(2)}) copy-start(bf16[768,768]{1,0:T(8,128)(2,1)S(1)} %collective-permute-done.29.refs_6_.refs_15_) | copy-start | bytes 3538948
  229.5 6.3 %copy-start.15 = (bf16[768,768]{1,0:T(8,128)(2,1)}, bf16[768,768]{1,0:T(8,128)(2,1)S(1)}, u32[]{:S(2)}) copy-start(bf16[768,768]{1,0:T(8,128)(2,1)S(1)} %collective-permute-done.31.refs_7_.refs_16_) | copy-start | bytes 3538948
  229.5 23.2 %collective-permute-start.32 = (bf16[768,512]{1,0:T(8,128)(2,1)}, bf16[768,512]{1,0:T(8,128)(2,1)}, u32[]{:S(2)}, u32[]{:S(2)}) collective-permute-start(bf16[768,512]{1,0:T(8,128)(2,1)} %slice.42), channel_id=1, source_target_pairs={{0,24},{4,28},{24,0},{28,4},{1,25},{5,29},{25,1},{29,5},{2,26},{6,... | collective-permute-start | bytes 2359304 | tf_op jit(solution)/shard_map/ppermute | solution.py:399
  235.2 21.4 %collective-permute-start.33 = (bf16[768,768]{1,0:T(8,128)(2,1)}, bf16[768,768]{1,0:T(8,128)(2,1)S(1)}, u32[]{:S(2)}, u32[]{:S(2)}) collective-permute-start(bf16[768,768]{1,0:T(8,128)(2,1)} %collective-permute-done.27.refs_5_.refs_22_), channel_id=1, source_target_pairs={{0,1},{1,0},{2,3},{3,2},{4,5},{5,4},{6,7},{7,6},{8,9},{9,8},{10,11... | collective-permute-start | bytes 3538952 | tf_op jit(solution)/shard_map/ppermute | solution.py:366
  254.1 6.9 %copy-start.28 = (bf16[768,256]{1,0:T(8,128)(2,1)S(1)}, bf16[768,256]{1,0:T(8,128)(2,1)}, u32[]{:S(2)}) copy-start(bf16[768,256]{1,0:T(8,128)(2,1)} %slice.40) | copy-start | bytes 1179652
  256.6 50.0 %collective-permute-start.35 = (bf16[768,256]{1,0:T(8,128)(2,1)S(1)}, bf16[768,256]{1,0:T(8,128)(2,1)S(1)}, u32[]{:S(2)}, u32[]{:S(2)}) collective-permute-start(bf16[768,256]{1,0:T(8,128)(2,1)S(1)} %copy-done.29), channel_id=1, source_target_pairs={{0,24},{4,28},{24,0},{28,4},{1,25},{5,29},{25,1},{29,5},{2,26},{6,... | collective-permute-start | bytes 1179656 | tf_op jit(solution)/shard_map/ppermute | solution.py:399
  261.0 46.6 %collective-permute-start.34 = (bf16[768,256]{1,0:T(8,128)(2,1)S(1)}, bf16[768,256]{1,0:T(8,128)(2,1)S(1)}, u32[]{:S(2)}, u32[]{:S(2)}) collective-permute-start(bf16[768,256]{1,0:T(8,128)(2,1)S(1)} %copy-done.28), channel_id=1, source_target_pairs={{8,0},{12,4},{16,24},{20,28},{0,16},{4,20},{24,8},{28,12},{9,1},{1... | collective-permute-start | bytes 1179656 | tf_op jit(solution)/shard_map/ppermute | solution.py:399
  295.6 7.9 %collective-permute-start.36 = (f32[2,128,128]{2,1,0:T(8,128)}, f32[2,128,128]{2,1,0:T(8,128)S(1)}, u32[]{:S(2)}, u32[]{:S(2)}) collective-permute-start(f32[2,128,128]{2,1,0:T(8,128)} %get-tuple-element.85), channel_id=1, source_target_pairs={{0,16},{4,20},{8,24},{12,28},{16,0},{20,4},{24,8},{28,12},{1,17},{... | collective-permute-start | bytes 393224 | tf_op jit(solution)/shard_map/ppermute | solution.py:363
  324.1 9.8 %copy-start.35 = (bf16[768,256]{1,0:T(8,128)(2,1)S(1)}, bf16[768,256]{1,0:T(8,128)(2,1)}, u32[]{:S(2)}) copy-start(bf16[768,256]{1,0:T(8,128)(2,1)} %get-tuple-element.88) | copy-start | bytes 1179652
  332.0 22.8 %collective-permute-start.37 = (bf16[768,256]{1,0:T(8,128)(2,1)}, bf16[768,256]{1,0:T(8,128)(2,1)S(1)}, u32[]{:S(2)}, u32[]{:S(2)}) collective-permute-start(bf16[768,256]{1,0:T(8,128)(2,1)} %get-tuple-element.90), channel_id=1, source_target_pairs={{0,4},{4,0},{8,12},{12,8},{16,20},{20,16},{24,28},{28,24},{1,5},{5... | collective-permute-start | bytes 1179656 | tf_op jit(solution)/shard_map/ppermute | solution.py:363
  333.9 20.9 %collective-permute-start.38 = (bf16[768,256]{1,0:T(8,128)(2,1)S(1)}, bf16[768,256]{1,0:T(8,128)(2,1)S(1)}, u32[]{:S(2)}, u32[]{:S(2)}) collective-permute-start(bf16[768,256]{1,0:T(8,128)(2,1)S(1)} %copy-done.35), channel_id=1, source_target_pairs={{0,8},{4,12},{8,0},{12,4},{16,24},{20,28},{24,16},{28,20},{1,9},{5... | collective-permute-start | bytes 1179656 | tf_op jit(solution)/shard_map/ppermute | solution.py:363
  334.9 12.0 %collective-permute-start.42 = (f32[1,768]{1,0:T(1,128)S(1)}, f32[1,768]{1,0:T(1,128)S(1)}, u32[]{:S(2)}, u32[]{:S(2)}) collective-permute-start(f32[1,768]{1,0:T(1,128)S(1)} %slice.38), channel_id=1, source_target_pairs={{0,4},{4,0},{8,12},{12,8},{16,20},{20,16},{24,28},{28,24},{1,5},{5... | collective-permute-start | bytes 9224 | tf_op jit(solution)/shard_map/ppermute | solution.py:363
  335.9 12.5 %collective-permute-start.41 = (f32[1,768]{1,0:T(1,128)S(1)}, f32[1,768]{1,0:T(1,128)S(1)}, u32[]{:S(2)}, u32[]{:S(2)}) collective-permute-start(f32[1,768]{1,0:T(1,128)S(1)} %slice.37), channel_id=1, source_target_pairs={{0,8},{4,12},{8,0},{12,4},{16,24},{20,28},{24,16},{28,20},{1,9},{5... | collective-permute-start | bytes 9224 | tf_op jit(solution)/shard_map/ppermute | solution.py:363
  338.3 8.6 %copy-start.34 = (bf16[768,256]{1,0:T(8,128)(2,1)S(1)}, bf16[768,256]{1,0:T(8,128)(2,1)}, u32[]{:S(2)}) copy-start(bf16[768,256]{1,0:T(8,128)(2,1)} %get-tuple-element.86) | copy-start | bytes 1179652
  338.3 14.4 %copy-start.33 = (bf16[1024]{0:T(1024)(128)(2,1)S(1)}, bf16[1024]{0:T(1024)(128)(2,1)}, u32[]{:S(2)}) copy-start(bf16[1024]{0:T(1024)(128)(2,1)} %param.9) | copy-start | bytes 6148
  338.3 10.0 %collective-permute-start.40 = (f32[1,768]{1,0:T(1,128)S(1)}, f32[1,768]{1,0:T(1,128)S(1)}, u32[]{:S(2)}, u32[]{:S(2)}) collective-permute-start(f32[1,768]{1,0:T(1,128)S(1)} %slice.36), channel_id=1, source_target_pairs={{0,12},{4,8},{8,4},{12,0},{16,28},{20,24},{24,20},{28,16},{1,13},{... | collective-permute-start | bytes 9224 | tf_op jit(solution)/shard_map/ppermute | solution.py:363
  346.9 8.7 %collective-permute-start.39 = (bf16[768,256]{1,0:T(8,128)(2,1)S(1)}, bf16[768,256]{1,0:T(8,128)(2,1)S(1)}, u32[]{:S(2)}, u32[]{:S(2)}) collective-permute-start(bf16[768,256]{1,0:T(8,128)(2,1)S(1)} %copy-done.34), channel_id=1, source_target_pairs={{0,12},{4,8},{8,4},{12,0},{16,28},{20,24},{24,20},{28,16},{1,13},{... | collective-permute-start | bytes 1179656 | tf_op jit(solution)/shard_map/ppermute | solution.py:363
  349.1 3.6 collective-permute-start.43
  352.7 1.2 collective-permute-start.44
  (18 other events, 39.6 us)

commit v3 on v0

--- a/solution.py
+++ b/solution.py
@@ -1,14 +1,521 @@
+import functools
+
 import jax
 import jax.numpy as jnp
 from jax import lax
+from jax.experimental import pallas as pl
+from jax.experimental.pallas import tpu as pltpu
 from jax.sharding import PartitionSpec as P
+
+MEMBERS = 4
+VMEM = 60 * 1024 * 1024
+VMEM_SMALL = 16 * 1024 * 1024
 
 
 def doc_index(positions, doc_ends):
     return jnp.sum((positions[:, None] >= doc_ends[None, :]).astype(jnp.int32), axis=1)
 
 
-def shards(tokens, w_query, w_keyval, doc_lengths, norm_gain):
+def silu(v):
+    return v / (1.0 + jnp.exp(-v))
+
+
+def params(limit=VMEM):
+    return pltpu.CompilerParams(vmem_limit_bytes=limit)
+
+
+def accumulate(step, ranges, t_refs, w_refs, total, start_refs):
+    edges, at = [], 0
+    for ref in t_refs:
+        edges.append((at, at + ref.shape[0]))
+        at += ref.shape[0]
+
+    @pl.when(step == 0)
+    def _():
+        at = 0
+        for ref in start_refs:
+            total[at : at + ref.shape[0], :] = ref[...]
+            at += ref.shape[0]
+        if at < total.shape[0]:
+            total[at:, :] = jnp.zeros((total.shape[0] - at, total.shape[1]), jnp.float32)
+
+    def run(w_ref, low, high):
+        chosen = [r[...] for r, (a, b) in zip(t_refs, edges) if low <= a and b <= high]
+        lhs = jnp.concatenate(chosen, axis=0) if len(chosen) > 1 else chosen[0]
+        total[low:high, :] += jnp.dot(lhs, w_ref[...], preferred_element_type=jnp.float32)
+
+    for w_ref, (first, end, low, high) in zip(w_refs, ranges):
+        pl.when((step >= first) & (step < end))(functools.partial(run, w_ref, low, high))
+
+
+def project_body(ranges, starts, *refs):
+    k_ref, refs = refs[0], refs[1:]
+    arrays = len(ranges)
+    parts = len(refs) - arrays - starts - 1
+    t_refs, w_refs, refs = refs[:parts], refs[parts : parts + arrays], refs[parts + arrays :]
+    accumulate(pl.program_id(0), ranges, t_refs, w_refs, refs[-1], refs[:starts])
+
+
+def settle(places, fsdp_size, where_ref, t_refs, total, out_ref):
+    m, f = where_ref[0], where_ref[1]
+    block_rows = out_ref.shape[0] // MEMBERS
+    at = 0
+    for ref, (j, spots) in zip(t_refs, places):
+        rows = ref.shape[0] // len(spots)
+        for e, offset in spots:
+            to = (m ^ j) * block_rows
+            if e is not None:
+                to = to + (f ^ e) * (block_rows // fsdp_size) + offset
+            to = pl.multiple_of(to, 16)
+            out_ref[pl.ds(to, rows), :] = silu(total[at : at + rows, :]).astype(out_ref.dtype)
+            at += rows
+
+
+def activate_body(places, fsdp_size, ranges, starts, where_ref, k_ref, *refs):
+    parts, arrays = len(places), len(ranges)
+    t_refs, w_refs, refs = refs[:parts], refs[parts : parts + arrays], refs[parts + arrays :]
+    start_refs, out_ref, total = refs[:starts], refs[-2], refs[-1]
+    step = pl.program_id(0)
+    accumulate(step, ranges, t_refs, w_refs, total, start_refs)
+
+    @pl.when(step == ranges[-1][1] - 1)
+    def _():
+        settle(places, fsdp_size, where_ref, t_refs, total, out_ref)
+
+
+def keyval_body(places, fsdp_size, ranges, starts, heads, where_ref, k_ref, ends_ref, *refs):
+    parts, arrays = len(places), len(ranges)
+    t_refs, w_refs, refs = refs[:parts], refs[parts : parts + arrays], refs[parts + arrays :]
+    start_refs, (out_ref, tails_ref, state_ref, total) = refs[:starts], refs[starts:]
+    step = pl.program_id(0)
+    accumulate(step, ranges, t_refs, w_refs, total, start_refs)
+
+    @pl.when(step == ranges[-1][1] - 1)
+    def _():
+        settle(places, fsdp_size, where_ref, t_refs, total, out_ref)
+        rows = out_ref.shape[0] // MEMBERS
+        size = out_ref.shape[1] // heads // 2
+        for b in range(MEMBERS):
+            start = (where_ref[2] * MEMBERS + b) * rows
+            last = doc_of_scalar(start + rows - 1, ends_ref)
+            before = doc_of_scalar(start - 1, ends_ref)
+            docs = doc_of(start + lax.broadcasted_iota(jnp.int32, (rows, 1), 0), ends_ref)
+            mask = docs == last
+            kept = jnp.where(before == last, 1.0, 0.0)
+            for h in range(heads):
+                at = 2 * h * size
+                keys = out_ref[b * rows : (b + 1) * rows, at : at + size]
+                keys = jnp.where(mask, keys.astype(jnp.float32), 0.0).astype(keys.dtype)
+                values = out_ref[b * rows : (b + 1) * rows, at + size : at + 2 * size]
+                tail = lax.dot_general(
+                    keys, values, (((0,), (0,)), ((), ())), preferred_element_type=jnp.float32
+                )
+                tails_ref[b, h] = tail
+                state_ref[h] = tail + kept * state_ref[h] if b else tail
+
+
+def part_rows(part, depth):
+    return part.shape[0] * part.shape[1] // (depth * lax.axis_size("seq"))
+
+
+def part_spec(part, depth, block):
+    if part.shape[1] == depth:
+        return pl.BlockSpec((part_rows(part, depth), depth), lambda *a: (block(*a), 0))
+    return pl.BlockSpec((part.shape[0], depth), lambda *a: (0, block(*a)))
+
+
+def project(where, k_blocks, parts, weights, depth, column, width, starts=(), kind="sum", ends=None):
+    counts = [part_rows(p, depth) for p, _ in parts]
+    rows = sum(counts)
+    ranges, spans, steps = [], [None] * len(parts), 0
+    for w, a, b in weights:
+        end = steps + w.shape[0] // depth
+        ranges.append((steps, end, sum(counts[:a]), sum(counts[:b])))
+        for i in range(a, b):
+            spans[i] = (spans[i][0] if spans[i] else steps, end)
+        steps = end
+    in_specs = [
+        part_spec(p, depth, lambda k, kb, *_, s=s: kb[jnp.clip(k, s[0], s[1] - 1)])
+        for (p, _), s in zip(parts, spans)
+    ]
+    in_specs += [
+        pl.BlockSpec(
+            (depth, width),
+            lambda k, *_, r=r, c=column if w.shape[1] > width else 0: (
+                jnp.clip(k - r[0], 0, r[1] - r[0] - 1),
+                c,
+            ),
+        )
+        for (w, _, _), r in zip(weights, ranges)
+    ]
+    in_specs += [
+        pl.BlockSpec((count, width), lambda k, *_, at=at, c=c: (at, c)) for _, at, count, c in starts
+    ]
+    operands = [p for p, _ in parts] + [w for w, _, _ in weights] + [a for a, _, _, _ in starts]
+    whole = pl.BlockSpec((rows, width), lambda k, *_: (0, 0))
+    scratch = [pltpu.VMEM((rows, width), jnp.float32)]
+    places, fsdp_size = [p for _, p in parts], lax.axis_size("fsdp")
+    if kind == "sum":
+        prefetch, scratch = [k_blocks], []
+        body = functools.partial(project_body, ranges, len(starts))
+        out_specs, out_shape = whole, jax.ShapeDtypeStruct((rows, width), jnp.float32)
+    elif kind == "query":
+        prefetch = [where, k_blocks]
+        body = functools.partial(activate_body, places, fsdp_size, ranges, len(starts))
+        out_specs, out_shape = whole, jax.ShapeDtypeStruct((rows, width), jnp.bfloat16)
+    else:
+        heads, size = kind
+        prefetch = [where, k_blocks, ends]
+        body = functools.partial(keyval_body, places, fsdp_size, ranges, len(starts), heads)
+        out_specs = [
+            whole,
+            pl.BlockSpec((MEMBERS, heads, size, size), lambda k, *_: (0, 0, 0, 0)),
+            pl.BlockSpec((heads, size, size), lambda k, *_: (0, 0, 0)),
+        ]
+        out_shape = [
+            jax.ShapeDtypeStruct((rows, width), jnp.bfloat16),
+            jax.ShapeDtypeStruct((MEMBERS, heads, size, size), jnp.float32),
+            jax.ShapeDtypeStruct((heads, size, size), jnp.float32),
+        ]
+    at = prefetch.index(k_blocks) if kind == "sum" else 1
+    if at:
+        for i, p in enumerate(parts):
+            s = spans[i]
+            in_specs[i] = part_spec(
+                p[0], depth, lambda k, wh, kb, *_, s=s: kb[jnp.clip(k, s[0], s[1] - 1)]
+            )
+    work = sum((r[1] - r[0]) * (r[3] - r[2]) for r in ranges)
+    return pl.pallas_call(
+        body,
+        grid_spec=pltpu.PrefetchScalarGridSpec(
+            num_scalar_prefetch=len(prefetch),
+            grid=(steps,),
+            in_specs=in_specs,
+            out_specs=out_specs,
+            scratch_shapes=scratch,
+        ),
+        out_shape=out_shape,
+        compiler_params=params(),
+        cost_estimate=pl.CostEstimate(
+            flops=2 * work * depth * width,
+            bytes_accessed=2 * depth * (work + steps * width) + 8 * rows * width,
+            transcendentals=0,
+        ),
+    )(*prefetch, *operands)
+
+
+def doc_of(positions, ends_ref):
+    total = jnp.zeros(positions.shape, jnp.int32)
+    for i in range(ends_ref.shape[0]):
+        total += (positions >= ends_ref[i]).astype(jnp.int32)
+    return total
+
+
+def doc_of_scalar(position, ends_ref):
+    total = jnp.int32(0)
+    for i in range(ends_ref.shape[0]):
+        total += (position >= ends_ref[i]).astype(jnp.int32)
+    return total
+
+
+def attend_body(place, cut, where_ref, ends_ref, q_ref, kv_ref, tails_ref, other_ref, out_ref, square_ref):
+    rows, width = q_ref.shape
+    heads, size = other_ref.shape[0], other_ref.shape[1]
+    m, g = where_ref[0], where_ref[2]
+    block = m ^ place
+    origin = g * MEMBERS * rows
+    start = origin + block * rows
+    before = doc_of_scalar(start - 1, ends_ref)
+
+    edge = doc_of_scalar(origin - 1, ends_ref)
+    owner = doc_of_scalar(((g ^ 1) + 1) * MEMBERS * rows - 1, ends_ref)
+    state = jnp.where((g == 1) & (owner == edge), 1.0, 0.0) * other_ref[...]
+    for i in range(MEMBERS - 1):
+        prior = doc_of_scalar(origin + i * rows - 1, ends_ref)
+        ended = doc_of_scalar(origin + (i + 1) * rows - 1, ends_ref)
+        follows = tails_ref[i] + jnp.where(prior == ended, 1.0, 0.0) * state
+        state = jnp.where(i < block, follows, state)
+    incoming = state.astype(jnp.bfloat16)
+
+    row_docs = doc_of(start + lax.broadcasted_iota(jnp.int32, (1, rows), 1), ends_ref)
+    for begin in range(0, rows, cut):
+        seen = begin + cut
+        docs = doc_of(start + begin + lax.broadcasted_iota(jnp.int32, (cut, 1), 0), ends_ref)
+        at = begin + lax.broadcasted_iota(jnp.int32, (cut, seen), 0)
+        behind = lax.broadcasted_iota(jnp.int32, (cut, seen), 1)
+        mask = (at >= behind) & (docs == row_docs[:, :seen])
+        mixed = []
+        for h in range(heads):
+            k_at, v_at = 2 * h * size, (2 * h + 1) * size
+            q = q_ref[begin:seen, h * size : (h + 1) * size]
+            scores = lax.dot_general(
+                q, kv_ref[:seen, k_at : k_at + size], (((1,), (1,)), ((), ())),
+                preferred_element_type=jnp.float32,
+            )
+            weights = jnp.where(mask, scores, 0.0).astype(jnp.bfloat16)
+            within = jnp.dot(
+                weights, kv_ref[:seen, v_at : v_at + size], preferred_element_type=jnp.float32
+            )
+            carried = jnp.dot(q, incoming[h], preferred_element_type=jnp.float32)
+            mixed.append(within + jnp.where(docs == before, carried, 0.0))
+        mixed = jnp.concatenate(mixed, axis=1)
+        out_ref[begin:seen, :] = mixed.astype(out_ref.dtype)
+        sums = lax.dot_general(
+            jnp.ones((8, width), jnp.float32), mixed * mixed, (((1,), (1,)), ((), ())),
+            preferred_element_type=jnp.float32,
+        )
+        square_ref[:, begin:seen] = sums[:1]
+
+
+def attend(where, ends, place, q, kv, tail, other):
+    rows, width = q.shape[0] // MEMBERS, q.shape[1]
+    heads, size = other.shape[0], other.shape[1]
+    cut = rows // 3 if rows % 384 == 0 else rows
+    return pl.pallas_call(
+        functools.partial(attend_body, place, cut),
+        grid_spec=pltpu.PrefetchScalarGridSpec(
+            num_scalar_prefetch=2,
+            grid=(1,),
+            in_specs=[
+                pl.BlockSpec((rows, width), lambda i, wh, en: (wh[0] ^ place, 0)),
+                pl.BlockSpec((rows, kv.shape[1]), lambda i, wh, en: (wh[0] ^ place, 0)),
+                pl.BlockSpec(tail.shape, lambda i, wh, en: (0, 0, 0, 0)),
+                pl.BlockSpec(other.shape, lambda i, wh, en: (0, 0, 0)),
+            ],
+            out_specs=[
+                pl.BlockSpec((rows, width), lambda i, wh, en: (0, 0)),
+                pl.BlockSpec((1, rows), lambda i, wh, en: (0, 0)),
+            ],
+        ),
+        out_shape=[
+            jax.ShapeDtypeStruct((rows, width), jnp.bfloat16),
+            jax.ShapeDtypeStruct((1, rows), jnp.float32),
+        ],
+        compiler_params=params(VMEM_SMALL),
+        cost_estimate=pl.CostEstimate(
+            flops=3 * rows * rows * width + 2 * rows * width * size,
+            bytes_accessed=8 * rows * width,
+            transcendentals=0,
+        ),
+    )(where, ends, q, kv, tail, other)
+
+
+def finish_body(count, where_ref, *refs):
+    squares_ref, gain_ref, out_ref = refs[MEMBERS:]
+    rows, width = refs[0].shape
+    inverse = lax.rsqrt(squares_ref[...] / count + 1e-06)
+    inverse = jnp.transpose(jnp.broadcast_to(inverse, (128, rows)))[:, :1]
+    for k in range(MEMBERS):
+        at = pl.multiple_of((where_ref[0] ^ k) * width, width)
+        gain = gain_ref[:, pl.ds(at, width)].astype(jnp.float32)
+        value = refs[k][...].astype(jnp.float32) * inverse * gain
+        out_ref[:, pl.ds(at, width)] = value.astype(out_ref.dtype)
+
+
+def finish(where, parts, squares, gain, count):
+    rows, width = parts[0].shape
+    cut = rows // 3 if rows % 384 == 0 else rows
+    return pl.pallas_call(
+        functools.partial(finish_body, count),
+        grid_spec=pltpu.PrefetchScalarGridSpec(
+            num_scalar_prefetch=1,
+            grid=(rows // cut,),
+            in_specs=[pl.BlockSpec((cut, width), lambda i, wh: (i, 0)) for _ in parts]
+            + [
+                pl.BlockSpec((1, cut), lambda i, wh: (0, i)),
+                pl.BlockSpec((1, MEMBERS * width), lambda i, wh: (0, 0)),
+            ],
+            out_specs=pl.BlockSpec((cut, MEMBERS * width), lambda i, wh: (i, 0)),
+        ),
+        out_shape=jax.ShapeDtypeStruct((rows, MEMBERS * width), jnp.bfloat16),
+        compiler_params=params(VMEM_SMALL),
+    )(where, *parts, squares, gain)
+
+
+def grouped(seq_size, fsdp_size, tokens, w_query, w_keyval, doc_lengths, norm_gain):
+    rows, model = tokens.shape
+    depth, head_count, size = w_query.shape
+    heads = head_count // MEMBERS
+    s = lax.axis_index("seq")
+    f = lax.axis_index("fsdp")
+    m = lax.rem(s, MEMBERS)
+    g = lax.div(s, MEMBERS)
+    where = jnp.stack([m, f, g]).astype(jnp.int32)
+    doc_ends = jnp.cumsum(doc_lengths)
+
+    inner = ((s >> 1) ^ (s >> 2)) & 1 == 1
+    inner_seq = [i for i in range(seq_size) if ((i >> 1) ^ (i >> 2)) & 1 == 1]
+    outer_seq = [i for i in range(seq_size) if i not in inner_seq]
+
+    def hop(value, k, only=range(seq_size)):
+        return lax.ppermute(value, "seq", [(i, i ^ k) for i in only])
+
+    def side(value, k):
+        return lax.ppermute(value, "fsdp", [(i, i ^ k) for i in range(fsdp_size)])
+
+    q_width, kv_width = heads * size, 2 * heads * size
+    width = kv_width + q_width
+    q_block = kv_width // q_width
+    flat_kv = w_keyval.reshape(depth, head_count * 2 * size)
+    flat_q = w_query.reshape(depth, head_count * size)
+
+    def columns(k):
+        at = m ^ k
+        return jnp.concatenate(
+            [
+                lax.dynamic_slice(flat_kv, (0, at * kv_width), (depth, kv_width)),
+                lax.dynamic_slice(flat_q, (0, at * q_width), (depth, q_width)),
+            ],
+            axis=1,
+        )
+
+    half = rows // fsdp_size // 2
+
+    def own(i):
+        chunk = lax.dynamic_slice(tokens, ((2 * f + i) * half, 0), (half, model))
+        return chunk.reshape(half, seq_size, depth).transpose(1, 0, 2).reshape(-1, depth)
+
+    history = [[], []]
+
+    def stage(extra, ops, ties="chain"):
+        found, before = [], history[-1]
+        for chain, move, operand in ops:
+            waits = list(extra)
+            if ties == "chain":
+                waits += [v for _, v in history[-2]] + [v for c_, v in before if c_ == chain]
+            elif ties == "all":
+                waits += [v for _, v in before]
+            if waits:
+                operand = lax.optimization_barrier((operand, tuple(waits)))[0]
+            found.append((chain, move(operand)))
+        history.append(found)
+        return [v for _, v in found]
+
+    def blocks(ks):
+        return jnp.stack([s ^ k for k in ks]).astype(jnp.int32)
+
+    def pairs(inner_hop, outer_hop):
+        moves = [(i, i ^ inner_hop) for i in inner_seq if inner_hop]
+        moves += [(i, i ^ outer_hop) for i in outer_seq if outer_hop]
+        return lambda value: lax.ppermute(value, "seq", moves)
+
+    def pick(a, b):
+        return jnp.where(inner, a, b)
+
+    def spread(j, first, second):
+        found = []
+        for offset, pieces in ((0, first), (half, second)):
+            found += [(p, (j, [(e, offset)])) for e, p in zip((0, 2, 1, 3), pieces)]
+        return found
+
+    def x(value):
+        return hop(value, 1)
+
+    def y(value):
+        return side(value, 2)
+
+    def c(value):
+        return side(value, 1)
+
+    both_ways = pairs(2, 2)
+    part0 = [(tokens, (0, [(None, 0)]))]
+    own1 = own(0)
+    wb = columns(2)
+    r1, tz1, tx1 = stage([], [("z", pairs(6, 0), wb), ("z", both_ways, own1), ("x", x, own1)])
+    wa, wc, wd, own2 = columns(0), columns(1), columns(3), own(1)
+    in2, in3 = pick(wa, own2), pick(own2, wa)
+    x_first, x_second = pick(wd, wc), pick(wc, wd)
+    r2, tx2, yx1, cx1, cz1 = stage(
+        [x_first, x_second, own2, in2, in3],
+        [("z", pairs(4, 2), in2), ("x", x, own2), ("y", y, tx1), ("c", c, tx1), ("c", c, tz1)],
+    )
+    r3, rx1, yx2, cx2, dx1 = stage(
+        [], [("z", pairs(2, 4), in3), ("x", x, x_first), ("y", y, tx2), ("c", c, tx2), ("c", c, yx1)]
+    )
+    r4, tzx1, yz1, dx2 = stage(
+        [], [("z", pairs(0, 6), wb), ("x", x, tz1), ("y", y, tz1), ("c", c, yx2)]
+    )
+    tz2, w4 = pick(r2, r3), pick(r3, r2)
+    rx1_kv, rx1_q = rx1[:, :kv_width], rx1[:, kv_width:]
+    part1 = spread(1, (tx1, yx1, cx1, dx1), (tx2, yx2, cx2, dx2))
+    r5, z5, rx2, yzx1, dz1 = stage(
+        [tz2, w4, rx1_kv, rx1_q],
+        [("z", pairs(6, 0), rx1), ("z", both_ways, wb), ("x", x, x_second), ("y", y, tzx1), ("c", c, yz1)],
+    )
+    w6 = pick(r1, r4)
+    near = part0 + part1
+    n = len(near)
+    acc_a = project(
+        where, blocks([0, 4, 6]), near, [(w, 0, n) for w in (wa, w4, w6)], depth, 0, width
+    )
+    r6, tzx2, yz2, czx1, dzx1 = stage(
+        [acc_a],
+        [("z", pairs(4, 2), rx2), ("x", x, tz2), ("y", y, tz2), ("c", c, tzx1), ("c", c, yzx1)],
+    )
+    rx2_kv, rx2_q = rx2[:, :kv_width], rx2[:, kv_width:]
+    rxa = pick(rx2, rx1)
+    five, w_five = [0, 4, 6, 1, 2], [wa, w4, w6, rxa, z5]
+    first2 = spread(2, (tz1, yz1, cz1, dz1), [None] * 4)[:4]
+    acc_a = project(
+        where, blocks(five), near + first2,
+        [(w, n, n + 4) for w in w_five[:3]] + [(w, 0, n + 4) for w in w_five[3:]], depth, 0, width,
+        starts=[(acc_a, 0, 2 * rows, 0)],
+    )
+    r7, yzx2, cz2, czx2, dz2 = stage(
+        [acc_a, rx2_kv, rx2_q],
+        [("z", pairs(2, 4), rx1_kv), ("y", y, tzx2), ("c", c, tz2), ("c", c, tzx2), ("c", c, yz2)],
+        "all",
+    )
+    sixth = (s ^ pick(3, 5))[None].astype(jnp.int32)
+    six = jnp.concatenate([blocks(five), sixth])
+    first3 = spread(3, (tzx1, yzx1, czx1, dzx1), [None] * 4)[:4]
+    most = near + first2 + first3
+    acc_b = project(
+        where, six, most, [(w, n + 4, n + 8) for w in w_five] + [(r6, 0, n + 8)], depth, 0, width,
+        starts=[(acc_a, 0, 2 * rows + rows // 2, 0)],
+    )
+    dzx2, r8 = stage([acc_b], [("c", c, yzx2), ("z", pairs(0, 6), rx2_kv)], "all")
+    rest = spread(2, [None] * 4, (tz2, yz2, cz2, dz2))[4:]
+    rest += spread(3, [None] * 4, (tzx2, yzx2, czx2, dzx2))[4:]
+    acc_c = project(where, six, rest, [(w, 0, 8) for w in w_five + [r6]], depth, 0, width)
+    r7q, r8q = stage(
+        [acc_c], [("z", pairs(2, 4), rx1_q), ("z", pairs(0, 6), rx2_q)], ties=None
+    )
+
+    r8 = lax.optimization_barrier((r8, acc_c))[0]
+    every = most + rest
+    last = jnp.stack([s ^ pick(5, 3), s ^ 7]).astype(jnp.int32)
+
+    def finals(column):
+        return [(acc_b, 0, 3 * rows, column), (acc_c, 0, rows, column)]
+
+    keyval, tail, state = project(
+        where, last, every, [(w, 0, len(every)) for w in (r7, pick(r5[:, :kv_width], r8))],
+        depth, 0, kv_width, starts=finals(0), kind=(heads, size), ends=doc_ends,
+    )
+    other = hop(state, MEMBERS)
+    queries = project(
+        where, last, every, [(w, 0, len(every)) for w in (r7q, pick(r5[:, kv_width:], r8q))],
+        depth, 0, q_width, starts=finals(q_block), kind="query",
+    )
+
+    outs, squares, sent = {}, 0.0, []
+    for k in (3, 2, 1, 0):
+        if k == 0:
+            queries = lax.optimization_barrier((queries, sent[0]))[0]
+        outs[k], square = attend(where, doc_ends, k, queries, keyval, tail, other)
+        if k:
+            outs[k], square = hop(outs[k], k), hop(square, k)
+            sent.append(outs[k])
+        squares = squares + square
+    squares = squares + sum(side(squares, k) for k in range(1, fsdp_size))
+    return finish(
+        where, [outs[k] for k in range(MEMBERS)], squares, norm_gain[None, :],
+        head_count * fsdp_size * size,
+    )
+
+
+def plain(tokens, w_query, w_keyval, doc_lengths, norm_gain):
     rows_here = tokens.shape[0]
     head_count = w_query.shape[1]
     head_size = w_query.shape[2]
@@ -63,8 +570,13 @@
 
 
 def solution(mesh):
+    seq_size, fsdp_size = mesh.shape["seq"], mesh.shape["fsdp"]
+    if seq_size == 2 * MEMBERS:
+        body = functools.partial(grouped, seq_size, fsdp_size)
+    else:
+        body = plain
     return jax.shard_map(
-        shards,
+        body,
         mesh=mesh,
         in_specs=(P("seq", None), P("seq", "fsdp", None), P("seq", "fsdp", None), P(), P("fsdp")),
         out_specs=P("seq", "fsdp"),

time: 766 us -> 307 us (0.40)
  waiting for transfers between devices: 659 us -> 99 us
  Pallas kernels: 0 us -> 101 us
  matrix products: 55 us -> 0 us
  starting transfers between devices: 0.08 us -> 53.2 us
  between operations: 13.2 us -> 0.88 us
  other arithmetic: 8.39 us -> 17.4 us
    all_gather x3 -> x0, waiting for transfers between devices: 657 us -> none  [the longest x1 482 us: shards(): keyval_sum = project(lax.all_gather(w_keyval, 'seq', axis=0, tiled=True))]
    pallas_call x0 -> x11, Pallas kernels: none -> 101 us  [the longest x6 88.6 us: project(): pl.pallas_call(body, grid_spec=pltpu.PrefetchScalarGridSpec(num_scalar_pr...]
    ppermute x0 -> x46, waiting for transfers between devices: none -> 99 us  [the longest x12 65.8 us: pairs(): return lambda value: lax.ppermute(value, 'seq', moves)]
    dot_general x5 -> x0, matrix products: 55 us -> none  [the longest x2 40.2 us: project(): return jnp.dot(tokens, panel, preferred_element_type=jnp.float32)]
    ppermute x0 -> x46, starting transfers between devices: none -> 53.2 us  [the longest x12 23 us: pairs(): return lambda value: lax.ppermute(value, 'seq', moves)]
    select_n x0 -> x7, other arithmetic: none -> 13.8 us  [pick(): return jnp.where(inner, a, b)]
    unnamed x11 -> x68, local copies, waits for them, and re-layouts: 20.4 us -> 12.5 us
  transfers between devices with their start and end apart: 3 -> 46, of which waited for: 3 -> 20; matrix products, arithmetic and copies ran while one was open for 10% -> 12% of each run, Pallas kernels for 0% -> 32%
where the time goes in v3:
time: 307 us; the launch traced here: 302 us
  Pallas kernels  101 us (33%)
  waiting for transfers between devices  99 us (32%)
  starting transfers between devices  53.2 us (17%)
  local copies, waits for them, and re-layouts  30.1 us (10%)
  other arithmetic  17.4 us (6%)
    pallas_call x6, Pallas kernels, project(): pl.pallas_call(body, grid_spec=pltpu.PrefetchScalarGridSpec(num_scalar_pr...  88.6 us
    ppermute x12, waiting for transfers between devices, pairs(): return lambda value: lax.ppermute(value, 'seq', moves)  65.8 us
    ppermute x12, starting transfers between devices, pairs(): return lambda value: lax.ppermute(value, 'seq', moves)  23 us
    ppermute x13, waiting for transfers between devices, hop(): return lax.ppermute(value, 'seq', [(i, i ^ k) for i in only])  22.9 us
    ppermute x13, starting transfers between devices, hop(): return lax.ppermute(value, 'seq', [(i, i ^ k) for i in only])  17 us
    select_n x7, other arithmetic, pick(): return jnp.where(inner, a, b)  13.8 us
    ppermute x21, starting transfers between devices, side(): return lax.ppermute(value, 'fsdp', [(i, i ^ k) for i in range(fsdp_size)])  13.2 us
    unnamed x68, local copies, waits for them, and re-layouts  12.5 us
  transfers between devices with their start and end apart: 46, of which 20 were waited for; matrix products, arithmetic and copies ran while one was open for 12% of the time, Pallas kernels for 32%

profile of v3, /device:TPU:0, one launch (start us, length us, event | category | flops | bytes accessed | tf_op | source)
XLA Modules:
  0.0 301.6 jit_solution(14923104385971871968)
XLA Ops:
  0.0 2.8 constant_dynamic-slice_fusion.4
  3.1 1.3 copy.6
  4.3 2.9 collective-permute-start
  7.3 4.7 %copy.9 = bf16[96,8,8,256]{3,1,2,0:T(8,128)(2,1)} copy(bf16[96,8,8,256]{3,2,1,0:T(8,128)(2,1)} %bitcast.43) | data formatting | bytes 6291456
  12.5 3.2 %constant_dynamic-slice_fusion.1 = (bf16[768,512]{1,0:T(8,128)(2,1)S(1)}, bf16[768,512]{1,0:T(8,128)(2,1)S(1)}, bf16[768,512]{1,0:T(8,128)(2,1)}, bf16[768,512]{1,0:T(8,128)(2,1)}) fusion(bf16[768,2048]{1,0:T(8,128)(2,1)} %bitcast.36, s32[]{:T(128)S(6)} %select_n.103, s32[]{:T(128)S(6)} %select_n.99, s32[]{:T(128)S(6)} %select_n.94, s32[]{:T(128)S(6)} %select_n.92), kind=kLoop, calls=%fused_computation.18 | loop fusion | bytes 6291472 | tf_op jit(solution)/shard_map/dynamic_slice | solution.py:366
  17.9 1.7 collective-permute-start.3
  19.6 3.4 %collective-permute-start.4 = (bf16[768,768]{1,0:T(8,128)(2,1)}, bf16[768,768]{1,0:T(8,128)(2,1)}, u32[]{:S(2)}, u32[]{:S(2)}) collective-permute-start(bf16[768,768]{1,0:T(8,128)(2,1)} %bitcast.8), channel_id=1, source_target_pairs={{8,0},{12,4},{16,24},{20,28},{0,8},{4,12},{24,16},{28,20},{9,1},{1... | collective-permute-start | bytes 3538952 | tf_op jit(solution)/shard_map/ppermute | solution.py:400
  24.8 1.5 broadcast_select_fusion.6
  26.3 1.5 broadcast_select_fusion.4
  27.9 5.6 %collective-permute-done.refs_2_.refs_1_ = bf16[768,768]{1,0:T(8,128)(2,1)S(1)} collective-permute-done((bf16[768,768]{1,0:T(8,128)(2,1)}, bf16[768,768]{1,0:T(8,128)(2,1)S(1)}, u32[]{:S(2)}, u32[]{:S(2)}) %collective-permute-start) | collective-permute-done | bytes 1179680 | tf_op jit(solution)/shard_map/ppermute | solution.py:351
  33.4 1.7 collective-permute-start.7
  35.2 13.5 %collective-permute-done.4.refs_10_.refs_9_ = bf16[768,768]{1,0:T(8,128)(2,1)} collective-permute-done((bf16[768,768]{1,0:T(8,128)(2,1)}, bf16[768,768]{1,0:T(8,128)(2,1)}, u32[]{:S(2)}, u32[]{:S(2)}) %collective-permute-start.4) | collective-permute-done | bytes 1179680 | tf_op jit(solution)/shard_map/ppermute | solution.py:400
  48.7 1.7 collective-permute-start.10
  51.0 1.5 collective-permute-start.1
  52.5 8.2 %collective-permute-done.7.refs_6_.refs_5_ = bf16[768,768]{1,0:T(8,128)(2,1)S(1)} collective-permute-done((bf16[768,768]{1,0:T(8,128)(2,1)S(1)}, bf16[768,768]{1,0:T(8,128)(2,1)S(1)}, u32[]{:S(2)}, u32[]{:S(2)}) %collective-permute-start.7) | collective-permute-done | bytes 1179680 | tf_op jit(solution)/shard_map/ppermute | solution.py:351
  60.7 1.4 collective-permute-start.14
  62.1 14.0 %collective-permute-done.10 = bf16[768,768]{1,0:T(8,128)(2,1)S(1)} collective-permute-done((bf16[768,768]{1,0:T(8,128)(2,1)S(1)}, bf16[768,768]{1,0:T(8,128)(2,1)S(1)}, u32[]{:S(2)}, u32[]{:S(2)}) %collective-permute-start.10) | collective-permute-done | bytes 1179680 | tf_op jit(solution)/shard_map/ppermute | solution.py:400
  76.6 2.2 collective-permute-done.1.refs_3_.refs_2_
  78.9 1.5 collective-permute-start.8
  80.9 6.3 %collective-permute-done.14 = bf16[768,768]{1,0:T(8,128)(2,1)} collective-permute-done((bf16[768,768]{1,0:T(8,128)(2,1)S(1)}, bf16[768,768]{1,0:T(8,128)(2,1)}, u32[]{:S(2)}, u32[]{:S(2)}) %collective-permute-start.14) | collective-permute-done | bytes 1179680 | tf_op jit(solution)/shard_map/ppermute | solution.py:351
  87.1 1.1 collective-permute-start.16
  88.3 13.5 %collective-permute-done.13 = bf16[768,768]{1,0:T(8,128)(2,1)S(1)} collective-permute-done((bf16[768,768]{1,0:T(8,128)(2,1)S(1)}, bf16[768,768]{1,0:T(8,128)(2,1)S(1)}, u32[]{:S(2)}, u32[]{:S(2)}) %collective-permute-start.13) | collective-permute-done | bytes 1179680 | tf_op jit(solution)/shard_map/ppermute | solution.py:400
  101.7 4.1 %collective-permute-start.18 = (bf16[768,768]{1,0:T(8,128)(2,1)}, bf16[768,768]{1,0:T(8,128)(2,1)S(1)}, u32[]{:S(2)}, u32[]{:S(2)}) collective-permute-start(bf16[768,768]{1,0:T(8,128)(2,1)} %pad_maximum_fusion.3), channel_id=1, source_target_pairs={{0,24},{4,28},{24,0},{28,4},{1,25},{5,29},{25,1},{29,5},{2,26},{6,... | collective-permute-start | bytes 3538952 | tf_op jit(solution)/shard_map/ppermute | solution.py:400
  106.0 1.5 collective-permute-start.12
  109.6 2.1 slice.24
  111.6 1.8 slice.25
  113.4 1.7 broadcast_select_fusion.2
  115.7 14.7 %collective-permute-done.18 = bf16[768,768]{1,0:T(8,128)(2,1)S(1)} collective-permute-done((bf16[768,768]{1,0:T(8,128)(2,1)}, bf16[768,768]{1,0:T(8,128)(2,1)S(1)}, u32[]{:S(2)}, u32[]{:S(2)}) %collective-permute-start.18) | collective-permute-done | bytes 1179680 | tf_op jit(solution)/shard_map/ppermute | solution.py:400
  130.4 2.0 collective-permute-start.24
  132.5 1.6 collective-permute-start.17
  135.8 2.4 broadcast_select_fusion.1.refs_12_.refs_16_.refs_20_.refs_11_
  138.2 12.4 %shard_map.55.refs_19_ = f32[1536,768]{1,0:T(8,128)} custom-call(s32[3]{0:T(128)} %pad_add_fusion.2.refs_0_, bf16[768,6144]{1,0:T(8,128)(2,1)} %refs_0_.3, bf16[768,768]{1,0:T(8,128)(2,1)} %copy-done.5, bf16[768,768]{1,0:T(8,128)(2,1)} %copy-done.8, bf16[768,768]{1,0:T(8,128)(2,1)} %copy-done.7, bf16[768,768]{1,0:T(8,128)(2,1)} %copy-done.11, ...), custom_call_target="tpu_custom_call" | custom-call | flops 5435817984 | bytes 20054016 | tf_op jit(solution)/shard_map/pallas_call | solution.py:188
  151.3 5.2 %collective-permute-done.23.refs_18_.refs_22_.refs_13_ = bf16[768,768]{1,0:T(8,128)(2,1)} collective-permute-done((bf16[768,768]{1,0:T(8,128)(2,1)}, bf16[768,768]{1,0:T(8,128)(2,1)}, u32[]{:S(2)}, u32[]{:S(2)}) %collective-permute-start.23) | collective-permute-done | bytes 1179680 | tf_op jit(solution)/shard_map/ppermute | solution.py:400
  157.8 1.5 collective-permute-start.21
  160.4 2.1 slice.26
  162.5 1.8 slice.27
  164.3 2.4 broadcast_select_fusion.refs_17_.refs_21_.refs_12_
  166.7 17.1 %shard_map.56.refs_24_ = f32[1920,768]{1,0:T(8,128)} custom-call(s32[5]{0:T(128)} %stack.63.refs_0_, bf16[768,6144]{1,0:T(8,128)(2,1)} %refs_0_.3, bf16[768,768]{1,0:T(8,128)(2,1)} %copy-done.5, bf16[768,768]{1,0:T(8,128)(2,1)} %copy-done.8, bf16[768,768]{1,0:T(8,128)(2,1)} %copy-done.7, bf16[768,768]{1,0:T(8,128)(2,1)} %copy-done.11, ...), custom_call_target="tpu_custom_call" | custom-call | flops 5888802816 | bytes 25362432 | tf_op jit(solution)/shard_map/pallas_call | solution.py:188
  184.7 1.5 collective-permute-start.29
  186.8 1.3 collective-permute-start.31
  188.6 17.7 %shard_map.57.refs_27_ = f32[2304,768]{1,0:T(8,128)} custom-call(s32[6]{0:T(128)} %concatenate.19.refs_0_, bf16[768,6144]{1,0:T(8,128)(2,1)} %refs_0_.3, bf16[768,768]{1,0:T(8,128)(2,1)} %copy-done.5, bf16[768,768]{1,0:T(8,128)(2,1)} %copy-done.8, bf16[768,768]{1,0:T(8,128)(2,1)} %copy-done.7, bf16[768,768]{1,0:T(8,128)(2,1)} %copy-done.11, ...), custom_call_target="tpu_custom_call" | custom-call | flops 4982833152 | bytes 27721728 | tf_op jit(solution)/shard_map/pallas_call | solution.py:188
  207.2 4.9 %collective-permute-done.29.refs_6_.refs_22_ = bf16[768,768]{1,0:T(8,128)(2,1)S(1)} collective-permute-done((bf16[768,768]{1,0:T(8,128)(2,1)}, bf16[768,768]{1,0:T(8,128)(2,1)S(1)}, u32[]{:S(2)}, u32[]{:S(2)}) %collective-permute-start.29) | collective-permute-done | bytes 1179680 | tf_op jit(solution)/shard_map/ppermute | solution.py:354
  212.2 3.6 %collective-permute-start.35 = (bf16[768,512]{1,0:T(8,128)(2,1)}, bf16[768,512]{1,0:T(8,128)(2,1)}, u32[]{:S(2)}, u32[]{:S(2)}) collective-permute-start(bf16[768,512]{1,0:T(8,128)(2,1)} %slice.26), channel_id=1, source_target_pairs={{0,24},{4,28},{24,0},{28,4},{1,25},{5,29},{25,1},{29,5},{2,26},{6,... | collective-permute-start | bytes 2359304 | tf_op jit(solution)/shard_map/ppermute | solution.py:400
  218.8 13.5 %shard_map.58.refs_28_ = f32[768,768]{1,0:T(8,128)} custom-call(s32[6]{0:T(128)} %concatenate.19.refs_0_, bf16[768,768]{1,0:T(8,128)(2,1)} %get-tuple-element.72.refs_1_.refs_17_, bf16[768,768]{1,0:T(8,128)(2,1)} %collective-permute-done.21.refs_2_.refs_18_, bf16[768,768]{1,0:T(8,128)(2,1)} %collective-permute-done.27.refs_3_.refs_19_, ...), custom_call_target="tpu_custom_call" | custom-call | flops 5435817984 | bytes 18874368 | tf_op jit(solution)/shard_map/pallas_call | solution.py:188
  232.3 3.9 %collective-permute-done.35 = bf16[768,512]{1,0:T(8,128)(2,1)} collective-permute-done((bf16[768,512]{1,0:T(8,128)(2,1)}, bf16[768,512]{1,0:T(8,128)(2,1)}, u32[]{:S(2)}, u32[]{:S(2)}) %collective-permute-start.35) | collective-permute-done | bytes 786464 | tf_op jit(solution)/shard_map/ppermute | solution.py:400
  236.1 3.6 %collective-permute-start.34 = (bf16[768,256]{1,0:T(8,128)(2,1)S(1)}, bf16[768,256]{1,0:T(8,128)(2,1)S(1)}, u32[]{:S(2)}, u32[]{:S(2)}) collective-permute-start(bf16[768,256]{1,0:T(8,128)(2,1)S(1)} %copy-done.29), channel_id=1, source_target_pairs={{0,24},{4,28},{24,0},{28,4},{1,25},{5,29},{25,1},{29,5},{2,26},{6,... | collective-permute-start | bytes 1179656 | tf_op jit(solution)/shard_map/ppermute | solution.py:400
  240.0 2.3 slice_select_fusion.refs_26_
  242.4 17.5 %shard_map.60 = (bf16[3072,512]{1,0:T(8,128)(2,1)}, f32[4,2,128,128]{3,2,1,0:T(8,128)}, f32[2,128,128]{2,1,0:T(8,128)}) custom-call(s32[3]{0:T(128)} %pad_add_fusion.where_ref, s32[2]{0:T(128)} %pad_add_fusion.1.k_ref, s32[8]{0:T(128)} %bitcast.31, bf16[768,6144]{1,0:T(8,128)(2,1)} %refs_0_.3, bf16[768,768]{1,0:T(8,128)(2,1)} %copy-done.5, ...), custom_call_target="tpu_custom_call" | custom-call | flops 4831838208 | bytes 23592960 | tf_op jit(solution)/shard_map/pallas_call | solution.py:188
  259.9 2.5 collective-permute-start.36
  262.4 1.8 slice_select_fusion.1.refs_26_
  264.2 10.4 %shard_map.59.q_ref = bf16[3072,256]{1,0:T(8,128)(2,1)} custom-call(s32[3]{0:T(128)} %pad_add_fusion.where_ref, s32[2]{0:T(128)} %pad_add_fusion.1.k_ref, bf16[768,6144]{1,0:T(8,128)(2,1)} %refs_0_.3, bf16[768,768]{1,0:T(8,128)(2,1)} %copy-done.5, bf16[768,768]{1,0:T(8,128)(2,1)} %copy-done.8, bf16[768,768]{1,0:T(8,128)(2,1)} %copy-done.7, ...), custom_call_target="tpu_custom_call" | custom-call | flops 2415919104 | bytes 16515072 | tf_op jit(solution)/shard_map/pallas_call | solution.py:188
  274.7 1.4 copy-done.1
  276.1 2.4 shard_map.61
  278.8 2.4 shard_map.64
  281.2 1.8 collective-permute-start.41
  282.9 2.4 shard_map.63
  285.3 1.5 collective-permute-start.42
  287.1 1.8 collective-permute-start.39
  288.8 1.2 collective-permute-done.37.refs_3_
  290.6 2.4 shard_map.62
  293.7 1.3 collective-permute-start.45
  295.0 1.8 collective-permute-done.44
  296.9 1.5 collective-permute-done.38.refs_1_
  298.4 2.8 shard_map.65
  (133 shorter events, 21.7 us)
Async XLA Ops:
  4.3 29.1 %collective-permute-start = (bf16[768,768]{1,0:T(8,128)(2,1)}, bf16[768,768]{1,0:T(8,128)(2,1)S(1)}, u32[]{:S(2)}, u32[]{:S(2)}) collective-permute-start(bf16[768,768]{1,0:T(8,128)(2,1)} %bitcast.8), channel_id=1, source_target_pairs={{0,4},{4,0},{8,12},{12,8},{16,20},{20,16},{24,28},{28,24},{1,5},{5... | collective-permute-start | bytes 3538952 | tf_op jit(solution)/shard_map/ppermute | solution.py:351
  16.8 6.2 %copy-start.21 = (bf16[96,6144]{1,0:T(8,128)(2,1)S(1)}, bf16[96,6144]{1,0:T(8,128)(2,1)}, u32[]{:S(2)}) copy-start(bf16[96,6144]{1,0:T(8,128)(2,1)} %get-tuple-element.93) | copy-start | bytes 3538948
  17.9 17.3 %collective-permute-start.3 = (bf16[768,768]{1,0:T(8,128)(2,1)}, bf16[768,768]{1,0:T(8,128)(2,1)}, u32[]{:S(2)}, u32[]{:S(2)}) collective-permute-start(bf16[768,768]{1,0:T(8,128)(2,1)} %pad_maximum_fusion.3), channel_id=1, source_target_pairs={{8,16},{12,20},{16,8},{20,12},{9,17},{13,21},{17,9},{21,13},{10,18... | collective-permute-start | bytes 3538952 | tf_op jit(solution)/shard_map/ppermute | solution.py:400
  19.6 29.1 %collective-permute-start.4 = (bf16[768,768]{1,0:T(8,128)(2,1)}, bf16[768,768]{1,0:T(8,128)(2,1)}, u32[]{:S(2)}, u32[]{:S(2)}) collective-permute-start(bf16[768,768]{1,0:T(8,128)(2,1)} %bitcast.8), channel_id=1, source_target_pairs={{8,0},{12,4},{16,24},{20,28},{0,8},{4,12},{24,16},{28,20},{9,1},{1... | collective-permute-start | bytes 3538952 | tf_op jit(solution)/shard_map/ppermute | solution.py:400
  33.4 80.0 %copy-start.5 = (bf16[768,768]{1,0:T(8,128)(2,1)}, bf16[768,768]{1,0:T(8,128)(2,1)S(1)}, u32[]{:S(2)}) copy-start(bf16[768,768]{1,0:T(8,128)(2,1)S(1)} %collective-permute-done.refs_2_.refs_1_) | copy-start | bytes 3538948
  33.4 27.3 %collective-permute-start.7 = (bf16[768,768]{1,0:T(8,128)(2,1)S(1)}, bf16[768,768]{1,0:T(8,128)(2,1)S(1)}, u32[]{:S(2)}, u32[]{:S(2)}) collective-permute-start(bf16[768,768]{1,0:T(8,128)(2,1)S(1)} %bitcast.42), channel_id=1, source_target_pairs={{0,4},{4,0},{8,12},{12,8},{16,20},{20,16},{24,28},{28,24},{1,5},{5... | collective-permute-start | bytes 3538952 | tf_op jit(solution)/shard_map/ppermute | solution.py:351
  48.7 27.4 %collective-permute-start.10 = (bf16[768,768]{1,0:T(8,128)(2,1)S(1)}, bf16[768,768]{1,0:T(8,128)(2,1)S(1)}, u32[]{:S(2)}, u32[]{:S(2)}) collective-permute-start(bf16[768,768]{1,0:T(8,128)(2,1)S(1)} %get-tuple-element.55), channel_id=1, source_target_pairs={{8,24},{12,28},{16,0},{20,4},{0,8},{4,12},{24,16},{28,20},{9,25},{... | collective-permute-start | bytes 3538952 | tf_op jit(solution)/shard_map/ppermute | solution.py:400
  50.5 26.2 %collective-permute-start.5 = (bf16[768,768]{1,0:T(8,128)(2,1)}, bf16[768,768]{1,0:T(8,128)(2,1)S(1)}, u32[]{:S(2)}, u32[]{:S(2)}) collective-permute-start(bf16[768,768]{1,0:T(8,128)(2,1)} %collective-permute-done.4.refs_10_.refs_9_), channel_id=1, source_target_pairs={{0,1},{1,0},{2,3},{3,2},{4,5},{5,4},{6,7},{7,6},{8,9},{9,8},{10,11... | collective-permute-start | bytes 3538952 | tf_op jit(solution)/shard_map/ppermute | solution.py:354
  50.5 26.2 %collective-permute-start.2 = (bf16[768,768]{1,0:T(8,128)(2,1)S(1)}, bf16[768,768]{1,0:T(8,128)(2,1)S(1)}, u32[]{:S(2)}, u32[]{:S(2)}) collective-permute-start(bf16[768,768]{1,0:T(8,128)(2,1)S(1)} %collective-permute-done.refs_2_.refs_1_), channel_id=1, source_target_pairs={{0,1},{1,0},{2,3},{3,2},{4,5},{5,4},{6,7},{7,6},{8,9},{9,8},{10,11... | collective-permute-start | bytes 3538952 | tf_op jit(solution)/shard_map/ppermute | solution.py:354
  51.0 27.9 %collective-permute-start.1 = (bf16[768,768]{1,0:T(8,128)(2,1)S(1)}, bf16[768,768]{1,0:T(8,128)(2,1)S(1)}, u32[]{:S(2)}, u32[]{:S(2)}) collective-permute-start(bf16[768,768]{1,0:T(8,128)(2,1)S(1)} %collective-permute-done.refs_2_.refs_1_), channel_id=1, source_target_pairs={{0,2},{1,3},{2,0},{3,1},{4,6},{5,7},{6,4},{7,5},{8,10},{9,11},{10,... | collective-permute-start | bytes 3538952 | tf_op jit(solution)/shard_map/ppermute | solution.py:354
  60.7 52.7 %copy-start.6 = (bf16[768,768]{1,0:T(8,128)(2,1)}, bf16[768,768]{1,0:T(8,128)(2,1)S(1)}, u32[]{:S(2)}) copy-start(bf16[768,768]{1,0:T(8,128)(2,1)S(1)} %collective-permute-done.7.refs_6_.refs_5_) | copy-start | bytes 3538948
  60.7 26.4 %collective-permute-start.14 = (bf16[768,768]{1,0:T(8,128)(2,1)S(1)}, bf16[768,768]{1,0:T(8,128)(2,1)}, u32[]{:S(2)}, u32[]{:S(2)}) collective-permute-start(bf16[768,768]{1,0:T(8,128)(2,1)S(1)} %get-tuple-element.59), channel_id=1, source_target_pairs={{0,4},{4,0},{8,12},{12,8},{16,20},{20,16},{24,28},{28,24},{1,5},{5... | collective-permute-start | bytes 3538952 | tf_op jit(solution)/shard_map/ppermute | solution.py:351
  76.1 25.6 %collective-permute-start.13 = (bf16[768,768]{1,0:T(8,128)(2,1)S(1)}, bf16[768,768]{1,0:T(8,128)(2,1)S(1)}, u32[]{:S(2)}, u32[]{:S(2)}) collective-permute-start(bf16[768,768]{1,0:T(8,128)(2,1)S(1)} %get-tuple-element.58), channel_id=1, source_target_pairs={{8,0},{12,4},{16,24},{20,28},{0,16},{4,20},{24,8},{28,12},{9,1},{1... | collective-permute-start | bytes 3538952 | tf_op jit(solution)/shard_map/ppermute | solution.py:400
  76.6 38.5 %copy-start.7 = (bf16[768,768]{1,0:T(8,128)(2,1)}, bf16[768,768]{1,0:T(8,128)(2,1)S(1)}, u32[]{:S(2)}) copy-start(bf16[768,768]{1,0:T(8,128)(2,1)S(1)} %collective-permute-done.2.refs_4_.refs_3_) | copy-start | bytes 3538948
  78.9 28.7 %copy-start.8 = (bf16[768,768]{1,0:T(8,128)(2,1)}, bf16[768,768]{1,0:T(8,128)(2,1)S(1)}, u32[]{:S(2)}) copy-start(bf16[768,768]{1,0:T(8,128)(2,1)S(1)} %collective-permute-done.1.refs_3_.refs_2_) | copy-start | bytes 3538948
  78.9 27.1 %collective-permute-start.8 = (bf16[768,768]{1,0:T(8,128)(2,1)S(1)}, bf16[768,768]{1,0:T(8,128)(2,1)S(1)}, u32[]{:S(2)}, u32[]{:S(2)}) collective-permute-start(bf16[768,768]{1,0:T(8,128)(2,1)S(1)} %collective-permute-done.7.refs_6_.refs_5_), channel_id=1, source_target_pairs={{0,2},{1,3},{2,0},{3,1},{4,6},{5,7},{6,4},{7,5},{8,10},{9,11},{10,... | collective-permute-start | bytes 3538952 | tf_op jit(solution)/shard_map/ppermute | solution.py:354
  80.4 27.1 %collective-permute-start.9 = (bf16[768,768]{1,0:T(8,128)(2,1)S(1)}, bf16[768,768]{1,0:T(8,128)(2,1)S(1)}, u32[]{:S(2)}, u32[]{:S(2)}) collective-permute-start(bf16[768,768]{1,0:T(8,128)(2,1)S(1)} %collective-permute-done.7.refs_6_.refs_5_), channel_id=1, source_target_pairs={{0,1},{1,0},{2,3},{3,2},{4,5},{5,4},{6,7},{7,6},{8,9},{9,8},{10,11... | collective-permute-start | bytes 3538952 | tf_op jit(solution)/shard_map/ppermute | solution.py:354
  80.4 27.1 %collective-permute-start.6 = (bf16[768,768]{1,0:T(8,128)(2,1)S(1)}, bf16[768,768]{1,0:T(8,128)(2,1)S(1)}, u32[]{:S(2)}, u32[]{:S(2)}) collective-permute-start(bf16[768,768]{1,0:T(8,128)(2,1)S(1)} %collective-permute-done.1.refs_3_.refs_2_), channel_id=1, source_target_pairs={{0,1},{1,0},{2,3},{3,2},{4,5},{5,4},{6,7},{7,6},{8,9},{9,8},{10,11... | collective-permute-start | bytes 3538952 | tf_op jit(solution)/shard_map/ppermute | solution.py:354
  87.1 28.0 %collective-permute-start.16 = (bf16[768,768]{1,0:T(8,128)(2,1)}, bf16[768,768]{1,0:T(8,128)(2,1)S(1)}, u32[]{:S(2)}, u32[]{:S(2)}) collective-permute-start(bf16[768,768]{1,0:T(8,128)(2,1)} %collective-permute-done.4.refs_10_.refs_9_), channel_id=1, source_target_pairs={{0,4},{4,0},{8,12},{12,8},{16,20},{20,16},{24,28},{28,24},{1,5},{5... | collective-permute-start | bytes 3538952 | tf_op jit(solution)/shard_map/ppermute | solution.py:351
  101.7 28.7 %collective-permute-start.18 = (bf16[768,768]{1,0:T(8,128)(2,1)}, bf16[768,768]{1,0:T(8,128)(2,1)S(1)}, u32[]{:S(2)}, u32[]{:S(2)}) collective-permute-start(bf16[768,768]{1,0:T(8,128)(2,1)} %pad_maximum_fusion.3), channel_id=1, source_target_pairs={{0,24},{4,28},{24,0},{28,4},{1,25},{5,29},{25,1},{29,5},{2,26},{6,... | collective-permute-start | bytes 3538952 | tf_op jit(solution)/shard_map/ppermute | solution.py:400
  106.0 9.1 %copy-start.9 = (bf16[768,768]{1,0:T(8,128)(2,1)}, bf16[768,768]{1,0:T(8,128)(2,1)S(1)}, u32[]{:S(2)}) copy-start(bf16[768,768]{1,0:T(8,128)(2,1)S(1)} %collective-permute-done.8.refs_7_.refs_6_) | copy-start | bytes 3538948
  106.0 26.5 %collective-permute-start.12 = (bf16[768,768]{1,0:T(8,128)(2,1)}, bf16[768,768]{1,0:T(8,128)(2,1)}, u32[]{:S(2)}, u32[]{:S(2)}) collective-permute-start(bf16[768,768]{1,0:T(8,128)(2,1)} %collective-permute-done.4.refs_10_.refs_9_), channel_id=1, source_target_pairs={{0,2},{1,3},{2,0},{3,1},{4,6},{5,7},{6,4},{7,5},{8,10},{9,11},{10,... | collective-permute-start | bytes 3538952 | tf_op jit(solution)/shard_map/ppermute | solution.py:354
  109.6 24.5 %collective-permute-start.11 = (bf16[768,768]{1,0:T(8,128)(2,1)S(1)}, bf16[768,768]{1,0:T(8,128)(2,1)S(1)}, u32[]{:S(2)}, u32[]{:S(2)}) collective-permute-start(bf16[768,768]{1,0:T(8,128)(2,1)S(1)} %collective-permute-done.8.refs_7_.refs_6_), channel_id=1, source_target_pairs={{0,1},{1,0},{2,3},{3,2},{4,5},{5,4},{6,7},{7,6},{8,9},{9,8},{10,11... | collective-permute-start | bytes 3538952 | tf_op jit(solution)/shard_map/ppermute | solution.py:354
  115.1 44.2 %copy-start.15 = (bf16[768,768]{1,0:T(8,128)(2,1)}, bf16[768,768]{1,0:T(8,128)(2,1)S(1)}, u32[]{:S(2)}) copy-start(bf16[768,768]{1,0:T(8,128)(2,1)S(1)} %collective-permute-done.16.refs_14_.refs_13_) | copy-start | bytes 3538948
  115.1 35.5 %collective-permute-start.22 = (bf16[768,768]{1,0:T(8,128)(2,1)}, bf16[768,768]{1,0:T(8,128)(2,1)}, u32[]{:S(2)}, u32[]{:S(2)}) collective-permute-start(bf16[768,768]{1,0:T(8,128)(2,1)} %get-tuple-element.67), channel_id=1, source_target_pairs={{0,4},{4,0},{8,12},{12,8},{16,20},{20,16},{24,28},{28,24},{1,5},{5... | collective-permute-start | bytes 3538952 | tf_op jit(solution)/shard_map/ppermute | solution.py:351
  130.4 20.8 %collective-permute-start.24 = (bf16[768,768]{1,0:T(8,128)(2,1)}, bf16[768,768]{1,0:T(8,128)(2,1)}, u32[]{:S(2)}, u32[]{:S(2)}) collective-permute-start(bf16[768,768]{1,0:T(8,128)(2,1)} %collective-permute-done.14), channel_id=1, source_target_pairs={{8,16},{12,20},{16,8},{20,12},{9,17},{13,21},{17,9},{21,13},{10,18... | collective-permute-start | bytes 3538952 | tf_op jit(solution)/shard_map/ppermute | solution.py:400
  132.4 24.1 %collective-permute-start.23 = (bf16[768,768]{1,0:T(8,128)(2,1)}, bf16[768,768]{1,0:T(8,128)(2,1)}, u32[]{:S(2)}, u32[]{:S(2)}) collective-permute-start(bf16[768,768]{1,0:T(8,128)(2,1)} %pad_maximum_fusion.3), channel_id=1, source_target_pairs={{8,0},{12,4},{16,24},{20,28},{0,8},{4,12},{24,16},{28,20},{9,1},{1... | collective-permute-start | bytes 3538952 | tf_op jit(solution)/shard_map/ppermute | solution.py:400
  132.5 25.3 %collective-permute-start.17 = (bf16[768,768]{1,0:T(8,128)(2,1)S(1)}, bf16[768,768]{1,0:T(8,128)(2,1)S(1)}, u32[]{:S(2)}, u32[]{:S(2)}) collective-permute-start(bf16[768,768]{1,0:T(8,128)(2,1)S(1)} %collective-permute-done.16.refs_14_.refs_13_), channel_id=1, source_target_pairs={{0,2},{1,3},{2,0},{3,1},{4,6},{5,7},{6,4},{7,5},{8,10},{9,11},{10,... | collective-permute-start | bytes 3538952 | tf_op jit(solution)/shard_map/ppermute | solution.py:354
  135.1 24.2 %collective-permute-start.15 = (bf16[768,768]{1,0:T(8,128)(2,1)}, bf16[768,768]{1,0:T(8,128)(2,1)S(1)}, u32[]{:S(2)}, u32[]{:S(2)}) collective-permute-start(bf16[768,768]{1,0:T(8,128)(2,1)} %collective-permute-done.12.refs_11_.refs_10_), channel_id=1, source_target_pairs={{0,1},{1,0},{2,3},{3,2},{4,5},{5,4},{6,7},{7,6},{8,9},{9,8},{10,11... | collective-permute-start | bytes 3538952 | tf_op jit(solution)/shard_map/ppermute | solution.py:354
  150.7 33.2 %collective-permute-start.26 = (bf16[768,768]{1,0:T(8,128)(2,1)}, bf16[768,768]{1,0:T(8,128)(2,1)}, u32[]{:S(2)}, u32[]{:S(2)}) collective-permute-start(bf16[768,768]{1,0:T(8,128)(2,1)} %get-tuple-element.72.refs_1_.refs_17_), channel_id=1, source_target_pairs={{0,4},{4,0},{8,12},{12,8},{16,20},{20,16},{24,28},{28,24},{1,5},{5... | collective-permute-start | bytes 3538952 | tf_op jit(solution)/shard_map/ppermute | solution.py:351
  156.5 27.5 %collective-permute-start.25 = (bf16[768,768]{1,0:T(8,128)(2,1)}, bf16[768,768]{1,0:T(8,128)(2,1)}, u32[]{:S(2)}, u32[]{:S(2)}) collective-permute-start(bf16[768,768]{1,0:T(8,128)(2,1)} %collective-permute-done.22), channel_id=1, source_target_pairs={{8,24},{12,28},{16,0},{20,4},{0,8},{4,12},{24,16},{28,20},{9,25},{... | collective-permute-start | bytes 3538952 | tf_op jit(solution)/shard_map/ppermute | solution.py:400
  157.8 6.5 %copy-start.16 = (bf16[768,768]{1,0:T(8,128)(2,1)}, bf16[768,768]{1,0:T(8,128)(2,1)S(1)}, u32[]{:S(2)}) copy-start(bf16[768,768]{1,0:T(8,128)(2,1)S(1)} %collective-permute-done.17.refs_15_.refs_14_) | copy-start | bytes 3538948
  157.8 26.9 %collective-permute-start.21 = (bf16[768,768]{1,0:T(8,128)(2,1)}, bf16[768,768]{1,0:T(8,128)(2,1)}, u32[]{:S(2)}, u32[]{:S(2)}) collective-permute-start(bf16[768,768]{1,0:T(8,128)(2,1)} %get-tuple-element.72.refs_1_.refs_17_), channel_id=1, source_target_pairs={{0,2},{1,3},{2,0},{3,1},{4,6},{5,7},{6,4},{7,5},{8,10},{9,11},{10,... | collective-permute-start | bytes 3538952 | tf_op jit(solution)/shard_map/ppermute | solution.py:354
  159.3 5.0 %copy-start.14 = (bf16[768,768]{1,0:T(8,128)(2,1)}, bf16[768,768]{1,0:T(8,128)(2,1)S(1)}, u32[]{:S(2)}) copy-start(bf16[768,768]{1,0:T(8,128)(2,1)S(1)} %collective-permute-done.15.refs_13_.refs_12_) | copy-start | bytes 3538948
  159.3 25.4 %collective-permute-start.20 = (bf16[768,768]{1,0:T(8,128)(2,1)S(1)}, bf16[768,768]{1,0:T(8,128)(2,1)}, u32[]{:S(2)}, u32[]{:S(2)}) collective-permute-start(bf16[768,768]{1,0:T(8,128)(2,1)S(1)} %collective-permute-done.17.refs_15_.refs_14_), channel_id=1, source_target_pairs={{0,1},{1,0},{2,3},{3,2},{4,5},{5,4},{6,7},{7,6},{8,9},{9,8},{10,11... | collective-permute-start | bytes 3538952 | tf_op jit(solution)/shard_map/ppermute | solution.py:354
  159.3 25.4 %collective-permute-start.19 = (bf16[768,768]{1,0:T(8,128)(2,1)S(1)}, bf16[768,768]{1,0:T(8,128)(2,1)}, u32[]{:S(2)}, u32[]{:S(2)}) collective-permute-start(bf16[768,768]{1,0:T(8,128)(2,1)S(1)} %collective-permute-done.16.refs_14_.refs_13_), channel_id=1, source_target_pairs={{0,1},{1,0},{2,3},{3,2},{4,5},{5,4},{6,7},{7,6},{8,9},{9,8},{10,11... | collective-permute-start | bytes 3538952 | tf_op jit(solution)/shard_map/ppermute | solution.py:354
  166.7 20.0 %copy-start.17 = (bf16[768,768]{1,0:T(8,128)(2,1)S(1)}, bf16[768,768]{1,0:T(8,128)(2,1)}, u32[]{:S(2)}) copy-start(bf16[768,768]{1,0:T(8,128)(2,1)} %get-tuple-element.72.refs_1_.refs_17_) | copy-start | bytes 3538948
  184.7 27.4 %collective-permute-start.29 = (bf16[768,768]{1,0:T(8,128)(2,1)}, bf16[768,768]{1,0:T(8,128)(2,1)S(1)}, u32[]{:S(2)}, u32[]{:S(2)}) collective-permute-start(bf16[768,768]{1,0:T(8,128)(2,1)} %collective-permute-done.26.refs_5_.refs_21_), channel_id=1, source_target_pairs={{0,2},{1,3},{2,0},{3,1},{4,6},{5,7},{6,4},{7,5},{8,10},{9,11},{10,... | collective-permute-start | bytes 3538952 | tf_op jit(solution)/shard_map/ppermute | solution.py:354
  186.3 25.8 %collective-permute-start.30 = (bf16[768,768]{1,0:T(8,128)(2,1)}, bf16[768,768]{1,0:T(8,128)(2,1)S(1)}, u32[]{:S(2)}, u32[]{:S(2)}) collective-permute-start(bf16[768,768]{1,0:T(8,128)(2,1)} %collective-permute-done.26.refs_5_.refs_21_), channel_id=1, source_target_pairs={{0,1},{1,0},{2,3},{3,2},{4,5},{5,4},{6,7},{7,6},{8,9},{9,8},{10,11... | collective-permute-start | bytes 3538952 | tf_op jit(solution)/shard_map/ppermute | solution.py:354
  186.3 25.8 %collective-permute-start.28 = (bf16[768,768]{1,0:T(8,128)(2,1)}, bf16[768,768]{1,0:T(8,128)(2,1)}, u32[]{:S(2)}, u32[]{:S(2)}) collective-permute-start(bf16[768,768]{1,0:T(8,128)(2,1)} %collective-permute-done.21.refs_2_.refs_18_), channel_id=1, source_target_pairs={{0,1},{1,0},{2,3},{3,2},{4,5},{5,4},{6,7},{7,6},{8,9},{9,8},{10,11... | collective-permute-start | bytes 3538952 | tf_op jit(solution)/shard_map/ppermute | solution.py:354
  186.8 25.3 %collective-permute-start.27 = (bf16[768,768]{1,0:T(8,128)(2,1)S(1)}, bf16[768,768]{1,0:T(8,128)(2,1)}, u32[]{:S(2)}, u32[]{:S(2)}) collective-permute-start(bf16[768,768]{1,0:T(8,128)(2,1)S(1)} %copy-done.17), channel_id=1, source_target_pairs={{0,1},{1,0},{2,3},{3,2},{4,5},{5,4},{6,7},{7,6},{8,9},{9,8},{10,11... | collective-permute-start | bytes 3538952 | tf_op jit(solution)/shard_map/ppermute | solution.py:354
  186.8 20.4 %collective-permute-start.31 = (bf16[768,512]{1,0:T(8,128)(2,1)}, bf16[768,512]{1,0:T(8,128)(2,1)}, u32[]{:S(2)}, u32[]{:S(2)}) collective-permute-start(bf16[768,512]{1,0:T(8,128)(2,1)} %slice.24), channel_id=1, source_target_pairs={{8,0},{12,4},{16,24},{20,28},{0,16},{4,20},{24,8},{28,12},{9,1},{1... | collective-permute-start | bytes 2359304 | tf_op jit(solution)/shard_map/ppermute | solution.py:400
  188.6 27.2 %copy-start.31 = (s32[8]{0:T(128)S(1)}, s32[8]{0:T(128)}, u32[]{:S(2)}) copy-start(s32[8]{0:T(128)} %param.8) | copy-start | bytes 100
  212.1 5.7 %copy-start.18 = (bf16[768,768]{1,0:T(8,128)(2,1)}, bf16[768,768]{1,0:T(8,128)(2,1)S(1)}, u32[]{:S(2)}) copy-start(bf16[768,768]{1,0:T(8,128)(2,1)S(1)} %collective-permute-done.29.refs_6_.refs_22_) | copy-start | bytes 3538948
  212.1 5.7 %copy-start.19 = (bf16[768,768]{1,0:T(8,128)(2,1)}, bf16[768,768]{1,0:T(8,128)(2,1)S(1)}, u32[]{:S(2)}) copy-start(bf16[768,768]{1,0:T(8,128)(2,1)S(1)} %collective-permute-done.30.refs_7_.refs_23_) | copy-start | bytes 3538948
  212.1 5.6 %collective-permute-start.32 = (bf16[768,768]{1,0:T(8,128)(2,1)S(1)}, bf16[768,768]{1,0:T(8,128)(2,1)S(1)}, u32[]{:S(2)}, u32[]{:S(2)}) collective-permute-start(bf16[768,768]{1,0:T(8,128)(2,1)S(1)} %collective-permute-done.29.refs_6_.refs_22_), channel_id=1, source_target_pairs={{0,1},{1,0},{2,3},{3,2},{4,5},{5,4},{6,7},{7,6},{8,9},{9,8},{10,11... | collective-permute-start | bytes 3538952 | tf_op jit(solution)/shard_map/ppermute | solution.py:354
  212.2 23.9 %collective-permute-start.35 = (bf16[768,512]{1,0:T(8,128)(2,1)}, bf16[768,512]{1,0:T(8,128)(2,1)}, u32[]{:S(2)}, u32[]{:S(2)}) collective-permute-start(bf16[768,512]{1,0:T(8,128)(2,1)} %slice.26), channel_id=1, source_target_pairs={{0,24},{4,28},{24,0},{28,4},{1,25},{5,29},{25,1},{29,5},{2,26},{6,... | collective-permute-start | bytes 2359304 | tf_op jit(solution)/shard_map/ppermute | solution.py:400
  217.8 18.4 %copy-start.29 = (bf16[768,256]{1,0:T(8,128)(2,1)S(1)}, bf16[768,256]{1,0:T(8,128)(2,1)}, u32[]{:S(2)}) copy-start(bf16[768,256]{1,0:T(8,128)(2,1)} %slice.27) | copy-start | bytes 1179652
  236.1 26.2 %collective-permute-start.34 = (bf16[768,256]{1,0:T(8,128)(2,1)S(1)}, bf16[768,256]{1,0:T(8,128)(2,1)S(1)}, u32[]{:S(2)}, u32[]{:S(2)}) collective-permute-start(bf16[768,256]{1,0:T(8,128)(2,1)S(1)} %copy-done.29), channel_id=1, source_target_pairs={{0,24},{4,28},{24,0},{28,4},{1,25},{5,29},{25,1},{29,5},{2,26},{6,... | collective-permute-start | bytes 1179656 | tf_op jit(solution)/shard_map/ppermute | solution.py:400
  239.7 24.5 %collective-permute-start.33 = (bf16[768,256]{1,0:T(8,128)(2,1)}, bf16[768,256]{1,0:T(8,128)(2,1)}, u32[]{:S(2)}, u32[]{:S(2)}) collective-permute-start(bf16[768,256]{1,0:T(8,128)(2,1)} %slice.25), channel_id=1, source_target_pairs={{8,0},{12,4},{16,24},{20,28},{0,16},{4,20},{24,8},{28,12},{9,1},{1... | collective-permute-start | bytes 1179656 | tf_op jit(solution)/shard_map/ppermute | solution.py:400
  259.9 14.8 %collective-permute-start.36 = (f32[2,128,128]{2,1,0:T(8,128)}, f32[2,128,128]{2,1,0:T(8,128)S(1)}, u32[]{:S(2)}, u32[]{:S(2)}) collective-permute-start(f32[2,128,128]{2,1,0:T(8,128)} %get-tuple-element.83), channel_id=1, source_target_pairs={{0,16},{4,20},{8,24},{12,28},{16,0},{20,4},{24,8},{28,12},{1,17},{... | collective-permute-start | bytes 393224 | tf_op jit(solution)/shard_map/ppermute | solution.py:351
  264.2 10.5 %copy-start.2 = (f32[4,2,128,128]{3,2,1,0:T(8,128)S(1)}, f32[4,2,128,128]{3,2,1,0:T(8,128)}, u32[]{:S(2)}) copy-start(f32[4,2,128,128]{3,2,1,0:T(8,128)} %get-tuple-element.82.tails_ref) | copy-start | bytes 1572868
  264.2 10.5 %copy-start.3 = (s32[3]{0:T(128)S(1)}, s32[3]{0:T(128)}, u32[]{:S(2)}) copy-start(s32[3]{0:T(128)} %pad_add_fusion.where_ref) | copy-start | bytes 40
  264.2 10.5 %copy-start.4 = (s32[8,1]{0,1:T(1,128)S(1)}, s32[8,1]{0,1:T(1,128)}, u32[]{:S(2)}) copy-start(s32[8,1]{0,1:T(1,128)} %reduce-window.9) | copy-start | bytes 100
  264.2 10.5 %copy-start = (bf16[3072,512]{1,0:T(8,128)(2,1)S(1)}, bf16[3072,512]{1,0:T(8,128)(2,1)}, u32[]{:S(2)}) copy-start(bf16[3072,512]{1,0:T(8,128)(2,1)} %get-tuple-element.81.kv_ref) | copy-start | bytes 9437188
  278.5 11.6 %collective-permute-start.37 = (bf16[768,256]{1,0:T(8,128)(2,1)S(1)}, bf16[768,256]{1,0:T(8,128)(2,1)S(1)}, u32[]{:S(2)}, u32[]{:S(2)}) collective-permute-start(bf16[768,256]{1,0:T(8,128)(2,1)S(1)} %get-tuple-element.84), channel_id=1, source_target_pairs={{0,12},{4,8},{8,4},{12,0},{16,28},{20,24},{24,20},{28,16},{1,13},{... | collective-permute-start | bytes 1179656 | tf_op jit(solution)/shard_map/ppermute | solution.py:351
  281.2 11.9 %collective-permute-start.41 = (f32[1,768]{1,0:T(1,128)S(1)}, f32[1,768]{1,0:T(1,128)S(1)}, u32[]{:S(2)}, u32[]{:S(2)}) collective-permute-start(f32[1,768]{1,0:T(1,128)S(1)} %get-tuple-element.90), channel_id=1, source_target_pairs={{0,8},{4,12},{8,0},{12,4},{16,24},{20,28},{24,16},{28,20},{1,9},{5... | collective-permute-start | bytes 9224 | tf_op jit(solution)/shard_map/ppermute | solution.py:351
  285.3 7.7 %collective-permute-start.42 = (f32[1,768]{1,0:T(1,128)S(1)}, f32[1,768]{1,0:T(1,128)S(1)}, u32[]{:S(2)}, u32[]{:S(2)}) collective-permute-start(f32[1,768]{1,0:T(1,128)S(1)} %get-tuple-element.91), channel_id=1, source_target_pairs={{0,4},{4,0},{8,12},{12,8},{16,20},{20,16},{24,28},{28,24},{1,5},{5... | collective-permute-start | bytes 9224 | tf_op jit(solution)/shard_map/ppermute | solution.py:351
  286.8 6.2 %collective-permute-start.40 = (f32[1,768]{1,0:T(1,128)S(1)}, f32[1,768]{1,0:T(1,128)S(1)}, u32[]{:S(2)}, u32[]{:S(2)}) collective-permute-start(f32[1,768]{1,0:T(1,128)S(1)} %get-tuple-element.89), channel_id=1, source_target_pairs={{0,12},{4,8},{8,4},{12,0},{16,28},{20,24},{24,20},{28,16},{1,13},{... | collective-permute-start | bytes 9224 | tf_op jit(solution)/shard_map/ppermute | solution.py:351
  287.1 9.9 %collective-permute-start.39 = (bf16[768,256]{1,0:T(8,128)(2,1)S(1)}, bf16[768,256]{1,0:T(8,128)(2,1)S(1)}, u32[]{:S(2)}, u32[]{:S(2)}) collective-permute-start(bf16[768,256]{1,0:T(8,128)(2,1)S(1)} %get-tuple-element.88), channel_id=1, source_target_pairs={{0,8},{4,12},{8,0},{12,4},{16,24},{20,28},{24,16},{28,20},{1,9},{5... | collective-permute-start | bytes 1179656 | tf_op jit(solution)/shard_map/ppermute | solution.py:351
  290.1 8.3 %collective-permute-start.38 = (bf16[768,256]{1,0:T(8,128)(2,1)S(1)}, bf16[768,256]{1,0:T(8,128)(2,1)S(1)}, u32[]{:S(2)}, u32[]{:S(2)}) collective-permute-start(bf16[768,256]{1,0:T(8,128)(2,1)S(1)} %get-tuple-element.87), channel_id=1, source_target_pairs={{0,4},{4,0},{8,12},{12,8},{16,20},{20,16},{24,28},{28,24},{1,5},{5... | collective-permute-start | bytes 1179656 | tf_op jit(solution)/shard_map/ppermute | solution.py:351
  293.1 2.0 collective-permute-start.43
  293.1 3.7 %collective-permute-start.44 = (f32[1,768]{1,0:T(1,128)S(1)}, f32[1,768]{1,0:T(1,128)S(1)}, u32[]{:S(2)}, u32[]{:S(2)}) collective-permute-start(f32[1,768]{1,0:T(1,128)S(1)} %add_add_fusion.1), channel_id=1, source_target_pairs={{0,2},{1,3},{2,0},{3,1},{4,6},{5,7},{6,4},{7,5},{8,10},{9,11},{10,... | collective-permute-start | bytes 9224 | tf_op jit(solution)/shard_map/ppermute | solution.py:354
  293.7 3.1 %collective-permute-start.45 = (f32[1,768]{1,0:T(1,128)S(1)}, f32[1,768]{1,0:T(1,128)S(1)}, u32[]{:S(2)}, u32[]{:S(2)}) collective-permute-start(f32[1,768]{1,0:T(1,128)S(1)} %add_add_fusion.1), channel_id=1, source_target_pairs={{0,3},{1,2},{2,1},{3,0},{4,7},{5,6},{6,5},{7,4},{8,11},{9,10},{10,... | collective-permute-start | bytes 9224 | tf_op jit(solution)/shard_map/ppermute | solution.py:354
  (14 other events, 28.1 us)

commit v4 on v3

--- a/solution.py
+++ b/solution.py
@@ -24,7 +24,7 @@
     return pltpu.CompilerParams(vmem_limit_bytes=limit)
 
 
-def accumulate(step, ranges, t_refs, w_refs, total, start_refs):
+def accumulate(step, ranges, t_refs, w_refs, total, start_refs, inner=None):
     edges, at = [], 0
     for ref in t_refs:
         edges.append((at, at + ref.shape[0]))
@@ -44,8 +44,11 @@
         lhs = jnp.concatenate(chosen, axis=0) if len(chosen) > 1 else chosen[0]
         total[low:high, :] += jnp.dot(lhs, w_ref[...], preferred_element_type=jnp.float32)
 
-    for w_ref, (first, end, low, high) in zip(w_refs, ranges):
-        pl.when((step >= first) & (step < end))(functools.partial(run, w_ref, low, high))
+    for w_ref, (first, end, low, high, place) in zip(w_refs, ranges):
+        here = (step >= first) & (step < end)
+        if place is not None:
+            here = here & (inner == place)
+        pl.when(here)(functools.partial(run, w_ref, low, high))
 
 
 def project_body(ranges, starts, *refs):
@@ -76,7 +79,7 @@
     t_refs, w_refs, refs = refs[:parts], refs[parts : parts + arrays], refs[parts + arrays :]
     start_refs, out_ref, total = refs[:starts], refs[-2], refs[-1]
     step = pl.program_id(0)
-    accumulate(step, ranges, t_refs, w_refs, total, start_refs)
+    accumulate(step, ranges, t_refs, w_refs, total, start_refs, where_ref[3])
 
     @pl.when(step == ranges[-1][1] - 1)
     def _():
@@ -88,7 +91,7 @@
     t_refs, w_refs, refs = refs[:parts], refs[parts : parts + arrays], refs[parts + arrays :]
     start_refs, (out_ref, tails_ref, state_ref, total) = refs[:starts], refs[starts:]
     step = pl.program_id(0)
-    accumulate(step, ranges, t_refs, w_refs, total, start_refs)
+    accumulate(step, ranges, t_refs, w_refs, total, start_refs, where_ref[3])
 
     @pl.when(step == ranges[-1][1] - 1)
     def _():
@@ -115,7 +118,7 @@
 
 
 def part_rows(part, depth):
-    return part.shape[0] * part.shape[1] // (depth * lax.axis_size("seq"))
+    return part.shape[-2] * part.shape[-1] // (depth * lax.axis_size("seq"))
 
 
 def part_spec(part, depth, block):
@@ -128,9 +131,14 @@
     counts = [part_rows(p, depth) for p, _ in parts]
     rows = sum(counts)
     ranges, spans, steps = [], [None] * len(parts), 0
+    arrays = []
     for w, a, b in weights:
-        end = steps + w.shape[0] // depth
-        ranges.append((steps, end, sum(counts[:a]), sum(counts[:b])))
+        choices = w if isinstance(w, tuple) else (w,)
+        end = steps + choices[0].shape[0] // depth
+        for place, choice in enumerate(choices):
+            place = place if len(choices) > 1 else None
+            ranges.append((steps, end, sum(counts[:a]), sum(counts[:b]), place))
+            arrays.append(choice)
         for i in range(a, b):
             spans[i] = (spans[i][0] if spans[i] else steps, end)
         steps = end
@@ -146,12 +154,12 @@
                 c,
             ),
         )
-        for (w, _, _), r in zip(weights, ranges)
+        for w, r in zip(arrays, ranges)
     ]
     in_specs += [
         pl.BlockSpec((count, width), lambda k, *_, at=at, c=c: (at, c)) for _, at, count, c in starts
     ]
-    operands = [p for p, _ in parts] + [w for w, _, _ in weights] + [a for a, _, _, _ in starts]
+    operands = [p for p, _ in parts] + arrays + [a for a, _, _, _ in starts]
     whole = pl.BlockSpec((rows, width), lambda k, *_: (0, 0))
     scratch = [pltpu.VMEM((rows, width), jnp.float32)]
     places, fsdp_size = [p for _, p in parts], lax.axis_size("fsdp")
@@ -332,6 +340,82 @@
     )(where, *parts, squares, gain)
 
 
+def stack_columns(out_ref, in_ref):
+    rows, depth = in_ref.shape[0], out_ref.shape[1]
+    for k in range(out_ref.shape[0] // rows):
+        out_ref[k * rows : (k + 1) * rows, :] = in_ref[:, k * depth : (k + 1) * depth]
+
+
+def stacked_body(where_ref, in_ref, out_ref):
+    stack_columns(out_ref, in_ref)
+
+
+def stacked(where, tokens, rows, depth):
+    model = tokens.shape[1]
+    return pl.pallas_call(
+        stacked_body,
+        grid_spec=pltpu.PrefetchScalarGridSpec(
+            num_scalar_prefetch=1,
+            grid=(1,),
+            in_specs=[pl.BlockSpec((rows, model), lambda i, wh: (2 * wh[1], 0))],
+            out_specs=pl.BlockSpec((model // depth * rows, depth), lambda i, wh: (0, 0)),
+        ),
+        out_shape=jax.ShapeDtypeStruct((model // depth * rows, depth), tokens.dtype),
+        compiler_params=params(),
+    )(where, tokens)
+
+
+def pack_body(where_ref, kv_ref, q_ref, tokens_ref, a_ref, b_ref, x1_ref, x2_ref, own_ref, in2_ref, in3_ref):
+    m, inner = where_ref[0], where_ref[3]
+    width = a_ref.shape[1]
+    q_width = q_ref.shape[1] // MEMBERS
+    kv_width = width - q_width
+
+    def put(ref, member):
+        at = pl.multiple_of(member * kv_width, 128)
+        ref[:, :kv_width] = kv_ref[:, pl.ds(at, kv_width)]
+        at = pl.multiple_of(member * q_width, 128)
+        ref[:, kv_width:] = q_ref[:, pl.ds(at, q_width)]
+
+    put(a_ref, m)
+    put(b_ref, m ^ 2)
+    put(x1_ref, m ^ (1 + 2 * inner))
+    put(x2_ref, m ^ (3 - 2 * inner))
+    stack_columns(own_ref, tokens_ref)
+
+    @pl.when(inner == 1)
+    def _():
+        put(in2_ref, m)
+        stack_columns(in3_ref, tokens_ref)
+
+    @pl.when(inner == 0)
+    def _():
+        put(in3_ref, m)
+        stack_columns(in2_ref, tokens_ref)
+
+
+def pack(where, kv, q, tokens, rows):
+    depth = kv.shape[0]
+    width = (kv.shape[1] + q.shape[1]) // MEMBERS
+    whole = lambda shape: pl.BlockSpec(shape, lambda i, wh: (0, 0))
+    piece = jax.ShapeDtypeStruct((depth, width), kv.dtype)
+    return pl.pallas_call(
+        pack_body,
+        grid_spec=pltpu.PrefetchScalarGridSpec(
+            num_scalar_prefetch=1,
+            grid=(1,),
+            in_specs=[
+                whole(kv.shape),
+                whole(q.shape),
+                pl.BlockSpec((rows, tokens.shape[1]), lambda i, wh: (2 * wh[1] + 1, 0)),
+            ],
+            out_specs=[whole((depth, width))] * 7,
+        ),
+        out_shape=[piece] * 7,
+        compiler_params=params(),
+    )(where, kv, q, tokens)
+
+
 def grouped(seq_size, fsdp_size, tokens, w_query, w_keyval, doc_lengths, norm_gain):
     rows, model = tokens.shape
     depth, head_count, size = w_query.shape
@@ -340,10 +424,10 @@
     f = lax.axis_index("fsdp")
     m = lax.rem(s, MEMBERS)
     g = lax.div(s, MEMBERS)
-    where = jnp.stack([m, f, g]).astype(jnp.int32)
     doc_ends = jnp.cumsum(doc_lengths)
 
     inner = ((s >> 1) ^ (s >> 2)) & 1 == 1
+    where = jnp.stack([m, f, g, inner]).astype(jnp.int32)
     inner_seq = [i for i in range(seq_size) if ((i >> 1) ^ (i >> 2)) & 1 == 1]
     outer_seq = [i for i in range(seq_size) if i not in inner_seq]
 
@@ -359,28 +443,15 @@
     flat_kv = w_keyval.reshape(depth, head_count * 2 * size)
     flat_q = w_query.reshape(depth, head_count * size)
 
-    def columns(k):
-        at = m ^ k
-        return jnp.concatenate(
-            [
-                lax.dynamic_slice(flat_kv, (0, at * kv_width), (depth, kv_width)),
-                lax.dynamic_slice(flat_q, (0, at * q_width), (depth, q_width)),
-            ],
-            axis=1,
-        )
-
     half = rows // fsdp_size // 2
-
-    def own(i):
-        chunk = lax.dynamic_slice(tokens, ((2 * f + i) * half, 0), (half, model))
-        return chunk.reshape(half, seq_size, depth).transpose(1, 0, 2).reshape(-1, depth)
 
     history = [[], []]
 
     def stage(extra, ops, ties="chain"):
         found, before = [], history[-1]
         for chain, move, operand in ops:
-            waits = list(extra)
+            waits = [v for v in extra if not isinstance(v, tuple)]
+            waits += [v[1] for v in extra if isinstance(v, tuple) and v[0] == chain]
             if ties == "chain":
                 waits += [v for _, v in history[-2]] + [v for c_, v in before if c_ == chain]
             elif ties == "all":
@@ -391,7 +462,7 @@
         history.append(found)
         return [v for _, v in found]
 
-    def blocks(ks):
+    def blocks(*ks):
         return jnp.stack([s ^ k for k in ks]).astype(jnp.int32)
 
     def pairs(inner_hop, outer_hop):
@@ -419,14 +490,19 @@
 
     both_ways = pairs(2, 2)
     part0 = [(tokens, (0, [(None, 0)]))]
-    own1 = own(0)
-    wb = columns(2)
-    r1, tz1, tx1 = stage([], [("z", pairs(6, 0), wb), ("z", both_ways, own1), ("x", x, own1)])
-    wa, wc, wd, own2 = columns(0), columns(1), columns(3), own(1)
-    in2, in3 = pick(wa, own2), pick(own2, wa)
-    x_first, x_second = pick(wd, wc), pick(wc, wd)
+    own1 = stacked(where, tokens, half, depth)
+    raw = [
+        lax.dynamic_slice(w, (0, (m ^ 2) * heads, 0), (depth, heads, w.shape[2]))
+        for w in (w_keyval, w_query)
+    ]
+    r1_kv, r1_q, tz1, tx1 = stage(
+        [],
+        [("z", pairs(6, 0), raw[0]), ("z", pairs(6, 0), raw[1]), ("z", both_ways, own1), ("x", x, own1)],
+    )
+    wa, wb, x_first, x_second, own2, in2, in3 = pack(where, flat_kv, flat_q, tokens, half)
+    r1 = jnp.concatenate([r1_kv.reshape(depth, -1), r1_q.reshape(depth, -1)], axis=1)
     r2, tx2, yx1, cx1, cz1 = stage(
-        [x_first, x_second, own2, in2, in3],
+        [doc_ends],
         [("z", pairs(4, 2), in2), ("x", x, own2), ("y", y, tx1), ("c", c, tx1), ("c", c, tz1)],
     )
     r3, rx1, yx2, cx2, dx1 = stage(
@@ -446,28 +522,28 @@
     near = part0 + part1
     n = len(near)
     acc_a = project(
-        where, blocks([0, 4, 6]), near, [(w, 0, n) for w in (wa, w4, w6)], depth, 0, width
+        where, blocks(0, 4, 6), near, [(w, 0, n) for w in (wa, w4, w6)], depth, 0, width
     )
     r6, tzx2, yz2, czx1, dzx1 = stage(
         [acc_a],
         [("z", pairs(4, 2), rx2), ("x", x, tz2), ("y", y, tz2), ("c", c, tzx1), ("c", c, yzx1)],
     )
     rx2_kv, rx2_q = rx2[:, :kv_width], rx2[:, kv_width:]
+    r5_q = r5[:, kv_width:]
     rxa = pick(rx2, rx1)
     five, w_five = [0, 4, 6, 1, 2], [wa, w4, w6, rxa, z5]
     first2 = spread(2, (tz1, yz1, cz1, dz1), [None] * 4)[:4]
     acc_a = project(
-        where, blocks(five), near + first2,
+        where, blocks(*five), near + first2,
         [(w, n, n + 4) for w in w_five[:3]] + [(w, 0, n + 4) for w in w_five[3:]], depth, 0, width,
         starts=[(acc_a, 0, 2 * rows, 0)],
     )
     r7, yzx2, cz2, czx2, dz2 = stage(
-        [acc_a, rx2_kv, rx2_q],
+        [acc_a, rx2_kv, rx2_q, r5_q],
         [("z", pairs(2, 4), rx1_kv), ("y", y, tzx2), ("c", c, tz2), ("c", c, tzx2), ("c", c, yz2)],
         "all",
     )
-    sixth = (s ^ pick(3, 5))[None].astype(jnp.int32)
-    six = jnp.concatenate([blocks(five), sixth])
+    six = blocks(*five, pick(3, 5))
     first3 = spread(3, (tzx1, yzx1, czx1, dzx1), [None] * 4)[:4]
     most = near + first2 + first3
     acc_b = project(
@@ -484,18 +560,18 @@
 
     r8 = lax.optimization_barrier((r8, acc_c))[0]
     every = most + rest
-    last = jnp.stack([s ^ pick(5, 3), s ^ 7]).astype(jnp.int32)
+    last = blocks(pick(5, 3), 7)
 
     def finals(column):
         return [(acc_b, 0, 3 * rows, column), (acc_c, 0, rows, column)]
 
     keyval, tail, state = project(
-        where, last, every, [(w, 0, len(every)) for w in (r7, pick(r5[:, :kv_width], r8))],
+        where, last, every, [(w, 0, len(every)) for w in (r7, (r8, r5))],
         depth, 0, kv_width, starts=finals(0), kind=(heads, size), ends=doc_ends,
     )
     other = hop(state, MEMBERS)
     queries = project(
-        where, last, every, [(w, 0, len(every)) for w in (r7q, pick(r5[:, kv_width:], r8q))],
+        where, last, every, [(w, 0, len(every)) for w in (r7q, (r8q, r5_q))],
         depth, 0, q_width, starts=finals(q_block), kind="query",
     )
 

time: 307 us -> 299 us (0.974)
  waiting for transfers between devices: 99 us -> 78 us
  Pallas kernels: 101 us -> 111 us
  other arithmetic: 17.4 us -> 8.19 us
  starting transfers between devices: 53.2 us -> 61.7 us
    ppermute x12 -> x13, waiting for transfers between devices: 65.8 us -> 32.4 us  [pairs(): return lambda value: lax.ppermute(value, 'seq', moves)]
    ppermute x13, waiting for transfers between devices: 22.9 us -> 37 us  [hop(): return lax.ppermute(value, 'seq', [(i, i ^ k) for i in only])]
    pallas_call x0 -> x2, Pallas kernels: none -> 10.3 us  [the longest x1 7.29 us: pack(): pl.pallas_call(pack_body, grid_spec=pltpu.PrefetchScalarGridSpec(num_scal...]
    select_n x7 -> x3, other arithmetic: 13.8 us -> 5.62 us  [pick(): return jnp.where(inner, a, b)]
    ppermute x12 -> x13, starting transfers between devices: 23 us -> 29.8 us  [pairs(): return lambda value: lax.ppermute(value, 'seq', moves)]
    reshape x0 -> x2, local copies, waits for them, and re-layouts: none -> 4.2 us  [the longest x1 2.29 us: grouped(): r1_kv.reshape(depth, -1)]
    unnamed x68 -> x64, local copies, waits for them, and re-layouts: 12.5 us -> 15.7 us
    ppermute x13, starting transfers between devices: 17 us -> 20.1 us  [hop(): return lax.ppermute(value, 'seq', [(i, i ^ k) for i in only])]
  transfers between devices with their start and end apart: 46 -> 47, of which waited for: 20 -> 19; matrix products, arithmetic and copies ran while one was open for 12% -> 12% of each run, Pallas kernels for 32% -> 35%
where the time goes in v4:
time: 299 us; the launch traced here: 293 us
  Pallas kernels  111 us (37%)
  waiting for transfers between devices  78 us (26%)
  starting transfers between devices  61.7 us (21%)
  local copies, waits for them, and re-layouts  33.1 us (11%)
  other arithmetic  8.19 us (3%)
    pallas_call x6, Pallas kernels, project(): pl.pallas_call(body, grid_spec=pltpu.PrefetchScalarGridSpec(num_scalar_pr...  88.7 us
    ppermute x13, waiting for transfers between devices, hop(): return lax.ppermute(value, 'seq', [(i, i ^ k) for i in only])  37 us
    ppermute x13, waiting for transfers between devices, pairs(): return lambda value: lax.ppermute(value, 'seq', moves)  32.4 us
    ppermute x13, starting transfers between devices, pairs(): return lambda value: lax.ppermute(value, 'seq', moves)  29.8 us
    ppermute x13, starting transfers between devices, hop(): return lax.ppermute(value, 'seq', [(i, i ^ k) for i in only])  20.1 us
    unnamed x64, local copies, waits for them, and re-layouts  15.7 us
    ppermute x21, starting transfers between devices, side(): return lax.ppermute(value, 'fsdp', [(i, i ^ k) for i in range(fsdp_size)])  11.9 us
    pallas_call x4, Pallas kernels, attend(): pl.pallas_call(functools.partial(attend_body, place, cut), grid_spec=pltp...  9.59 us
  transfers between devices with their start and end apart: 47, of which 19 were waited for; matrix products, arithmetic and copies ran while one was open for 12% of the time, Pallas kernels for 35%

profile of v4, /device:TPU:0, one launch (start us, length us, event | category | flops | bytes accessed | tf_op | source)
XLA Modules:
  0.0 293.0 jit_solution(6941088458357522552)
XLA Ops:
  0.7 3.0 %shard_map.55 = bf16[768,768]{1,0:T(8,128)(2,1)} custom-call(s32[4]{0:T(128)} %pad_add_fusion.where_ref, bf16[768,6144]{1,0:T(8,128)(2,1)} %refs_0_.3), custom_call_target="tpu_custom_call" | custom-call | tf_op jit(solution)/shard_map/pallas_call | solution.py:355
  3.7 2.9 %collective-permute-start = (bf16[768,768]{1,0:T(8,128)(2,1)}, bf16[768,768]{1,0:T(8,128)(2,1)S(1)}, u32[]{:S(2)}, u32[]{:S(2)}) collective-permute-start(bf16[768,768]{1,0:T(8,128)(2,1)} %shard_map.55), channel_id=1, source_target_pairs={{0,4},{4,0},{8,12},{12,8},{16,20},{20,16},{24,28},{28,24},{1,5},{5... | collective-permute-start | bytes 3538952 | tf_op jit(solution)/shard_map/ppermute | solution.py:435
  6.6 1.6 collective-permute-start.5
  8.2 2.7 constant_dynamic-slice_fusion.1
  10.9 1.8 copy.10
  13.4 1.8 constant_dynamic-slice_fusion
  17.0 4.7 %copy.12 = bf16[96,8,8,256]{3,1,2,0:T(8,128)(2,1)} copy(bf16[96,8,8,256]{3,2,1,0:T(8,128)(2,1)} %bitcast.29) | data formatting | bytes 6291456
  21.8 1.6 copy.15
  24.1 7.3 %shard_map.56 = (bf16[768,768]{1,0:T(8,128)(2,1)}, bf16[768,768]{1,0:T(8,128)(2,1)}, bf16[768,768]{1,0:T(8,128)(2,1)}, bf16[768,768]{1,0:T(8,128)(2,1)}, bf16[76...) custom-call(s32[4]{0:T(128)} %pad_add_fusion.where_ref, bf16[768,2048]{1,0:T(8,128)(2,1)} %bitcast.27, ...), custom_call_target="tpu_custom_call" | custom-call | tf_op jit(solution)/shard_map/pallas_call | solution.py:402
  31.4 1.4 collective-permute-done.refs_2_.refs_1_
  32.8 1.7 collective-permute-start.8
  34.6 8.9 %collective-permute-start.11 = (bf16[768,768]{1,0:T(8,128)(2,1)}, bf16[768,768]{1,0:T(8,128)(2,1)S(1)}, u32[]{:S(2)}, u32[]{:S(2)}) collective-permute-start(bf16[768,768]{1,0:T(8,128)(2,1)} %get-tuple-element.64), channel_id=1, source_target_pairs={{8,24},{12,28},{16,0},{20,4},{0,8},{4,12},{24,16},{28,20},{9,25},{... | collective-permute-start | bytes 3538952 | tf_op jit(solution)/shard_map/ppermute | solution.py:471
  44.0 1.5 collective-permute-start.1
  45.5 14.7 %collective-permute-done.8.refs_6_.refs_5_ = bf16[768,768]{1,0:T(8,128)(2,1)S(1)} collective-permute-done((bf16[768,768]{1,0:T(8,128)(2,1)}, bf16[768,768]{1,0:T(8,128)(2,1)S(1)}, u32[]{:S(2)}, u32[]{:S(2)}) %collective-permute-start.8) | collective-permute-done | bytes 1179680 | tf_op jit(solution)/shard_map/ppermute | solution.py:435
  60.2 1.5 collective-permute-start.15
  61.7 7.7 %collective-permute-done.11 = bf16[768,768]{1,0:T(8,128)(2,1)S(1)} collective-permute-done((bf16[768,768]{1,0:T(8,128)(2,1)}, bf16[768,768]{1,0:T(8,128)(2,1)S(1)}, u32[]{:S(2)}, u32[]{:S(2)}) %collective-permute-start.11) | collective-permute-done | bytes 1179680 | tf_op jit(solution)/shard_map/ppermute | solution.py:471
  69.3 1.7 collective-permute-start.14
  71.9 1.5 collective-permute-start.9
  73.9 12.8 %collective-permute-done.15 = bf16[768,768]{1,0:T(8,128)(2,1)S(1)} collective-permute-done((bf16[768,768]{1,0:T(8,128)(2,1)}, bf16[768,768]{1,0:T(8,128)(2,1)S(1)}, u32[]{:S(2)}, u32[]{:S(2)}) %collective-permute-start.15) | collective-permute-done | bytes 1179680 | tf_op jit(solution)/shard_map/ppermute | solution.py:435
  86.7 1.3 collective-permute-start.17
  88.0 7.1 %collective-permute-done.14 = bf16[768,768]{1,0:T(8,128)(2,1)S(1)} collective-permute-done((bf16[768,768]{1,0:T(8,128)(2,1)}, bf16[768,768]{1,0:T(8,128)(2,1)S(1)}, u32[]{:S(2)}, u32[]{:S(2)}) %collective-permute-start.14) | collective-permute-done | bytes 1179680 | tf_op jit(solution)/shard_map/ppermute | solution.py:471
  95.1 3.7 %collective-permute-start.19 = (bf16[768,768]{1,0:T(8,128)(2,1)}, bf16[768,768]{1,0:T(8,128)(2,1)S(1)}, u32[]{:S(2)}, u32[]{:S(2)}) collective-permute-start(bf16[768,768]{1,0:T(8,128)(2,1)} %get-tuple-element.82), channel_id=1, source_target_pairs={{0,24},{4,28},{24,0},{28,4},{1,25},{5,29},{25,1},{29,5},{2,26},{6,... | collective-permute-start | bytes 3538952 | tf_op jit(solution)/shard_map/ppermute | solution.py:471
  98.9 1.5 collective-permute-start.13
  100.4 1.1 copy-done.10
  104.3 1.6 broadcast_select_fusion.1
  105.8 6.8 %collective-permute-done.17.refs_14_.refs_13_ = bf16[768,768]{1,0:T(8,128)(2,1)} collective-permute-done((bf16[768,768]{1,0:T(8,128)(2,1)S(1)}, bf16[768,768]{1,0:T(8,128)(2,1)}, u32[]{:S(2)}, u32[]{:S(2)}) %collective-permute-start.17) | collective-permute-done | bytes 1179680 | tf_op jit(solution)/shard_map/ppermute | solution.py:435
  112.6 1.3 collective-permute-start.23
  113.9 9.9 %collective-permute-done.19 = bf16[768,768]{1,0:T(8,128)(2,1)S(1)} collective-permute-done((bf16[768,768]{1,0:T(8,128)(2,1)}, bf16[768,768]{1,0:T(8,128)(2,1)S(1)}, u32[]{:S(2)}, u32[]{:S(2)}) %collective-permute-start.19) | collective-permute-done | bytes 1179680 | tf_op jit(solution)/shard_map/ppermute | solution.py:471
  123.9 1.9 collective-permute-start.25
  125.9 1.6 collective-permute-start.18
  127.5 1.1 copy-done.12
  129.1 1.9 copy.9
  131.1 2.3 copy.8
  133.3 2.9 maximum_select_fusion.refs_12_.refs_16_.refs_20_.refs_11_
  136.3 12.4 %shard_map.57.refs_19_ = f32[1536,768]{1,0:T(8,128)} custom-call(s32[3]{0:T(128)} %pad_add_fusion.2.refs_0_, bf16[768,6144]{1,0:T(8,128)(2,1)} %refs_0_.3, bf16[768,768]{1,0:T(8,128)(2,1)} %copy-done.5, bf16[768,768]{1,0:T(8,128)(2,1)} %copy-done.8, bf16[768,768]{1,0:T(8,128)(2,1)} %copy-done.7, bf16[768,768]{1,0:T(8,128)(2,1)} %copy-done.11, ...), custom_call_target="tpu_custom_call" | custom-call | flops 5435817984 | bytes 20054016 | tf_op jit(solution)/shard_map/pallas_call | solution.py:196
  149.9 1.1 collective-permute-start.26
  151.1 1.1 collective-permute-start.22
  153.3 1.8 slice.24.refs_27_
  155.1 2.2 slice.22
  157.3 1.8 slice.23
  159.1 1.1 broadcast_select_fusion.refs_17_.refs_21_.refs_12_
  160.2 17.0 %shard_map.58.refs_24_ = f32[1920,768]{1,0:T(8,128)} custom-call(s32[5]{0:T(128)} %stack.77.refs_0_, bf16[768,6144]{1,0:T(8,128)(2,1)} %refs_0_.3, bf16[768,768]{1,0:T(8,128)(2,1)} %copy-done.5, bf16[768,768]{1,0:T(8,128)(2,1)} %copy-done.8, bf16[768,768]{1,0:T(8,128)(2,1)} %copy-done.7, bf16[768,768]{1,0:T(8,128)(2,1)} %copy-done.11, ...), custom_call_target="tpu_custom_call" | custom-call | flops 5888802816 | bytes 25362432 | tf_op jit(solution)/shard_map/pallas_call | solution.py:196
  177.5 1.4 collective-permute-done.26.refs_23_.refs_14_
  180.3 2.1 collective-permute-start.32
  183.0 17.6 %shard_map.59.refs_28_ = f32[2304,768]{1,0:T(8,128)} custom-call(s32[6]{0:T(128)} %stack.79.refs_0_, bf16[768,6144]{1,0:T(8,128)(2,1)} %refs_0_.3, bf16[768,768]{1,0:T(8,128)(2,1)} %copy-done.5, bf16[768,768]{1,0:T(8,128)(2,1)} %copy-done.8, bf16[768,768]{1,0:T(8,128)(2,1)} %copy-done.7, bf16[768,768]{1,0:T(8,128)(2,1)} %copy-done.11, ...), custom_call_target="tpu_custom_call" | custom-call | flops 4982833152 | bytes 27721728 | tf_op jit(solution)/shard_map/pallas_call | solution.py:196
  201.0 5.5 %collective-permute-done.30.refs_6_.refs_22_ = bf16[768,768]{1,0:T(8,128)(2,1)S(1)} collective-permute-done((bf16[768,768]{1,0:T(8,128)(2,1)}, bf16[768,768]{1,0:T(8,128)(2,1)S(1)}, u32[]{:S(2)}, u32[]{:S(2)}) %collective-permute-start.30) | collective-permute-done | bytes 1179680 | tf_op jit(solution)/shard_map/ppermute | solution.py:438
  206.6 3.6 %collective-permute-start.36 = (bf16[768,512]{1,0:T(8,128)(2,1)}, bf16[768,512]{1,0:T(8,128)(2,1)}, u32[]{:S(2)}, u32[]{:S(2)}) collective-permute-start(bf16[768,512]{1,0:T(8,128)(2,1)} %slice.22), channel_id=1, source_target_pairs={{0,24},{4,28},{24,0},{28,4},{1,25},{5,29},{25,1},{29,5},{2,26},{6,... | collective-permute-start | bytes 2359304 | tf_op jit(solution)/shard_map/ppermute | solution.py:471
  211.8 13.4 %shard_map.60.refs_29_ = f32[768,768]{1,0:T(8,128)} custom-call(s32[6]{0:T(128)} %stack.79.refs_0_, bf16[768,768]{1,0:T(8,128)(2,1)} %get-tuple-element.86.refs_1_.refs_17_, bf16[768,768]{1,0:T(8,128)(2,1)} %collective-permute-done.22.refs_2_.refs_18_, bf16[768,768]{1,0:T(8,128)(2,1)} %collective-permute-done.28.refs_3_.refs_19_, ...), custom_call_target="tpu_custom_call" | custom-call | flops 5435817984 | bytes 18874368 | tf_op jit(solution)/shard_map/pallas_call | solution.py:196
  225.2 5.3 %collective-permute-done.36.refs_26_ = bf16[768,512]{1,0:T(8,128)(2,1)} collective-permute-done((bf16[768,512]{1,0:T(8,128)(2,1)}, bf16[768,512]{1,0:T(8,128)(2,1)}, u32[]{:S(2)}, u32[]{:S(2)}) %collective-permute-start.36) | collective-permute-done | bytes 786464 | tf_op jit(solution)/shard_map/ppermute | solution.py:471
  230.5 3.6 %collective-permute-start.35 = (bf16[768,256]{1,0:T(8,128)(2,1)}, bf16[768,256]{1,0:T(8,128)(2,1)S(1)}, u32[]{:S(2)}, u32[]{:S(2)}) collective-permute-start(bf16[768,256]{1,0:T(8,128)(2,1)} %slice.23), channel_id=1, source_target_pairs={{0,24},{4,28},{24,0},{28,4},{1,25},{5,29},{25,1},{29,5},{2,26},{6,... | collective-permute-start | bytes 1179656 | tf_op jit(solution)/shard_map/ppermute | solution.py:471
  234.3 17.8 %shard_map.62 = (bf16[3072,512]{1,0:T(8,128)(2,1)}, f32[4,2,128,128]{3,2,1,0:T(8,128)}, f32[2,128,128]{2,1,0:T(8,128)}) custom-call(s32[4]{0:T(128)} %pad_add_fusion.where_ref, s32[2]{0:T(128)} %pad_add_fusion.1.k_ref, s32[8]{0:T(128)} %bitcast.22, bf16[768,6144]{1,0:T(8,128)(2,1)} %refs_0_.3, bf16[768,768]{1,0:T(8,128)(2,1)} %copy-done.5, ...), custom_call_target="tpu_custom_call" | custom-call | flops 7247757312 | bytes 28311552 | tf_op jit(solution)/shard_map/pallas_call | solution.py:196
  252.1 2.7 collective-permute-start.37
  255.6 10.5 %shard_map.61.q_ref = bf16[3072,256]{1,0:T(8,128)(2,1)} custom-call(s32[4]{0:T(128)} %pad_add_fusion.where_ref, s32[2]{0:T(128)} %pad_add_fusion.1.k_ref, bf16[768,6144]{1,0:T(8,128)(2,1)} %refs_0_.3, bf16[768,768]{1,0:T(8,128)(2,1)} %copy-done.5, bf16[768,768]{1,0:T(8,128)(2,1)} %copy-done.8, bf16[768,768]{1,0:T(8,128)(2,1)} %copy-done.7, ...), custom_call_target="tpu_custom_call" | custom-call | flops 3623878656 | bytes 21233664 | tf_op jit(solution)/shard_map/pallas_call | solution.py:196
  266.1 1.4 copy-done.1
  267.5 2.4 shard_map.63
  270.9 2.4 shard_map.66
  273.3 2.0 collective-permute-start.42
  275.3 2.4 shard_map.65
  279.2 2.0 collective-permute-start.40
  281.7 1.5 collective-permute-start.39
  283.2 2.4 shard_map.64
  286.3 1.3 collective-permute-start.46
  287.6 1.8 collective-permute-done.45
  290.0 2.8 shard_map.67
  (128 shorter events, 21.3 us)
Async XLA Ops:
  3.7 29.1 %collective-permute-start = (bf16[768,768]{1,0:T(8,128)(2,1)}, bf16[768,768]{1,0:T(8,128)(2,1)S(1)}, u32[]{:S(2)}, u32[]{:S(2)}) collective-permute-start(bf16[768,768]{1,0:T(8,128)(2,1)} %shard_map.55), channel_id=1, source_target_pairs={{0,4},{4,0},{8,12},{12,8},{16,20},{20,16},{24,28},{28,24},{1,5},{5... | collective-permute-start | bytes 3538952 | tf_op jit(solution)/shard_map/ppermute | solution.py:435
  6.6 27.9 %collective-permute-start.5 = (bf16[768,768]{1,0:T(8,128)(2,1)}, bf16[768,768]{1,0:T(8,128)(2,1)S(1)}, u32[]{:S(2)}, u32[]{:S(2)}) collective-permute-start(bf16[768,768]{1,0:T(8,128)(2,1)} %shard_map.55), channel_id=1, source_target_pairs={{8,0},{12,4},{16,24},{20,28},{0,8},{4,12},{24,16},{28,20},{9,1},{1... | collective-permute-start | bytes 3538952 | tf_op jit(solution)/shard_map/ppermute | solution.py:471
  12.7 21.8 %collective-permute-start.3 = (bf16[768,2,256]{0,2,1:T(8,128)(2,1)}, bf16[768,2,256]{0,2,1:T(8,128)(2,1)S(1)}, u32[]{:S(2)}, u32[]{:S(2)}) collective-permute-start(bf16[768,2,256]{0,2,1:T(8,128)(2,1)} %copy.10), channel_id=1, source_target_pairs={{8,16},{12,20},{16,8},{20,12},{9,17},{13,21},{17,9},{21,13},{10,18... | collective-permute-start | bytes 2359304 | tf_op jit(solution)/shard_map/ppermute | solution.py:471
  16.3 18.2 %collective-permute-start.4 = (bf16[768,2,128]{0,2,1:T(8,128)(2,1)}, bf16[768,2,128]{0,2,1:T(8,128)(2,1)S(1)}, u32[]{:S(2)}, u32[]{:S(2)}) collective-permute-start(bf16[768,2,128]{0,2,1:T(8,128)(2,1)} %copy.11), channel_id=1, source_target_pairs={{8,16},{12,20},{16,8},{20,12},{9,17},{13,21},{17,9},{21,13},{10,18... | collective-permute-start | bytes 1179656 | tf_op jit(solution)/shard_map/ppermute | solution.py:471
  32.8 71.4 %copy-start.5 = (bf16[768,768]{1,0:T(8,128)(2,1)}, bf16[768,768]{1,0:T(8,128)(2,1)S(1)}, u32[]{:S(2)}) copy-start(bf16[768,768]{1,0:T(8,128)(2,1)S(1)} %collective-permute-done.refs_2_.refs_1_) | copy-start | bytes 3538948
  32.8 27.4 %collective-permute-start.8 = (bf16[768,768]{1,0:T(8,128)(2,1)}, bf16[768,768]{1,0:T(8,128)(2,1)S(1)}, u32[]{:S(2)}, u32[]{:S(2)}) collective-permute-start(bf16[768,768]{1,0:T(8,128)(2,1)} %get-tuple-element.60), channel_id=1, source_target_pairs={{0,4},{4,0},{8,12},{12,8},{16,20},{20,16},{24,28},{28,24},{1,5},{5... | collective-permute-start | bytes 3538952 | tf_op jit(solution)/shard_map/ppermute | solution.py:435
  34.6 25.6 %copy-start.27 = (bf16[768,2,128]{0,2,1:T(8,128)(2,1)}, bf16[768,2,128]{0,2,1:T(8,128)(2,1)S(1)}, u32[]{:S(2)}) copy-start(bf16[768,2,128]{0,2,1:T(8,128)(2,1)S(1)} %collective-permute-done.4) | copy-start | bytes 1179652
  34.6 25.6 %copy-start.25 = (bf16[768,2,256]{0,2,1:T(8,128)(2,1)}, bf16[768,2,256]{0,2,1:T(8,128)(2,1)S(1)}, u32[]{:S(2)}) copy-start(bf16[768,2,256]{0,2,1:T(8,128)(2,1)S(1)} %collective-permute-done.3) | copy-start | bytes 2359300
  34.6 71.2 %copy-start.13 = (bf16[768,768]{1,0:T(8,128)(2,1)}, bf16[768,768]{1,0:T(8,128)(2,1)S(1)}, u32[]{:S(2)}) copy-start(bf16[768,768]{1,0:T(8,128)(2,1)S(1)} %collective-permute-done.5.refs_10_.refs_9_) | copy-start | bytes 3538948
  34.6 34.7 %collective-permute-start.11 = (bf16[768,768]{1,0:T(8,128)(2,1)}, bf16[768,768]{1,0:T(8,128)(2,1)S(1)}, u32[]{:S(2)}, u32[]{:S(2)}) collective-permute-start(bf16[768,768]{1,0:T(8,128)(2,1)} %get-tuple-element.64), channel_id=1, source_target_pairs={{8,24},{12,28},{16,0},{20,4},{0,8},{4,12},{24,16},{28,20},{9,25},{... | collective-permute-start | bytes 3538952 | tf_op jit(solution)/shard_map/ppermute | solution.py:471
  43.5 27.6 %collective-permute-start.2 = (bf16[768,768]{1,0:T(8,128)(2,1)S(1)}, bf16[768,768]{1,0:T(8,128)(2,1)S(1)}, u32[]{:S(2)}, u32[]{:S(2)}) collective-permute-start(bf16[768,768]{1,0:T(8,128)(2,1)S(1)} %collective-permute-done.refs_2_.refs_1_), channel_id=1, source_target_pairs={{0,1},{1,0},{2,3},{3,2},{4,5},{5,4},{6,7},{7,6},{8,9},{9,8},{10,11... | collective-permute-start | bytes 3538952 | tf_op jit(solution)/shard_map/ppermute | solution.py:438
  43.5 27.6 %collective-permute-start.6 = (bf16[768,768]{1,0:T(8,128)(2,1)S(1)}, bf16[768,768]{1,0:T(8,128)(2,1)S(1)}, u32[]{:S(2)}, u32[]{:S(2)}) collective-permute-start(bf16[768,768]{1,0:T(8,128)(2,1)S(1)} %collective-permute-done.5.refs_10_.refs_9_), channel_id=1, source_target_pairs={{0,1},{1,0},{2,3},{3,2},{4,5},{5,4},{6,7},{7,6},{8,9},{9,8},{10,11... | collective-permute-start | bytes 3538952 | tf_op jit(solution)/shard_map/ppermute | solution.py:438
  44.0 27.9 %collective-permute-start.1 = (bf16[768,768]{1,0:T(8,128)(2,1)S(1)}, bf16[768,768]{1,0:T(8,128)(2,1)S(1)}, u32[]{:S(2)}, u32[]{:S(2)}) collective-permute-start(bf16[768,768]{1,0:T(8,128)(2,1)S(1)} %collective-permute-done.refs_2_.refs_1_), channel_id=1, source_target_pairs={{0,2},{1,3},{2,0},{3,1},{4,6},{5,7},{6,4},{7,5},{8,10},{9,11},{10,... | collective-permute-start | bytes 3538952 | tf_op jit(solution)/shard_map/ppermute | solution.py:438
  60.2 44.1 %copy-start.6 = (bf16[768,768]{1,0:T(8,128)(2,1)}, bf16[768,768]{1,0:T(8,128)(2,1)S(1)}, u32[]{:S(2)}) copy-start(bf16[768,768]{1,0:T(8,128)(2,1)S(1)} %collective-permute-done.8.refs_6_.refs_5_) | copy-start | bytes 3538948
  60.2 26.5 %collective-permute-start.15 = (bf16[768,768]{1,0:T(8,128)(2,1)}, bf16[768,768]{1,0:T(8,128)(2,1)S(1)}, u32[]{:S(2)}, u32[]{:S(2)}) collective-permute-start(bf16[768,768]{1,0:T(8,128)(2,1)} %get-tuple-element.70), channel_id=1, source_target_pairs={{0,4},{4,0},{8,12},{12,8},{16,20},{20,16},{24,28},{28,24},{1,5},{5... | collective-permute-start | bytes 3538952 | tf_op jit(solution)/shard_map/ppermute | solution.py:435
  69.3 25.8 %collective-permute-start.14 = (bf16[768,768]{1,0:T(8,128)(2,1)}, bf16[768,768]{1,0:T(8,128)(2,1)S(1)}, u32[]{:S(2)}, u32[]{:S(2)}) collective-permute-start(bf16[768,768]{1,0:T(8,128)(2,1)} %get-tuple-element.68), channel_id=1, source_target_pairs={{8,0},{12,4},{16,24},{20,28},{0,16},{4,20},{24,8},{28,12},{9,1},{1... | collective-permute-start | bytes 3538952 | tf_op jit(solution)/shard_map/ppermute | solution.py:471
  71.1 34.7 %copy-start.7 = (bf16[768,768]{1,0:T(8,128)(2,1)}, bf16[768,768]{1,0:T(8,128)(2,1)S(1)}, u32[]{:S(2)}) copy-start(bf16[768,768]{1,0:T(8,128)(2,1)S(1)} %collective-permute-done.2.refs_4_.refs_3_) | copy-start | bytes 3538948
  71.1 34.7 %copy-start.14 = (bf16[768,768]{1,0:T(8,128)(2,1)}, bf16[768,768]{1,0:T(8,128)(2,1)S(1)}, u32[]{:S(2)}) copy-start(bf16[768,768]{1,0:T(8,128)(2,1)S(1)} %collective-permute-done.6.refs_12_.refs_11_) | copy-start | bytes 3538948
  71.9 28.6 %copy-start.8 = (bf16[768,768]{1,0:T(8,128)(2,1)}, bf16[768,768]{1,0:T(8,128)(2,1)S(1)}, u32[]{:S(2)}) copy-start(bf16[768,768]{1,0:T(8,128)(2,1)S(1)} %collective-permute-done.1.refs_3_.refs_2_) | copy-start | bytes 3538948
  71.9 27.0 %collective-permute-start.9 = (bf16[768,768]{1,0:T(8,128)(2,1)S(1)}, bf16[768,768]{1,0:T(8,128)(2,1)S(1)}, u32[]{:S(2)}, u32[]{:S(2)}) collective-permute-start(bf16[768,768]{1,0:T(8,128)(2,1)S(1)} %collective-permute-done.8.refs_6_.refs_5_), channel_id=1, source_target_pairs={{0,2},{1,3},{2,0},{3,1},{4,6},{5,7},{6,4},{7,5},{8,10},{9,11},{10,... | collective-permute-start | bytes 3538952 | tf_op jit(solution)/shard_map/ppermute | solution.py:438
  73.4 27.0 %collective-permute-start.10 = (bf16[768,768]{1,0:T(8,128)(2,1)S(1)}, bf16[768,768]{1,0:T(8,128)(2,1)S(1)}, u32[]{:S(2)}, u32[]{:S(2)}) collective-permute-start(bf16[768,768]{1,0:T(8,128)(2,1)S(1)} %collective-permute-done.8.refs_6_.refs_5_), channel_id=1, source_target_pairs={{0,1},{1,0},{2,3},{3,2},{4,5},{5,4},{6,7},{7,6},{8,9},{9,8},{10,11... | collective-permute-start | bytes 3538952 | tf_op jit(solution)/shard_map/ppermute | solution.py:438
  73.4 27.0 %collective-permute-start.7 = (bf16[768,768]{1,0:T(8,128)(2,1)S(1)}, bf16[768,768]{1,0:T(8,128)(2,1)S(1)}, u32[]{:S(2)}, u32[]{:S(2)}) collective-permute-start(bf16[768,768]{1,0:T(8,128)(2,1)S(1)} %collective-permute-done.1.refs_3_.refs_2_), channel_id=1, source_target_pairs={{0,1},{1,0},{2,3},{3,2},{4,5},{5,4},{6,7},{7,6},{8,9},{9,8},{10,11... | collective-permute-start | bytes 3538952 | tf_op jit(solution)/shard_map/ppermute | solution.py:438
  86.7 37.2 %copy-start.21 = (bf16[768,768]{1,0:T(8,128)(2,1)}, bf16[768,768]{1,0:T(8,128)(2,1)S(1)}, u32[]{:S(2)}) copy-start(bf16[768,768]{1,0:T(8,128)(2,1)S(1)} %collective-permute-done.15) | copy-start | bytes 3538948
  86.7 25.9 %collective-permute-start.17 = (bf16[768,768]{1,0:T(8,128)(2,1)S(1)}, bf16[768,768]{1,0:T(8,128)(2,1)}, u32[]{:S(2)}, u32[]{:S(2)}) collective-permute-start(bf16[768,768]{1,0:T(8,128)(2,1)S(1)} %collective-permute-done.5.refs_10_.refs_9_), channel_id=1, source_target_pairs={{0,4},{4,0},{8,12},{12,8},{16,20},{20,16},{24,28},{28,24},{1,5},{5... | collective-permute-start | bytes 3538952 | tf_op jit(solution)/shard_map/ppermute | solution.py:435
  95.1 28.8 %collective-permute-start.19 = (bf16[768,768]{1,0:T(8,128)(2,1)}, bf16[768,768]{1,0:T(8,128)(2,1)S(1)}, u32[]{:S(2)}, u32[]{:S(2)}) collective-permute-start(bf16[768,768]{1,0:T(8,128)(2,1)} %get-tuple-element.82), channel_id=1, source_target_pairs={{0,24},{4,28},{24,0},{28,4},{1,25},{5,29},{25,1},{29,5},{2,26},{6,... | collective-permute-start | bytes 3538952 | tf_op jit(solution)/shard_map/ppermute | solution.py:471
  98.9 6.9 %copy-start.9 = (bf16[768,768]{1,0:T(8,128)(2,1)}, bf16[768,768]{1,0:T(8,128)(2,1)S(1)}, u32[]{:S(2)}) copy-start(bf16[768,768]{1,0:T(8,128)(2,1)S(1)} %collective-permute-done.9.refs_7_.refs_6_) | copy-start | bytes 3538948
  98.9 27.0 %collective-permute-start.13 = (bf16[768,768]{1,0:T(8,128)(2,1)S(1)}, bf16[768,768]{1,0:T(8,128)(2,1)}, u32[]{:S(2)}, u32[]{:S(2)}) collective-permute-start(bf16[768,768]{1,0:T(8,128)(2,1)S(1)} %collective-permute-done.5.refs_10_.refs_9_), channel_id=1, source_target_pairs={{0,2},{1,3},{2,0},{3,1},{4,6},{5,7},{6,4},{7,5},{8,10},{9,11},{10,... | collective-permute-start | bytes 3538952 | tf_op jit(solution)/shard_map/ppermute | solution.py:438
  102.5 24.9 %collective-permute-start.12 = (bf16[768,768]{1,0:T(8,128)(2,1)S(1)}, bf16[768,768]{1,0:T(8,128)(2,1)S(1)}, u32[]{:S(2)}, u32[]{:S(2)}) collective-permute-start(bf16[768,768]{1,0:T(8,128)(2,1)S(1)} %collective-permute-done.9.refs_7_.refs_6_), channel_id=1, source_target_pairs={{0,1},{1,0},{2,3},{3,2},{4,5},{5,4},{6,7},{7,6},{8,9},{9,8},{10,11... | collective-permute-start | bytes 3538952 | tf_op jit(solution)/shard_map/ppermute | solution.py:438
  112.6 36.1 %collective-permute-start.23 = (bf16[768,768]{1,0:T(8,128)(2,1)}, bf16[768,768]{1,0:T(8,128)(2,1)}, u32[]{:S(2)}, u32[]{:S(2)}) collective-permute-start(bf16[768,768]{1,0:T(8,128)(2,1)} %get-tuple-element.81), channel_id=1, source_target_pairs={{0,4},{4,0},{8,12},{12,8},{16,20},{20,16},{24,28},{28,24},{1,5},{5... | collective-permute-start | bytes 3538952 | tf_op jit(solution)/shard_map/ppermute | solution.py:435
  123.9 25.4 %collective-permute-start.25 = (bf16[768,768]{1,0:T(8,128)(2,1)S(1)}, bf16[768,768]{1,0:T(8,128)(2,1)}, u32[]{:S(2)}, u32[]{:S(2)}) collective-permute-start(bf16[768,768]{1,0:T(8,128)(2,1)S(1)} %collective-permute-done.15), channel_id=1, source_target_pairs={{8,16},{12,20},{16,8},{20,12},{9,17},{13,21},{17,9},{21,13},{10,18... | collective-permute-start | bytes 3538952 | tf_op jit(solution)/shard_map/ppermute | solution.py:471
  125.8 24.2 %collective-permute-start.24 = (bf16[768,768]{1,0:T(8,128)(2,1)}, bf16[768,768]{1,0:T(8,128)(2,1)}, u32[]{:S(2)}, u32[]{:S(2)}) collective-permute-start(bf16[768,768]{1,0:T(8,128)(2,1)} %get-tuple-element.82), channel_id=1, source_target_pairs={{8,0},{12,4},{16,24},{20,28},{0,8},{4,12},{24,16},{28,20},{9,1},{1... | collective-permute-start | bytes 3538952 | tf_op jit(solution)/shard_map/ppermute | solution.py:471
  125.9 25.2 %collective-permute-start.18 = (bf16[768,768]{1,0:T(8,128)(2,1)}, bf16[768,768]{1,0:T(8,128)(2,1)S(1)}, u32[]{:S(2)}, u32[]{:S(2)}) collective-permute-start(bf16[768,768]{1,0:T(8,128)(2,1)} %collective-permute-done.17.refs_14_.refs_13_), channel_id=1, source_target_pairs={{0,2},{1,3},{2,0},{3,1},{4,6},{5,7},{6,4},{7,5},{8,10},{9,11},{10,... | collective-permute-start | bytes 3538952 | tf_op jit(solution)/shard_map/ppermute | solution.py:438
  128.6 23.6 %collective-permute-start.16 = (bf16[768,768]{1,0:T(8,128)(2,1)}, bf16[768,768]{1,0:T(8,128)(2,1)S(1)}, u32[]{:S(2)}, u32[]{:S(2)}) collective-permute-start(bf16[768,768]{1,0:T(8,128)(2,1)} %collective-permute-done.13.refs_11_.refs_10_), channel_id=1, source_target_pairs={{0,1},{1,0},{2,3},{3,2},{4,5},{5,4},{6,7},{7,6},{8,9},{9,8},{10,11... | collective-permute-start | bytes 3538952 | tf_op jit(solution)/shard_map/ppermute | solution.py:438
  148.7 28.8 %collective-permute-start.27 = (bf16[768,768]{1,0:T(8,128)(2,1)}, bf16[768,768]{1,0:T(8,128)(2,1)}, u32[]{:S(2)}, u32[]{:S(2)}) collective-permute-start(bf16[768,768]{1,0:T(8,128)(2,1)} %get-tuple-element.86.refs_1_.refs_17_), channel_id=1, source_target_pairs={{0,4},{4,0},{8,12},{12,8},{16,20},{20,16},{24,28},{28,24},{1,5},{5... | collective-permute-start | bytes 3538952 | tf_op jit(solution)/shard_map/ppermute | solution.py:435
  149.9 28.9 %collective-permute-start.26 = (bf16[768,768]{1,0:T(8,128)(2,1)}, bf16[768,768]{1,0:T(8,128)(2,1)}, u32[]{:S(2)}, u32[]{:S(2)}) collective-permute-start(bf16[768,768]{1,0:T(8,128)(2,1)} %collective-permute-done.23), channel_id=1, source_target_pairs={{8,24},{12,28},{16,0},{20,4},{0,8},{4,12},{24,16},{28,20},{9,25},{... | collective-permute-start | bytes 3538952 | tf_op jit(solution)/shard_map/ppermute | solution.py:471
  151.1 6.2 %copy-start.16 = (bf16[768,768]{1,0:T(8,128)(2,1)}, bf16[768,768]{1,0:T(8,128)(2,1)S(1)}, u32[]{:S(2)}) copy-start(bf16[768,768]{1,0:T(8,128)(2,1)S(1)} %collective-permute-done.18.refs_15_.refs_14_) | copy-start | bytes 3538948
  151.1 28.1 %collective-permute-start.22 = (bf16[768,768]{1,0:T(8,128)(2,1)}, bf16[768,768]{1,0:T(8,128)(2,1)}, u32[]{:S(2)}, u32[]{:S(2)}) collective-permute-start(bf16[768,768]{1,0:T(8,128)(2,1)} %get-tuple-element.86.refs_1_.refs_17_), channel_id=1, source_target_pairs={{0,2},{1,3},{2,0},{3,1},{4,6},{5,7},{6,4},{7,5},{8,10},{9,11},{10,... | collective-permute-start | bytes 3538952 | tf_op jit(solution)/shard_map/ppermute | solution.py:438
  152.2 5.1 %copy-start.15 = (bf16[768,768]{1,0:T(8,128)(2,1)}, bf16[768,768]{1,0:T(8,128)(2,1)S(1)}, u32[]{:S(2)}) copy-start(bf16[768,768]{1,0:T(8,128)(2,1)S(1)} %collective-permute-done.16.refs_13_.refs_12_) | copy-start | bytes 3538948
  152.2 27.0 %collective-permute-start.21 = (bf16[768,768]{1,0:T(8,128)(2,1)S(1)}, bf16[768,768]{1,0:T(8,128)(2,1)S(1)}, u32[]{:S(2)}, u32[]{:S(2)}) collective-permute-start(bf16[768,768]{1,0:T(8,128)(2,1)S(1)} %collective-permute-done.18.refs_15_.refs_14_), channel_id=1, source_target_pairs={{0,1},{1,0},{2,3},{3,2},{4,5},{5,4},{6,7},{7,6},{8,9},{9,8},{10,11... | collective-permute-start | bytes 3538952 | tf_op jit(solution)/shard_map/ppermute | solution.py:438
  152.2 27.0 %collective-permute-start.20 = (bf16[768,768]{1,0:T(8,128)(2,1)}, bf16[768,768]{1,0:T(8,128)(2,1)}, u32[]{:S(2)}, u32[]{:S(2)}) collective-permute-start(bf16[768,768]{1,0:T(8,128)(2,1)} %collective-permute-done.17.refs_14_.refs_13_), channel_id=1, source_target_pairs={{0,1},{1,0},{2,3},{3,2},{4,5},{5,4},{6,7},{7,6},{8,9},{9,8},{10,11... | collective-permute-start | bytes 3538952 | tf_op jit(solution)/shard_map/ppermute | solution.py:438
  179.2 27.2 %collective-permute-start.30 = (bf16[768,768]{1,0:T(8,128)(2,1)}, bf16[768,768]{1,0:T(8,128)(2,1)S(1)}, u32[]{:S(2)}, u32[]{:S(2)}) collective-permute-start(bf16[768,768]{1,0:T(8,128)(2,1)} %collective-permute-done.27.refs_5_.refs_21_), channel_id=1, source_target_pairs={{0,2},{1,3},{2,0},{3,1},{4,6},{5,7},{6,4},{7,5},{8,10},{9,11},{10,... | collective-permute-start | bytes 3538952 | tf_op jit(solution)/shard_map/ppermute | solution.py:438
  179.8 26.7 %collective-permute-start.31 = (bf16[768,768]{1,0:T(8,128)(2,1)}, bf16[768,768]{1,0:T(8,128)(2,1)S(1)}, u32[]{:S(2)}, u32[]{:S(2)}) collective-permute-start(bf16[768,768]{1,0:T(8,128)(2,1)} %collective-permute-done.27.refs_5_.refs_21_), channel_id=1, source_target_pairs={{0,1},{1,0},{2,3},{3,2},{4,5},{5,4},{6,7},{7,6},{8,9},{9,8},{10,11... | collective-permute-start | bytes 3538952 | tf_op jit(solution)/shard_map/ppermute | solution.py:438
  179.8 26.7 %collective-permute-start.29 = (bf16[768,768]{1,0:T(8,128)(2,1)}, bf16[768,768]{1,0:T(8,128)(2,1)}, u32[]{:S(2)}, u32[]{:S(2)}) collective-permute-start(bf16[768,768]{1,0:T(8,128)(2,1)} %collective-permute-done.22.refs_2_.refs_18_), channel_id=1, source_target_pairs={{0,1},{1,0},{2,3},{3,2},{4,5},{5,4},{6,7},{7,6},{8,9},{9,8},{10,11... | collective-permute-start | bytes 3538952 | tf_op jit(solution)/shard_map/ppermute | solution.py:438
  180.3 26.2 %collective-permute-start.28 = (bf16[768,768]{1,0:T(8,128)(2,1)}, bf16[768,768]{1,0:T(8,128)(2,1)}, u32[]{:S(2)}, u32[]{:S(2)}) collective-permute-start(bf16[768,768]{1,0:T(8,128)(2,1)} %get-tuple-element.86.refs_1_.refs_17_), channel_id=1, source_target_pairs={{0,1},{1,0},{2,3},{3,2},{4,5},{5,4},{6,7},{7,6},{8,9},{9,8},{10,11... | collective-permute-start | bytes 3538952 | tf_op jit(solution)/shard_map/ppermute | solution.py:438
  180.3 20.7 %collective-permute-start.32 = (bf16[768,512]{1,0:T(8,128)(2,1)}, bf16[768,512]{1,0:T(8,128)(2,1)}, u32[]{:S(2)}, u32[]{:S(2)}) collective-permute-start(bf16[768,512]{1,0:T(8,128)(2,1)} %slice.20), channel_id=1, source_target_pairs={{8,0},{12,4},{16,24},{20,28},{0,16},{4,20},{24,8},{28,12},{9,1},{1... | collective-permute-start | bytes 2359304 | tf_op jit(solution)/shard_map/ppermute | solution.py:471
  206.5 4.2 %collective-permute-start.33 = (bf16[768,768]{1,0:T(8,128)(2,1)S(1)}, bf16[768,768]{1,0:T(8,128)(2,1)S(1)}, u32[]{:S(2)}, u32[]{:S(2)}) collective-permute-start(bf16[768,768]{1,0:T(8,128)(2,1)S(1)} %collective-permute-done.30.refs_6_.refs_22_), channel_id=1, source_target_pairs={{0,1},{1,0},{2,3},{3,2},{4,5},{5,4},{6,7},{7,6},{8,9},{9,8},{10,11... | collective-permute-start | bytes 3538952 | tf_op jit(solution)/shard_map/ppermute | solution.py:438
  206.6 23.9 %collective-permute-start.36 = (bf16[768,512]{1,0:T(8,128)(2,1)}, bf16[768,512]{1,0:T(8,128)(2,1)}, u32[]{:S(2)}, u32[]{:S(2)}) collective-permute-start(bf16[768,512]{1,0:T(8,128)(2,1)} %slice.22), channel_id=1, source_target_pairs={{0,24},{4,28},{24,0},{28,4},{1,25},{5,29},{25,1},{29,5},{2,26},{6,... | collective-permute-start | bytes 2359304 | tf_op jit(solution)/shard_map/ppermute | solution.py:471
  230.5 24.3 %collective-permute-start.35 = (bf16[768,256]{1,0:T(8,128)(2,1)}, bf16[768,256]{1,0:T(8,128)(2,1)S(1)}, u32[]{:S(2)}, u32[]{:S(2)}) collective-permute-start(bf16[768,256]{1,0:T(8,128)(2,1)} %slice.23), channel_id=1, source_target_pairs={{0,24},{4,28},{24,0},{28,4},{1,25},{5,29},{25,1},{29,5},{2,26},{6,... | collective-permute-start | bytes 1179656 | tf_op jit(solution)/shard_map/ppermute | solution.py:471
  234.1 21.5 %collective-permute-start.34 = (bf16[768,256]{1,0:T(8,128)(2,1)}, bf16[768,256]{1,0:T(8,128)(2,1)}, u32[]{:S(2)}, u32[]{:S(2)}) collective-permute-start(bf16[768,256]{1,0:T(8,128)(2,1)} %slice.21), channel_id=1, source_target_pairs={{8,0},{12,4},{16,24},{20,28},{0,16},{4,20},{24,8},{28,12},{9,1},{1... | collective-permute-start | bytes 1179656 | tf_op jit(solution)/shard_map/ppermute | solution.py:471
  252.1 14.0 %copy-start.2 = (f32[4,2,128,128]{3,2,1,0:T(8,128)S(1)}, f32[4,2,128,128]{3,2,1,0:T(8,128)}, u32[]{:S(2)}) copy-start(f32[4,2,128,128]{3,2,1,0:T(8,128)} %get-tuple-element.96.tails_ref) | copy-start | bytes 1572868
  252.1 14.0 %copy-start.3 = (s32[4]{0:T(128)S(1)}, s32[4]{0:T(128)}, u32[]{:S(2)}) copy-start(s32[4]{0:T(128)} %pad_add_fusion.where_ref) | copy-start | bytes 52
  252.1 14.0 %copy-start.4 = (s32[8,1]{0,1:T(1,128)S(1)}, s32[8,1]{0,1:T(1,128)}, u32[]{:S(2)}) copy-start(s32[8,1]{0,1:T(1,128)} %reduce-window.9) | copy-start | bytes 100
  252.1 13.9 %collective-permute-start.37 = (f32[2,128,128]{2,1,0:T(8,128)}, f32[2,128,128]{2,1,0:T(8,128)S(1)}, u32[]{:S(2)}, u32[]{:S(2)}) collective-permute-start(f32[2,128,128]{2,1,0:T(8,128)} %get-tuple-element.97), channel_id=1, source_target_pairs={{0,16},{4,20},{8,24},{12,28},{16,0},{20,4},{24,8},{28,12},{1,17},{... | collective-permute-start | bytes 393224 | tf_op jit(solution)/shard_map/ppermute | solution.py:435
  255.6 10.5 %copy-start = (bf16[3072,512]{1,0:T(8,128)(2,1)S(1)}, bf16[3072,512]{1,0:T(8,128)(2,1)}, u32[]{:S(2)}) copy-start(bf16[3072,512]{1,0:T(8,128)(2,1)} %get-tuple-element.95.kv_ref) | copy-start | bytes 9437188
  269.9 11.8 %collective-permute-start.38 = (bf16[768,256]{1,0:T(8,128)(2,1)S(1)}, bf16[768,256]{1,0:T(8,128)(2,1)S(1)}, u32[]{:S(2)}, u32[]{:S(2)}) collective-permute-start(bf16[768,256]{1,0:T(8,128)(2,1)S(1)} %get-tuple-element.98), channel_id=1, source_target_pairs={{0,12},{4,8},{8,4},{12,0},{16,28},{20,24},{24,20},{28,16},{1,13},{... | collective-permute-start | bytes 1179656 | tf_op jit(solution)/shard_map/ppermute | solution.py:435
  273.3 12.2 %collective-permute-start.42 = (f32[1,768]{1,0:T(1,128)S(1)}, f32[1,768]{1,0:T(1,128)S(1)}, u32[]{:S(2)}, u32[]{:S(2)}) collective-permute-start(f32[1,768]{1,0:T(1,128)S(1)} %get-tuple-element.104), channel_id=1, source_target_pairs={{0,8},{4,12},{8,0},{12,4},{16,24},{20,28},{24,16},{28,20},{1,9},{5... | collective-permute-start | bytes 9224 | tf_op jit(solution)/shard_map/ppermute | solution.py:435
  277.7 7.9 %collective-permute-start.43 = (f32[1,768]{1,0:T(1,128)S(1)}, f32[1,768]{1,0:T(1,128)S(1)}, u32[]{:S(2)}, u32[]{:S(2)}) collective-permute-start(f32[1,768]{1,0:T(1,128)S(1)} %get-tuple-element.105), channel_id=1, source_target_pairs={{0,4},{4,0},{8,12},{12,8},{16,20},{20,16},{24,28},{28,24},{1,5},{5... | collective-permute-start | bytes 9224 | tf_op jit(solution)/shard_map/ppermute | solution.py:435
  278.2 7.3 %collective-permute-start.41 = (f32[1,768]{1,0:T(1,128)S(1)}, f32[1,768]{1,0:T(1,128)S(1)}, u32[]{:S(2)}, u32[]{:S(2)}) collective-permute-start(f32[1,768]{1,0:T(1,128)S(1)} %get-tuple-element.103), channel_id=1, source_target_pairs={{0,12},{4,8},{8,4},{12,0},{16,28},{20,24},{24,20},{28,16},{1,13},{... | collective-permute-start | bytes 9224 | tf_op jit(solution)/shard_map/ppermute | solution.py:435
  279.2 10.1 %collective-permute-start.40 = (bf16[768,256]{1,0:T(8,128)(2,1)S(1)}, bf16[768,256]{1,0:T(8,128)(2,1)S(1)}, u32[]{:S(2)}, u32[]{:S(2)}) collective-permute-start(bf16[768,256]{1,0:T(8,128)(2,1)S(1)} %get-tuple-element.102), channel_id=1, source_target_pairs={{0,8},{4,12},{8,0},{12,4},{16,24},{20,28},{24,16},{28,20},{1,9},{5... | collective-permute-start | bytes 1179656 | tf_op jit(solution)/shard_map/ppermute | solution.py:435
  281.7 5.9 %copy-start.28 = (bf16[1024]{0:T(1024)(128)(2,1)S(1)}, bf16[1024]{0:T(1024)(128)(2,1)}, u32[]{:S(2)}) copy-start(bf16[1024]{0:T(1024)(128)(2,1)} %param.9) | copy-start | bytes 6148
  281.7 8.3 %collective-permute-start.39 = (bf16[768,256]{1,0:T(8,128)(2,1)S(1)}, bf16[768,256]{1,0:T(8,128)(2,1)S(1)}, u32[]{:S(2)}, u32[]{:S(2)}) collective-permute-start(bf16[768,256]{1,0:T(8,128)(2,1)S(1)} %get-tuple-element.101), channel_id=1, source_target_pairs={{0,4},{4,0},{8,12},{12,8},{16,20},{20,16},{24,28},{28,24},{1,5},{5... | collective-permute-start | bytes 1179656 | tf_op jit(solution)/shard_map/ppermute | solution.py:435
  285.6 2.0 collective-permute-start.44
  285.7 3.7 %collective-permute-start.45 = (f32[1,768]{1,0:T(1,128)S(1)}, f32[1,768]{1,0:T(1,128)S(1)}, u32[]{:S(2)}, u32[]{:S(2)}) collective-permute-start(f32[1,768]{1,0:T(1,128)S(1)} %add_add_fusion.1), channel_id=1, source_target_pairs={{0,2},{1,3},{2,0},{3,1},{4,6},{5,7},{6,4},{7,5},{8,10},{9,11},{10,... | collective-permute-start | bytes 9224 | tf_op jit(solution)/shard_map/ppermute | solution.py:438
  286.3 3.1 %collective-permute-start.46 = (f32[1,768]{1,0:T(1,128)S(1)}, f32[1,768]{1,0:T(1,128)S(1)}, u32[]{:S(2)}, u32[]{:S(2)}) collective-permute-start(f32[1,768]{1,0:T(1,128)S(1)} %add_add_fusion.1), channel_id=1, source_target_pairs={{0,3},{1,2},{2,1},{3,0},{4,7},{5,6},{6,5},{7,4},{8,11},{9,10},{10,... | collective-permute-start | bytes 9224 | tf_op jit(solution)/shard_map/ppermute | solution.py:438
  (13 other events, 32.6 us)

commit v5 on v4

--- a/solution.py
+++ b/solution.py
@@ -59,7 +59,28 @@
     accumulate(pl.program_id(0), ranges, t_refs, w_refs, refs[-1], refs[:starts])
 
 
-def settle(places, fsdp_size, where_ref, t_refs, total, out_ref):
+def fetch(step, starts, start_refs, held, sems, body):
+    width = held.shape[1]
+    copies, at = [], 0
+    for i, (ref, (block, count, column)) in enumerate(zip(start_refs, starts)):
+        part = ref.at[pl.ds(block * count, count), pl.ds(column * width, width)]
+        copies.append(pltpu.make_async_copy(part, held.at[pl.ds(at, count), :], sems.at[i]))
+        at += count
+
+    @pl.when(step == 0)
+    def _():
+        for copy in copies:
+            copy.start()
+
+    body()
+
+    @pl.when(step == pl.num_programs(0) - 1)
+    def _():
+        for copy in copies:
+            copy.wait()
+
+
+def settle(places, fsdp_size, where_ref, t_refs, total, held, out_ref):
     m, f = where_ref[0], where_ref[1]
     block_rows = out_ref.shape[0] // MEMBERS
     at = 0
@@ -70,32 +91,36 @@
             if e is not None:
                 to = to + (f ^ e) * (block_rows // fsdp_size) + offset
             to = pl.multiple_of(to, 16)
-            out_ref[pl.ds(to, rows), :] = silu(total[at : at + rows, :]).astype(out_ref.dtype)
+            value = silu(total[at : at + rows, :] + held[at : at + rows, :])
+            out_ref[pl.ds(to, rows), :] = value.astype(out_ref.dtype)
             at += rows
 
 
 def activate_body(places, fsdp_size, ranges, starts, where_ref, k_ref, *refs):
     parts, arrays = len(places), len(ranges)
     t_refs, w_refs, refs = refs[:parts], refs[parts : parts + arrays], refs[parts + arrays :]
-    start_refs, out_ref, total = refs[:starts], refs[-2], refs[-1]
+    start_refs, (out_ref, total, held, sems) = refs[: len(starts)], refs[len(starts) :]
     step = pl.program_id(0)
-    accumulate(step, ranges, t_refs, w_refs, total, start_refs, where_ref[3])
+    run = functools.partial(accumulate, step, ranges, t_refs, w_refs, total, (), where_ref[3])
+    fetch(step, starts, start_refs, held, sems, run)
 
     @pl.when(step == ranges[-1][1] - 1)
     def _():
-        settle(places, fsdp_size, where_ref, t_refs, total, out_ref)
+        settle(places, fsdp_size, where_ref, t_refs, total, held, out_ref)
 
 
 def keyval_body(places, fsdp_size, ranges, starts, heads, where_ref, k_ref, ends_ref, *refs):
     parts, arrays = len(places), len(ranges)
     t_refs, w_refs, refs = refs[:parts], refs[parts : parts + arrays], refs[parts + arrays :]
-    start_refs, (out_ref, tails_ref, state_ref, total) = refs[:starts], refs[starts:]
+    start_refs, refs = refs[: len(starts)], refs[len(starts) :]
+    out_ref, tails_ref, state_ref, total, held, sems = refs
     step = pl.program_id(0)
-    accumulate(step, ranges, t_refs, w_refs, total, start_refs, where_ref[3])
+    run = functools.partial(accumulate, step, ranges, t_refs, w_refs, total, (), where_ref[3])
+    fetch(step, starts, start_refs, held, sems, run)
 
     @pl.when(step == ranges[-1][1] - 1)
     def _():
-        settle(places, fsdp_size, where_ref, t_refs, total, out_ref)
+        settle(places, fsdp_size, where_ref, t_refs, total, held, out_ref)
         rows = out_ref.shape[0] // MEMBERS
         size = out_ref.shape[1] // heads // 2
         for b in range(MEMBERS):
@@ -156,12 +181,21 @@
         )
         for w, r in zip(arrays, ranges)
     ]
-    in_specs += [
-        pl.BlockSpec((count, width), lambda k, *_, at=at, c=c: (at, c)) for _, at, count, c in starts
-    ]
+    if kind == "sum":
+        in_specs += [
+            pl.BlockSpec((count, width), lambda k, *_, at=at, c=c: (at, c))
+            for _, at, count, c in starts
+        ]
+    else:
+        in_specs += [pl.BlockSpec(memory_space=pl.ANY) for _ in starts]
     operands = [p for p, _ in parts] + arrays + [a for a, _, _, _ in starts]
     whole = pl.BlockSpec((rows, width), lambda k, *_: (0, 0))
-    scratch = [pltpu.VMEM((rows, width), jnp.float32)]
+    scratch = [
+        pltpu.VMEM((rows, width), jnp.float32),
+        pltpu.VMEM((rows, width), jnp.float32),
+        pltpu.SemaphoreType.DMA((max(len(starts), 1),)),
+    ]
+    spots = [(at, count, c) for _, at, count, c in starts]
     places, fsdp_size = [p for _, p in parts], lax.axis_size("fsdp")
     if kind == "sum":
         prefetch, scratch = [k_blocks], []
@@ -169,12 +203,12 @@
         out_specs, out_shape = whole, jax.ShapeDtypeStruct((rows, width), jnp.float32)
     elif kind == "query":
         prefetch = [where, k_blocks]
-        body = functools.partial(activate_body, places, fsdp_size, ranges, len(starts))
+        body = functools.partial(activate_body, places, fsdp_size, ranges, spots)
         out_specs, out_shape = whole, jax.ShapeDtypeStruct((rows, width), jnp.bfloat16)
     else:
         heads, size = kind
         prefetch = [where, k_blocks, ends]
-        body = functools.partial(keyval_body, places, fsdp_size, ranges, len(starts), heads)
+        body = functools.partial(keyval_body, places, fsdp_size, ranges, spots, heads)
         out_specs = [
             whole,
             pl.BlockSpec((MEMBERS, heads, size, size), lambda k, *_: (0, 0, 0, 0)),
@@ -532,6 +566,7 @@
     r5_q = r5[:, kv_width:]
     rxa = pick(rx2, rx1)
     five, w_five = [0, 4, 6, 1, 2], [wa, w4, w6, rxa, z5]
+    six, last = blocks(*five, pick(3, 5)), blocks(pick(5, 3), 7)
     first2 = spread(2, (tz1, yz1, cz1, dz1), [None] * 4)[:4]
     acc_a = project(
         where, blocks(*five), near + first2,
@@ -539,11 +574,10 @@
         starts=[(acc_a, 0, 2 * rows, 0)],
     )
     r7, yzx2, cz2, czx2, dz2 = stage(
-        [acc_a, rx2_kv, rx2_q, r5_q],
+        [acc_a, rx2_kv, rx2_q, r5_q, six, last],
         [("z", pairs(2, 4), rx1_kv), ("y", y, tzx2), ("c", c, tz2), ("c", c, tzx2), ("c", c, yz2)],
         "all",
     )
-    six = blocks(*five, pick(3, 5))
     first3 = spread(3, (tzx1, yzx1, czx1, dzx1), [None] * 4)[:4]
     most = near + first2 + first3
     acc_b = project(
@@ -560,7 +594,6 @@
 
     r8 = lax.optimization_barrier((r8, acc_c))[0]
     every = most + rest
-    last = blocks(pick(5, 3), 7)
 
     def finals(column):
         return [(acc_b, 0, 3 * rows, column), (acc_c, 0, rows, column)]
@@ -647,10 +680,14 @@
 
 def solution(mesh):
     seq_size, fsdp_size = mesh.shape["seq"], mesh.shape["fsdp"]
-    if seq_size == 2 * MEMBERS:
-        body = functools.partial(grouped, seq_size, fsdp_size)
-    else:
-        body = plain
+
+    def body(tokens, w_query, *rest):
+        rows, (depth, head_count, _) = tokens.shape[0], w_query.shape
+        fits = seq_size == 2 * MEMBERS and fsdp_size == 4 and head_count % MEMBERS == 0
+        if fits and rows == depth and rows % 128 == 0:
+            return grouped(seq_size, fsdp_size, tokens, w_query, *rest)
+        return plain(tokens, w_query, *rest)
+
     return jax.shard_map(
         body,
         mesh=mesh,

time: 299 us -> 298 us (level)
    ppermute x13, starting transfers between devices: 29.8 us -> 32.8 us  [pairs(): return lambda value: lax.ppermute(value, 'seq', moves)]
    unnamed x64 -> x66, local copies, waits for them, and re-layouts: 15.7 us -> 15.6 us
  transfers between devices with their start and end apart: 47 -> 47, of which waited for: 19 -> 19; matrix products, arithmetic and copies ran while one was open for 12% -> 12% of each run, Pallas kernels for 35% -> 34%
where the time goes in v5:
time: 298 us; the launch traced here: 292 us
  Pallas kernels  109 us (37%)
  waiting for transfers between devices  78.4 us (26%)
  starting transfers between devices  63.3 us (21%)
  local copies, waits for them, and re-layouts  33.1 us (11%)
  other arithmetic  8.18 us (3%)
    pallas_call x6, Pallas kernels, project(): pl.pallas_call(body, grid_spec=pltpu.PrefetchScalarGridSpec(num_scalar_pr...  85.7 us
    ppermute x13, waiting for transfers between devices, hop(): return lax.ppermute(value, 'seq', [(i, i ^ k) for i in only])  38.5 us
    ppermute x13, starting transfers between devices, pairs(): return lambda value: lax.ppermute(value, 'seq', moves)  32.8 us
    ppermute x13, waiting for transfers between devices, pairs(): return lambda value: lax.ppermute(value, 'seq', moves)  31.6 us
    ppermute x13, starting transfers between devices, hop(): return lax.ppermute(value, 'seq', [(i, i ^ k) for i in only])  18.5 us
    unnamed x66, local copies, waits for them, and re-layouts  15.6 us
    ppermute x21, starting transfers between devices, side(): return lax.ppermute(value, 'fsdp', [(i, i ^ k) for i in range(fsdp_size)])  12 us
    pallas_call x4, Pallas kernels, attend(): pl.pallas_call(functools.partial(attend_body, place, cut), grid_spec=pltp...  9.59 us
  transfers between devices with their start and end apart: 47, of which 19 were waited for; matrix products, arithmetic and copies ran while one was open for 12% of the time, Pallas kernels for 34%

profile of v5, /device:TPU:0, one launch (start us, length us, event | category | flops | bytes accessed | tf_op | source)
XLA Modules:
  0.0 292.1 jit_solution(1889870617660706052)
XLA Ops:
  0.6 3.0 %shard_map.55 = bf16[768,768]{1,0:T(8,128)(2,1)} custom-call(s32[4]{0:T(128)} %pad_add_fusion.where_ref, bf16[768,6144]{1,0:T(8,128)(2,1)} %refs_0_.3), custom_call_target="tpu_custom_call" | custom-call | tf_op jit(solution)/shard_map/pallas_call | solution.py:389
  3.6 2.9 %collective-permute-start = (bf16[768,768]{1,0:T(8,128)(2,1)}, bf16[768,768]{1,0:T(8,128)(2,1)S(1)}, u32[]{:S(2)}, u32[]{:S(2)}) collective-permute-start(bf16[768,768]{1,0:T(8,128)(2,1)} %shard_map.55), channel_id=1, source_target_pairs={{0,4},{4,0},{8,12},{12,8},{16,20},{20,16},{24,28},{28,24},{1,5},{5... | collective-permute-start | bytes 3538952 | tf_op jit(solution)/shard_map/ppermute | solution.py:469
  6.6 1.6 collective-permute-start.5
  8.1 2.7 constant_dynamic-slice_fusion.1
  10.8 1.8 copy.10
  13.4 1.8 constant_dynamic-slice_fusion
  17.0 4.7 %copy.12 = bf16[96,8,8,256]{3,1,2,0:T(8,128)(2,1)} copy(bf16[96,8,8,256]{3,2,1,0:T(8,128)(2,1)} %bitcast.29) | data formatting | bytes 6291456
  21.7 1.6 copy.15
  24.0 7.4 %shard_map.56 = (bf16[768,768]{1,0:T(8,128)(2,1)}, bf16[768,768]{1,0:T(8,128)(2,1)}, bf16[768,768]{1,0:T(8,128)(2,1)}, bf16[768,768]{1,0:T(8,128)(2,1)}, bf16[76...) custom-call(s32[4]{0:T(128)} %pad_add_fusion.where_ref, bf16[768,2048]{1,0:T(8,128)(2,1)} %bitcast.27, ...), custom_call_target="tpu_custom_call" | custom-call | tf_op jit(solution)/shard_map/pallas_call | solution.py:436
  31.5 1.3 collective-permute-done.refs_2_.refs_1_
  32.7 1.7 collective-permute-start.8
  34.5 8.9 %collective-permute-start.11 = (bf16[768,768]{1,0:T(8,128)(2,1)}, bf16[768,768]{1,0:T(8,128)(2,1)S(1)}, u32[]{:S(2)}, u32[]{:S(2)}) collective-permute-start(bf16[768,768]{1,0:T(8,128)(2,1)} %get-tuple-element.64), channel_id=1, source_target_pairs={{8,24},{12,28},{16,0},{20,4},{0,8},{4,12},{24,16},{28,20},{9,25},{... | collective-permute-start | bytes 3538952 | tf_op jit(solution)/shard_map/ppermute | solution.py:505
  43.9 1.5 collective-permute-start.1
  45.5 14.7 %collective-permute-done.8.refs_6_.refs_5_ = bf16[768,768]{1,0:T(8,128)(2,1)S(1)} collective-permute-done((bf16[768,768]{1,0:T(8,128)(2,1)}, bf16[768,768]{1,0:T(8,128)(2,1)S(1)}, u32[]{:S(2)}, u32[]{:S(2)}) %collective-permute-start.8) | collective-permute-done | bytes 1179680 | tf_op jit(solution)/shard_map/ppermute | solution.py:469
  60.1 1.5 collective-permute-start.15
  61.6 7.7 %collective-permute-done.11 = bf16[768,768]{1,0:T(8,128)(2,1)S(1)} collective-permute-done((bf16[768,768]{1,0:T(8,128)(2,1)}, bf16[768,768]{1,0:T(8,128)(2,1)S(1)}, u32[]{:S(2)}, u32[]{:S(2)}) %collective-permute-start.11) | collective-permute-done | bytes 1179680 | tf_op jit(solution)/shard_map/ppermute | solution.py:505
  69.3 1.7 collective-permute-start.14
  71.8 1.5 collective-permute-start.9
  73.8 12.8 %collective-permute-done.15 = bf16[768,768]{1,0:T(8,128)(2,1)S(1)} collective-permute-done((bf16[768,768]{1,0:T(8,128)(2,1)}, bf16[768,768]{1,0:T(8,128)(2,1)S(1)}, u32[]{:S(2)}, u32[]{:S(2)}) %collective-permute-start.15) | collective-permute-done | bytes 1179680 | tf_op jit(solution)/shard_map/ppermute | solution.py:469
  86.6 1.3 collective-permute-start.17
  87.9 7.1 %collective-permute-done.14 = bf16[768,768]{1,0:T(8,128)(2,1)S(1)} collective-permute-done((bf16[768,768]{1,0:T(8,128)(2,1)}, bf16[768,768]{1,0:T(8,128)(2,1)S(1)}, u32[]{:S(2)}, u32[]{:S(2)}) %collective-permute-start.14) | collective-permute-done | bytes 1179680 | tf_op jit(solution)/shard_map/ppermute | solution.py:505
  95.1 3.7 %collective-permute-start.19 = (bf16[768,768]{1,0:T(8,128)(2,1)}, bf16[768,768]{1,0:T(8,128)(2,1)S(1)}, u32[]{:S(2)}, u32[]{:S(2)}) collective-permute-start(bf16[768,768]{1,0:T(8,128)(2,1)} %get-tuple-element.82), channel_id=1, source_target_pairs={{0,24},{4,28},{24,0},{28,4},{1,25},{5,29},{25,1},{29,5},{2,26},{6,... | collective-permute-start | bytes 3538952 | tf_op jit(solution)/shard_map/ppermute | solution.py:505
  98.8 1.5 collective-permute-start.13
  104.2 1.6 broadcast_select_fusion.1
  105.8 6.7 %collective-permute-done.17.refs_14_.refs_13_ = bf16[768,768]{1,0:T(8,128)(2,1)} collective-permute-done((bf16[768,768]{1,0:T(8,128)(2,1)S(1)}, bf16[768,768]{1,0:T(8,128)(2,1)}, u32[]{:S(2)}, u32[]{:S(2)}) %collective-permute-start.17) | collective-permute-done | bytes 1179680 | tf_op jit(solution)/shard_map/ppermute | solution.py:469
  112.5 1.3 collective-permute-start.23
  113.9 10.0 %collective-permute-done.19 = bf16[768,768]{1,0:T(8,128)(2,1)S(1)} collective-permute-done((bf16[768,768]{1,0:T(8,128)(2,1)}, bf16[768,768]{1,0:T(8,128)(2,1)S(1)}, u32[]{:S(2)}, u32[]{:S(2)}) %collective-permute-start.19) | collective-permute-done | bytes 1179680 | tf_op jit(solution)/shard_map/ppermute | solution.py:505
  123.8 1.8 collective-permute-start.25
  125.8 1.6 collective-permute-start.18
  129.0 1.9 copy.9
  130.9 2.3 copy.8
  133.2 3.0 %maximum_select_fusion.refs_12_.refs_16_.refs_20_.refs_11_ = bf16[768,768]{1,0:T(8,128)(2,1)} fusion(bf16[768,768]{1,0:T(8,128)(2,1)} %copy-done.24, bf16[768,256]{1,0:T(8,128)(2,1)} %copy.9, bf16[768,512]{1,0:T(8,128)(2,1)} %copy.8, pred[]{:T(512)S(6)} %eq.3), kind=kLoop, calls=%fused_computation.1 | loop fusion | flops 2949120 | bytes 3538945 | tf_op jit(solution)/shard_map/jit(_where)/select_n | solution.py:508
  136.1 12.3 %shard_map.57.refs_19_ = f32[1536,768]{1,0:T(8,128)} custom-call(s32[3]{0:T(128)} %pad_add_fusion.2.refs_0_, bf16[768,6144]{1,0:T(8,128)(2,1)} %refs_0_.3, bf16[768,768]{1,0:T(8,128)(2,1)} %copy-done.5, bf16[768,768]{1,0:T(8,128)(2,1)} %copy-done.8, bf16[768,768]{1,0:T(8,128)(2,1)} %copy-done.7, bf16[768,768]{1,0:T(8,128)(2,1)} %copy-done.11, ...), custom_call_target="tpu_custom_call" | custom-call | flops 5435817984 | bytes 20054016 | tf_op jit(solution)/shard_map/pallas_call | solution.py:230
  150.9 1.3 collective-permute-start.22
  154.5 1.8 slice.24.refs_27_
  156.3 2.2 slice.22
  158.5 1.8 slice.23
  160.3 1.2 broadcast_select_fusion.refs_17_.refs_21_.refs_12_
  161.4 16.9 %shard_map.58.refs_24_ = f32[1920,768]{1,0:T(8,128)} custom-call(s32[5]{0:T(128)} %stack.77.refs_0_, bf16[768,6144]{1,0:T(8,128)(2,1)} %refs_0_.3, bf16[768,768]{1,0:T(8,128)(2,1)} %copy-done.5, bf16[768,768]{1,0:T(8,128)(2,1)} %copy-done.8, bf16[768,768]{1,0:T(8,128)(2,1)} %copy-done.7, bf16[768,768]{1,0:T(8,128)(2,1)} %copy-done.11, ...), custom_call_target="tpu_custom_call" | custom-call | flops 5888802816 | bytes 25362432 | tf_op jit(solution)/shard_map/pallas_call | solution.py:230
  180.1 3.3 %collective-permute-start.32 = (bf16[768,512]{1,0:T(8,128)(2,1)}, bf16[768,512]{1,0:T(8,128)(2,1)}, u32[]{:S(2)}, u32[]{:S(2)}) collective-permute-start(bf16[768,512]{1,0:T(8,128)(2,1)} %slice.20), channel_id=1, source_target_pairs={{8,0},{12,4},{16,24},{20,28},{0,16},{4,20},{24,8},{28,12},{9,1},{1... | collective-permute-start | bytes 2359304 | tf_op jit(solution)/shard_map/ppermute | solution.py:505
  183.4 17.7 %shard_map.59.refs_28_ = f32[2304,768]{1,0:T(8,128)} custom-call(s32[6]{0:T(128)} %stack.79.refs_0_, bf16[768,6144]{1,0:T(8,128)(2,1)} %refs_0_.3, bf16[768,768]{1,0:T(8,128)(2,1)} %copy-done.5, bf16[768,768]{1,0:T(8,128)(2,1)} %copy-done.8, bf16[768,768]{1,0:T(8,128)(2,1)} %copy-done.7, bf16[768,768]{1,0:T(8,128)(2,1)} %copy-done.11, ...), custom_call_target="tpu_custom_call" | custom-call | flops 4982833152 | bytes 27721728 | tf_op jit(solution)/shard_map/pallas_call | solution.py:230
  202.0 4.6 %collective-permute-done.30.refs_6_.refs_22_ = bf16[768,768]{1,0:T(8,128)(2,1)S(1)} collective-permute-done((bf16[768,768]{1,0:T(8,128)(2,1)}, bf16[768,768]{1,0:T(8,128)(2,1)S(1)}, u32[]{:S(2)}, u32[]{:S(2)}) %collective-permute-start.30) | collective-permute-done | bytes 1179680 | tf_op jit(solution)/shard_map/ppermute | solution.py:472
  206.7 4.6 %collective-permute-start.36 = (bf16[768,512]{1,0:T(8,128)(2,1)}, bf16[768,512]{1,0:T(8,128)(2,1)}, u32[]{:S(2)}, u32[]{:S(2)}) collective-permute-start(bf16[768,512]{1,0:T(8,128)(2,1)} %slice.22), channel_id=1, source_target_pairs={{0,24},{4,28},{24,0},{28,4},{1,25},{5,29},{25,1},{29,5},{2,26},{6,... | collective-permute-start | bytes 2359304 | tf_op jit(solution)/shard_map/ppermute | solution.py:505
  212.3 13.4 %shard_map.60.refs_29_ = f32[768,768]{1,0:T(8,128)} custom-call(s32[6]{0:T(128)} %stack.79.refs_0_, bf16[768,768]{1,0:T(8,128)(2,1)} %get-tuple-element.86.refs_1_.refs_17_, bf16[768,768]{1,0:T(8,128)(2,1)} %collective-permute-done.22.refs_2_.refs_18_, bf16[768,768]{1,0:T(8,128)(2,1)} %collective-permute-done.28.refs_3_.refs_19_, ...), custom_call_target="tpu_custom_call" | custom-call | flops 5435817984 | bytes 18874368 | tf_op jit(solution)/shard_map/pallas_call | solution.py:230
  225.7 5.0 %collective-permute-done.36.refs_26_ = bf16[768,512]{1,0:T(8,128)(2,1)} collective-permute-done((bf16[768,512]{1,0:T(8,128)(2,1)}, bf16[768,512]{1,0:T(8,128)(2,1)}, u32[]{:S(2)}, u32[]{:S(2)}) %collective-permute-start.36) | collective-permute-done | bytes 786464 | tf_op jit(solution)/shard_map/ppermute | solution.py:505
  230.6 4.5 %collective-permute-start.35 = (bf16[768,256]{1,0:T(8,128)(2,1)}, bf16[768,256]{1,0:T(8,128)(2,1)S(1)}, u32[]{:S(2)}, u32[]{:S(2)}) collective-permute-start(bf16[768,256]{1,0:T(8,128)(2,1)} %slice.23), channel_id=1, source_target_pairs={{0,24},{4,28},{24,0},{28,4},{1,25},{5,29},{25,1},{29,5},{2,26},{6,... | collective-permute-start | bytes 1179656 | tf_op jit(solution)/shard_map/ppermute | solution.py:505
  235.4 15.9 %shard_map.62 = (bf16[3072,512]{1,0:T(8,128)(2,1)}, f32[4,2,128,128]{3,2,1,0:T(8,128)}, f32[2,128,128]{2,1,0:T(8,128)}) custom-call(s32[4]{0:T(128)} %pad_add_fusion.where_ref, s32[2]{0:T(128)} %pad_add_fusion.1.k_ref, s32[8]{0:T(128)} %bitcast.22, bf16[768,6144]{1,0:T(8,128)(2,1)} %refs_0_.3, bf16[768,768]{1,0:T(8,128)(2,1)} %copy-done.5, ...), custom_call_target="tpu_custom_call" | custom-call | flops 7247757312 | bytes 28311552 | tf_op jit(solution)/shard_map/pallas_call | solution.py:230
  251.4 1.7 collective-permute-start.37
  253.9 9.5 %shard_map.61.q_ref = bf16[3072,256]{1,0:T(8,128)(2,1)} custom-call(s32[4]{0:T(128)} %pad_add_fusion.where_ref, s32[2]{0:T(128)} %pad_add_fusion.1.k_ref, bf16[768,6144]{1,0:T(8,128)(2,1)} %refs_0_.3, bf16[768,768]{1,0:T(8,128)(2,1)} %copy-done.5, bf16[768,768]{1,0:T(8,128)(2,1)} %copy-done.8, bf16[768,768]{1,0:T(8,128)(2,1)} %copy-done.7, ...), custom_call_target="tpu_custom_call" | custom-call | flops 3623878656 | bytes 21233664 | tf_op jit(solution)/shard_map/pallas_call | solution.py:230
  263.4 1.4 copy-done.1
  264.8 2.4 shard_map.63
  267.2 1.1 collective-permute-start.38
  268.3 2.4 shard_map.66
  270.7 1.5 collective-permute-start.42
  272.3 2.4 shard_map.65
  275.5 1.1 collective-permute-start.41
  276.6 1.5 collective-permute-start.40
  278.2 1.9 collective-permute-done.38.refs_3_
  280.0 1.2 collective-permute-start.39
  281.2 2.4 shard_map.64
  283.7 1.1 collective-permute-start.45
  285.6 1.8 collective-permute-done.45
  287.9 1.2 collective-permute-done.39.refs_1_
  289.1 2.8 shard_map.67
  (130 shorter events, 22.9 us)
Async XLA Ops:
  3.6 29.1 %collective-permute-start = (bf16[768,768]{1,0:T(8,128)(2,1)}, bf16[768,768]{1,0:T(8,128)(2,1)S(1)}, u32[]{:S(2)}, u32[]{:S(2)}) collective-permute-start(bf16[768,768]{1,0:T(8,128)(2,1)} %shard_map.55), channel_id=1, source_target_pairs={{0,4},{4,0},{8,12},{12,8},{16,20},{20,16},{24,28},{28,24},{1,5},{5... | collective-permute-start | bytes 3538952 | tf_op jit(solution)/shard_map/ppermute | solution.py:469
  6.6 27.9 %collective-permute-start.5 = (bf16[768,768]{1,0:T(8,128)(2,1)}, bf16[768,768]{1,0:T(8,128)(2,1)S(1)}, u32[]{:S(2)}, u32[]{:S(2)}) collective-permute-start(bf16[768,768]{1,0:T(8,128)(2,1)} %shard_map.55), channel_id=1, source_target_pairs={{8,0},{12,4},{16,24},{20,28},{0,8},{4,12},{24,16},{28,20},{9,1},{1... | collective-permute-start | bytes 3538952 | tf_op jit(solution)/shard_map/ppermute | solution.py:505
  12.7 21.8 %collective-permute-start.3 = (bf16[768,2,256]{0,2,1:T(8,128)(2,1)}, bf16[768,2,256]{0,2,1:T(8,128)(2,1)S(1)}, u32[]{:S(2)}, u32[]{:S(2)}) collective-permute-start(bf16[768,2,256]{0,2,1:T(8,128)(2,1)} %copy.10), channel_id=1, source_target_pairs={{8,16},{12,20},{16,8},{20,12},{9,17},{13,21},{17,9},{21,13},{10,18... | collective-permute-start | bytes 2359304 | tf_op jit(solution)/shard_map/ppermute | solution.py:505
  16.3 18.2 %collective-permute-start.4 = (bf16[768,2,128]{0,2,1:T(8,128)(2,1)}, bf16[768,2,128]{0,2,1:T(8,128)(2,1)S(1)}, u32[]{:S(2)}, u32[]{:S(2)}) collective-permute-start(bf16[768,2,128]{0,2,1:T(8,128)(2,1)} %copy.11), channel_id=1, source_target_pairs={{8,16},{12,20},{16,8},{20,12},{9,17},{13,21},{17,9},{21,13},{10,18... | collective-permute-start | bytes 1179656 | tf_op jit(solution)/shard_map/ppermute | solution.py:505
  32.7 71.5 %copy-start.5 = (bf16[768,768]{1,0:T(8,128)(2,1)}, bf16[768,768]{1,0:T(8,128)(2,1)S(1)}, u32[]{:S(2)}) copy-start(bf16[768,768]{1,0:T(8,128)(2,1)S(1)} %collective-permute-done.refs_2_.refs_1_) | copy-start | bytes 3538948
  32.7 27.4 %collective-permute-start.8 = (bf16[768,768]{1,0:T(8,128)(2,1)}, bf16[768,768]{1,0:T(8,128)(2,1)S(1)}, u32[]{:S(2)}, u32[]{:S(2)}) collective-permute-start(bf16[768,768]{1,0:T(8,128)(2,1)} %get-tuple-element.60), channel_id=1, source_target_pairs={{0,4},{4,0},{8,12},{12,8},{16,20},{20,16},{24,28},{28,24},{1,5},{5... | collective-permute-start | bytes 3538952 | tf_op jit(solution)/shard_map/ppermute | solution.py:469
  34.5 25.6 %copy-start.28 = (bf16[768,2,128]{0,2,1:T(8,128)(2,1)}, bf16[768,2,128]{0,2,1:T(8,128)(2,1)S(1)}, u32[]{:S(2)}) copy-start(bf16[768,2,128]{0,2,1:T(8,128)(2,1)S(1)} %collective-permute-done.4) | copy-start | bytes 1179652
  34.5 25.6 %copy-start.25 = (bf16[768,2,256]{0,2,1:T(8,128)(2,1)}, bf16[768,2,256]{0,2,1:T(8,128)(2,1)S(1)}, u32[]{:S(2)}) copy-start(bf16[768,2,256]{0,2,1:T(8,128)(2,1)S(1)} %collective-permute-done.3) | copy-start | bytes 2359300
  34.5 71.3 %copy-start.13 = (bf16[768,768]{1,0:T(8,128)(2,1)}, bf16[768,768]{1,0:T(8,128)(2,1)S(1)}, u32[]{:S(2)}) copy-start(bf16[768,768]{1,0:T(8,128)(2,1)S(1)} %collective-permute-done.5.refs_10_.refs_9_) | copy-start | bytes 3538948
  34.5 34.8 %collective-permute-start.11 = (bf16[768,768]{1,0:T(8,128)(2,1)}, bf16[768,768]{1,0:T(8,128)(2,1)S(1)}, u32[]{:S(2)}, u32[]{:S(2)}) collective-permute-start(bf16[768,768]{1,0:T(8,128)(2,1)} %get-tuple-element.64), channel_id=1, source_target_pairs={{8,24},{12,28},{16,0},{20,4},{0,8},{4,12},{24,16},{28,20},{9,25},{... | collective-permute-start | bytes 3538952 | tf_op jit(solution)/shard_map/ppermute | solution.py:505
  43.4 27.6 %collective-permute-start.2 = (bf16[768,768]{1,0:T(8,128)(2,1)S(1)}, bf16[768,768]{1,0:T(8,128)(2,1)S(1)}, u32[]{:S(2)}, u32[]{:S(2)}) collective-permute-start(bf16[768,768]{1,0:T(8,128)(2,1)S(1)} %collective-permute-done.refs_2_.refs_1_), channel_id=1, source_target_pairs={{0,1},{1,0},{2,3},{3,2},{4,5},{5,4},{6,7},{7,6},{8,9},{9,8},{10,11... | collective-permute-start | bytes 3538952 | tf_op jit(solution)/shard_map/ppermute | solution.py:472
  43.4 27.6 %collective-permute-start.6 = (bf16[768,768]{1,0:T(8,128)(2,1)S(1)}, bf16[768,768]{1,0:T(8,128)(2,1)S(1)}, u32[]{:S(2)}, u32[]{:S(2)}) collective-permute-start(bf16[768,768]{1,0:T(8,128)(2,1)S(1)} %collective-permute-done.5.refs_10_.refs_9_), channel_id=1, source_target_pairs={{0,1},{1,0},{2,3},{3,2},{4,5},{5,4},{6,7},{7,6},{8,9},{9,8},{10,11... | collective-permute-start | bytes 3538952 | tf_op jit(solution)/shard_map/ppermute | solution.py:472
  43.9 27.9 %collective-permute-start.1 = (bf16[768,768]{1,0:T(8,128)(2,1)S(1)}, bf16[768,768]{1,0:T(8,128)(2,1)S(1)}, u32[]{:S(2)}, u32[]{:S(2)}) collective-permute-start(bf16[768,768]{1,0:T(8,128)(2,1)S(1)} %collective-permute-done.refs_2_.refs_1_), channel_id=1, source_target_pairs={{0,2},{1,3},{2,0},{3,1},{4,6},{5,7},{6,4},{7,5},{8,10},{9,11},{10,... | collective-permute-start | bytes 3538952 | tf_op jit(solution)/shard_map/ppermute | solution.py:472
  60.1 44.1 %copy-start.6 = (bf16[768,768]{1,0:T(8,128)(2,1)}, bf16[768,768]{1,0:T(8,128)(2,1)S(1)}, u32[]{:S(2)}) copy-start(bf16[768,768]{1,0:T(8,128)(2,1)S(1)} %collective-permute-done.8.refs_6_.refs_5_) | copy-start | bytes 3538948
  60.1 26.5 %collective-permute-start.15 = (bf16[768,768]{1,0:T(8,128)(2,1)}, bf16[768,768]{1,0:T(8,128)(2,1)S(1)}, u32[]{:S(2)}, u32[]{:S(2)}) collective-permute-start(bf16[768,768]{1,0:T(8,128)(2,1)} %get-tuple-element.70), channel_id=1, source_target_pairs={{0,4},{4,0},{8,12},{12,8},{16,20},{20,16},{24,28},{28,24},{1,5},{5... | collective-permute-start | bytes 3538952 | tf_op jit(solution)/shard_map/ppermute | solution.py:469
  69.3 25.8 %collective-permute-start.14 = (bf16[768,768]{1,0:T(8,128)(2,1)}, bf16[768,768]{1,0:T(8,128)(2,1)S(1)}, u32[]{:S(2)}, u32[]{:S(2)}) collective-permute-start(bf16[768,768]{1,0:T(8,128)(2,1)} %get-tuple-element.68), channel_id=1, source_target_pairs={{8,0},{12,4},{16,24},{20,28},{0,16},{4,20},{24,8},{28,12},{9,1},{1... | collective-permute-start | bytes 3538952 | tf_op jit(solution)/shard_map/ppermute | solution.py:505
  71.0 34.8 %copy-start.7 = (bf16[768,768]{1,0:T(8,128)(2,1)}, bf16[768,768]{1,0:T(8,128)(2,1)S(1)}, u32[]{:S(2)}) copy-start(bf16[768,768]{1,0:T(8,128)(2,1)S(1)} %collective-permute-done.2.refs_4_.refs_3_) | copy-start | bytes 3538948
  71.0 34.8 %copy-start.14 = (bf16[768,768]{1,0:T(8,128)(2,1)}, bf16[768,768]{1,0:T(8,128)(2,1)S(1)}, u32[]{:S(2)}) copy-start(bf16[768,768]{1,0:T(8,128)(2,1)S(1)} %collective-permute-done.6.refs_12_.refs_11_) | copy-start | bytes 3538948
  71.8 28.6 %copy-start.8 = (bf16[768,768]{1,0:T(8,128)(2,1)}, bf16[768,768]{1,0:T(8,128)(2,1)S(1)}, u32[]{:S(2)}) copy-start(bf16[768,768]{1,0:T(8,128)(2,1)S(1)} %collective-permute-done.1.refs_3_.refs_2_) | copy-start | bytes 3538948
  71.8 27.0 %collective-permute-start.9 = (bf16[768,768]{1,0:T(8,128)(2,1)S(1)}, bf16[768,768]{1,0:T(8,128)(2,1)S(1)}, u32[]{:S(2)}, u32[]{:S(2)}) collective-permute-start(bf16[768,768]{1,0:T(8,128)(2,1)S(1)} %collective-permute-done.8.refs_6_.refs_5_), channel_id=1, source_target_pairs={{0,2},{1,3},{2,0},{3,1},{4,6},{5,7},{6,4},{7,5},{8,10},{9,11},{10,... | collective-permute-start | bytes 3538952 | tf_op jit(solution)/shard_map/ppermute | solution.py:472
  73.3 27.0 %collective-permute-start.10 = (bf16[768,768]{1,0:T(8,128)(2,1)S(1)}, bf16[768,768]{1,0:T(8,128)(2,1)S(1)}, u32[]{:S(2)}, u32[]{:S(2)}) collective-permute-start(bf16[768,768]{1,0:T(8,128)(2,1)S(1)} %collective-permute-done.8.refs_6_.refs_5_), channel_id=1, source_target_pairs={{0,1},{1,0},{2,3},{3,2},{4,5},{5,4},{6,7},{7,6},{8,9},{9,8},{10,11... | collective-permute-start | bytes 3538952 | tf_op jit(solution)/shard_map/ppermute | solution.py:472
  73.3 27.0 %collective-permute-start.7 = (bf16[768,768]{1,0:T(8,128)(2,1)S(1)}, bf16[768,768]{1,0:T(8,128)(2,1)S(1)}, u32[]{:S(2)}, u32[]{:S(2)}) collective-permute-start(bf16[768,768]{1,0:T(8,128)(2,1)S(1)} %collective-permute-done.1.refs_3_.refs_2_), channel_id=1, source_target_pairs={{0,1},{1,0},{2,3},{3,2},{4,5},{5,4},{6,7},{7,6},{8,9},{9,8},{10,11... | collective-permute-start | bytes 3538952 | tf_op jit(solution)/shard_map/ppermute | solution.py:472
  86.6 37.2 %copy-start.21 = (bf16[768,768]{1,0:T(8,128)(2,1)}, bf16[768,768]{1,0:T(8,128)(2,1)S(1)}, u32[]{:S(2)}) copy-start(bf16[768,768]{1,0:T(8,128)(2,1)S(1)} %collective-permute-done.15) | copy-start | bytes 3538948
  86.6 25.9 %collective-permute-start.17 = (bf16[768,768]{1,0:T(8,128)(2,1)S(1)}, bf16[768,768]{1,0:T(8,128)(2,1)}, u32[]{:S(2)}, u32[]{:S(2)}) collective-permute-start(bf16[768,768]{1,0:T(8,128)(2,1)S(1)} %collective-permute-done.5.refs_10_.refs_9_), channel_id=1, source_target_pairs={{0,4},{4,0},{8,12},{12,8},{16,20},{20,16},{24,28},{28,24},{1,5},{5... | collective-permute-start | bytes 3538952 | tf_op jit(solution)/shard_map/ppermute | solution.py:469
  95.1 28.8 %collective-permute-start.19 = (bf16[768,768]{1,0:T(8,128)(2,1)}, bf16[768,768]{1,0:T(8,128)(2,1)S(1)}, u32[]{:S(2)}, u32[]{:S(2)}) collective-permute-start(bf16[768,768]{1,0:T(8,128)(2,1)} %get-tuple-element.82), channel_id=1, source_target_pairs={{0,24},{4,28},{24,0},{28,4},{1,25},{5,29},{25,1},{29,5},{2,26},{6,... | collective-permute-start | bytes 3538952 | tf_op jit(solution)/shard_map/ppermute | solution.py:505
  98.8 7.0 %copy-start.9 = (bf16[768,768]{1,0:T(8,128)(2,1)}, bf16[768,768]{1,0:T(8,128)(2,1)S(1)}, u32[]{:S(2)}) copy-start(bf16[768,768]{1,0:T(8,128)(2,1)S(1)} %collective-permute-done.9.refs_7_.refs_6_) | copy-start | bytes 3538948
  98.8 26.9 %collective-permute-start.13 = (bf16[768,768]{1,0:T(8,128)(2,1)S(1)}, bf16[768,768]{1,0:T(8,128)(2,1)}, u32[]{:S(2)}, u32[]{:S(2)}) collective-permute-start(bf16[768,768]{1,0:T(8,128)(2,1)S(1)} %collective-permute-done.5.refs_10_.refs_9_), channel_id=1, source_target_pairs={{0,2},{1,3},{2,0},{3,1},{4,6},{5,7},{6,4},{7,5},{8,10},{9,11},{10,... | collective-permute-start | bytes 3538952 | tf_op jit(solution)/shard_map/ppermute | solution.py:472
  102.5 24.9 %collective-permute-start.12 = (bf16[768,768]{1,0:T(8,128)(2,1)S(1)}, bf16[768,768]{1,0:T(8,128)(2,1)S(1)}, u32[]{:S(2)}, u32[]{:S(2)}) collective-permute-start(bf16[768,768]{1,0:T(8,128)(2,1)S(1)} %collective-permute-done.9.refs_7_.refs_6_), channel_id=1, source_target_pairs={{0,1},{1,0},{2,3},{3,2},{4,5},{5,4},{6,7},{7,6},{8,9},{9,8},{10,11... | collective-permute-start | bytes 3538952 | tf_op jit(solution)/shard_map/ppermute | solution.py:472
  112.5 35.9 %collective-permute-start.23 = (bf16[768,768]{1,0:T(8,128)(2,1)}, bf16[768,768]{1,0:T(8,128)(2,1)}, u32[]{:S(2)}, u32[]{:S(2)}) collective-permute-start(bf16[768,768]{1,0:T(8,128)(2,1)} %get-tuple-element.81), channel_id=1, source_target_pairs={{0,4},{4,0},{8,12},{12,8},{16,20},{20,16},{24,28},{28,24},{1,5},{5... | collective-permute-start | bytes 3538952 | tf_op jit(solution)/shard_map/ppermute | solution.py:469
  123.8 25.3 %collective-permute-start.25 = (bf16[768,768]{1,0:T(8,128)(2,1)S(1)}, bf16[768,768]{1,0:T(8,128)(2,1)}, u32[]{:S(2)}, u32[]{:S(2)}) collective-permute-start(bf16[768,768]{1,0:T(8,128)(2,1)S(1)} %collective-permute-done.15), channel_id=1, source_target_pairs={{8,16},{12,20},{16,8},{20,12},{9,17},{13,21},{17,9},{21,13},{10,18... | collective-permute-start | bytes 3538952 | tf_op jit(solution)/shard_map/ppermute | solution.py:505
  125.7 24.2 %collective-permute-start.24 = (bf16[768,768]{1,0:T(8,128)(2,1)}, bf16[768,768]{1,0:T(8,128)(2,1)}, u32[]{:S(2)}, u32[]{:S(2)}) collective-permute-start(bf16[768,768]{1,0:T(8,128)(2,1)} %get-tuple-element.82), channel_id=1, source_target_pairs={{8,0},{12,4},{16,24},{20,28},{0,8},{4,12},{24,16},{28,20},{9,1},{1... | collective-permute-start | bytes 3538952 | tf_op jit(solution)/shard_map/ppermute | solution.py:505
  125.8 25.1 %collective-permute-start.18 = (bf16[768,768]{1,0:T(8,128)(2,1)}, bf16[768,768]{1,0:T(8,128)(2,1)S(1)}, u32[]{:S(2)}, u32[]{:S(2)}) collective-permute-start(bf16[768,768]{1,0:T(8,128)(2,1)} %collective-permute-done.17.refs_14_.refs_13_), channel_id=1, source_target_pairs={{0,2},{1,3},{2,0},{3,1},{4,6},{5,7},{6,4},{7,5},{8,10},{9,11},{10,... | collective-permute-start | bytes 3538952 | tf_op jit(solution)/shard_map/ppermute | solution.py:472
  128.4 23.8 %collective-permute-start.16 = (bf16[768,768]{1,0:T(8,128)(2,1)}, bf16[768,768]{1,0:T(8,128)(2,1)S(1)}, u32[]{:S(2)}, u32[]{:S(2)}) collective-permute-start(bf16[768,768]{1,0:T(8,128)(2,1)} %collective-permute-done.13.refs_11_.refs_10_), channel_id=1, source_target_pairs={{0,1},{1,0},{2,3},{3,2},{4,5},{5,4},{6,7},{7,6},{8,9},{9,8},{10,11... | collective-permute-start | bytes 3538952 | tf_op jit(solution)/shard_map/ppermute | solution.py:472
  148.5 29.8 %collective-permute-start.27 = (bf16[768,768]{1,0:T(8,128)(2,1)}, bf16[768,768]{1,0:T(8,128)(2,1)}, u32[]{:S(2)}, u32[]{:S(2)}) collective-permute-start(bf16[768,768]{1,0:T(8,128)(2,1)} %get-tuple-element.86.refs_1_.refs_17_), channel_id=1, source_target_pairs={{0,4},{4,0},{8,12},{12,8},{16,20},{20,16},{24,28},{28,24},{1,5},{5... | collective-permute-start | bytes 3538952 | tf_op jit(solution)/shard_map/ppermute | solution.py:469
  149.8 28.8 %collective-permute-start.26 = (bf16[768,768]{1,0:T(8,128)(2,1)}, bf16[768,768]{1,0:T(8,128)(2,1)}, u32[]{:S(2)}, u32[]{:S(2)}) collective-permute-start(bf16[768,768]{1,0:T(8,128)(2,1)} %collective-permute-done.23), channel_id=1, source_target_pairs={{8,24},{12,28},{16,0},{20,4},{0,8},{4,12},{24,16},{28,20},{9,25},{... | collective-permute-start | bytes 3538952 | tf_op jit(solution)/shard_map/ppermute | solution.py:505
  150.9 7.6 %copy-start.16 = (bf16[768,768]{1,0:T(8,128)(2,1)}, bf16[768,768]{1,0:T(8,128)(2,1)S(1)}, u32[]{:S(2)}) copy-start(bf16[768,768]{1,0:T(8,128)(2,1)S(1)} %collective-permute-done.18.refs_15_.refs_14_) | copy-start | bytes 3538948
  150.9 28.1 %collective-permute-start.22 = (bf16[768,768]{1,0:T(8,128)(2,1)}, bf16[768,768]{1,0:T(8,128)(2,1)}, u32[]{:S(2)}, u32[]{:S(2)}) collective-permute-start(bf16[768,768]{1,0:T(8,128)(2,1)} %get-tuple-element.86.refs_1_.refs_17_), channel_id=1, source_target_pairs={{0,2},{1,3},{2,0},{3,1},{4,6},{5,7},{6,4},{7,5},{8,10},{9,11},{10,... | collective-permute-start | bytes 3538952 | tf_op jit(solution)/shard_map/ppermute | solution.py:472
  152.2 6.3 %copy-start.15 = (bf16[768,768]{1,0:T(8,128)(2,1)}, bf16[768,768]{1,0:T(8,128)(2,1)S(1)}, u32[]{:S(2)}) copy-start(bf16[768,768]{1,0:T(8,128)(2,1)S(1)} %collective-permute-done.16.refs_13_.refs_12_) | copy-start | bytes 3538948
  152.2 26.9 %collective-permute-start.21 = (bf16[768,768]{1,0:T(8,128)(2,1)S(1)}, bf16[768,768]{1,0:T(8,128)(2,1)S(1)}, u32[]{:S(2)}, u32[]{:S(2)}) collective-permute-start(bf16[768,768]{1,0:T(8,128)(2,1)S(1)} %collective-permute-done.18.refs_15_.refs_14_), channel_id=1, source_target_pairs={{0,1},{1,0},{2,3},{3,2},{4,5},{5,4},{6,7},{7,6},{8,9},{9,8},{10,11... | collective-permute-start | bytes 3538952 | tf_op jit(solution)/shard_map/ppermute | solution.py:472
  152.2 26.9 %collective-permute-start.20 = (bf16[768,768]{1,0:T(8,128)(2,1)}, bf16[768,768]{1,0:T(8,128)(2,1)}, u32[]{:S(2)}, u32[]{:S(2)}) collective-permute-start(bf16[768,768]{1,0:T(8,128)(2,1)} %collective-permute-done.17.refs_14_.refs_13_), channel_id=1, source_target_pairs={{0,1},{1,0},{2,3},{3,2},{4,5},{5,4},{6,7},{7,6},{8,9},{9,8},{10,11... | collective-permute-start | bytes 3538952 | tf_op jit(solution)/shard_map/ppermute | solution.py:472
  179.0 27.6 %collective-permute-start.30 = (bf16[768,768]{1,0:T(8,128)(2,1)}, bf16[768,768]{1,0:T(8,128)(2,1)S(1)}, u32[]{:S(2)}, u32[]{:S(2)}) collective-permute-start(bf16[768,768]{1,0:T(8,128)(2,1)} %collective-permute-done.27.refs_5_.refs_21_), channel_id=1, source_target_pairs={{0,2},{1,3},{2,0},{3,1},{4,6},{5,7},{6,4},{7,5},{8,10},{9,11},{10,... | collective-permute-start | bytes 3538952 | tf_op jit(solution)/shard_map/ppermute | solution.py:472
  179.6 27.0 %collective-permute-start.31 = (bf16[768,768]{1,0:T(8,128)(2,1)}, bf16[768,768]{1,0:T(8,128)(2,1)S(1)}, u32[]{:S(2)}, u32[]{:S(2)}) collective-permute-start(bf16[768,768]{1,0:T(8,128)(2,1)} %collective-permute-done.27.refs_5_.refs_21_), channel_id=1, source_target_pairs={{0,1},{1,0},{2,3},{3,2},{4,5},{5,4},{6,7},{7,6},{8,9},{9,8},{10,11... | collective-permute-start | bytes 3538952 | tf_op jit(solution)/shard_map/ppermute | solution.py:472
  179.6 27.0 %collective-permute-start.29 = (bf16[768,768]{1,0:T(8,128)(2,1)}, bf16[768,768]{1,0:T(8,128)(2,1)}, u32[]{:S(2)}, u32[]{:S(2)}) collective-permute-start(bf16[768,768]{1,0:T(8,128)(2,1)} %collective-permute-done.22.refs_2_.refs_18_), channel_id=1, source_target_pairs={{0,1},{1,0},{2,3},{3,2},{4,5},{5,4},{6,7},{7,6},{8,9},{9,8},{10,11... | collective-permute-start | bytes 3538952 | tf_op jit(solution)/shard_map/ppermute | solution.py:472
  180.1 26.5 %collective-permute-start.28 = (bf16[768,768]{1,0:T(8,128)(2,1)}, bf16[768,768]{1,0:T(8,128)(2,1)}, u32[]{:S(2)}, u32[]{:S(2)}) collective-permute-start(bf16[768,768]{1,0:T(8,128)(2,1)} %get-tuple-element.86.refs_1_.refs_17_), channel_id=1, source_target_pairs={{0,1},{1,0},{2,3},{3,2},{4,5},{5,4},{6,7},{7,6},{8,9},{9,8},{10,11... | collective-permute-start | bytes 3538952 | tf_op jit(solution)/shard_map/ppermute | solution.py:472
  180.1 21.9 %collective-permute-start.32 = (bf16[768,512]{1,0:T(8,128)(2,1)}, bf16[768,512]{1,0:T(8,128)(2,1)}, u32[]{:S(2)}, u32[]{:S(2)}) collective-permute-start(bf16[768,512]{1,0:T(8,128)(2,1)} %slice.20), channel_id=1, source_target_pairs={{8,0},{12,4},{16,24},{20,28},{0,16},{4,20},{24,8},{28,12},{9,1},{1... | collective-permute-start | bytes 2359304 | tf_op jit(solution)/shard_map/ppermute | solution.py:505
  201.1 34.1 %copy-start.27 = (bf16[768,256]{1,0:T(8,128)(2,1)S(1)}, bf16[768,256]{1,0:T(8,128)(2,1)}, u32[]{:S(2)}) copy-start(bf16[768,256]{1,0:T(8,128)(2,1)} %slice.21) | copy-start | bytes 1179652
  206.6 4.6 %collective-permute-start.33 = (bf16[768,768]{1,0:T(8,128)(2,1)S(1)}, bf16[768,768]{1,0:T(8,128)(2,1)S(1)}, u32[]{:S(2)}, u32[]{:S(2)}) collective-permute-start(bf16[768,768]{1,0:T(8,128)(2,1)S(1)} %collective-permute-done.30.refs_6_.refs_22_), channel_id=1, source_target_pairs={{0,1},{1,0},{2,3},{3,2},{4,5},{5,4},{6,7},{7,6},{8,9},{9,8},{10,11... | collective-permute-start | bytes 3538952 | tf_op jit(solution)/shard_map/ppermute | solution.py:472
  206.7 23.9 %collective-permute-start.36 = (bf16[768,512]{1,0:T(8,128)(2,1)}, bf16[768,512]{1,0:T(8,128)(2,1)}, u32[]{:S(2)}, u32[]{:S(2)}) collective-permute-start(bf16[768,512]{1,0:T(8,128)(2,1)} %slice.22), channel_id=1, source_target_pairs={{0,24},{4,28},{24,0},{28,4},{1,25},{5,29},{25,1},{29,5},{2,26},{6,... | collective-permute-start | bytes 2359304 | tf_op jit(solution)/shard_map/ppermute | solution.py:505
  230.6 22.5 %collective-permute-start.35 = (bf16[768,256]{1,0:T(8,128)(2,1)}, bf16[768,256]{1,0:T(8,128)(2,1)S(1)}, u32[]{:S(2)}, u32[]{:S(2)}) collective-permute-start(bf16[768,256]{1,0:T(8,128)(2,1)} %slice.23), channel_id=1, source_target_pairs={{0,24},{4,28},{24,0},{28,4},{1,25},{5,29},{25,1},{29,5},{2,26},{6,... | collective-permute-start | bytes 1179656 | tf_op jit(solution)/shard_map/ppermute | solution.py:505
  235.2 18.7 %collective-permute-start.34 = (bf16[768,256]{1,0:T(8,128)(2,1)S(1)}, bf16[768,256]{1,0:T(8,128)(2,1)}, u32[]{:S(2)}, u32[]{:S(2)}) collective-permute-start(bf16[768,256]{1,0:T(8,128)(2,1)S(1)} %copy-done.27), channel_id=1, source_target_pairs={{8,0},{12,4},{16,24},{20,28},{0,16},{4,20},{24,8},{28,12},{9,1},{1... | collective-permute-start | bytes 1179656 | tf_op jit(solution)/shard_map/ppermute | solution.py:505
  251.4 12.0 %copy-start.2 = (f32[4,2,128,128]{3,2,1,0:T(8,128)S(1)}, f32[4,2,128,128]{3,2,1,0:T(8,128)}, u32[]{:S(2)}) copy-start(f32[4,2,128,128]{3,2,1,0:T(8,128)} %get-tuple-element.96.tails_ref) | copy-start | bytes 1572868
  251.4 12.0 %copy-start.3 = (s32[4]{0:T(128)S(1)}, s32[4]{0:T(128)}, u32[]{:S(2)}) copy-start(s32[4]{0:T(128)} %pad_add_fusion.where_ref) | copy-start | bytes 52
  251.4 12.0 %copy-start.4 = (s32[8,1]{0,1:T(1,128)S(1)}, s32[8,1]{0,1:T(1,128)}, u32[]{:S(2)}) copy-start(s32[8,1]{0,1:T(1,128)} %reduce-window.9) | copy-start | bytes 100
  251.4 12.0 %collective-permute-start.37 = (f32[2,128,128]{2,1,0:T(8,128)}, f32[2,128,128]{2,1,0:T(8,128)S(1)}, u32[]{:S(2)}, u32[]{:S(2)}) collective-permute-start(f32[2,128,128]{2,1,0:T(8,128)} %get-tuple-element.97), channel_id=1, source_target_pairs={{0,16},{4,20},{8,24},{12,28},{16,0},{20,4},{24,8},{28,12},{1,17},{... | collective-permute-start | bytes 393224 | tf_op jit(solution)/shard_map/ppermute | solution.py:469
  253.9 9.5 %copy-start = (bf16[3072,512]{1,0:T(8,128)(2,1)S(1)}, bf16[3072,512]{1,0:T(8,128)(2,1)}, u32[]{:S(2)}) copy-start(bf16[3072,512]{1,0:T(8,128)(2,1)} %get-tuple-element.95.kv_ref) | copy-start | bytes 9437188
  267.2 12.8 %collective-permute-start.38 = (bf16[768,256]{1,0:T(8,128)(2,1)S(1)}, bf16[768,256]{1,0:T(8,128)(2,1)S(1)}, u32[]{:S(2)}, u32[]{:S(2)}) collective-permute-start(bf16[768,256]{1,0:T(8,128)(2,1)S(1)} %get-tuple-element.98), channel_id=1, source_target_pairs={{0,12},{4,8},{8,4},{12,0},{16,28},{20,24},{24,20},{28,16},{1,13},{... | collective-permute-start | bytes 1179656 | tf_op jit(solution)/shard_map/ppermute | solution.py:469
  270.7 12.9 %collective-permute-start.42 = (f32[1,768]{1,0:T(1,128)S(1)}, f32[1,768]{1,0:T(1,128)S(1)}, u32[]{:S(2)}, u32[]{:S(2)}) collective-permute-start(f32[1,768]{1,0:T(1,128)S(1)} %get-tuple-element.104), channel_id=1, source_target_pairs={{0,8},{4,12},{8,0},{12,4},{16,24},{20,28},{24,16},{28,20},{1,9},{5... | collective-permute-start | bytes 9224 | tf_op jit(solution)/shard_map/ppermute | solution.py:469
  274.7 8.9 %collective-permute-start.43 = (f32[1,768]{1,0:T(1,128)S(1)}, f32[1,768]{1,0:T(1,128)S(1)}, u32[]{:S(2)}, u32[]{:S(2)}) collective-permute-start(f32[1,768]{1,0:T(1,128)S(1)} %get-tuple-element.105), channel_id=1, source_target_pairs={{0,4},{4,0},{8,12},{12,8},{16,20},{20,16},{24,28},{28,24},{1,5},{5... | collective-permute-start | bytes 9224 | tf_op jit(solution)/shard_map/ppermute | solution.py:469
  275.5 8.1 %collective-permute-start.41 = (f32[1,768]{1,0:T(1,128)S(1)}, f32[1,768]{1,0:T(1,128)S(1)}, u32[]{:S(2)}, u32[]{:S(2)}) collective-permute-start(f32[1,768]{1,0:T(1,128)S(1)} %get-tuple-element.103), channel_id=1, source_target_pairs={{0,12},{4,8},{8,4},{12,0},{16,28},{20,24},{24,20},{28,16},{1,13},{... | collective-permute-start | bytes 9224 | tf_op jit(solution)/shard_map/ppermute | solution.py:469
  276.6 11.3 %collective-permute-start.40 = (bf16[768,256]{1,0:T(8,128)(2,1)S(1)}, bf16[768,256]{1,0:T(8,128)(2,1)S(1)}, u32[]{:S(2)}, u32[]{:S(2)}) collective-permute-start(bf16[768,256]{1,0:T(8,128)(2,1)S(1)} %get-tuple-element.102), channel_id=1, source_target_pairs={{0,8},{4,12},{8,0},{12,4},{16,24},{20,28},{24,16},{28,20},{1,9},{5... | collective-permute-start | bytes 1179656 | tf_op jit(solution)/shard_map/ppermute | solution.py:469
  280.0 9.1 %collective-permute-start.39 = (bf16[768,256]{1,0:T(8,128)(2,1)S(1)}, bf16[768,256]{1,0:T(8,128)(2,1)S(1)}, u32[]{:S(2)}, u32[]{:S(2)}) collective-permute-start(bf16[768,256]{1,0:T(8,128)(2,1)S(1)} %get-tuple-element.101), channel_id=1, source_target_pairs={{0,4},{4,0},{8,12},{12,8},{16,20},{20,16},{24,28},{28,24},{1,5},{5... | collective-permute-start | bytes 1179656 | tf_op jit(solution)/shard_map/ppermute | solution.py:469
  283.6 2.0 collective-permute-start.44
  283.7 3.7 %collective-permute-start.45 = (f32[1,768]{1,0:T(1,128)S(1)}, f32[1,768]{1,0:T(1,128)S(1)}, u32[]{:S(2)}, u32[]{:S(2)}) collective-permute-start(f32[1,768]{1,0:T(1,128)S(1)} %add_add_fusion.1), channel_id=1, source_target_pairs={{0,2},{1,3},{2,0},{3,1},{4,6},{5,7},{6,4},{7,5},{8,10},{9,11},{10,... | collective-permute-start | bytes 9224 | tf_op jit(solution)/shard_map/ppermute | solution.py:472
  284.9 3.0 %collective-permute-start.46 = (f32[1,768]{1,0:T(1,128)S(1)}, f32[1,768]{1,0:T(1,128)S(1)}, u32[]{:S(2)}, u32[]{:S(2)}) collective-permute-start(f32[1,768]{1,0:T(1,128)S(1)} %add_add_fusion.1), channel_id=1, source_target_pairs={{0,3},{1,2},{2,1},{3,0},{4,7},{5,6},{6,5},{7,4},{8,11},{9,10},{10,... | collective-permute-start | bytes 9224 | tf_op jit(solution)/shard_map/ppermute | solution.py:472
  (14 other events, 39.4 us)

commit v6 on v5

--- a/solution.py
+++ b/solution.py
@@ -356,7 +356,7 @@
 
 def finish(where, parts, squares, gain, count):
     rows, width = parts[0].shape
-    cut = rows // 3 if rows % 384 == 0 else rows
+    cut = rows // 2 if rows % 256 == 0 else rows
     return pl.pallas_call(
         functools.partial(finish_body, count),
         grid_spec=pltpu.PrefetchScalarGridSpec(

time: 298 us -> 297 us (level)
  no operation moved by 1% of the time
where the time goes in v6:
time: 297 us; the launch traced here: 292 us
  Pallas kernels  108 us (36%)
  waiting for transfers between devices  78.4 us (26%)
  starting transfers between devices  63.3 us (21%)
  local copies, waits for them, and re-layouts  33.1 us (11%)
  other arithmetic  8.18 us (3%)
    pallas_call x6, Pallas kernels, project(): pl.pallas_call(body, grid_spec=pltpu.PrefetchScalarGridSpec(num_scalar_pr...  85.7 us
    ppermute x13, waiting for transfers between devices, hop(): return lax.ppermute(value, 'seq', [(i, i ^ k) for i in only])  38.5 us
    ppermute x13, starting transfers between devices, pairs(): return lambda value: lax.ppermute(value, 'seq', moves)  32.8 us
    ppermute x13, waiting for transfers between devices, pairs(): return lambda value: lax.ppermute(value, 'seq', moves)  31.6 us
    ppermute x13, starting transfers between devices, hop(): return lax.ppermute(value, 'seq', [(i, i ^ k) for i in only])  18.5 us
    unnamed x66, local copies, waits for them, and re-layouts  15.6 us
    ppermute x21, starting transfers between devices, side(): return lax.ppermute(value, 'fsdp', [(i, i ^ k) for i in range(fsdp_size)])  12 us
    pallas_call x4, Pallas kernels, attend(): pl.pallas_call(functools.partial(attend_body, place, cut), grid_spec=pltp...  9.59 us
  transfers between devices with their start and end apart: 47, of which 19 were waited for; matrix products, arithmetic and copies ran while one was open for 12% of the time, Pallas kernels for 34%

profile of v6, /device:TPU:0, one launch (start us, length us, event | category | flops | bytes accessed | tf_op | source)
XLA Modules:
  0.0 291.7 jit_solution(17742343516306981468)
XLA Ops:
  0.6 3.0 %shard_map.55 = bf16[768,768]{1,0:T(8,128)(2,1)} custom-call(s32[4]{0:T(128)} %pad_add_fusion.where_ref, bf16[768,6144]{1,0:T(8,128)(2,1)} %refs_0_.3), custom_call_target="tpu_custom_call" | custom-call | tf_op jit(solution)/shard_map/pallas_call | solution.py:389
  3.6 2.9 %collective-permute-start = (bf16[768,768]{1,0:T(8,128)(2,1)}, bf16[768,768]{1,0:T(8,128)(2,1)S(1)}, u32[]{:S(2)}, u32[]{:S(2)}) collective-permute-start(bf16[768,768]{1,0:T(8,128)(2,1)} %shard_map.55), channel_id=1, source_target_pairs={{0,4},{4,0},{8,12},{12,8},{16,20},{20,16},{24,28},{28,24},{1,5},{5... | collective-permute-start | bytes 3538952 | tf_op jit(solution)/shard_map/ppermute | solution.py:469
  6.6 1.6 collective-permute-start.5
  8.1 2.7 constant_dynamic-slice_fusion.1
  10.8 1.8 copy.10
  13.4 1.8 constant_dynamic-slice_fusion
  17.0 4.7 %copy.12 = bf16[96,8,8,256]{3,1,2,0:T(8,128)(2,1)} copy(bf16[96,8,8,256]{3,2,1,0:T(8,128)(2,1)} %bitcast.29) | data formatting | bytes 6291456
  21.7 1.6 copy.15
  24.0 7.4 %shard_map.56 = (bf16[768,768]{1,0:T(8,128)(2,1)}, bf16[768,768]{1,0:T(8,128)(2,1)}, bf16[768,768]{1,0:T(8,128)(2,1)}, bf16[768,768]{1,0:T(8,128)(2,1)}, bf16[76...) custom-call(s32[4]{0:T(128)} %pad_add_fusion.where_ref, bf16[768,2048]{1,0:T(8,128)(2,1)} %bitcast.27, ...), custom_call_target="tpu_custom_call" | custom-call | tf_op jit(solution)/shard_map/pallas_call | solution.py:436
  31.5 1.3 collective-permute-done.refs_2_.refs_1_
  32.7 1.7 collective-permute-start.8
  34.5 8.9 %collective-permute-start.11 = (bf16[768,768]{1,0:T(8,128)(2,1)}, bf16[768,768]{1,0:T(8,128)(2,1)S(1)}, u32[]{:S(2)}, u32[]{:S(2)}) collective-permute-start(bf16[768,768]{1,0:T(8,128)(2,1)} %get-tuple-element.64), channel_id=1, source_target_pairs={{8,24},{12,28},{16,0},{20,4},{0,8},{4,12},{24,16},{28,20},{9,25},{... | collective-permute-start | bytes 3538952 | tf_op jit(solution)/shard_map/ppermute | solution.py:505
  43.9 1.5 collective-permute-start.1
  45.5 14.7 %collective-permute-done.8.refs_6_.refs_5_ = bf16[768,768]{1,0:T(8,128)(2,1)S(1)} collective-permute-done((bf16[768,768]{1,0:T(8,128)(2,1)}, bf16[768,768]{1,0:T(8,128)(2,1)S(1)}, u32[]{:S(2)}, u32[]{:S(2)}) %collective-permute-start.8) | collective-permute-done | bytes 1179680 | tf_op jit(solution)/shard_map/ppermute | solution.py:469
  60.1 1.5 collective-permute-start.15
  61.6 7.7 %collective-permute-done.11 = bf16[768,768]{1,0:T(8,128)(2,1)S(1)} collective-permute-done((bf16[768,768]{1,0:T(8,128)(2,1)}, bf16[768,768]{1,0:T(8,128)(2,1)S(1)}, u32[]{:S(2)}, u32[]{:S(2)}) %collective-permute-start.11) | collective-permute-done | bytes 1179680 | tf_op jit(solution)/shard_map/ppermute | solution.py:505
  69.3 1.7 collective-permute-start.14
  71.8 1.5 collective-permute-start.9
  73.8 12.8 %collective-permute-done.15 = bf16[768,768]{1,0:T(8,128)(2,1)S(1)} collective-permute-done((bf16[768,768]{1,0:T(8,128)(2,1)}, bf16[768,768]{1,0:T(8,128)(2,1)S(1)}, u32[]{:S(2)}, u32[]{:S(2)}) %collective-permute-start.15) | collective-permute-done | bytes 1179680 | tf_op jit(solution)/shard_map/ppermute | solution.py:469
  86.6 1.3 collective-permute-start.17
  87.9 7.1 %collective-permute-done.14 = bf16[768,768]{1,0:T(8,128)(2,1)S(1)} collective-permute-done((bf16[768,768]{1,0:T(8,128)(2,1)}, bf16[768,768]{1,0:T(8,128)(2,1)S(1)}, u32[]{:S(2)}, u32[]{:S(2)}) %collective-permute-start.14) | collective-permute-done | bytes 1179680 | tf_op jit(solution)/shard_map/ppermute | solution.py:505
  95.1 3.7 %collective-permute-start.19 = (bf16[768,768]{1,0:T(8,128)(2,1)}, bf16[768,768]{1,0:T(8,128)(2,1)S(1)}, u32[]{:S(2)}, u32[]{:S(2)}) collective-permute-start(bf16[768,768]{1,0:T(8,128)(2,1)} %get-tuple-element.82), channel_id=1, source_target_pairs={{0,24},{4,28},{24,0},{28,4},{1,25},{5,29},{25,1},{29,5},{2,26},{6,... | collective-permute-start | bytes 3538952 | tf_op jit(solution)/shard_map/ppermute | solution.py:505
  98.8 1.5 collective-permute-start.13
  104.2 1.6 broadcast_select_fusion.1
  105.8 6.7 %collective-permute-done.17.refs_14_.refs_13_ = bf16[768,768]{1,0:T(8,128)(2,1)} collective-permute-done((bf16[768,768]{1,0:T(8,128)(2,1)S(1)}, bf16[768,768]{1,0:T(8,128)(2,1)}, u32[]{:S(2)}, u32[]{:S(2)}) %collective-permute-start.17) | collective-permute-done | bytes 1179680 | tf_op jit(solution)/shard_map/ppermute | solution.py:469
  112.5 1.3 collective-permute-start.23
  113.9 10.0 %collective-permute-done.19 = bf16[768,768]{1,0:T(8,128)(2,1)S(1)} collective-permute-done((bf16[768,768]{1,0:T(8,128)(2,1)}, bf16[768,768]{1,0:T(8,128)(2,1)S(1)}, u32[]{:S(2)}, u32[]{:S(2)}) %collective-permute-start.19) | collective-permute-done | bytes 1179680 | tf_op jit(solution)/shard_map/ppermute | solution.py:505
  123.8 1.8 collective-permute-start.25
  125.8 1.6 collective-permute-start.18
  129.0 1.9 copy.9
  130.9 2.3 copy.8
  133.2 3.0 %maximum_select_fusion.refs_12_.refs_16_.refs_20_.refs_11_ = bf16[768,768]{1,0:T(8,128)(2,1)} fusion(bf16[768,768]{1,0:T(8,128)(2,1)} %copy-done.24, bf16[768,256]{1,0:T(8,128)(2,1)} %copy.9, bf16[768,512]{1,0:T(8,128)(2,1)} %copy.8, pred[]{:T(512)S(6)} %eq.3), kind=kLoop, calls=%fused_computation.1 | loop fusion | flops 2949120 | bytes 3538945 | tf_op jit(solution)/shard_map/jit(_where)/select_n | solution.py:508
  136.1 12.3 %shard_map.57.refs_19_ = f32[1536,768]{1,0:T(8,128)} custom-call(s32[3]{0:T(128)} %pad_add_fusion.2.refs_0_, bf16[768,6144]{1,0:T(8,128)(2,1)} %refs_0_.3, bf16[768,768]{1,0:T(8,128)(2,1)} %copy-done.5, bf16[768,768]{1,0:T(8,128)(2,1)} %copy-done.8, bf16[768,768]{1,0:T(8,128)(2,1)} %copy-done.7, bf16[768,768]{1,0:T(8,128)(2,1)} %copy-done.11, ...), custom_call_target="tpu_custom_call" | custom-call | flops 5435817984 | bytes 20054016 | tf_op jit(solution)/shard_map/pallas_call | solution.py:230
  150.9 1.3 collective-permute-start.22
  154.5 1.8 slice.24.refs_27_
  156.3 2.2 slice.22
  158.5 1.8 slice.23
  160.3 1.2 broadcast_select_fusion.refs_17_.refs_21_.refs_12_
  161.4 16.9 %shard_map.58.refs_24_ = f32[1920,768]{1,0:T(8,128)} custom-call(s32[5]{0:T(128)} %stack.77.refs_0_, bf16[768,6144]{1,0:T(8,128)(2,1)} %refs_0_.3, bf16[768,768]{1,0:T(8,128)(2,1)} %copy-done.5, bf16[768,768]{1,0:T(8,128)(2,1)} %copy-done.8, bf16[768,768]{1,0:T(8,128)(2,1)} %copy-done.7, bf16[768,768]{1,0:T(8,128)(2,1)} %copy-done.11, ...), custom_call_target="tpu_custom_call" | custom-call | flops 5888802816 | bytes 25362432 | tf_op jit(solution)/shard_map/pallas_call | solution.py:230
  180.1 3.3 %collective-permute-start.32 = (bf16[768,512]{1,0:T(8,128)(2,1)}, bf16[768,512]{1,0:T(8,128)(2,1)}, u32[]{:S(2)}, u32[]{:S(2)}) collective-permute-start(bf16[768,512]{1,0:T(8,128)(2,1)} %slice.20), channel_id=1, source_target_pairs={{8,0},{12,4},{16,24},{20,28},{0,16},{4,20},{24,8},{28,12},{9,1},{1... | collective-permute-start | bytes 2359304 | tf_op jit(solution)/shard_map/ppermute | solution.py:505
  183.4 17.7 %shard_map.59.refs_28_ = f32[2304,768]{1,0:T(8,128)} custom-call(s32[6]{0:T(128)} %stack.79.refs_0_, bf16[768,6144]{1,0:T(8,128)(2,1)} %refs_0_.3, bf16[768,768]{1,0:T(8,128)(2,1)} %copy-done.5, bf16[768,768]{1,0:T(8,128)(2,1)} %copy-done.8, bf16[768,768]{1,0:T(8,128)(2,1)} %copy-done.7, bf16[768,768]{1,0:T(8,128)(2,1)} %copy-done.11, ...), custom_call_target="tpu_custom_call" | custom-call | flops 4982833152 | bytes 27721728 | tf_op jit(solution)/shard_map/pallas_call | solution.py:230
  202.0 4.6 %collective-permute-done.30.refs_6_.refs_22_ = bf16[768,768]{1,0:T(8,128)(2,1)S(1)} collective-permute-done((bf16[768,768]{1,0:T(8,128)(2,1)}, bf16[768,768]{1,0:T(8,128)(2,1)S(1)}, u32[]{:S(2)}, u32[]{:S(2)}) %collective-permute-start.30) | collective-permute-done | bytes 1179680 | tf_op jit(solution)/shard_map/ppermute | solution.py:472
  206.7 4.6 %collective-permute-start.36 = (bf16[768,512]{1,0:T(8,128)(2,1)}, bf16[768,512]{1,0:T(8,128)(2,1)}, u32[]{:S(2)}, u32[]{:S(2)}) collective-permute-start(bf16[768,512]{1,0:T(8,128)(2,1)} %slice.22), channel_id=1, source_target_pairs={{0,24},{4,28},{24,0},{28,4},{1,25},{5,29},{25,1},{29,5},{2,26},{6,... | collective-permute-start | bytes 2359304 | tf_op jit(solution)/shard_map/ppermute | solution.py:505
  212.3 13.4 %shard_map.60.refs_29_ = f32[768,768]{1,0:T(8,128)} custom-call(s32[6]{0:T(128)} %stack.79.refs_0_, bf16[768,768]{1,0:T(8,128)(2,1)} %get-tuple-element.86.refs_1_.refs_17_, bf16[768,768]{1,0:T(8,128)(2,1)} %collective-permute-done.22.refs_2_.refs_18_, bf16[768,768]{1,0:T(8,128)(2,1)} %collective-permute-done.28.refs_3_.refs_19_, ...), custom_call_target="tpu_custom_call" | custom-call | flops 5435817984 | bytes 18874368 | tf_op jit(solution)/shard_map/pallas_call | solution.py:230
  225.7 5.0 %collective-permute-done.36.refs_26_ = bf16[768,512]{1,0:T(8,128)(2,1)} collective-permute-done((bf16[768,512]{1,0:T(8,128)(2,1)}, bf16[768,512]{1,0:T(8,128)(2,1)}, u32[]{:S(2)}, u32[]{:S(2)}) %collective-permute-start.36) | collective-permute-done | bytes 786464 | tf_op jit(solution)/shard_map/ppermute | solution.py:505
  230.6 4.5 %collective-permute-start.35 = (bf16[768,256]{1,0:T(8,128)(2,1)}, bf16[768,256]{1,0:T(8,128)(2,1)S(1)}, u32[]{:S(2)}, u32[]{:S(2)}) collective-permute-start(bf16[768,256]{1,0:T(8,128)(2,1)} %slice.23), channel_id=1, source_target_pairs={{0,24},{4,28},{24,0},{28,4},{1,25},{5,29},{25,1},{29,5},{2,26},{6,... | collective-permute-start | bytes 1179656 | tf_op jit(solution)/shard_map/ppermute | solution.py:505
  235.4 15.9 %shard_map.62 = (bf16[3072,512]{1,0:T(8,128)(2,1)}, f32[4,2,128,128]{3,2,1,0:T(8,128)}, f32[2,128,128]{2,1,0:T(8,128)}) custom-call(s32[4]{0:T(128)} %pad_add_fusion.where_ref, s32[2]{0:T(128)} %pad_add_fusion.1.k_ref, s32[8]{0:T(128)} %bitcast.22, bf16[768,6144]{1,0:T(8,128)(2,1)} %refs_0_.3, bf16[768,768]{1,0:T(8,128)(2,1)} %copy-done.5, ...), custom_call_target="tpu_custom_call" | custom-call | flops 7247757312 | bytes 28311552 | tf_op jit(solution)/shard_map/pallas_call | solution.py:230
  251.4 1.7 collective-permute-start.37
  253.9 9.5 %shard_map.61.q_ref = bf16[3072,256]{1,0:T(8,128)(2,1)} custom-call(s32[4]{0:T(128)} %pad_add_fusion.where_ref, s32[2]{0:T(128)} %pad_add_fusion.1.k_ref, bf16[768,6144]{1,0:T(8,128)(2,1)} %refs_0_.3, bf16[768,768]{1,0:T(8,128)(2,1)} %copy-done.5, bf16[768,768]{1,0:T(8,128)(2,1)} %copy-done.8, bf16[768,768]{1,0:T(8,128)(2,1)} %copy-done.7, ...), custom_call_target="tpu_custom_call" | custom-call | flops 3623878656 | bytes 21233664 | tf_op jit(solution)/shard_map/pallas_call | solution.py:230
  263.4 1.4 copy-done.1
  264.8 2.4 shard_map.63
  267.2 1.1 collective-permute-start.38
  268.3 2.4 shard_map.66
  270.7 1.5 collective-permute-start.42
  272.3 2.4 shard_map.65
  275.5 1.1 collective-permute-start.41
  276.6 1.5 collective-permute-start.40
  278.2 1.9 collective-permute-done.38.refs_3_
  280.0 1.2 collective-permute-start.39
  281.2 2.4 shard_map.64
  283.7 1.1 collective-permute-start.45
  285.6 1.8 collective-permute-done.45
  287.9 1.2 collective-permute-done.39.refs_1_
  289.1 2.3 shard_map.67
  (130 shorter events, 22.9 us)
Async XLA Ops:
  3.6 29.1 %collective-permute-start = (bf16[768,768]{1,0:T(8,128)(2,1)}, bf16[768,768]{1,0:T(8,128)(2,1)S(1)}, u32[]{:S(2)}, u32[]{:S(2)}) collective-permute-start(bf16[768,768]{1,0:T(8,128)(2,1)} %shard_map.55), channel_id=1, source_target_pairs={{0,4},{4,0},{8,12},{12,8},{16,20},{20,16},{24,28},{28,24},{1,5},{5... | collective-permute-start | bytes 3538952 | tf_op jit(solution)/shard_map/ppermute | solution.py:469
  6.6 27.9 %collective-permute-start.5 = (bf16[768,768]{1,0:T(8,128)(2,1)}, bf16[768,768]{1,0:T(8,128)(2,1)S(1)}, u32[]{:S(2)}, u32[]{:S(2)}) collective-permute-start(bf16[768,768]{1,0:T(8,128)(2,1)} %shard_map.55), channel_id=1, source_target_pairs={{8,0},{12,4},{16,24},{20,28},{0,8},{4,12},{24,16},{28,20},{9,1},{1... | collective-permute-start | bytes 3538952 | tf_op jit(solution)/shard_map/ppermute | solution.py:505
  12.7 21.8 %collective-permute-start.3 = (bf16[768,2,256]{0,2,1:T(8,128)(2,1)}, bf16[768,2,256]{0,2,1:T(8,128)(2,1)S(1)}, u32[]{:S(2)}, u32[]{:S(2)}) collective-permute-start(bf16[768,2,256]{0,2,1:T(8,128)(2,1)} %copy.10), channel_id=1, source_target_pairs={{8,16},{12,20},{16,8},{20,12},{9,17},{13,21},{17,9},{21,13},{10,18... | collective-permute-start | bytes 2359304 | tf_op jit(solution)/shard_map/ppermute | solution.py:505
  16.3 18.2 %collective-permute-start.4 = (bf16[768,2,128]{0,2,1:T(8,128)(2,1)}, bf16[768,2,128]{0,2,1:T(8,128)(2,1)S(1)}, u32[]{:S(2)}, u32[]{:S(2)}) collective-permute-start(bf16[768,2,128]{0,2,1:T(8,128)(2,1)} %copy.11), channel_id=1, source_target_pairs={{8,16},{12,20},{16,8},{20,12},{9,17},{13,21},{17,9},{21,13},{10,18... | collective-permute-start | bytes 1179656 | tf_op jit(solution)/shard_map/ppermute | solution.py:505
  32.7 71.5 %copy-start.5 = (bf16[768,768]{1,0:T(8,128)(2,1)}, bf16[768,768]{1,0:T(8,128)(2,1)S(1)}, u32[]{:S(2)}) copy-start(bf16[768,768]{1,0:T(8,128)(2,1)S(1)} %collective-permute-done.refs_2_.refs_1_) | copy-start | bytes 3538948
  32.7 27.4 %collective-permute-start.8 = (bf16[768,768]{1,0:T(8,128)(2,1)}, bf16[768,768]{1,0:T(8,128)(2,1)S(1)}, u32[]{:S(2)}, u32[]{:S(2)}) collective-permute-start(bf16[768,768]{1,0:T(8,128)(2,1)} %get-tuple-element.60), channel_id=1, source_target_pairs={{0,4},{4,0},{8,12},{12,8},{16,20},{20,16},{24,28},{28,24},{1,5},{5... | collective-permute-start | bytes 3538952 | tf_op jit(solution)/shard_map/ppermute | solution.py:469
  34.5 25.6 %copy-start.28 = (bf16[768,2,128]{0,2,1:T(8,128)(2,1)}, bf16[768,2,128]{0,2,1:T(8,128)(2,1)S(1)}, u32[]{:S(2)}) copy-start(bf16[768,2,128]{0,2,1:T(8,128)(2,1)S(1)} %collective-permute-done.4) | copy-start | bytes 1179652
  34.5 25.6 %copy-start.25 = (bf16[768,2,256]{0,2,1:T(8,128)(2,1)}, bf16[768,2,256]{0,2,1:T(8,128)(2,1)S(1)}, u32[]{:S(2)}) copy-start(bf16[768,2,256]{0,2,1:T(8,128)(2,1)S(1)} %collective-permute-done.3) | copy-start | bytes 2359300
  34.5 71.3 %copy-start.13 = (bf16[768,768]{1,0:T(8,128)(2,1)}, bf16[768,768]{1,0:T(8,128)(2,1)S(1)}, u32[]{:S(2)}) copy-start(bf16[768,768]{1,0:T(8,128)(2,1)S(1)} %collective-permute-done.5.refs_10_.refs_9_) | copy-start | bytes 3538948
  34.5 34.8 %collective-permute-start.11 = (bf16[768,768]{1,0:T(8,128)(2,1)}, bf16[768,768]{1,0:T(8,128)(2,1)S(1)}, u32[]{:S(2)}, u32[]{:S(2)}) collective-permute-start(bf16[768,768]{1,0:T(8,128)(2,1)} %get-tuple-element.64), channel_id=1, source_target_pairs={{8,24},{12,28},{16,0},{20,4},{0,8},{4,12},{24,16},{28,20},{9,25},{... | collective-permute-start | bytes 3538952 | tf_op jit(solution)/shard_map/ppermute | solution.py:505
  43.4 27.6 %collective-permute-start.2 = (bf16[768,768]{1,0:T(8,128)(2,1)S(1)}, bf16[768,768]{1,0:T(8,128)(2,1)S(1)}, u32[]{:S(2)}, u32[]{:S(2)}) collective-permute-start(bf16[768,768]{1,0:T(8,128)(2,1)S(1)} %collective-permute-done.refs_2_.refs_1_), channel_id=1, source_target_pairs={{0,1},{1,0},{2,3},{3,2},{4,5},{5,4},{6,7},{7,6},{8,9},{9,8},{10,11... | collective-permute-start | bytes 3538952 | tf_op jit(solution)/shard_map/ppermute | solution.py:472
  43.4 27.6 %collective-permute-start.6 = (bf16[768,768]{1,0:T(8,128)(2,1)S(1)}, bf16[768,768]{1,0:T(8,128)(2,1)S(1)}, u32[]{:S(2)}, u32[]{:S(2)}) collective-permute-start(bf16[768,768]{1,0:T(8,128)(2,1)S(1)} %collective-permute-done.5.refs_10_.refs_9_), channel_id=1, source_target_pairs={{0,1},{1,0},{2,3},{3,2},{4,5},{5,4},{6,7},{7,6},{8,9},{9,8},{10,11... | collective-permute-start | bytes 3538952 | tf_op jit(solution)/shard_map/ppermute | solution.py:472
  43.9 27.9 %collective-permute-start.1 = (bf16[768,768]{1,0:T(8,128)(2,1)S(1)}, bf16[768,768]{1,0:T(8,128)(2,1)S(1)}, u32[]{:S(2)}, u32[]{:S(2)}) collective-permute-start(bf16[768,768]{1,0:T(8,128)(2,1)S(1)} %collective-permute-done.refs_2_.refs_1_), channel_id=1, source_target_pairs={{0,2},{1,3},{2,0},{3,1},{4,6},{5,7},{6,4},{7,5},{8,10},{9,11},{10,... | collective-permute-start | bytes 3538952 | tf_op jit(solution)/shard_map/ppermute | solution.py:472
  60.1 44.1 %copy-start.6 = (bf16[768,768]{1,0:T(8,128)(2,1)}, bf16[768,768]{1,0:T(8,128)(2,1)S(1)}, u32[]{:S(2)}) copy-start(bf16[768,768]{1,0:T(8,128)(2,1)S(1)} %collective-permute-done.8.refs_6_.refs_5_) | copy-start | bytes 3538948
  60.1 26.5 %collective-permute-start.15 = (bf16[768,768]{1,0:T(8,128)(2,1)}, bf16[768,768]{1,0:T(8,128)(2,1)S(1)}, u32[]{:S(2)}, u32[]{:S(2)}) collective-permute-start(bf16[768,768]{1,0:T(8,128)(2,1)} %get-tuple-element.70), channel_id=1, source_target_pairs={{0,4},{4,0},{8,12},{12,8},{16,20},{20,16},{24,28},{28,24},{1,5},{5... | collective-permute-start | bytes 3538952 | tf_op jit(solution)/shard_map/ppermute | solution.py:469
  69.3 25.8 %collective-permute-start.14 = (bf16[768,768]{1,0:T(8,128)(2,1)}, bf16[768,768]{1,0:T(8,128)(2,1)S(1)}, u32[]{:S(2)}, u32[]{:S(2)}) collective-permute-start(bf16[768,768]{1,0:T(8,128)(2,1)} %get-tuple-element.68), channel_id=1, source_target_pairs={{8,0},{12,4},{16,24},{20,28},{0,16},{4,20},{24,8},{28,12},{9,1},{1... | collective-permute-start | bytes 3538952 | tf_op jit(solution)/shard_map/ppermute | solution.py:505
  71.0 34.8 %copy-start.7 = (bf16[768,768]{1,0:T(8,128)(2,1)}, bf16[768,768]{1,0:T(8,128)(2,1)S(1)}, u32[]{:S(2)}) copy-start(bf16[768,768]{1,0:T(8,128)(2,1)S(1)} %collective-permute-done.2.refs_4_.refs_3_) | copy-start | bytes 3538948
  71.0 34.8 %copy-start.14 = (bf16[768,768]{1,0:T(8,128)(2,1)}, bf16[768,768]{1,0:T(8,128)(2,1)S(1)}, u32[]{:S(2)}) copy-start(bf16[768,768]{1,0:T(8,128)(2,1)S(1)} %collective-permute-done.6.refs_12_.refs_11_) | copy-start | bytes 3538948
  71.8 28.6 %copy-start.8 = (bf16[768,768]{1,0:T(8,128)(2,1)}, bf16[768,768]{1,0:T(8,128)(2,1)S(1)}, u32[]{:S(2)}) copy-start(bf16[768,768]{1,0:T(8,128)(2,1)S(1)} %collective-permute-done.1.refs_3_.refs_2_) | copy-start | bytes 3538948
  71.8 27.0 %collective-permute-start.9 = (bf16[768,768]{1,0:T(8,128)(2,1)S(1)}, bf16[768,768]{1,0:T(8,128)(2,1)S(1)}, u32[]{:S(2)}, u32[]{:S(2)}) collective-permute-start(bf16[768,768]{1,0:T(8,128)(2,1)S(1)} %collective-permute-done.8.refs_6_.refs_5_), channel_id=1, source_target_pairs={{0,2},{1,3},{2,0},{3,1},{4,6},{5,7},{6,4},{7,5},{8,10},{9,11},{10,... | collective-permute-start | bytes 3538952 | tf_op jit(solution)/shard_map/ppermute | solution.py:472
  73.3 27.0 %collective-permute-start.10 = (bf16[768,768]{1,0:T(8,128)(2,1)S(1)}, bf16[768,768]{1,0:T(8,128)(2,1)S(1)}, u32[]{:S(2)}, u32[]{:S(2)}) collective-permute-start(bf16[768,768]{1,0:T(8,128)(2,1)S(1)} %collective-permute-done.8.refs_6_.refs_5_), channel_id=1, source_target_pairs={{0,1},{1,0},{2,3},{3,2},{4,5},{5,4},{6,7},{7,6},{8,9},{9,8},{10,11... | collective-permute-start | bytes 3538952 | tf_op jit(solution)/shard_map/ppermute | solution.py:472
  73.3 27.0 %collective-permute-start.7 = (bf16[768,768]{1,0:T(8,128)(2,1)S(1)}, bf16[768,768]{1,0:T(8,128)(2,1)S(1)}, u32[]{:S(2)}, u32[]{:S(2)}) collective-permute-start(bf16[768,768]{1,0:T(8,128)(2,1)S(1)} %collective-permute-done.1.refs_3_.refs_2_), channel_id=1, source_target_pairs={{0,1},{1,0},{2,3},{3,2},{4,5},{5,4},{6,7},{7,6},{8,9},{9,8},{10,11... | collective-permute-start | bytes 3538952 | tf_op jit(solution)/shard_map/ppermute | solution.py:472
  86.6 37.2 %copy-start.21 = (bf16[768,768]{1,0:T(8,128)(2,1)}, bf16[768,768]{1,0:T(8,128)(2,1)S(1)}, u32[]{:S(2)}) copy-start(bf16[768,768]{1,0:T(8,128)(2,1)S(1)} %collective-permute-done.15) | copy-start | bytes 3538948
  86.6 25.9 %collective-permute-start.17 = (bf16[768,768]{1,0:T(8,128)(2,1)S(1)}, bf16[768,768]{1,0:T(8,128)(2,1)}, u32[]{:S(2)}, u32[]{:S(2)}) collective-permute-start(bf16[768,768]{1,0:T(8,128)(2,1)S(1)} %collective-permute-done.5.refs_10_.refs_9_), channel_id=1, source_target_pairs={{0,4},{4,0},{8,12},{12,8},{16,20},{20,16},{24,28},{28,24},{1,5},{5... | collective-permute-start | bytes 3538952 | tf_op jit(solution)/shard_map/ppermute | solution.py:469
  95.1 28.8 %collective-permute-start.19 = (bf16[768,768]{1,0:T(8,128)(2,1)}, bf16[768,768]{1,0:T(8,128)(2,1)S(1)}, u32[]{:S(2)}, u32[]{:S(2)}) collective-permute-start(bf16[768,768]{1,0:T(8,128)(2,1)} %get-tuple-element.82), channel_id=1, source_target_pairs={{0,24},{4,28},{24,0},{28,4},{1,25},{5,29},{25,1},{29,5},{2,26},{6,... | collective-permute-start | bytes 3538952 | tf_op jit(solution)/shard_map/ppermute | solution.py:505
  98.8 7.0 %copy-start.9 = (bf16[768,768]{1,0:T(8,128)(2,1)}, bf16[768,768]{1,0:T(8,128)(2,1)S(1)}, u32[]{:S(2)}) copy-start(bf16[768,768]{1,0:T(8,128)(2,1)S(1)} %collective-permute-done.9.refs_7_.refs_6_) | copy-start | bytes 3538948
  98.8 26.9 %collective-permute-start.13 = (bf16[768,768]{1,0:T(8,128)(2,1)S(1)}, bf16[768,768]{1,0:T(8,128)(2,1)}, u32[]{:S(2)}, u32[]{:S(2)}) collective-permute-start(bf16[768,768]{1,0:T(8,128)(2,1)S(1)} %collective-permute-done.5.refs_10_.refs_9_), channel_id=1, source_target_pairs={{0,2},{1,3},{2,0},{3,1},{4,6},{5,7},{6,4},{7,5},{8,10},{9,11},{10,... | collective-permute-start | bytes 3538952 | tf_op jit(solution)/shard_map/ppermute | solution.py:472
  102.5 24.9 %collective-permute-start.12 = (bf16[768,768]{1,0:T(8,128)(2,1)S(1)}, bf16[768,768]{1,0:T(8,128)(2,1)S(1)}, u32[]{:S(2)}, u32[]{:S(2)}) collective-permute-start(bf16[768,768]{1,0:T(8,128)(2,1)S(1)} %collective-permute-done.9.refs_7_.refs_6_), channel_id=1, source_target_pairs={{0,1},{1,0},{2,3},{3,2},{4,5},{5,4},{6,7},{7,6},{8,9},{9,8},{10,11... | collective-permute-start | bytes 3538952 | tf_op jit(solution)/shard_map/ppermute | solution.py:472
  112.5 35.9 %collective-permute-start.23 = (bf16[768,768]{1,0:T(8,128)(2,1)}, bf16[768,768]{1,0:T(8,128)(2,1)}, u32[]{:S(2)}, u32[]{:S(2)}) collective-permute-start(bf16[768,768]{1,0:T(8,128)(2,1)} %get-tuple-element.81), channel_id=1, source_target_pairs={{0,4},{4,0},{8,12},{12,8},{16,20},{20,16},{24,28},{28,24},{1,5},{5... | collective-permute-start | bytes 3538952 | tf_op jit(solution)/shard_map/ppermute | solution.py:469
  123.8 25.3 %collective-permute-start.25 = (bf16[768,768]{1,0:T(8,128)(2,1)S(1)}, bf16[768,768]{1,0:T(8,128)(2,1)}, u32[]{:S(2)}, u32[]{:S(2)}) collective-permute-start(bf16[768,768]{1,0:T(8,128)(2,1)S(1)} %collective-permute-done.15), channel_id=1, source_target_pairs={{8,16},{12,20},{16,8},{20,12},{9,17},{13,21},{17,9},{21,13},{10,18... | collective-permute-start | bytes 3538952 | tf_op jit(solution)/shard_map/ppermute | solution.py:505
  125.7 24.2 %collective-permute-start.24 = (bf16[768,768]{1,0:T(8,128)(2,1)}, bf16[768,768]{1,0:T(8,128)(2,1)}, u32[]{:S(2)}, u32[]{:S(2)}) collective-permute-start(bf16[768,768]{1,0:T(8,128)(2,1)} %get-tuple-element.82), channel_id=1, source_target_pairs={{8,0},{12,4},{16,24},{20,28},{0,8},{4,12},{24,16},{28,20},{9,1},{1... | collective-permute-start | bytes 3538952 | tf_op jit(solution)/shard_map/ppermute | solution.py:505
  125.8 25.1 %collective-permute-start.18 = (bf16[768,768]{1,0:T(8,128)(2,1)}, bf16[768,768]{1,0:T(8,128)(2,1)S(1)}, u32[]{:S(2)}, u32[]{:S(2)}) collective-permute-start(bf16[768,768]{1,0:T(8,128)(2,1)} %collective-permute-done.17.refs_14_.refs_13_), channel_id=1, source_target_pairs={{0,2},{1,3},{2,0},{3,1},{4,6},{5,7},{6,4},{7,5},{8,10},{9,11},{10,... | collective-permute-start | bytes 3538952 | tf_op jit(solution)/shard_map/ppermute | solution.py:472
  128.4 23.8 %collective-permute-start.16 = (bf16[768,768]{1,0:T(8,128)(2,1)}, bf16[768,768]{1,0:T(8,128)(2,1)S(1)}, u32[]{:S(2)}, u32[]{:S(2)}) collective-permute-start(bf16[768,768]{1,0:T(8,128)(2,1)} %collective-permute-done.13.refs_11_.refs_10_), channel_id=1, source_target_pairs={{0,1},{1,0},{2,3},{3,2},{4,5},{5,4},{6,7},{7,6},{8,9},{9,8},{10,11... | collective-permute-start | bytes 3538952 | tf_op jit(solution)/shard_map/ppermute | solution.py:472
  148.5 29.8 %collective-permute-start.27 = (bf16[768,768]{1,0:T(8,128)(2,1)}, bf16[768,768]{1,0:T(8,128)(2,1)}, u32[]{:S(2)}, u32[]{:S(2)}) collective-permute-start(bf16[768,768]{1,0:T(8,128)(2,1)} %get-tuple-element.86.refs_1_.refs_17_), channel_id=1, source_target_pairs={{0,4},{4,0},{8,12},{12,8},{16,20},{20,16},{24,28},{28,24},{1,5},{5... | collective-permute-start | bytes 3538952 | tf_op jit(solution)/shard_map/ppermute | solution.py:469
  149.8 28.8 %collective-permute-start.26 = (bf16[768,768]{1,0:T(8,128)(2,1)}, bf16[768,768]{1,0:T(8,128)(2,1)}, u32[]{:S(2)}, u32[]{:S(2)}) collective-permute-start(bf16[768,768]{1,0:T(8,128)(2,1)} %collective-permute-done.23), channel_id=1, source_target_pairs={{8,24},{12,28},{16,0},{20,4},{0,8},{4,12},{24,16},{28,20},{9,25},{... | collective-permute-start | bytes 3538952 | tf_op jit(solution)/shard_map/ppermute | solution.py:505
  150.9 7.6 %copy-start.16 = (bf16[768,768]{1,0:T(8,128)(2,1)}, bf16[768,768]{1,0:T(8,128)(2,1)S(1)}, u32[]{:S(2)}) copy-start(bf16[768,768]{1,0:T(8,128)(2,1)S(1)} %collective-permute-done.18.refs_15_.refs_14_) | copy-start | bytes 3538948
  150.9 28.1 %collective-permute-start.22 = (bf16[768,768]{1,0:T(8,128)(2,1)}, bf16[768,768]{1,0:T(8,128)(2,1)}, u32[]{:S(2)}, u32[]{:S(2)}) collective-permute-start(bf16[768,768]{1,0:T(8,128)(2,1)} %get-tuple-element.86.refs_1_.refs_17_), channel_id=1, source_target_pairs={{0,2},{1,3},{2,0},{3,1},{4,6},{5,7},{6,4},{7,5},{8,10},{9,11},{10,... | collective-permute-start | bytes 3538952 | tf_op jit(solution)/shard_map/ppermute | solution.py:472
  152.2 6.3 %copy-start.15 = (bf16[768,768]{1,0:T(8,128)(2,1)}, bf16[768,768]{1,0:T(8,128)(2,1)S(1)}, u32[]{:S(2)}) copy-start(bf16[768,768]{1,0:T(8,128)(2,1)S(1)} %collective-permute-done.16.refs_13_.refs_12_) | copy-start | bytes 3538948
  152.2 26.9 %collective-permute-start.21 = (bf16[768,768]{1,0:T(8,128)(2,1)S(1)}, bf16[768,768]{1,0:T(8,128)(2,1)S(1)}, u32[]{:S(2)}, u32[]{:S(2)}) collective-permute-start(bf16[768,768]{1,0:T(8,128)(2,1)S(1)} %collective-permute-done.18.refs_15_.refs_14_), channel_id=1, source_target_pairs={{0,1},{1,0},{2,3},{3,2},{4,5},{5,4},{6,7},{7,6},{8,9},{9,8},{10,11... | collective-permute-start | bytes 3538952 | tf_op jit(solution)/shard_map/ppermute | solution.py:472
  152.2 26.9 %collective-permute-start.20 = (bf16[768,768]{1,0:T(8,128)(2,1)}, bf16[768,768]{1,0:T(8,128)(2,1)}, u32[]{:S(2)}, u32[]{:S(2)}) collective-permute-start(bf16[768,768]{1,0:T(8,128)(2,1)} %collective-permute-done.17.refs_14_.refs_13_), channel_id=1, source_target_pairs={{0,1},{1,0},{2,3},{3,2},{4,5},{5,4},{6,7},{7,6},{8,9},{9,8},{10,11... | collective-permute-start | bytes 3538952 | tf_op jit(solution)/shard_map/ppermute | solution.py:472
  179.0 27.6 %collective-permute-start.30 = (bf16[768,768]{1,0:T(8,128)(2,1)}, bf16[768,768]{1,0:T(8,128)(2,1)S(1)}, u32[]{:S(2)}, u32[]{:S(2)}) collective-permute-start(bf16[768,768]{1,0:T(8,128)(2,1)} %collective-permute-done.27.refs_5_.refs_21_), channel_id=1, source_target_pairs={{0,2},{1,3},{2,0},{3,1},{4,6},{5,7},{6,4},{7,5},{8,10},{9,11},{10,... | collective-permute-start | bytes 3538952 | tf_op jit(solution)/shard_map/ppermute | solution.py:472
  179.6 27.0 %collective-permute-start.31 = (bf16[768,768]{1,0:T(8,128)(2,1)}, bf16[768,768]{1,0:T(8,128)(2,1)S(1)}, u32[]{:S(2)}, u32[]{:S(2)}) collective-permute-start(bf16[768,768]{1,0:T(8,128)(2,1)} %collective-permute-done.27.refs_5_.refs_21_), channel_id=1, source_target_pairs={{0,1},{1,0},{2,3},{3,2},{4,5},{5,4},{6,7},{7,6},{8,9},{9,8},{10,11... | collective-permute-start | bytes 3538952 | tf_op jit(solution)/shard_map/ppermute | solution.py:472
  179.6 27.0 %collective-permute-start.29 = (bf16[768,768]{1,0:T(8,128)(2,1)}, bf16[768,768]{1,0:T(8,128)(2,1)}, u32[]{:S(2)}, u32[]{:S(2)}) collective-permute-start(bf16[768,768]{1,0:T(8,128)(2,1)} %collective-permute-done.22.refs_2_.refs_18_), channel_id=1, source_target_pairs={{0,1},{1,0},{2,3},{3,2},{4,5},{5,4},{6,7},{7,6},{8,9},{9,8},{10,11... | collective-permute-start | bytes 3538952 | tf_op jit(solution)/shard_map/ppermute | solution.py:472
  180.1 26.5 %collective-permute-start.28 = (bf16[768,768]{1,0:T(8,128)(2,1)}, bf16[768,768]{1,0:T(8,128)(2,1)}, u32[]{:S(2)}, u32[]{:S(2)}) collective-permute-start(bf16[768,768]{1,0:T(8,128)(2,1)} %get-tuple-element.86.refs_1_.refs_17_), channel_id=1, source_target_pairs={{0,1},{1,0},{2,3},{3,2},{4,5},{5,4},{6,7},{7,6},{8,9},{9,8},{10,11... | collective-permute-start | bytes 3538952 | tf_op jit(solution)/shard_map/ppermute | solution.py:472
  180.1 21.9 %collective-permute-start.32 = (bf16[768,512]{1,0:T(8,128)(2,1)}, bf16[768,512]{1,0:T(8,128)(2,1)}, u32[]{:S(2)}, u32[]{:S(2)}) collective-permute-start(bf16[768,512]{1,0:T(8,128)(2,1)} %slice.20), channel_id=1, source_target_pairs={{8,0},{12,4},{16,24},{20,28},{0,16},{4,20},{24,8},{28,12},{9,1},{1... | collective-permute-start | bytes 2359304 | tf_op jit(solution)/shard_map/ppermute | solution.py:505
  201.1 34.1 %copy-start.27 = (bf16[768,256]{1,0:T(8,128)(2,1)S(1)}, bf16[768,256]{1,0:T(8,128)(2,1)}, u32[]{:S(2)}) copy-start(bf16[768,256]{1,0:T(8,128)(2,1)} %slice.21) | copy-start | bytes 1179652
  206.6 4.6 %collective-permute-start.33 = (bf16[768,768]{1,0:T(8,128)(2,1)S(1)}, bf16[768,768]{1,0:T(8,128)(2,1)S(1)}, u32[]{:S(2)}, u32[]{:S(2)}) collective-permute-start(bf16[768,768]{1,0:T(8,128)(2,1)S(1)} %collective-permute-done.30.refs_6_.refs_22_), channel_id=1, source_target_pairs={{0,1},{1,0},{2,3},{3,2},{4,5},{5,4},{6,7},{7,6},{8,9},{9,8},{10,11... | collective-permute-start | bytes 3538952 | tf_op jit(solution)/shard_map/ppermute | solution.py:472
  206.7 23.9 %collective-permute-start.36 = (bf16[768,512]{1,0:T(8,128)(2,1)}, bf16[768,512]{1,0:T(8,128)(2,1)}, u32[]{:S(2)}, u32[]{:S(2)}) collective-permute-start(bf16[768,512]{1,0:T(8,128)(2,1)} %slice.22), channel_id=1, source_target_pairs={{0,24},{4,28},{24,0},{28,4},{1,25},{5,29},{25,1},{29,5},{2,26},{6,... | collective-permute-start | bytes 2359304 | tf_op jit(solution)/shard_map/ppermute | solution.py:505
  230.6 22.5 %collective-permute-start.35 = (bf16[768,256]{1,0:T(8,128)(2,1)}, bf16[768,256]{1,0:T(8,128)(2,1)S(1)}, u32[]{:S(2)}, u32[]{:S(2)}) collective-permute-start(bf16[768,256]{1,0:T(8,128)(2,1)} %slice.23), channel_id=1, source_target_pairs={{0,24},{4,28},{24,0},{28,4},{1,25},{5,29},{25,1},{29,5},{2,26},{6,... | collective-permute-start | bytes 1179656 | tf_op jit(solution)/shard_map/ppermute | solution.py:505
  235.2 18.7 %collective-permute-start.34 = (bf16[768,256]{1,0:T(8,128)(2,1)S(1)}, bf16[768,256]{1,0:T(8,128)(2,1)}, u32[]{:S(2)}, u32[]{:S(2)}) collective-permute-start(bf16[768,256]{1,0:T(8,128)(2,1)S(1)} %copy-done.27), channel_id=1, source_target_pairs={{8,0},{12,4},{16,24},{20,28},{0,16},{4,20},{24,8},{28,12},{9,1},{1... | collective-permute-start | bytes 1179656 | tf_op jit(solution)/shard_map/ppermute | solution.py:505
  251.4 12.0 %copy-start.2 = (f32[4,2,128,128]{3,2,1,0:T(8,128)S(1)}, f32[4,2,128,128]{3,2,1,0:T(8,128)}, u32[]{:S(2)}) copy-start(f32[4,2,128,128]{3,2,1,0:T(8,128)} %get-tuple-element.96.tails_ref) | copy-start | bytes 1572868
  251.4 12.0 %copy-start.3 = (s32[4]{0:T(128)S(1)}, s32[4]{0:T(128)}, u32[]{:S(2)}) copy-start(s32[4]{0:T(128)} %pad_add_fusion.where_ref) | copy-start | bytes 52
  251.4 12.0 %copy-start.4 = (s32[8,1]{0,1:T(1,128)S(1)}, s32[8,1]{0,1:T(1,128)}, u32[]{:S(2)}) copy-start(s32[8,1]{0,1:T(1,128)} %reduce-window.9) | copy-start | bytes 100
  251.4 12.0 %collective-permute-start.37 = (f32[2,128,128]{2,1,0:T(8,128)}, f32[2,128,128]{2,1,0:T(8,128)S(1)}, u32[]{:S(2)}, u32[]{:S(2)}) collective-permute-start(f32[2,128,128]{2,1,0:T(8,128)} %get-tuple-element.97), channel_id=1, source_target_pairs={{0,16},{4,20},{8,24},{12,28},{16,0},{20,4},{24,8},{28,12},{1,17},{... | collective-permute-start | bytes 393224 | tf_op jit(solution)/shard_map/ppermute | solution.py:469
  253.9 9.5 %copy-start = (bf16[3072,512]{1,0:T(8,128)(2,1)S(1)}, bf16[3072,512]{1,0:T(8,128)(2,1)}, u32[]{:S(2)}) copy-start(bf16[3072,512]{1,0:T(8,128)(2,1)} %get-tuple-element.95.kv_ref) | copy-start | bytes 9437188
  267.2 12.8 %collective-permute-start.38 = (bf16[768,256]{1,0:T(8,128)(2,1)S(1)}, bf16[768,256]{1,0:T(8,128)(2,1)S(1)}, u32[]{:S(2)}, u32[]{:S(2)}) collective-permute-start(bf16[768,256]{1,0:T(8,128)(2,1)S(1)} %get-tuple-element.98), channel_id=1, source_target_pairs={{0,12},{4,8},{8,4},{12,0},{16,28},{20,24},{24,20},{28,16},{1,13},{... | collective-permute-start | bytes 1179656 | tf_op jit(solution)/shard_map/ppermute | solution.py:469
  270.7 12.9 %collective-permute-start.42 = (f32[1,768]{1,0:T(1,128)S(1)}, f32[1,768]{1,0:T(1,128)S(1)}, u32[]{:S(2)}, u32[]{:S(2)}) collective-permute-start(f32[1,768]{1,0:T(1,128)S(1)} %get-tuple-element.104), channel_id=1, source_target_pairs={{0,8},{4,12},{8,0},{12,4},{16,24},{20,28},{24,16},{28,20},{1,9},{5... | collective-permute-start | bytes 9224 | tf_op jit(solution)/shard_map/ppermute | solution.py:469
  274.7 8.9 %collective-permute-start.43 = (f32[1,768]{1,0:T(1,128)S(1)}, f32[1,768]{1,0:T(1,128)S(1)}, u32[]{:S(2)}, u32[]{:S(2)}) collective-permute-start(f32[1,768]{1,0:T(1,128)S(1)} %get-tuple-element.105), channel_id=1, source_target_pairs={{0,4},{4,0},{8,12},{12,8},{16,20},{20,16},{24,28},{28,24},{1,5},{5... | collective-permute-start | bytes 9224 | tf_op jit(solution)/shard_map/ppermute | solution.py:469
  275.5 8.1 %collective-permute-start.41 = (f32[1,768]{1,0:T(1,128)S(1)}, f32[1,768]{1,0:T(1,128)S(1)}, u32[]{:S(2)}, u32[]{:S(2)}) collective-permute-start(f32[1,768]{1,0:T(1,128)S(1)} %get-tuple-element.103), channel_id=1, source_target_pairs={{0,12},{4,8},{8,4},{12,0},{16,28},{20,24},{24,20},{28,16},{1,13},{... | collective-permute-start | bytes 9224 | tf_op jit(solution)/shard_map/ppermute | solution.py:469
  276.6 11.3 %collective-permute-start.40 = (bf16[768,256]{1,0:T(8,128)(2,1)S(1)}, bf16[768,256]{1,0:T(8,128)(2,1)S(1)}, u32[]{:S(2)}, u32[]{:S(2)}) collective-permute-start(bf16[768,256]{1,0:T(8,128)(2,1)S(1)} %get-tuple-element.102), channel_id=1, source_target_pairs={{0,8},{4,12},{8,0},{12,4},{16,24},{20,28},{24,16},{28,20},{1,9},{5... | collective-permute-start | bytes 1179656 | tf_op jit(solution)/shard_map/ppermute | solution.py:469
  280.0 9.1 %collective-permute-start.39 = (bf16[768,256]{1,0:T(8,128)(2,1)S(1)}, bf16[768,256]{1,0:T(8,128)(2,1)S(1)}, u32[]{:S(2)}, u32[]{:S(2)}) collective-permute-start(bf16[768,256]{1,0:T(8,128)(2,1)S(1)} %get-tuple-element.101), channel_id=1, source_target_pairs={{0,4},{4,0},{8,12},{12,8},{16,20},{20,16},{24,28},{28,24},{1,5},{5... | collective-permute-start | bytes 1179656 | tf_op jit(solution)/shard_map/ppermute | solution.py:469
  283.6 2.0 collective-permute-start.44
  283.7 3.7 %collective-permute-start.45 = (f32[1,768]{1,0:T(1,128)S(1)}, f32[1,768]{1,0:T(1,128)S(1)}, u32[]{:S(2)}, u32[]{:S(2)}) collective-permute-start(f32[1,768]{1,0:T(1,128)S(1)} %add_add_fusion.1), channel_id=1, source_target_pairs={{0,2},{1,3},{2,0},{3,1},{4,6},{5,7},{6,4},{7,5},{8,10},{9,11},{10,... | collective-permute-start | bytes 9224 | tf_op jit(solution)/shard_map/ppermute | solution.py:472
  284.9 3.0 %collective-permute-start.46 = (f32[1,768]{1,0:T(1,128)S(1)}, f32[1,768]{1,0:T(1,128)S(1)}, u32[]{:S(2)}, u32[]{:S(2)}) collective-permute-start(f32[1,768]{1,0:T(1,128)S(1)} %add_add_fusion.1), channel_id=1, source_target_pairs={{0,3},{1,2},{2,1},{3,0},{4,7},{5,6},{6,5},{7,4},{8,11},{9,10},{10,... | collective-permute-start | bytes 9224 | tf_op jit(solution)/shard_map/ppermute | solution.py:472
  (14 other events, 39.4 us)
